TPU v7x, 32 devices: a whole 2x2x4 slice. The times are simulated.
32 devices in a mesh: state: 16 (over z, y, core), det: 2 (over x).
Axes of the slice: x: 2, y: 2, z: 4, core: 2. Of those that a mesh axis runs over, the one named last changes fastest.
Arguments:
- amplitudes: bfloat16 [64, 4096, 324], P('state', 'det'), may hold values from -0.09375 to 0.09375
Outputs:
- density_tiles: float32 [2, 256, 324, 324], P(None, ('state', 'det'))
All inputs are finite; a program needn't handle non-finite values.
Results may differ from a plain program's by a relative error of at most 0.0003.
Values may be sent and summed in bfloat16 or wider, within the bound.
No kernel may reach another device: no remote copies, remote signals or barrier semaphores. Data moves between devices by JAX's collectives and lax.ppermute only.
A program may use at most 128 MiB of HBM per device.

v0:
```python
import jax
import jax.numpy as jnp
from jax import lax
from jax.sharding import PartitionSpec as P


def partner_2(value, axis, stride):
    mask = 2**stride
    pairs = [(source, source ^ mask) for source in range(lax.axis_size(axis))]
    return lax.ppermute(value, axis, pairs)


def pair_terms(own_block, partner, count):
    operators = own_block.shape[2]
    terms = jnp.einsum("adp,bdq->abpq", own_block, partner, preferred_element_type=jnp.float32)
    return terms.reshape(count, operators, operators)


def on_device(amplitudes):
    blocks = lax.axis_size("state")
    far_bit = blocks.bit_length() - 2
    states = amplitudes.shape[0]
    owned = states * states // lax.axis_size("det")
    gathered = []
    for bit in (far_bit, 0):
        partner = partner_2(amplitudes, "state", bit)
        gathered.append(
            lax.psum_scatter(
                pair_terms(amplitudes, partner, owned * lax.axis_size("det")),
                "det",
                scatter_dimension=0,
                tiled=True,
            )
        )
    return jnp.stack(gathered)


def solution(mesh):
    placed = (P("state", "det", None),)
    return jax.shard_map(
        on_device,
        mesh=mesh,
        in_specs=placed,
        out_specs=P(None, ("state", "det"), None, None),
        check_vma=False,
    )
```

profile of v0, /device:TPU:0, one launch (start us, length us, event | category | flops | bytes accessed | tf_op | source)
XLA Modules:
  0.0 482.4 jit_solution(329127471639433035)
XLA Ops:
  6.5 0.0 reduce-scatter.3.cloned.1.call-start
  6.5 4.0 collective-permute-start
  10.6 228.4 %collective-permute-done = bf16[4,2048,324]{1,0,2:T(4,128)(2,1)S(1)} collective-permute-done((bf16[4,2048,324]{1,0,2:T(4,128)(2,1)}, bf16[4,2048,324]{1,0,2:T(4,128)(2,1)S(1)}, u32[]{:S(2)}, u32[]{:S(2)}) %collective-permute-start) | collective-permute-done | bytes 5308448 | tf_op jit(solution)/shard_map/ppermute | solution.py:10
  239.0 23.9 %fusion.8 = f32[4,4,324,324]{2,3,0,1:T(8,128)} fusion(bf16[4,2048,324]{1,0,2:T(4,128)(2,1)} %param.1, bf16[4,2048,324,1]{1,0,2,3:T(4,128)(2,1)S(1)} %bitcast.24), kind=kOutput, calls=%fused_computation.9 | convolution fusion | flops 6879707136 | bytes 17335296 | tf_op jit(solution)/shard_map/adp,bdq->abpq/dot_general | solution.py:15
  262.9 8.9 %copy.15 = f32[4,4,324,324]{3,2,1,0:T(8,128)} copy(f32[4,4,324,324]{2,3,0,1:T(8,128)} %fusion.8) | data formatting | bytes 13436928 | tf_op jit(solution)/shard_map/adp,bdq->abpq/transpose | solution.py:15
  271.8 0.0 reduce-scatter.3.cloned.1.call-update
  271.8 0.2 reduce-scatter.5.cloned.1.call-start
  272.0 0.1 collective-permute-start.1
  272.1 8.9 %collective-permute-done.1 = bf16[4,2048,324]{1,0,2:T(4,128)(2,1)S(1)} collective-permute-done((bf16[4,2048,324]{1,0,2:T(4,128)(2,1)}, bf16[4,2048,324]{1,0,2:T(4,128)(2,1)S(1)}, u32[]{:S(2)}, u32[]{:S(2)}) %collective-permute-start.1) | collective-permute-done | bytes 5308448 | tf_op jit(solution)/shard_map/ppermute | solution.py:10
  281.0 23.9 %fusion.13 = f32[4,4,324,324]{2,3,0,1:T(8,128)} fusion(bf16[4,2048,324]{1,0,2:T(4,128)(2,1)} %param.1, bf16[4,2048,324,1]{1,0,2,3:T(4,128)(2,1)S(1)} %bitcast.25), kind=kOutput, calls=%fused_computation.10 | convolution fusion | flops 6879707136 | bytes 17335296 | tf_op jit(solution)/shard_map/adp,bdq->abpq/dot_general | solution.py:15
  304.9 8.8 %copy.18 = f32[4,4,324,324]{3,2,1,0:T(8,128)} copy(f32[4,4,324,324]{2,3,0,1:T(8,128)} %fusion.13) | data formatting | bytes 13436928 | tf_op jit(solution)/shard_map/adp,bdq->abpq/transpose | solution.py:15
  313.8 0.0 reduce-scatter.5.cloned.1.call-update
  313.8 55.0 %reduce-scatter.3.cloned.1.call-done = f32[8,324,324]{2,1,0:T(8,128)} async-done(((f32[16,324,324]{2,1,0:T(8,128)}), f32[8,324,324]{2,1,0:T(8,128)}) %reduce-scatter.3.cloned.1.call-update) | async-done | bytes 3359248 | tf_op jit(solution)/shard_map/reduce_scatter | solution.py:28
  368.8 98.1 %reduce-scatter.5.cloned.1.call-done = f32[8,324,324]{2,1,0:T(8,128)} async-done(((f32[16,324,324]{2,1,0:T(8,128)}), f32[8,324,324]{2,1,0:T(8,128)}) %reduce-scatter.5.cloned.1.call-update) | async-done | bytes 3359248 | tf_op jit(solution)/shard_map/reduce_scatter | solution.py:28
  466.9 3.9 pad_maximum_fusion
  470.8 4.8 copy.19
Async XLA Ops:
  6.5 362.3 %reduce-scatter.3.cloned.1.call-start = ((), (), s32[]{:S(2)}) async-start(), calls=%async_computation.2 | async-start | bytes 12091392 | tf_op jit(solution)/shard_map/reduce_scatter | solution.py:28
  6.5 232.4 %collective-permute-start = (bf16[4,2048,324]{1,0,2:T(4,128)(2,1)}, bf16[4,2048,324]{1,0,2:T(4,128)(2,1)S(1)}, u32[]{:S(2)}, u32[]{:S(2)}) collective-permute-start(bf16[4,2048,324]{1,0,2:T(4,128)(2,1)} %param.1), channel_id=1, source_target_pairs={{0,16},{2,18},{4,20},{6,22},{8,24},{10,26},{12,28},{14,30},{16,0},... | collective-permute-start | bytes 15925256 | tf_op jit(solution)/shard_map/ppermute | solution.py:10
  271.8 195.1 %reduce-scatter.5.cloned.1.call-start = ((), (), s32[]{:S(2)}) async-start(), calls=%async_computation.3 | async-start | bytes 12091392 | tf_op jit(solution)/shard_map/reduce_scatter | solution.py:28
  272.0 9.0 %collective-permute-start.1 = (bf16[4,2048,324]{1,0,2:T(4,128)(2,1)}, bf16[4,2048,324]{1,0,2:T(4,128)(2,1)S(1)}, u32[]{:S(2)}, u32[]{:S(2)}) collective-permute-start(bf16[4,2048,324]{1,0,2:T(4,128)(2,1)} %param.1), channel_id=1, source_target_pairs={{0,2},{2,0},{4,6},{6,4},{8,10},{10,8},{12,14},{14,12},{16,18},{18,... | collective-permute-start | bytes 15925256 | tf_op jit(solution)/shard_map/ppermute | solution.py:10
Sparse Core Ops, SparseCore 0:
  271.9 96.8 reduce-scatter.2
  371.1 95.7 reduce-scatter.4
where the time goes:
time: 483 us; the launch traced here: 482 us
  waiting for transfers between devices  390 us (81%)
  matrix products  47.8 us (10%)
  local copies, waits for them, and re-layouts  22.5 us (5%)
  between operations  13.4 us (3%)
    ppermute x2, waiting for transfers between devices, partner_2(): return lax.ppermute(value, axis, pairs)  237 us
    reduce_scatter x2, waiting for transfers between devices, on_device(): lax.psum_scatter(pair_terms(amplitudes, partner, owned * lax.axis_size('d...  153 us
    dot_general x2, matrix products, pair_terms(): jnp.einsum('adp,bdq->abpq', own_block, partner, preferred_element_type=jn...  47.8 us
    transpose x2, local copies, waits for them, and re-layouts, pair_terms(): jnp.einsum('adp,bdq->abpq', own_block, partner, preferred_element_type=jn...  17.7 us
  transfers between devices with their start and end apart: 4, of which 4 were waited for; matrix products, arithmetic and copies ran while one was open for 7% of the time, Pallas kernels for 0%

commit v1 on v0

v1 whole, which is shorter than its diff:
```python
import functools

import jax
import jax.numpy as jnp
from jax import lax
from jax.experimental import pallas as pl
from jax.experimental.pallas import tpu as pltpu
from jax.sharding import PartitionSpec as P

LANES = 128
VMEM_LIMIT = 40 * 2**20
SQUARE_TOP = 2.0**13


def contract_last(left, right):
    return lax.dot_general(left, right, (((1,), (1,)), ((), ())), preferred_element_type=jnp.float32)


def call(body, grid, scalars, in_specs, out_specs, out_shape, flops, moved, aliases={}):
    return pl.pallas_call(
        body,
        grid_spec=pltpu.PrefetchScalarGridSpec(
            num_scalar_prefetch=scalars, grid=grid, in_specs=in_specs, out_specs=out_specs
        ),
        out_shape=out_shape,
        input_output_aliases=aliases,
        compiler_params=pltpu.CompilerParams(vmem_limit_bytes=VMEM_LIMIT),
        cost_estimate=pl.CostEstimate(flops=flops, bytes_accessed=moved, transcendentals=0),
    )


def f32(*shape):
    return jax.ShapeDtypeStruct(shape, jnp.float32)


def whole(shape):
    return pl.BlockSpec(shape, lambda *_: (0,) * len(shape))


def near_send(det, own, partner):
    states, ops, depth = own.shape
    half, wide = states // 2, ops // LANES * LANES

    def body(x_ref, own_ref, partner_ref, main_ref, rest_ref):
        main_ref[0] = contract_last(own_ref[0], partner_ref[0, :wide])
        rest_ref[0] = contract_last(partner_ref[0, wide:], own_ref[0])

    return call(
        body,
        (half, states),
        1,
        [
            pl.BlockSpec((1, ops, depth), lambda a, b, x: (half * (1 - x[0]) + a, 0, 0)),
            pl.BlockSpec((1, ops, depth), lambda a, b, x: (b, 0, 0)),
        ],
        [
            pl.BlockSpec((1, ops, wide), lambda a, b, x: (a * states + b, 0, 0)),
            pl.BlockSpec((1, ops - wide, ops), lambda a, b, x: (a * states + b, 0, 0)),
        ],
        [f32(half * states, ops, wide), f32(half * states, ops - wide, ops)],
        half * states * ops * ops * depth * 2,
        half * states * ops * (ops * 4 + depth * 2),
    )(det, own, partner)


def near_keep(det, own, partner):
    states, ops, depth = own.shape
    half = states // 2

    def body(x_ref, own_ref, partner_ref, tile_ref):
        tile_ref[0] = contract_last(own_ref[0], partner_ref[0])

    return call(
        body,
        (half, states),
        1,
        [
            pl.BlockSpec((1, ops, depth), lambda a, b, x: (half * x[0] + a, 0, 0)),
            pl.BlockSpec((1, ops, depth), lambda a, b, x: (b, 0, 0)),
        ],
        pl.BlockSpec((1, ops, ops), lambda a, b, x: (a * states + b, 0, 0)),
        f32(half * states, ops, ops),
        half * states * ops * ops * depth * 2,
        half * states * ops * (ops * 4 + depth * 2),
    )(det, own, partner)


def near_sum(keep, main, rest):
    tiles, ops, _ = keep.shape
    wide = main.shape[2]

    def body(keep_ref, main_ref, rest_ref, out_ref):
        out_ref[0, 0, :, :wide] = keep_ref[0, :, :wide] + main_ref[0]
        out_ref[0, 0, :, wide:] = keep_ref[0, :, wide:] + rest_ref[0].T

    return call(
        body,
        (tiles,),
        0,
        [
            pl.BlockSpec((1, ops, ops), lambda t: (t, 0, 0)),
            pl.BlockSpec((1, ops, wide), lambda t: (t, 0, 0)),
            pl.BlockSpec((1, ops - wide, ops), lambda t: (t, 0, 0)),
        ],
        pl.BlockSpec((1, 1, ops, ops), lambda t: (1, t, 0, 0)),
        f32(2, tiles, ops, ops),
        tiles * ops * ops,
        tiles * ops * ops * 12,
    )(keep, main, rest)


def far_terms(det, own, got, turned):
    states, ops, depth = own.shape
    half = states // 2
    width = got.size // (states * depth)
    tile = (ops, width) if turned else (width, ops)
    count = half * states + half * half

    def body(x_ref, own_ref, got_ref, send_ref, keep_ref):
        x, step = x_ref[0], pl.program_id(0)
        v = (step + half * x) % states
        if turned:
            def terms(first):
                block = got_ref[pl.ds(first, half)].reshape(half * width, depth)
                both = contract_last(own_ref[0], block)
                return [both[:, a * width : (a + 1) * width] for a in range(half)]

            other, mine = terms(half * (1 - x)), terms(half * x)
        else:
            every = contract_last(got_ref[...], own_ref[0])
            parts = [every[u * width : (u + 1) * width] for u in range(states)]
            low, high = parts[:half], parts[half:]
            other = [jnp.where(x == 0, q, p) for p, q in zip(low, high)]
            mine = [jnp.where(x == 0, p, q) for p, q in zip(low, high)]
        for a in range(half):
            send_ref[a * states + v] = other[a]
            keep_ref[a * states + v] = mine[a]

        @pl.when(step < half)
        def _():
            for a in range(half):
                keep_ref[half * states + step * half + a] = other[a]

        @pl.when(step >= half)
        def _():
            for a in range(half):
                send_ref[half * states + (step - half) * half + a] = mine[a]

    return call(
        body,
        (states,),
        1,
        [
            pl.BlockSpec((1, ops, depth), lambda g, x: ((g + half * x[0]) % states, 0, 0)),
            whole(got.shape),
        ],
        [whole((count, *tile))] * 2,
        [f32(count, *tile)] * 2,
        states * states * ops * width * depth * 2,
        states * ops * depth * 2 + got.size * 2 + 2 * count * ops * width * 4,
    )(det, own, got)


def far_sum(det, keep, came, states):
    count, rows, lanes = keep.shape
    half = states // 2
    back = half * states
    under = rows + 8 - rows % 8

    def body(x_ref, keep_ref, came_ref, back_ref, own_ref):
        x = x_ref[0]
        top = jnp.zeros((rows, lanes), jnp.float32)
        for t in range(back):
            tile = keep_ref[t] + came_ref[t]
            back_ref[t, :rows] = tile
            top = jnp.maximum(top, jnp.abs(tile))
        back_ref[0, rows:] = jnp.broadcast_to(jnp.max(top, keepdims=True), (under - rows, lanes))
        for b in range(half):
            for a in range(half):
                own_ref[b * states + half * x + a] = back_ref[a * states + half * x + b, :rows]
                t = back + b * half + a
                own_ref[b * states + half * (1 - x) + a] = keep_ref[t] + came_ref[t]

    return call(
        body,
        (1,),
        1,
        [whole((count, rows, lanes))] * 2,
        [whole((back, under, lanes)), whole((back, rows, lanes))],
        [f32(back, under, lanes), f32(back, rows, lanes)],
        2 * count * rows * lanes,
        (2 * count + 2 * back) * rows * lanes * 4,
    )(det, keep, came)


def squared(sums, rows):
    exponent = jnp.floor(jnp.log2(jnp.maximum(sums[0, rows, 0], 2.0**-120)))
    scaled = sums * jnp.exp2(-exponent)
    row = lax.broadcasted_iota(jnp.int32, sums.shape, 1)
    return jnp.where(row < rows, scaled * jnp.abs(scaled) * SQUARE_TOP, exponent).astype(jnp.float16)


def rooted(code, rows):
    exponent = code[0, rows, 0].astype(jnp.float32)
    values = code[:, :rows].astype(jnp.float32)
    root = jnp.sqrt(jnp.abs(values)) * (jnp.exp2(exponent) * SQUARE_TOP**-0.5)
    return jnp.where(values < 0, -root, root)


def place(receiver, out, owned, came):
    _, tiles, ops, _ = out.shape
    full = len(came)
    wide = full * LANES

    def body(role_ref, out_in, *refs):
        owned_refs, came_refs, out_ref = refs[: full + 1], refs[full:-1][1:], refs[-1]

        @pl.when(role_ref[0] == 1)
        def _():
            for k in range(full):
                out_ref[0, 0, :, k * LANES : (k + 1) * LANES] = owned_refs[k][0]
            out_ref[0, 0, :, wide:] = owned_refs[full][0].T

        @pl.when(role_ref[0] == 0)
        def _():
            for k in range(full):
                out_ref[0, 0, k * LANES : (k + 1) * LANES, :] = came_refs[k][0].T

    turned = pl.BlockSpec((1, ops, LANES), lambda t, r: (t, 0, 0))
    return call(
        body,
        (tiles,),
        1,
        [pl.BlockSpec(memory_space=pl.ANY)]
        + [turned] * full
        + [pl.BlockSpec((1, ops - wide, ops), lambda t, r: (t, 0, 0))]
        + [turned] * full,
        pl.BlockSpec((1, 1, ops, ops), lambda t, r: (0, t, 0, 0)),
        f32(*out.shape),
        tiles * ops * ops,
        tiles * ops * ops * 12,
        {1: 0},
    )(receiver, out, *owned, *came)


def paired(amplitudes):
    blocks = lax.axis_size("state")
    far = blocks.bit_length() - 2
    states, depth, ops = amplitudes.shape
    half, full = states // 2, ops // LANES
    wide = full * LANES
    both = ("state", "det")
    senders = [s for s in range(blocks) if (s & 1) == (s >> far & 1)]
    receivers = [s for s in range(blocks) if s not in senders]
    over = [(2 * s + x, 2 * (s ^ 1 << far) + x) for s in senders for x in range(2)]
    back = [(b, a) for a, b in over]
    across = [(2 * s + x, 2 * s + 1 - x) for s in receivers for x in range(2)]

    state = lax.axis_index("state")
    det = lax.axis_index("det").astype(jnp.int32)[None]
    receiver = ((state & 1) ^ (state >> far & 1)).astype(jnp.int32)[None]

    own = jnp.transpose(amplitudes, (0, 2, 1))
    chunks = [own[:, k * LANES : (k + 1) * LANES] for k in range(full)]
    chunks.append(own[:, wide:].reshape(states * (ops - wide), depth))
    got = [lax.ppermute(c, both, over) for c in chunks]

    partner = lax.ppermute(own, "state", [(s, s ^ 1) for s in range(blocks)])
    main, rest = near_send(det, own, partner)
    main, rest = (lax.ppermute(v, "det", [(0, 1), (1, 0)]) for v in (main, rest))
    keep = near_keep(det, own, partner)

    returned, owned = [], []
    for k, block in enumerate(got):
        send, kept = far_terms(det, own, block, k < full)
        came = lax.ppermute(send, both, across)
        sums, mine = far_sum(det, kept, came, states)
        rows = kept.shape[1]
        returned.append(rooted(lax.ppermute(squared(sums, rows), both, back), rows))
        owned.append(mine)

    out = near_sum(keep, main, rest)
    out = place(receiver, out, owned, returned[:full])
    last = jnp.where(receiver[0] == 1, out[0, :, wide:], returned[full])
    return lax.dynamic_update_slice(out, last[None], (0, 0, wide, 0))


def partner_2(value, axis, stride):
    mask = 2**stride
    pairs = [(source, source ^ mask) for source in range(lax.axis_size(axis))]
    return lax.ppermute(value, axis, pairs)


def pair_terms(own_block, partner, count):
    operators = own_block.shape[2]
    terms = jnp.einsum("adp,bdq->abpq", own_block, partner, preferred_element_type=jnp.float32)
    return terms.reshape(count, operators, operators)


def exchanged(amplitudes):
    blocks = lax.axis_size("state")
    far_bit = blocks.bit_length() - 2
    states = amplitudes.shape[0]
    gathered = []
    for bit in (far_bit, 0):
        partner = partner_2(amplitudes, "state", bit)
        terms = pair_terms(amplitudes, partner, states * states)
        gathered.append(lax.psum_scatter(terms, "det", scatter_dimension=0, tiled=True))
    return jnp.stack(gathered)


def on_device(amplitudes):
    states, _, ops = amplitudes.shape
    two = lax.axis_size("det") == 2 and lax.axis_size("state") >= 4
    if two and states % 2 == 0 and ops > LANES and ops % LANES % 8:
        return paired(amplitudes)
    return exchanged(amplitudes)


def solution(mesh):
    return jax.shard_map(
        on_device,
        mesh=mesh,
        in_specs=(P("state", "det", None),),
        out_specs=P(None, ("state", "det"), None, None),
        check_vma=False,
    )
```

time: 483 us -> 288 us (0.60)
  the two profiles are of different devices: /device:TPU:0 before, /device:TPU:1 now
where the time goes in v1:
time: 288 us; the launch traced here: 287 us
  waiting for transfers between devices  152 us (53%)
  local copies, waits for them, and re-layouts  54.4 us (19%)
  Pallas kernels  49.4 us (17%)
  starting transfers between devices  19.1 us (7%)
  other arithmetic  8.14 us (3%)
  between operations  4.37 us (2%)
    ppermute x3, waiting for transfers between devices, paired(): got = [lax.ppermute(c, both, over) for c in chunks]  94.7 us
    ppermute x3, waiting for transfers between devices, paired(): came = lax.ppermute(send, both, across)  47.5 us
    unnamed x41, local copies, waits for them, and re-layouts  16.8 us
    pallas_call x3, Pallas kernels, far_terms(): call(body, (states,), 1, [pl.BlockSpec((1, ops, depth), lambda g, x: ((g...  16.2 us
    pallas_call x1, Pallas kernels, near_keep(): call(body, (half, states), 1, [pl.BlockSpec((1, ops, depth), lambda a, b,...  10.1 us
    ppermute x3, starting transfers between devices, paired(): came = lax.ppermute(send, both, across)  9.45 us
    ppermute x3, waiting for transfers between devices, paired(): returned.append(rooted(lax.ppermute(squared(sums, rows), both, back), rows))  9.35 us
    dynamic_update_slice x1, local copies, waits for them, and re-layouts, paired(): return lax.dynamic_update_slice(out, last[None], (0, 0, wide, 0))  8.08 us
  transfers between devices with their start and end apart: 12, of which 6 were waited for; matrix products, arithmetic and copies ran while one was open for 9% of the time, Pallas kernels for 15%

profile of v1, /device:TPU:1, one launch (start us, length us, event | category | flops | bytes accessed | tf_op | source)
XLA Modules:
  0.0 287.1 jit_solution(10145607696624530341)
XLA Ops:
  0.0 5.4 %copy.17 = bf16[4,2048,324]{1,2,0:T(8,128)(2,1)S(1)} copy(bf16[4,2048,324]{1,0,2:T(4,128)(2,1)} %param.1) | data formatting | bytes 10616832 | tf_op args[0]
  5.4 0.0 copy-start
  5.4 6.5 %copy.8 = bf16[4,324,2048]{2,0,1:T(4,128)(2,1)} copy(bf16[4,324,2048]{2,1,0:T(8,128)(2,1)S(1)} %bitcast.17) | data formatting | bytes 10616832 | tf_op jit(solution)/shard_map/transpose | solution.py:263
  11.9 0.1 collective-permute-start
  11.9 2.4 fusion.18
  14.3 1.3 collective-permute-start.5
  15.6 1.3 collective-permute-start.3
  16.9 83.0 %collective-permute-done.5.got_ref = bf16[4,128,2048]{2,1,0:T(8,128)(2,1)} collective-permute-done((bf16[4,128,2048]{2,1,0:T(8,128)(2,1)}, bf16[4,128,2048]{2,1,0:T(8,128)(2,1)}, u32[]{:S(2)}, u32[]{:S(2)}) %collective-permute-start.5) | collective-permute-done | bytes 2097184 | tf_op jit(solution)/shard_map/ppermute | solution.py:266
  99.9 2.5 copy-done.1
  102.5 6.8 %shard_map.22 = (f32[12,324,128]{2,1,0:T(8,128)}, f32[12,324,128]{2,1,0:T(8,128)S(1)}) custom-call(s32[1]{0:T(128)} %bitcast.1.x_ref, bf16[4,324,2048]{2,1,0:T(8,128)(2,1)S(1)} %bitcast.19, bf16[4,128,2048]{2,1,0:T(8,128)(2,1)} %collective-permute-done.5.got_ref), custom_call_target="tpu_custom_call" | custom-call | flops 2717908992 | bytes 11386880 | tf_op jit(solution)/shard_map/pallas_call | solution.py:149
  109.2 3.8 %collective-permute-start.6 = (f32[12,324,128]{2,1,0:T(8,128)}, f32[12,324,128]{2,1,0:T(8,128)}, u32[]{:S(2)}, u32[]{:S(2)}) collective-permute-start(f32[12,324,128]{2,1,0:T(8,128)} %get-tuple-element.25), channel_id=1, source_target_pairs={{2,3},{3,2},{6,7},{7,6},{10,11},{11,10},{14,15},{15,14},{16,17},{1... | collective-permute-start | bytes 5971976 | tf_op jit(solution)/shard_map/ppermute | solution.py:276
  113.0 9.3 %collective-permute-done.3.got_ref = bf16[4,128,2048]{2,1,0:T(8,128)(2,1)S(1)} collective-permute-done((bf16[4,128,2048]{2,1,0:T(8,128)(2,1)}, bf16[4,128,2048]{2,1,0:T(8,128)(2,1)S(1)}, u32[]{:S(2)}, u32[]{:S(2)}) %collective-permute-start.3) | collective-permute-done | bytes 2097184 | tf_op jit(solution)/shard_map/ppermute | solution.py:266
  122.3 1.4 copy-done.14
  123.7 1.6 copy-done.15
  125.3 5.1 %shard_map.20 = (f32[12,324,128]{2,1,0:T(8,128)}, f32[12,324,128]{2,1,0:T(8,128)S(1)}) custom-call(s32[1]{0:T(128)} %bitcast.1.x_ref, bf16[4,324,2048]{2,1,0:T(8,128)(2,1)S(1)} %bitcast.20, bf16[4,128,2048]{2,1,0:T(8,128)(2,1)S(1)} %copy-done.15), custom_call_target="tpu_custom_call" | custom-call | flops 2717908992 | bytes 11386880 | tf_op jit(solution)/shard_map/pallas_call | solution.py:149
  130.4 3.8 %collective-permute-start.4 = (f32[12,324,128]{2,1,0:T(8,128)}, f32[12,324,128]{2,1,0:T(8,128)}, u32[]{:S(2)}, u32[]{:S(2)}) collective-permute-start(f32[12,324,128]{2,1,0:T(8,128)} %get-tuple-element.22), channel_id=1, source_target_pairs={{2,3},{3,2},{6,7},{7,6},{10,11},{11,10},{14,15},{15,14},{16,17},{1... | collective-permute-start | bytes 5971976 | tf_op jit(solution)/shard_map/ppermute | solution.py:276
  134.1 1.2 slice.54
  135.4 2.3 reshape.39
  137.6 1.7 collective-permute-start.7
  139.4 0.0 collective-permute-done
  139.4 5.4 %copy.9.partner_ref = bf16[4,324,2048]{2,1,0:T(8,128)(2,1)S(1)} copy(bf16[4,324,2048]{2,0,1:T(4,128)(2,1)} %collective-permute-done) | data formatting | bytes 10616832 | tf_op jit(solution)/shard_map/ppermute | solution.py:268
  144.8 7.4 %shard_map.18 = (f32[8,324,256]{2,1,0:T(8,128)S(1)}, f32[8,68,324]{2,1,0:T(8,128)S(1)}) custom-call(s32[1]{0:T(128)} %bitcast.1.x_ref, bf16[4,324,2048]{2,1,0:T(8,128)(2,1)S(1)} %bitcast.24, bf16[4,324,2048]{2,1,0:T(8,128)(2,1)S(1)} %copy.9.partner_ref), custom_call_target="tpu_custom_call" | custom-call | flops 3439853568 | bytes 13976064 | tf_op jit(solution)/shard_map/pallas_call | solution.py:48
  152.3 2.3 copy.11
  154.6 0.0 collective-permute-start.1
  154.6 2.4 collective-permute-done.7.got_ref
  157.0 4.3 %shard_map.24 = (f32[12,68,324]{2,1,0:T(8,128)}, f32[12,68,324]{2,1,0:T(8,128)S(1)}) custom-call(s32[1]{0:T(128)} %bitcast.1.x_ref, bf16[4,324,2048]{2,1,0:T(8,128)(2,1)S(1)} %bitcast.25, bf16[272,2048]{1,0:T(8,128)(2,1)S(1)} %collective-permute-done.7.got_ref), custom_call_target="tpu_custom_call" | custom-call | flops 1443889152 | bytes 8537600 | tf_op jit(solution)/shard_map/pallas_call | solution.py:149
  161.3 1.1 copy-done.10
  162.4 1.9 collective-permute-start.8
  164.3 0.0 collective-permute-done.6.came_ref
  164.3 3.2 %shard_map.23 = (f32[8,328,128]{2,1,0:T(8,128)}, f32[8,324,128]{2,1,0:T(8,128)S(1)}) custom-call(s32[1]{0:T(128)} %bitcast.1.x_ref, f32[12,324,128]{2,1,0:T(8,128)S(1)} %copy-done.5, f32[12,324,128]{2,1,0:T(8,128)} %collective-permute-done.6.came_ref), custom_call_target="tpu_custom_call" | custom-call | flops 995328 | bytes 6635520 | tf_op jit(solution)/shard_map/pallas_call | solution.py:184
  167.5 1.1 copy-done.6
  168.6 1.2 slice.45
  170.5 10.7 %collective-permute-done.4.came_ref = f32[12,324,128]{2,1,0:T(8,128)} collective-permute-done((f32[12,324,128]{2,1,0:T(8,128)}, f32[12,324,128]{2,1,0:T(8,128)}, u32[]{:S(2)}, u32[]{:S(2)}) %collective-permute-start.4) | collective-permute-done | bytes 1990688 | tf_op jit(solution)/shard_map/ppermute | solution.py:276
  181.1 3.1 %shard_map.21 = (f32[8,328,128]{2,1,0:T(8,128)}, f32[8,324,128]{2,1,0:T(8,128)S(1)}) custom-call(s32[1]{0:T(128)} %bitcast.1.x_ref, f32[12,324,128]{2,1,0:T(8,128)S(1)} %get-tuple-element.21.keep_ref, f32[12,324,128]{2,1,0:T(8,128)} %collective-permute-done.4.came_ref), custom_call_target="tpu_custom_call" | custom-call | flops 995328 | bytes 6635520 | tf_op jit(solution)/shard_map/pallas_call | solution.py:184
  184.2 1.1 copy-done.8
  185.3 1.2 slice.42
  187.2 3.6 %fusion.9 = (f16[8,328,128]{2,1,0:T(8,128)(2,1)}, f16[8,328,128]{2,1,0:T(8,128)(2,1)}) fusion(f32[8,328,128]{2,1,0:T(8,128)} %get-tuple-element.31, f32[]{:T(128)} %bitcast.5, f32[]{:T(128)S(6)} %exp2.47, pred[328]{0:T(512)(128)(4,1)S(1)} %iota_compare_fusion, f32[]{:T(128)} %bitcast.3, f32[8,328,128]{2,1,0:T(8,128)} %get-tuple-element.30, f32[]{:T(128)S(6)} %exp2.43), kind=kLoop, calls=%fused_computation.18 | loop fusion | flops 4030464 | bytes 4030808 | tf_op jit(solution)/shard_map/convert_element_type | solution.py:200
  190.7 1.3 collective-permute-start.9
  192.1 36.9 %collective-permute-done.8.came_ref = f32[12,68,324]{2,1,0:T(8,128)} collective-permute-done((f32[12,68,324]{2,1,0:T(8,128)}, f32[12,68,324]{2,1,0:T(8,128)}, u32[]{:S(2)}, u32[]{:S(2)}) %collective-permute-start.8) | collective-permute-done | bytes 1057568 | tf_op jit(solution)/shard_map/ppermute | solution.py:276
  229.0 1.7 shard_map.25
  230.7 0.6 slice.49
  232.0 2.2 collective-permute-start.10
  234.1 1.0 fusion.14
  235.1 1.5 collective-permute-start.11
  236.7 9.3 %collective-permute-done.11 = f16[8,72,324]{2,1,0:T(8,128)(2,1)S(1)} collective-permute-done((f16[8,72,324]{2,1,0:T(8,128)(2,1)}, f16[8,72,324]{2,1,0:T(8,128)(2,1)S(1)}, u32[]{:S(2)}, u32[]{:S(2)}) %collective-permute-start.11) | collective-permute-done | bytes 373280 | tf_op jit(solution)/shard_map/ppermute | solution.py:279
  246.0 0.6 slice.61
  247.4 0.5 slice.56
  248.6 0.2 copy.12
  248.8 0.3 collective-permute-start.2
  249.1 0.6 negate_select_fusion.1.refs_3_
  249.7 1.2 slice.58
  251.5 1.7 negate_select_fusion.refs_4_
  253.1 0.0 copy-start.2
  253.1 2.5 copy-done.2
  255.7 10.1 %shard_map.17.keep_ref = f32[8,324,324]{2,1,0:T(8,128)S(1)} custom-call(s32[1]{0:T(128)} %bitcast.1.x_ref, bf16[4,324,2048]{2,1,0:T(8,128)(2,1)S(1)} %bitcast.26, bf16[4,324,2048]{2,1,0:T(8,128)(2,1)} %copy-done.3), custom_call_target="tpu_custom_call" | custom-call | flops 3439853568 | bytes 13976064 | tf_op jit(solution)/shard_map/pallas_call | solution.py:73
  265.8 0.0 collective-permute-done.2
  265.8 0.2 copy.14.rest_ref
  265.9 0.0 collective-permute-done.1
  265.9 2.6 copy.13.main_ref
  268.6 4.0 %shard_map.19.out_in = f32[2,8,324,324]{3,2,1,0:T(8,128)} custom-call(f32[8,324,324]{2,1,0:T(8,128)S(1)} %shard_map.17.keep_ref, f32[8,324,256]{2,1,0:T(8,128)S(1)} %copy.13.main_ref, f32[8,68,324]{2,1,0:T(8,128)S(1)} %copy.14.rest_ref), custom_call_target="tpu_custom_call" | custom-call | flops 839808 | bytes 10077696 | tf_op jit(solution)/shard_map/pallas_call | solution.py:96
  272.5 3.8 %shard_map.26 = f32[2,8,324,324]{3,2,1,0:T(8,128)} custom-call(s32[1]{0:T(128)} %bitcast.role_ref, f32[2,8,324,324]{3,2,1,0:T(8,128)} %shard_map.19.out_in, f32[8,324,128]{2,1,0:T(8,128)S(1)} %copy-done.9, f32[8,324,128]{2,1,0:T(8,128)S(1)} %copy-done.7, f32[8,68,324]{2,1,0:T(8,128)S(1)} %get-tuple-element.29.refs_2_, ...), custom_call_target="tpu_custom_call", output_to_operand_aliasing={{}: (1, {})} | custom-call | flops 839808 | bytes 10077696 | tf_op jit(solution)/shard_map/pallas_call | solution.py:230
  276.3 1.3 slice_bitcast_fusion
  277.6 1.3 fusion.17
  279.0 8.1 %copy.15 = f32[2,8,324,324]{3,1,2,0:T(8,128)} copy(f32[2,8,324,324]{3,2,1,0:T(8,128)} %fusion.17) | data formatting | bytes 13436928 | tf_op jit(solution)/shard_map/dynamic_update_slice | solution.py:285
  (36 shorter events, 0.1 us)
Async XLA Ops:
  5.4 6.5 %copy-start = (bf16[4,2048,324]{1,2,0:T(8,128)(2,1)}, bf16[4,2048,324]{1,2,0:T(8,128)(2,1)S(1)}, u32[]{:S(2)}) copy-start(bf16[4,2048,324]{1,2,0:T(8,128)(2,1)S(1)} %copy.17) | copy-start | bytes 15925252
  11.9 127.5 %collective-permute-start = (bf16[4,324,2048]{2,0,1:T(4,128)(2,1)}, bf16[4,324,2048]{2,0,1:T(4,128)(2,1)}, u32[]{:S(2)}, u32[]{:S(2)}) collective-permute-start(bf16[4,324,2048]{2,0,1:T(4,128)(2,1)} %copy.8), channel_id=1, source_target_pairs={{0,2},{2,0},{4,6},{6,4},{8,10},{10,8},{12,14},{14,12},{16,18},{18,... | collective-permute-start | bytes 15925256 | tf_op jit(solution)/shard_map/ppermute | solution.py:268
  14.3 85.6 %collective-permute-start.5 = (bf16[4,128,2048]{2,1,0:T(8,128)(2,1)}, bf16[4,128,2048]{2,1,0:T(8,128)(2,1)}, u32[]{:S(2)}, u32[]{:S(2)}) collective-permute-start(bf16[4,128,2048]{2,1,0:T(8,128)(2,1)} %get-tuple-element.33), channel_id=1, source_target_pairs={{0,16},{1,17},{4,20},{5,21},{8,24},{9,25},{12,28},{13,29},{18,2},{... | collective-permute-start | bytes 6291464 | tf_op jit(solution)/shard_map/ppermute | solution.py:266
  15.6 106.7 %collective-permute-start.3 = (bf16[4,128,2048]{2,1,0:T(8,128)(2,1)}, bf16[4,128,2048]{2,1,0:T(8,128)(2,1)S(1)}, u32[]{:S(2)}, u32[]{:S(2)}) collective-permute-start(bf16[4,128,2048]{2,1,0:T(8,128)(2,1)} %get-tuple-element.34), channel_id=1, source_target_pairs={{0,16},{1,17},{4,20},{5,21},{8,24},{9,25},{12,28},{13,29},{18,2},{... | collective-permute-start | bytes 6291464 | tf_op jit(solution)/shard_map/ppermute | solution.py:266
  99.9 2.5 copy-start.1
  109.2 21.1 %copy-start.4 = (f32[12,324,128]{2,1,0:T(8,128)}, f32[12,324,128]{2,1,0:T(8,128)S(1)}, u32[]{:S(2)}) copy-start(f32[12,324,128]{2,1,0:T(8,128)S(1)} %get-tuple-element.24.keep_ref) | copy-start | bytes 5971972
  109.2 55.1 %collective-permute-start.6 = (f32[12,324,128]{2,1,0:T(8,128)}, f32[12,324,128]{2,1,0:T(8,128)}, u32[]{:S(2)}, u32[]{:S(2)}) collective-permute-start(f32[12,324,128]{2,1,0:T(8,128)} %get-tuple-element.25), channel_id=1, source_target_pairs={{2,3},{3,2},{6,7},{7,6},{10,11},{11,10},{14,15},{15,14},{16,17},{1... | collective-permute-start | bytes 5971976 | tf_op jit(solution)/shard_map/ppermute | solution.py:276
  122.3 1.4 copy-start.14
  123.7 1.6 copy-start.15
  130.4 50.7 %collective-permute-start.4 = (f32[12,324,128]{2,1,0:T(8,128)}, f32[12,324,128]{2,1,0:T(8,128)}, u32[]{:S(2)}, u32[]{:S(2)}) collective-permute-start(f32[12,324,128]{2,1,0:T(8,128)} %get-tuple-element.22), channel_id=1, source_target_pairs={{2,3},{3,2},{6,7},{7,6},{10,11},{11,10},{14,15},{15,14},{16,17},{1... | collective-permute-start | bytes 5971976 | tf_op jit(solution)/shard_map/ppermute | solution.py:276
  135.4 9.4 %slice-start = ((s8[5373952]{0:T(1024)(128)(4,1)}), s8[1179648]{0:T(1024)(128)(4,1)S(1)}, s32[]{:S(2)}) async-start(s8[5373952]{0:T(1024)(128)(4,1)} %bitcast.22), calls=%async_computation | async-start | bytes 2359296
  137.6 7.2 %slice-start.1 = ((s8[5373952]{0:T(1024)(128)(4,1)}), s8[4194304]{0:T(1024)(128)(4,1)S(1)}, s32[]{:S(2)}) async-start(s8[5373952]{0:T(1024)(128)(4,1)} %bitcast.22), calls=%async_computation.1 | async-start | bytes 8388608
  137.6 19.3 %collective-permute-start.7 = (bf16[272,2048]{1,0:T(8,128)(2,1)}, bf16[272,2048]{1,0:T(8,128)(2,1)S(1)}, u32[]{:S(2)}, u32[]{:S(2)}) collective-permute-start(bf16[272,2048]{1,0:T(8,128)(2,1)} %reshape.39), channel_id=1, source_target_pairs={{0,16},{1,17},{4,20},{5,21},{8,24},{9,25},{12,28},{13,29},{18,2},{... | collective-permute-start | bytes 3342344 | tf_op jit(solution)/shard_map/ppermute | solution.py:266
  144.8 7.4 %copy-start.3 = (bf16[4,324,2048]{2,1,0:T(8,128)(2,1)}, bf16[4,324,2048]{2,1,0:T(8,128)(2,1)S(1)}, u32[]{:S(2)}) copy-start(bf16[4,324,2048]{2,1,0:T(8,128)(2,1)S(1)} %copy.9.partner_ref) | copy-start | bytes 15925252
  152.3 2.3 copy-start.12
  154.6 111.3 %collective-permute-start.1 = (f32[8,324,256]{2,0,1:T(8,128)}, f32[8,324,256]{2,0,1:T(8,128)}, u32[]{:S(2)}, u32[]{:S(2)}) collective-permute-start(f32[8,324,256]{2,0,1:T(8,128)} %copy.11), channel_id=1, source_target_pairs={{0,1},{1,0},{2,3},{3,2},{4,5},{5,4},{6,7},{7,6},{8,9},{9,8},{10,11... | collective-permute-start | bytes 7962632 | tf_op jit(solution)/shard_map/ppermute | solution.py:270
  157.0 7.3 %copy-start.5 = (f32[12,324,128]{2,1,0:T(8,128)S(1)}, f32[12,324,128]{2,1,0:T(8,128)}, u32[]{:S(2)}) copy-start(f32[12,324,128]{2,1,0:T(8,128)} %copy-done.4) | copy-start | bytes 5971972
  161.3 1.1 copy-start.10
  162.4 66.6 %collective-permute-start.8 = (f32[12,68,324]{2,1,0:T(8,128)}, f32[12,68,324]{2,1,0:T(8,128)}, u32[]{:S(2)}, u32[]{:S(2)}) collective-permute-start(f32[12,68,324]{2,1,0:T(8,128)} %get-tuple-element.28), channel_id=1, source_target_pairs={{2,3},{3,2},{6,7},{7,6},{10,11},{11,10},{14,15},{15,14},{16,17},{1... | collective-permute-start | bytes 3172616 | tf_op jit(solution)/shard_map/ppermute | solution.py:276
  167.5 1.1 copy-start.6
  184.2 1.1 copy-start.8
  187.2 41.8 %copy-start.11 = (f32[12,68,324]{2,1,0:T(8,128)S(1)}, f32[12,68,324]{2,1,0:T(8,128)}, u32[]{:S(2)}) copy-start(f32[12,68,324]{2,1,0:T(8,128)} %copy-done.10) | copy-start | bytes 3172612
  190.7 56.6 %collective-permute-start.9 = (f16[8,328,128]{2,1,0:T(8,128)(2,1)}, f16[8,328,128]{2,1,0:T(8,128)(2,1)S(1)}, u32[]{:S(2)}, u32[]{:S(2)}) collective-permute-start(f16[8,328,128]{2,1,0:T(8,128)(2,1)} %get-tuple-element.36), channel_id=1, source_target_pairs={{16,0},{17,1},{20,4},{21,5},{24,8},{25,9},{28,12},{29,13},{2,18},{... | collective-permute-start | bytes 2015240 | tf_op jit(solution)/shard_map/ppermute | solution.py:279
  230.7 18.0 %copy-start.13 = (f32[8,68,324]{2,1,0:T(8,128)S(1)}, f32[8,68,324]{2,1,0:T(8,128)}, u32[]{:S(2)}) copy-start(f32[8,68,324]{2,1,0:T(8,128)} %copy-done.12) | copy-start | bytes 2115076
  232.0 17.7 %collective-permute-start.10 = (f16[8,328,128]{2,1,0:T(8,128)(2,1)}, f16[8,328,128]{2,1,0:T(8,128)(2,1)}, u32[]{:S(2)}, u32[]{:S(2)}) collective-permute-start(f16[8,328,128]{2,1,0:T(8,128)(2,1)} %get-tuple-element.35), channel_id=1, source_target_pairs={{16,0},{17,1},{20,4},{21,5},{24,8},{25,9},{28,12},{29,13},{2,18},{... | collective-permute-start | bytes 2015240 | tf_op jit(solution)/shard_map/ppermute | solution.py:279
  235.1 10.9 %collective-permute-start.11 = (f16[8,72,324]{2,1,0:T(8,128)(2,1)}, f16[8,72,324]{2,1,0:T(8,128)(2,1)S(1)}, u32[]{:S(2)}, u32[]{:S(2)}) collective-permute-start(f16[8,72,324]{2,1,0:T(8,128)(2,1)} %fusion.14), channel_id=1, source_target_pairs={{16,0},{17,1},{20,4},{21,5},{24,8},{25,9},{28,12},{29,13},{2,18},{... | collective-permute-start | bytes 1119752 | tf_op jit(solution)/shard_map/ppermute | solution.py:279
  246.0 2.6 copy-start.16
  248.8 17.0 %collective-permute-start.2 = (f32[8,68,324]{2,0,1:T(8,128)S(1)}, f32[8,68,324]{2,0,1:T(8,128)S(1)}, u32[]{:S(2)}, u32[]{:S(2)}) collective-permute-start(f32[8,68,324]{2,0,1:T(8,128)S(1)} %copy.12), channel_id=1, source_target_pairs={{0,1},{1,0},{2,3},{3,2},{4,5},{5,4},{6,7},{7,6},{8,9},{9,8},{10,11... | collective-permute-start | bytes 2115080 | tf_op jit(solution)/shard_map/ppermute | solution.py:270
  253.1 2.5 copy-start.2
  268.6 4.0 %copy-start.7 = (f32[8,324,128]{2,1,0:T(8,128)S(1)}, f32[8,324,128]{2,1,0:T(8,128)}, u32[]{:S(2)}) copy-start(f32[8,324,128]{2,1,0:T(8,128)} %copy-done.6) | copy-start | bytes 3981316
  268.6 4.0 %copy-start.9 = (f32[8,324,128]{2,1,0:T(8,128)S(1)}, f32[8,324,128]{2,1,0:T(8,128)}, u32[]{:S(2)}) copy-start(f32[8,324,128]{2,1,0:T(8,128)} %copy-done.8) | copy-start | bytes 3981316
  276.3 1.3 copy-start.17

commit v2 on v1

v2 whole, which is shorter than its diff:
```python
import functools

import jax
import jax.numpy as jnp
from jax import lax
from jax.experimental import pallas as pl
from jax.experimental.pallas import tpu as pltpu
from jax.sharding import PartitionSpec as P

LANES = 128
VMEM_LIMIT = 40 * 2**20
SQUARE_TOP = 2.0**13
SHORT, LONG = 10**3, 10**10


def contract_last(left, right):
    return lax.dot_general(left, right, (((1,), (1,)), ((), ())), preferred_element_type=jnp.float32)


def call(body, grid, scalars, in_specs, out_specs, out_shape, declared, aliases={}):
    return pl.pallas_call(
        body,
        grid_spec=pltpu.PrefetchScalarGridSpec(
            num_scalar_prefetch=scalars, grid=grid, in_specs=in_specs, out_specs=out_specs
        ),
        out_shape=out_shape,
        input_output_aliases=aliases,
        compiler_params=pltpu.CompilerParams(vmem_limit_bytes=VMEM_LIMIT),
        cost_estimate=pl.CostEstimate(flops=declared, bytes_accessed=declared // 100, transcendentals=0),
    )


def f32(*shape):
    return jax.ShapeDtypeStruct(shape, jnp.float32)


def up(size, unit):
    return -(-size // unit) * unit


def after(value, *done):
    return lax.optimization_barrier((value, *done))[0]


def whole(shape):
    return pl.BlockSpec(shape, lambda *_: (0,) * len(shape))


def near_send(det, own, partner):
    states, ops, depth = own.shape
    half, wide = states // 2, ops // LANES * LANES
    rest, lanes = ops - wide, up(ops, LANES)

    def body(x_ref, own_ref, partner_ref, main_ref, rest_ref):
        main_ref[0, :ops] = contract_last(own_ref[0], partner_ref[0, :wide])
        rest_ref[0, :rest, :ops] = contract_last(partner_ref[0, wide:], own_ref[0])

    shapes = [(up(ops, 8), wide), (up(rest, 8), lanes)]
    return call(
        body,
        (half, states),
        1,
        [
            pl.BlockSpec((1, ops, depth), lambda a, b, x: (half * (1 - x[0]) + a, 0, 0)),
            pl.BlockSpec((1, ops, depth), lambda a, b, x: (b, 0, 0)),
        ],
        [pl.BlockSpec((1, *s), lambda a, b, x: (a * states + b, 0, 0)) for s in shapes],
        [f32(half * states, *s) for s in shapes],
        SHORT,
    )(det, own, partner)


def near_keep(det, own, partner):
    states, ops, depth = own.shape
    half = states // 2

    def body(x_ref, own_ref, partner_ref, tile_ref):
        tile_ref[0] = contract_last(own_ref[0], partner_ref[0])

    return call(
        body,
        (half, states),
        1,
        [
            pl.BlockSpec((1, ops, depth), lambda a, b, x: (half * x[0] + a, 0, 0)),
            pl.BlockSpec((1, ops, depth), lambda a, b, x: (b, 0, 0)),
        ],
        pl.BlockSpec((1, ops, ops), lambda a, b, x: (a * states + b, 0, 0)),
        f32(half * states, ops, ops),
        SHORT,
    )(det, own, partner)


def near_sum(keep, main, rest):
    tiles, ops, _ = keep.shape
    wide = main.shape[2]

    def body(keep_ref, main_ref, rest_ref, out_ref):
        for t in range(tiles):
            out_ref[0, :, t, :wide] = keep_ref[t, :, :wide] + main_ref[t]
            out_ref[0, :, t, wide:] = keep_ref[t, :, wide:] + rest_ref[t].T[:, : ops - wide]

    return call(
        body,
        (pl.cdiv(ops, LANES),),
        0,
        [
            pl.BlockSpec((tiles, LANES, ops), lambda i: (0, i, 0)),
            pl.BlockSpec((tiles, LANES, wide), lambda i: (0, i, 0)),
            pl.BlockSpec((tiles, rest.shape[1], LANES), lambda i: (0, 0, i)),
        ],
        pl.BlockSpec((1, LANES, tiles, ops), lambda i: (1, i, 0, 0)),
        f32(2, ops, tiles, ops),
        LONG,
    )(keep, main, rest)


def far_terms(det, own, got, turned):
    states, ops, depth = own.shape
    half = states // 2
    width = got.size // (states * depth)
    tile = (ops, width) if turned else (width, ops)
    count = half * states + half * half

    def body(x_ref, own_ref, got_ref, send_ref, keep_ref):
        x, step = x_ref[0], pl.program_id(0)
        v = (step + half * x) % states
        if turned:
            def terms(first):
                block = got_ref[pl.ds(first, half)].reshape(half * width, depth)
                both = contract_last(own_ref[0], block)
                return [both[:, a * width : (a + 1) * width] for a in range(half)]

            other, mine = terms(half * (1 - x)), terms(half * x)
        else:
            every = contract_last(got_ref[...], own_ref[0])
            parts = [every[u * width : (u + 1) * width] for u in range(states)]
            low, high = parts[:half], parts[half:]
            other = [jnp.where(x == 0, q, p) for p, q in zip(low, high)]
            mine = [jnp.where(x == 0, p, q) for p, q in zip(low, high)]
        for a in range(half):
            send_ref[a * states + v] = other[a]
            keep_ref[a * states + v] = mine[a]

        @pl.when(step < half)
        def _():
            for a in range(half):
                keep_ref[half * states + step * half + a] = other[a]

        @pl.when(step >= half)
        def _():
            for a in range(half):
                send_ref[half * states + (step - half) * half + a] = mine[a]

    return call(
        body,
        (states,),
        1,
        [
            pl.BlockSpec((1, ops, depth), lambda g, x: ((g + half * x[0]) % states, 0, 0)),
            whole(got.shape),
        ],
        [whole((count, *tile))] * 2,
        [f32(count, *tile)] * 2,
        SHORT,
    )(det, own, got)


def far_sum(det, keep, came, states, turned):
    count, rows, lanes = keep.shape
    half = states // 2
    back = half * states
    shape = (back, up(rows + 1, 16), lanes) if turned else (rows + 1, back, lanes)

    def body(x_ref, keep_ref, came_ref, back_ref, own_ref):
        x = x_ref[0]
        top = jnp.zeros((rows, lanes), jnp.float32)
        for a in range(half):
            for v in range(states):
                t = a * states + v
                tile = keep_ref[t] + came_ref[t]
                if turned:
                    back_ref[t, :rows] = tile
                else:
                    back_ref[:rows, t] = tile
                top = jnp.maximum(top, jnp.abs(tile))

                @pl.when(v // half == x)
                def _():
                    own_ref[v % half * states + half * x + a] = tile

        top = jnp.max(top, keepdims=True)
        if turned:
            back_ref[0, rows:] = jnp.broadcast_to(top, (shape[1] - rows, lanes))
        else:
            back_ref[rows] = jnp.broadcast_to(top, (back, lanes))
        for b in range(half):
            for a in range(half):
                t = back + b * half + a
                own_ref[b * states + half * (1 - x) + a] = keep_ref[t] + came_ref[t]

    return call(
        body,
        (1,),
        1,
        [whole((count, rows, lanes))] * 2,
        [whole(shape), whole((back, rows, lanes))],
        [f32(*shape), f32(back, rows, lanes)],
        LONG,
    )(det, keep, came)


def squared(sums, axis, rows):
    largest = sums[0, rows, 0] if axis else sums[rows, 0, 0]
    exponent = jnp.floor(jnp.log2(jnp.maximum(largest, 2.0**-120)))
    scaled = sums * jnp.exp2(-exponent)
    row = lax.broadcasted_iota(jnp.int32, sums.shape, axis)
    return jnp.where(row < rows, scaled * jnp.abs(scaled) * SQUARE_TOP, exponent).astype(jnp.float16)


def rooted(code, axis, rows):
    exponent = (code[0, rows, 0] if axis else code[rows, 0, 0]).astype(jnp.float32)
    values = lax.slice_in_dim(code, 0, rows, axis=axis).astype(jnp.float32)
    root = jnp.sqrt(jnp.abs(values)) * (jnp.exp2(exponent) * SQUARE_TOP**-0.5)
    return jnp.where(values < 0, -root, root)


def place(receiver, out, owned, came):
    _, ops, tiles, _ = out.shape
    full = len(came)
    wide = full * LANES

    def body(role_ref, out_in, *refs):
        owned_refs, came_refs, out_ref = refs[: full + 1], refs[full + 1 : -1], refs[-1]

        @pl.when(role_ref[0] == 1)
        def _():
            for t in range(tiles):
                for k in range(full):
                    out_ref[0, :, t, k * LANES : (k + 1) * LANES] = owned_refs[k][t]
                out_ref[0, :, t, wide:] = owned_refs[full][t].T

        for k in range(full):

            @pl.when((role_ref[0] == 0) & (pl.program_id(0) == k))
            def _():
                for t in range(tiles):
                    out_ref[0, :, t] = came_refs[k][t].T

    return call(
        body,
        (pl.cdiv(ops, LANES),),
        1,
        [pl.BlockSpec(memory_space=pl.ANY)]
        + [pl.BlockSpec((tiles, LANES, LANES), lambda i, r: (0, i, 0))] * full
        + [pl.BlockSpec((tiles, ops - wide, LANES), lambda i, r: (0, 0, i))]
        + [whole((tiles, ops, LANES))] * full,
        pl.BlockSpec((1, LANES, tiles, ops), lambda i, r: (0, i, 0, 0)),
        f32(*out.shape),
        LONG,
        {1: 0},
    )(receiver, out, *owned, *came)


def finish(receiver, out, last):
    _, ops, tiles, _ = out.shape
    rest = last.shape[0]

    def body(role_ref, out_in, last_ref, out_ref, sem):
        @pl.when(role_ref[0] == 0)
        def _():
            copy = pltpu.make_async_copy(last_ref, out_ref.at[0, pl.ds(ops - rest, rest)], sem)
            copy.start()
            copy.wait()

    return pl.pallas_call(
        body,
        in_specs=[pl.BlockSpec(memory_space=pltpu.SMEM)] + [pl.BlockSpec(memory_space=pl.ANY)] * 2,
        out_specs=pl.BlockSpec(memory_space=pl.ANY),
        out_shape=f32(*out.shape),
        input_output_aliases={1: 0},
        scratch_shapes=[pltpu.SemaphoreType.DMA],
        cost_estimate=pl.CostEstimate(flops=0, bytes_accessed=SHORT, transcendentals=0),
    )(receiver, out, last)


def paired(amplitudes):
    blocks = lax.axis_size("state")
    far = blocks.bit_length() - 2
    states, depth, ops = amplitudes.shape
    full = ops // LANES
    wide = full * LANES
    both = ("state", "det")
    senders = [s for s in range(blocks) if (s & 1) == (s >> far & 1)]
    receivers = [s for s in range(blocks) if s not in senders]
    over = [(2 * s + x, 2 * (s ^ 1 << far) + x) for s in senders for x in range(2)]
    back = [(b, a) for a, b in over]
    across = [(2 * s + x, 2 * s + 1 - x) for s in receivers for x in range(2)]

    state = lax.axis_index("state")
    det = lax.axis_index("det").astype(jnp.int32)[None]
    receiver = ((state & 1) ^ (state >> far & 1)).astype(jnp.int32)[None]

    partner = lax.ppermute(amplitudes, "state", [(s, s ^ 1) for s in range(blocks)])
    chunks, seen = [], amplitudes
    for k in range(full + 1):
        chunk = seen[:, :, k * LANES : (k + 1) * LANES].transpose(0, 2, 1)
        if k == full:
            chunk = chunk.reshape(states * (ops - wide), depth)
        seen = after(amplitudes, chunk)
        chunks.append(chunk)
    got = [lax.ppermute(c, both, over) for c in chunks]

    own = seen.transpose(0, 2, 1)
    partner = after(partner, own).transpose(0, 2, 1)
    main, rest = near_send(det, own, partner)
    keep = near_keep(after(det, main), own, partner)
    main, rest = (lax.ppermute(v, "det", [(0, 1), (1, 0)]) for v in (main, rest))

    def terms(k, done):
        send, kept = far_terms(after(det, done), own, got[k], k < full)
        return lax.ppermute(send, both, across), kept

    def sums(k, pair, done):
        came, kept = pair
        axis, rows = int(k < full), kept.shape[1]
        home, mine = far_sum(after(det, done), kept, came, states, k < full)
        sent = squared(home, axis, rows)
        return sent, mine, lax.ppermute(sent, both, back), axis, rows

    pairs, done = [], keep
    for k in range(full + 1):
        pairs.append(terms(k, done))
        done = pairs[k][1]
    out = near_sum(after(keep, done), main, rest)
    done, codes = out, []
    for k in range(full + 1):
        codes.append(sums(k, pairs[k], done))
        done = codes[k][0]

    returned = [rooted(*c[2:]) for c in codes[:full]]
    out = place(after(receiver, done), out, [c[1] for c in codes], returned)
    out = finish(receiver, out, rooted(after(codes[full][2], out), *codes[full][3:]))
    return out.transpose(0, 2, 1, 3)


def partner_2(value, axis, stride):
    mask = 2**stride
    pairs = [(source, source ^ mask) for source in range(lax.axis_size(axis))]
    return lax.ppermute(value, axis, pairs)


def pair_terms(own_block, partner, count):
    operators = own_block.shape[2]
    terms = jnp.einsum("adp,bdq->abpq", own_block, partner, preferred_element_type=jnp.float32)
    return terms.reshape(count, operators, operators)


def exchanged(amplitudes):
    blocks = lax.axis_size("state")
    far_bit = blocks.bit_length() - 2
    states = amplitudes.shape[0]
    gathered = []
    for bit in (far_bit, 0):
        partner = partner_2(amplitudes, "state", bit)
        terms = pair_terms(amplitudes, partner, states * states)
        gathered.append(lax.psum_scatter(terms, "det", scatter_dimension=0, tiled=True))
    return jnp.stack(gathered)


def on_device(amplitudes):
    states, _, ops = amplitudes.shape
    two = lax.axis_size("det") == 2 and lax.axis_size("state") >= 4
    if two and states % 2 == 0 and ops > LANES and ops % LANES % 8:
        return paired(amplitudes)
    return exchanged(amplitudes)


def solution(mesh):
    return jax.shard_map(
        on_device,
        mesh=mesh,
        in_specs=(P("state", "det", None),),
        out_specs=P(None, ("state", "det"), None, None),
        check_vma=False,
    )
```

time: 288 us -> 230 us (0.80)
  the two profiles are of different devices: /device:TPU:1 before, /device:TPU:0 now
where the time goes in v2:
time: 230 us; the launch traced here: 229 us
  waiting for transfers between devices  81.3 us (35%)
  Pallas kernels  77.1 us (34%)
  local copies, waits for them, and re-layouts  37.6 us (16%)
  starting transfers between devices  22 us (10%)
  other arithmetic  6.23 us (3%)
  between operations  4.59 us (2%)
    ppermute x3, waiting for transfers between devices, sums(): return (sent, mine, lax.ppermute(sent, both, back), axis, rows)  56.5 us
    pallas_call x1, Pallas kernels, finish(): pl.pallas_call(body, in_specs=[pl.BlockSpec(memory_space=pltpu.SMEM)] + [...  26.4 us
    ppermute x2, waiting for transfers between devices, paired(): lax.ppermute(v, 'det', [(0, 1), (1, 0)])  21.8 us
    pallas_call x3, Pallas kernels, far_terms(): call(body, (states,), 1, [pl.BlockSpec((1, ops, depth), lambda g, x: ((g...  17.6 us
    optimization_barrier x3, local copies, waits for them, and re-layouts, after(): return lax.optimization_barrier((value, *done))[0]  16.3 us
    unnamed x39, local copies, waits for them, and re-layouts  10.7 us
    pallas_call x1, Pallas kernels, near_keep(): call(body, (half, states), 1, [pl.BlockSpec((1, ops, depth), lambda a, b,...  10.1 us
    ppermute x3, starting transfers between devices, paired(): got = [lax.ppermute(c, both, over) for c in chunks]  9.78 us
  transfers between devices with their start and end apart: 12, of which 4 were waited for; matrix products, arithmetic and copies ran while one was open for 15% of the time, Pallas kernels for 22%

profile of v2, /device:TPU:0, one launch (start us, length us, event | category | flops | bytes accessed | tf_op | source)
XLA Modules:
  0.0 228.8 jit_solution(3182757540922293795)
XLA Ops:
  0.0 0.5 collective-permute-start
  0.5 2.8 %slice.36 = bf16[4,2048,128]{1,0,2:T(4,128)(2,1)S(1)} slice(bf16[4,2048,324]{1,0,2:T(4,128)(2,1)} %param.1), slice={[0:4], [0:2048], [0:128]} | slice | bytes 4194304 | tf_op jit(solution)/shard_map/slice | solution.py:307
  3.2 2.5 %copy.25 = bf16[4,2048,128]{1,2,0:T(8,128)(2,1)} copy(bf16[4,2048,128]{1,0,2:T(4,128)(2,1)S(1)} %slice.36) | data formatting | bytes 4194304
  5.7 6.8 %collective-permute-start.1 = (bf16[4,128,2048]{2,1,0:T(8,128)(2,1)}, bf16[4,128,2048]{2,1,0:T(8,128)(2,1)}, u32[]{:S(2)}, u32[]{:S(2)}) collective-permute-start(bf16[4,128,2048]{2,1,0:T(8,128)(2,1)} %bitcast.21), channel_id=1, source_target_pairs={{0,16},{1,17},{4,20},{5,21},{8,24},{9,25},{12,28},{13,29},{18,2},{... | collective-permute-start | bytes 6291464 | tf_op jit(solution)/shard_map/ppermute | solution.py:312
  12.5 0.0 copy-done.16
  12.5 2.9 %copy.15 = bf16[4,2048,324]{1,2,0:T(8,128)(2,1)S(1)} copy(bf16[4,2048,324]{1,0,2:T(4,128)(2,1)S(1)} %copy-done.16) | data formatting | bytes 10616832 | tf_op jit(solution)/shard_map/optimization_barrier | solution.py:42
  15.4 1.7 slice_bitcast_fusion
  17.1 0.5 slice_bitcast_fusion.1
  17.6 0.6 copy.16
  18.2 1.2 reshape.39
  19.4 7.8 %copy.24 = bf16[4,2048,324]{1,2,0:T(8,128)(2,1)} copy(bf16[4,2048,324]{1,0,2:T(4,128)(2,1)} %param.1) | data formatting | bytes 10616832 | tf_op jit(solution)/shard_map/optimization_barrier | solution.py:42
  27.2 0.0 collective-permute-done
  27.2 5.6 %copy.23 = bf16[4,2048,324]{1,2,0:T(8,128)(2,1)S(1)} copy(bf16[4,2048,324]{1,0,2:T(4,128)(2,1)} %collective-permute-done) | data formatting | bytes 10616832 | tf_op jit(solution)/shard_map/optimization_barrier | solution.py:42
  32.8 0.0 copy-start.1
  32.8 8.6 %shard_map.17 = (f32[8,328,256]{2,1,0:T(8,128)}, f32[8,72,384]{2,1,0:T(8,128)}) custom-call(s32[1]{0:T(128)} %bitcast.1.x_ref, bf16[4,324,2048]{2,1,0:T(8,128)(2,1)S(1)} %bitcast.24, bf16[4,324,2048]{2,1,0:T(8,128)(2,1)S(1)} %bitcast.29), custom_call_target="tpu_custom_call" | custom-call | flops 1000 | bytes 10 | tf_op jit(solution)/shard_map/pallas_call | solution.py:59
  41.4 1.5 collective-permute-start.4
  42.9 1.4 collective-permute-start.2
  44.3 1.6 collective-permute-start.3
  45.9 10.1 %shard_map.18.keep_ref = f32[8,324,324]{2,1,0:T(8,128)S(1)} custom-call(s32[1]{0:T(128)} %bitcast.1.x_ref, bf16[4,324,2048]{2,1,0:T(8,128)(2,1)S(1)} %bitcast.25, bf16[4,324,2048]{2,1,0:T(8,128)(2,1)} %bitcast.30), custom_call_target="tpu_custom_call" | custom-call | flops 1000 | bytes 10 | tf_op jit(solution)/shard_map/pallas_call | solution.py:80
  56.0 0.0 collective-permute-done.1.got_ref
  56.0 8.1 %shard_map.19 = (f32[12,324,128]{2,1,0:T(8,128)}, f32[12,324,128]{2,1,0:T(8,128)S(1)}) custom-call(s32[1]{0:T(128)} %bitcast.1.x_ref, bf16[4,324,2048]{2,1,0:T(8,128)(2,1)S(1)} %bitcast.26, bf16[4,128,2048]{2,1,0:T(8,128)(2,1)} %collective-permute-done.1.got_ref), custom_call_target="tpu_custom_call" | custom-call | flops 1000 | bytes 10 | tf_op jit(solution)/shard_map/pallas_call | solution.py:155
  64.1 1.3 copy-done.4
  65.4 2.0 collective-permute-start.6
  67.4 0.5 collective-permute-start.5
  68.0 0.1 collective-permute-done.2.got_ref
  68.1 2.5 %copy-done = bf16[4,2048,324]{1,2,0:T(8,128)(2,1)S(1)} copy-done((bf16[4,2048,324]{1,2,0:T(8,128)(2,1)S(1)}, bf16[4,2048,324]{1,2,0:T(8,128)(2,1)}, u32[]{:S(2)}) %copy-start) | copy-done | bytes 5308440
  70.6 5.2 %shard_map.20 = (f32[12,324,128]{2,1,0:T(8,128)}, f32[12,324,128]{2,1,0:T(8,128)S(1)}) custom-call(s32[1]{0:T(128)} %bitcast.1.x_ref, bf16[4,324,2048]{2,1,0:T(8,128)(2,1)S(1)} %bitcast.27, bf16[4,128,2048]{2,1,0:T(8,128)(2,1)S(1)} %collective-permute-done.2.got_ref), custom_call_target="tpu_custom_call" | custom-call | flops 1000 | bytes 10 | tf_op jit(solution)/shard_map/pallas_call | solution.py:155
  75.8 1.3 copy-done.6
  77.0 3.0 %collective-permute-done.3.got_ref = bf16[272,2048]{1,0:T(8,128)(2,1)S(1)} collective-permute-done((bf16[272,2048]{1,0:T(8,128)(2,1)}, bf16[272,2048]{1,0:T(8,128)(2,1)S(1)}, u32[]{:S(2)}, u32[]{:S(2)}) %collective-permute-start.3) | collective-permute-done | bytes 1114144 | tf_op jit(solution)/shard_map/ppermute | solution.py:312
  80.0 4.3 %shard_map.21 = (f32[12,68,324]{2,1,0:T(8,128)}, f32[12,68,324]{2,1,0:T(8,128)S(1)}) custom-call(s32[1]{0:T(128)} %bitcast.1.x_ref, bf16[4,324,2048]{2,1,0:T(8,128)(2,1)S(1)} %bitcast.28, bf16[272,2048]{1,0:T(8,128)(2,1)S(1)} %collective-permute-done.3.got_ref), custom_call_target="tpu_custom_call" | custom-call | flops 1000 | bytes 10 | tf_op jit(solution)/shard_map/pallas_call | solution.py:155
  84.3 2.0 collective-permute-start.7
  86.3 1.9 collective-permute-start.8
  88.2 21.8 %collective-permute-done.5.rest_ref = f32[8,72,384]{2,1,0:T(8,128)} collective-permute-done((f32[8,72,384]{2,1,0:T(8,128)}, f32[8,72,384]{2,1,0:T(8,128)}, u32[]{:S(2)}, u32[]{:S(2)}) %collective-permute-start.5) | collective-permute-done | bytes 884768 | tf_op jit(solution)/shard_map/ppermute | solution.py:318
  110.0 0.0 collective-permute-done.4.main_ref
  110.0 5.6 %shard_map.22.out_in = f32[2,324,8,324]{3,2,1,0:T(8,128)} custom-call(f32[8,324,324]{2,1,0:T(8,128)S(1)} %copy-done.3, f32[8,328,256]{2,1,0:T(8,128)} %collective-permute-done.4.main_ref, f32[8,72,384]{2,1,0:T(8,128)} %collective-permute-done.5.rest_ref), custom_call_target="tpu_custom_call" | custom-call | flops 10000000000 | bytes 100000000 | tf_op jit(solution)/shard_map/pallas_call | solution.py:103
  115.6 0.0 collective-permute-done.6.came_ref
  115.6 1.9 shard_map.23
  117.6 1.1 copy-done.10
  118.7 0.5 slice.39
  119.9 1.2 fusion.2
  121.1 1.3 collective-permute-start.9
  122.4 0.0 collective-permute-done.7.came_ref
  122.4 1.9 shard_map.24
  124.4 1.1 copy-done.12
  125.5 0.5 slice.40
  126.7 1.2 fusion.5
  127.9 1.3 collective-permute-start.10
  129.2 0.0 collective-permute-done.8.came_ref
  129.2 1.8 shard_map.25
  131.0 0.9 copy-done.14
  132.0 0.5 slice.41
  133.1 0.2 fusion.12
  133.3 1.3 collective-permute-start.11
  134.6 56.4 %collective-permute-done.10 = f16[8,336,128]{2,1,0:T(8,128)(2,1)S(1)} collective-permute-done((f16[8,336,128]{2,1,0:T(8,128)(2,1)}, f16[8,336,128]{2,1,0:T(8,128)(2,1)S(1)}, u32[]{:S(2)}, u32[]{:S(2)}) %collective-permute-start.10) | collective-permute-done | bytes 688160 | tf_op jit(solution)/shard_map/ppermute | solution.py:329
  191.1 0.5 slice.52
  192.2 0.0 collective-permute-done.9
  192.2 1.2 slice.50
  194.1 0.6 negate_select_fusion.refs_4_
  194.7 1.8 negate_select_fusion.1.refs_3_
  196.6 3.2 %shard_map.26.out_in = f32[2,324,8,324]{3,2,1,0:T(8,128)} custom-call(s32[1]{0:T(128)} %bitcast.role_ref, f32[2,324,8,324]{3,2,1,0:T(8,128)} %shard_map.22.out_in, f32[8,324,128]{2,1,0:T(8,128)S(1)} %copy-done.11, f32[8,324,128]{2,1,0:T(8,128)S(1)} %copy-done.13, f32[8,68,324]{2,1,0:T(8,128)S(1)} %copy-done.15, ...), custom_call_target="tpu_custom_call", output_to_operand_aliasing={{}: (1, {})} | custom-call | flops 10000000000 | bytes 100000000 | tf_op jit(solution)/shard_map/pallas_call | solution.py:250
  199.8 0.0 collective-permute-done.11
  199.8 0.5 slice.47
  201.0 1.3 negate_select_fusion.2.last_ref
  202.2 26.4 %shard_map.27 = f32[2,324,8,324]{3,2,1,0:T(8,128)} custom-call(s32[1]{0:T(128)} %bitcast.role_ref, f32[2,324,8,324]{3,2,1,0:T(8,128)} %shard_map.26.out_in, f32[68,8,324]{2,1,0:T(8,128)} %negate_select_fusion.2.last_ref), custom_call_target="tpu_custom_call", output_to_operand_aliasing={{}: (1, {})} | custom-call | bytes 1000 | tf_op jit(solution)/shard_map/pallas_call | solution.py:276
  (33 shorter events, 0.1 us)
Async XLA Ops:
  0.0 27.2 %collective-permute-start = (bf16[4,2048,324]{1,0,2:T(4,128)(2,1)}, bf16[4,2048,324]{1,0,2:T(4,128)(2,1)}, u32[]{:S(2)}, u32[]{:S(2)}) collective-permute-start(bf16[4,2048,324]{1,0,2:T(4,128)(2,1)} %param.1), channel_id=1, source_target_pairs={{0,2},{2,0},{4,6},{6,4},{8,10},{10,8},{12,14},{14,12},{16,18},{18,... | collective-permute-start | bytes 15925256 | tf_op jit(solution)/shard_map/ppermute | solution.py:304
  0.5 12.0 %copy-start.16 = (bf16[4,2048,324]{1,0,2:T(4,128)(2,1)S(1)}, bf16[4,2048,324]{1,0,2:T(4,128)(2,1)}, u32[]{:S(2)}) copy-start(bf16[4,2048,324]{1,0,2:T(4,128)(2,1)} %param.1) | copy-start | bytes 15925252
  5.7 50.3 %collective-permute-start.1 = (bf16[4,128,2048]{2,1,0:T(8,128)(2,1)}, bf16[4,128,2048]{2,1,0:T(8,128)(2,1)}, u32[]{:S(2)}, u32[]{:S(2)}) collective-permute-start(bf16[4,128,2048]{2,1,0:T(8,128)(2,1)} %bitcast.21), channel_id=1, source_target_pairs={{0,16},{1,17},{4,20},{5,21},{8,24},{9,25},{12,28},{13,29},{18,2},{... | collective-permute-start | bytes 6291464 | tf_op jit(solution)/shard_map/ppermute | solution.py:312
  27.2 5.6 %slice-start = ((s8[5373952]{0:T(1024)(128)(4,1)}), s8[4194304]{0:T(1024)(128)(4,1)S(1)}, s32[]{:S(2)}) async-start(s8[5373952]{0:T(1024)(128)(4,1)} %bitcast.22), calls=%async_computation | async-start | bytes 8388608
  27.2 5.6 %slice-start.1 = ((s8[5373952]{0:T(1024)(128)(4,1)}), s8[1179648]{0:T(1024)(128)(4,1)S(1)}, s32[]{:S(2)}) async-start(s8[5373952]{0:T(1024)(128)(4,1)} %bitcast.22), calls=%async_computation.1 | async-start | bytes 2359296
  32.8 8.6 %copy-start.1 = (bf16[4,2048,324]{1,2,0:T(8,128)(2,1)}, bf16[4,2048,324]{1,2,0:T(8,128)(2,1)S(1)}, u32[]{:S(2)}) copy-start(bf16[4,2048,324]{1,2,0:T(8,128)(2,1)S(1)} %copy.23) | copy-start | bytes 15925252
  41.4 68.6 %collective-permute-start.4 = (f32[8,328,256]{2,1,0:T(8,128)}, f32[8,328,256]{2,1,0:T(8,128)}, u32[]{:S(2)}, u32[]{:S(2)}) collective-permute-start(f32[8,328,256]{2,1,0:T(8,128)} %get-tuple-element.37), channel_id=1, source_target_pairs={{0,1},{1,0},{2,3},{3,2},{4,5},{5,4},{6,7},{7,6},{8,9},{9,8},{10,11... | collective-permute-start | bytes 8060936 | tf_op jit(solution)/shard_map/ppermute | solution.py:318
  42.9 25.2 %collective-permute-start.2 = (bf16[4,128,2048]{2,1,0:T(8,128)(2,1)}, bf16[4,128,2048]{2,1,0:T(8,128)(2,1)S(1)}, u32[]{:S(2)}, u32[]{:S(2)}) collective-permute-start(bf16[4,128,2048]{2,1,0:T(8,128)(2,1)} %slice_bitcast_fusion), channel_id=1, source_target_pairs={{0,16},{1,17},{4,20},{5,21},{8,24},{9,25},{12,28},{13,29},{18,2},{... | collective-permute-start | bytes 6291464 | tf_op jit(solution)/shard_map/ppermute | solution.py:312
  44.3 35.7 %collective-permute-start.3 = (bf16[272,2048]{1,0:T(8,128)(2,1)}, bf16[272,2048]{1,0:T(8,128)(2,1)S(1)}, u32[]{:S(2)}, u32[]{:S(2)}) collective-permute-start(bf16[272,2048]{1,0:T(8,128)(2,1)} %reshape.39), channel_id=1, source_target_pairs={{0,16},{1,17},{4,20},{5,21},{8,24},{9,25},{12,28},{13,29},{18,2},{... | collective-permute-start | bytes 3342344 | tf_op jit(solution)/shard_map/ppermute | solution.py:312
  56.0 8.1 %copy-start.2 = (f32[8,324,324]{2,1,0:T(8,128)}, f32[8,324,324]{2,1,0:T(8,128)S(1)}, u32[]{:S(2)}) copy-start(f32[8,324,324]{2,1,0:T(8,128)S(1)} %shard_map.18.keep_ref) | copy-start | bytes 10077700
  64.1 1.3 copy-start.4
  65.4 50.1 %collective-permute-start.6 = (f32[12,324,128]{2,1,0:T(8,128)}, f32[12,324,128]{2,1,0:T(8,128)}, u32[]{:S(2)}, u32[]{:S(2)}) collective-permute-start(f32[12,324,128]{2,1,0:T(8,128)} %get-tuple-element.48), channel_id=1, source_target_pairs={{2,3},{3,2},{6,7},{7,6},{10,11},{11,10},{14,15},{15,14},{16,17},{1... | collective-permute-start | bytes 5971976 | tf_op jit(solution)/shard_map/ppermute | solution.py:322
  67.4 42.5 %collective-permute-start.5 = (f32[8,72,384]{2,1,0:T(8,128)}, f32[8,72,384]{2,1,0:T(8,128)}, u32[]{:S(2)}, u32[]{:S(2)}) collective-permute-start(f32[8,72,384]{2,1,0:T(8,128)} %get-tuple-element.46), channel_id=1, source_target_pairs={{0,1},{1,0},{2,3},{3,2},{4,5},{5,4},{6,7},{7,6},{8,9},{9,8},{10,11... | collective-permute-start | bytes 2654216 | tf_op jit(solution)/shard_map/ppermute | solution.py:318
  68.1 2.5 %copy-start = (bf16[4,2048,324]{1,2,0:T(8,128)(2,1)S(1)}, bf16[4,2048,324]{1,2,0:T(8,128)(2,1)}, u32[]{:S(2)}) copy-start(bf16[4,2048,324]{1,2,0:T(8,128)(2,1)} %copy.24) | copy-start | bytes 15925252
  75.8 1.3 copy-start.6
  77.0 33.0 %copy-start.3 = (f32[8,324,324]{2,1,0:T(8,128)S(1)}, f32[8,324,324]{2,1,0:T(8,128)}, u32[]{:S(2)}) copy-start(f32[8,324,324]{2,1,0:T(8,128)} %copy-done.2) | copy-start | bytes 10077700
  84.3 31.3 %copy-start.8 = (f32[12,68,324]{2,1,0:T(8,128)}, f32[12,68,324]{2,1,0:T(8,128)S(1)}, u32[]{:S(2)}) copy-start(f32[12,68,324]{2,1,0:T(8,128)S(1)} %get-tuple-element.44.keep_ref) | copy-start | bytes 3172612
  84.3 38.1 %collective-permute-start.7 = (f32[12,324,128]{2,1,0:T(8,128)}, f32[12,324,128]{2,1,0:T(8,128)}, u32[]{:S(2)}, u32[]{:S(2)}) collective-permute-start(f32[12,324,128]{2,1,0:T(8,128)} %get-tuple-element.51), channel_id=1, source_target_pairs={{2,3},{3,2},{6,7},{7,6},{10,11},{11,10},{14,15},{15,14},{16,17},{1... | collective-permute-start | bytes 5971976 | tf_op jit(solution)/shard_map/ppermute | solution.py:322
  86.3 29.3 %copy-start.5 = (f32[12,324,128]{2,1,0:T(8,128)S(1)}, f32[12,324,128]{2,1,0:T(8,128)}, u32[]{:S(2)}) copy-start(f32[12,324,128]{2,1,0:T(8,128)} %copy-done.4) | copy-start | bytes 5971972
  86.3 42.9 %collective-permute-start.8 = (f32[12,68,324]{2,1,0:T(8,128)}, f32[12,68,324]{2,1,0:T(8,128)}, u32[]{:S(2)}, u32[]{:S(2)}) collective-permute-start(f32[12,68,324]{2,1,0:T(8,128)} %get-tuple-element.54), channel_id=1, source_target_pairs={{2,3},{3,2},{6,7},{7,6},{10,11},{11,10},{14,15},{15,14},{16,17},{1... | collective-permute-start | bytes 3172616 | tf_op jit(solution)/shard_map/ppermute | solution.py:322
  117.5 1.1 copy-start.10
  118.7 3.8 %copy-start.7 = (f32[12,324,128]{2,1,0:T(8,128)S(1)}, f32[12,324,128]{2,1,0:T(8,128)}, u32[]{:S(2)}) copy-start(f32[12,324,128]{2,1,0:T(8,128)} %copy-done.6) | copy-start | bytes 5971972
  121.1 71.1 %collective-permute-start.9 = (f16[8,336,128]{2,1,0:T(8,128)(2,1)}, f16[8,336,128]{2,1,0:T(8,128)(2,1)}, u32[]{:S(2)}, u32[]{:S(2)}) collective-permute-start(f16[8,336,128]{2,1,0:T(8,128)(2,1)} %fusion.2), channel_id=1, source_target_pairs={{16,0},{17,1},{20,4},{21,5},{24,8},{25,9},{28,12},{29,13},{2,18},{... | collective-permute-start | bytes 2064392 | tf_op jit(solution)/shard_map/ppermute | solution.py:329
  124.4 1.1 copy-start.12
  125.5 3.7 %copy-start.9 = (f32[12,68,324]{2,1,0:T(8,128)S(1)}, f32[12,68,324]{2,1,0:T(8,128)}, u32[]{:S(2)}) copy-start(f32[12,68,324]{2,1,0:T(8,128)} %copy-done.8) | copy-start | bytes 3172612
  127.9 63.2 %collective-permute-start.10 = (f16[8,336,128]{2,1,0:T(8,128)(2,1)}, f16[8,336,128]{2,1,0:T(8,128)(2,1)S(1)}, u32[]{:S(2)}, u32[]{:S(2)}) collective-permute-start(f16[8,336,128]{2,1,0:T(8,128)(2,1)} %fusion.5), channel_id=1, source_target_pairs={{16,0},{17,1},{20,4},{21,5},{24,8},{25,9},{28,12},{29,13},{2,18},{... | collective-permute-start | bytes 2064392 | tf_op jit(solution)/shard_map/ppermute | solution.py:329
  131.0 0.9 copy-start.14
  133.3 66.4 %collective-permute-start.11 = (f16[69,8,324]{2,1,0:T(8,128)(2,1)S(1)}, f16[69,8,324]{2,1,0:T(8,128)(2,1)S(1)}, u32[]{:S(2)}, u32[]{:S(2)}) collective-permute-start(f16[69,8,324]{2,1,0:T(8,128)(2,1)S(1)} %fusion.12), channel_id=1, source_target_pairs={{16,0},{17,1},{20,4},{21,5},{24,8},{25,9},{28,12},{29,13},{2,18},{... | collective-permute-start | bytes 1073096 | tf_op jit(solution)/shard_map/ppermute | solution.py:329
  194.1 2.4 %copy-start.13 = (f32[8,324,128]{2,1,0:T(8,128)S(1)}, f32[8,324,128]{2,1,0:T(8,128)}, u32[]{:S(2)}) copy-start(f32[8,324,128]{2,1,0:T(8,128)} %copy-done.12) | copy-start | bytes 3981316
  194.1 2.4 %copy-start.15 = (f32[8,68,324]{2,1,0:T(8,128)S(1)}, f32[8,68,324]{2,1,0:T(8,128)}, u32[]{:S(2)}) copy-start(f32[8,68,324]{2,1,0:T(8,128)} %copy-done.14) | copy-start | bytes 2115076
  194.7 1.8 copy-start.11

commit v3 on v0

v3 whole, which is shorter than its diff:
```python
import functools

import jax
import jax.numpy as jnp
from jax import lax
from jax.experimental import pallas as pl
from jax.experimental.pallas import tpu as pltpu
from jax.sharding import PartitionSpec as P

LANES = 128
VMEM_LIMIT = 40 * 2**20
SQUARE_TOP = 2.0**13
SMALLEST = 2.0**-120


def contract_last(left, right):
    return lax.dot_general(left, right, (((1,), (1,)), ((), ())), preferred_element_type=jnp.float32)


def call(body, grid, scalars, in_specs, out_specs, out_shape, after=(), aliases={}):
    idle = len(after)

    def waiting(*refs):
        first = scalars + len(in_specs)
        body(*refs[:first], *refs[first + idle :])

    kernel = pl.pallas_call(
        waiting,
        grid_spec=pltpu.PrefetchScalarGridSpec(
            num_scalar_prefetch=scalars,
            grid=grid,
            in_specs=in_specs + [pl.BlockSpec(memory_space=pl.ANY)] * idle,
            out_specs=out_specs,
        ),
        out_shape=out_shape,
        input_output_aliases=aliases,
        compiler_params=pltpu.CompilerParams(vmem_limit_bytes=VMEM_LIMIT),
    )
    return lambda *operands: kernel(*operands, *after)


def f32(*shape):
    return jax.ShapeDtypeStruct(shape, jnp.float32)


def up(size, unit):
    return -(-size // unit) * unit


def whole(shape):
    return pl.BlockSpec(shape, lambda *_: (0,) * len(shape))


class Packing:
    def __init__(self, tiles, ops):
        self.ops, self.wide = ops, ops // LANES * LANES
        self.rest, self.below = ops - self.wide, up(ops, 8)
        self.each = self.below + up(self.rest, 8)
        beside = self.wide // LANES
        self.corners = [
            (tiles * self.each + t // beside * up(self.rest, 8), t % beside * LANES) for t in range(tiles)
        ]
        self.shape = (tiles * self.each + pl.cdiv(tiles, beside) * up(self.rest, 8), self.wide)

    def store(self, wire_ref, t, main, turned):
        row, lane = self.corners[t]
        wire_ref[t * self.each : t * self.each + self.ops] = main
        start = t * self.each + self.below
        wire_ref[start : start + self.rest] = turned[:, : self.wide]
        wire_ref[row : row + self.rest, lane : lane + self.rest] = turned[:, self.wide :]

    def parts(self, wire_ref, t):
        row, lane = self.corners[t]
        start, padded = t * self.each + self.below, up(self.rest, 8)
        head, tail = slice(0, self.wide), slice(self.wide, self.ops)
        side = wire_ref[start : start + padded].T[:, : self.rest]
        corner = wire_ref[row : row + padded, lane : lane + LANES].T[: self.rest, : self.rest]
        main = wire_ref[t * self.each : t * self.each + self.ops]
        return [(slice(0, self.ops), head, main), (head, tail, side), (tail, tail, corner)]


def near_send(det, own, partner, to_mine, after=()):
    states, ops, depth = own.shape
    half, tiles = states // 2, (states // 2) ** 2
    packing = Packing(tiles, ops)

    def body(x_ref, own_ref, partner_ref, wire_ref):
        main = contract_last(own_ref[0], partner_ref[0, : packing.wide])
        turned = contract_last(partner_ref[0, packing.wide :], own_ref[0])
        for t in range(tiles):

            @pl.when(pl.program_id(0) == t)
            def _():
                packing.store(wire_ref, t, main, turned)

    def second(x):
        return half * (1 - x[0]) if to_mine else half * x[0]

    return call(
        body,
        (tiles,),
        1,
        [
            pl.BlockSpec((1, ops, depth), lambda t, x: (half * (1 - x[0]) + t // half, 0, 0)),
            pl.BlockSpec((1, ops, depth), lambda t, x: (second(x) + t % half, 0, 0)),
        ],
        whole(packing.shape),
        f32(*packing.shape),
        after,
    )(det, own, partner)


def near_keep(det, own, partner, after=()):
    states, ops, depth = own.shape
    half = states // 2

    def body(x_ref, own_ref, partner_ref, tile_ref):
        tile_ref[0] = contract_last(own_ref[0], partner_ref[0])

    return call(
        body,
        (half, states),
        1,
        [
            pl.BlockSpec((1, ops, depth), lambda a, b, x: (half * x[0] + a, 0, 0)),
            pl.BlockSpec((1, ops, depth), lambda a, b, x: (b, 0, 0)),
        ],
        pl.BlockSpec((1, ops, ops), lambda a, b, x: (a * states + b, 0, 0)),
        f32(half * states, ops, ops),
        after,
    )(det, own, partner)


def near_share(det, keep, doubled, states, after=()):
    _, ops, _ = keep.shape
    half, tiles = states // 2, (states // 2) ** 2
    packing = Packing(tiles, ops)
    shape = (tiles, up(ops, 8), up(ops, LANES))

    def body(x_ref, keep_ref, wire_ref, tile_ref):
        for t in range(tiles):
            kept = t // half * states + half * x_ref[0] + t % half
            for rows, columns, values in packing.parts(wire_ref, t):
                tile_ref[t, rows, columns] = keep_ref[kept, rows, columns] + values

    return call(
        body, (1,), 1, [whole(keep.shape), whole(packing.shape)], whole(shape), f32(*shape), after
    )(det, keep, doubled)


def near_sum(place_in, keep, crossed, share, given, states, after=()):
    tiles, ops, _ = keep.shape
    half = states // 2
    packing = Packing(half * half, ops)

    def body(s_ref, keep_ref, wire_ref, share_ref, given_ref, out_ref):
        x, core = s_ref[0], s_ref[1]
        for a in range(half):
            for b in range(states):
                t, one, turned = a * states + b, a * half + b % half, b % half * half + a

                @pl.when(b // half != x)
                def _():
                    for rows, columns, values in packing.parts(wire_ref, one):
                        out_ref[0, rows, t, columns] = keep_ref[t, rows, columns] + values

                @pl.when((b // half == x) & (core == 0))
                def _():
                    out_ref[0, :, t] = share_ref[one, :ops, :ops]

                @pl.when((b // half == x) & (core == 1))
                def _():
                    out_ref[0, :, t] = given_ref[turned].T[:ops, :ops]

    return call(
        body,
        (1,),
        1,
        [whole(keep.shape), whole(packing.shape), whole(share.shape), whole(given.shape)],
        pl.BlockSpec((1, ops, tiles, ops), lambda i, s: (1, 0, 0, 0)),
        f32(2, ops, tiles, ops),
        after,
    )(place_in, keep, crossed, share, given)


def far_terms(det, own, got, turned, mine, after=()):
    states, ops, depth = own.shape
    half = states // 2
    width = got.size // (states * depth)
    rows = ops if turned else width
    tile = (up(ops, 8), width) if turned else (up(width, 8), ops)

    def body(x_ref, own_ref, got_ref, out_ref):
        if turned:
            every = contract_last(own_ref[0], got_ref[...].reshape(states * width, depth))
        else:
            every = contract_last(got_ref[...], own_ref[0])
        for u in range(states):
            part = slice(u * width, (u + 1) * width)
            out_ref[u, :rows] = every[:, part] if turned else every[part]

    def state(b, x):
        return ((half * x[0] if mine else half * (1 - x[0])) + b, 0, 0)

    return call(
        body,
        (half,),
        1,
        [pl.BlockSpec((1, ops, depth), state), whole(got.shape)],
        pl.BlockSpec((states, *tile), lambda b, x: (b, 0, 0)),
        f32(half * states, *tile),
        after,
    )(det, own, got)


def far_sum(det, keep, came, states, rows, turned, after=()):
    tiles, padded, lanes = keep.shape
    half = states // 2
    shape = (half * half, up(rows + 1, 16), lanes) if turned else (rows + 1, half * half, lanes)

    def body(x_ref, keep_ref, came_ref, own_ref, straight_ref, across_ref):
        x = x_ref[0]
        top = jnp.zeros((rows, lanes), jnp.float32)
        for t in range(tiles):
            tile = keep_ref[t, :rows] + came_ref[t, :rows]
            own_ref[t] = tile
            top = jnp.maximum(top, jnp.abs(tile))
        exponent = jnp.floor(jnp.log2(jnp.maximum(jnp.max(top, keepdims=True), SMALLEST)))
        scale = jnp.exp2(-exponent)
        for to_ref, first in ((straight_ref, half * x), (across_ref, half * (1 - x))):
            for a in range(half):
                for b in range(half):
                    scaled = own_ref[b * states + first + a] * scale
                    code = scaled * jnp.abs(scaled) * SQUARE_TOP
                    if turned:
                        to_ref[a * half + b, :rows] = code
                        to_ref[a * half + b, rows:] = jnp.broadcast_to(exponent, (shape[1] - rows, lanes))
                    else:
                        to_ref[:rows, a * half + b] = code
            if not turned:
                to_ref[rows] = jnp.broadcast_to(exponent, (half * half, lanes))

    return call(
        body,
        (1,),
        1,
        [whole((tiles, padded, lanes))] * 2,
        [whole((tiles, rows, lanes)), whole(shape), whole(shape)],
        [f32(tiles, rows, lanes), f32(*shape), f32(*shape)],
        after,
    )(det, keep, came)


def decoded(values, exponent):
    root = jnp.sqrt(jnp.abs(values)) * (jnp.exp2(exponent) * SQUARE_TOP**-0.5)
    return jnp.where(values < 0, -root, root)


def place(place_in, out, owned, came, states, after=()):
    _, ops, tiles, _ = out.shape
    full, half = len(came), states // 2
    wide = full * LANES
    code = came[0][0].shape

    def body(s_ref, out_in, *refs):
        owned_refs, came_refs, out_ref = refs[: full + 1], refs[full + 1 : -1], refs[-1]
        x = s_ref[0]

        @pl.when(s_ref[1] == 1)
        def _():
            for t in range(tiles):
                for k in range(full):
                    out_ref[0, :, t, k * LANES : (k + 1) * LANES] = owned_refs[k][t]
                out_ref[0, :, t, wide:] = owned_refs[full][t].T

        for k in range(full):
            straight, across = came_refs[2 * k : 2 * k + 2]

            @pl.when((s_ref[1] == 0) & (pl.program_id(0) == k))
            def _():
                for a in range(half):
                    for v in range(states):
                        one = a * half + v % half
                        block = jnp.where(v // half == x, straight[one], across[one])
                        tile = decoded(block[:ops], block[ops : ops + 1])
                        out_ref[0, :, a * states + v] = tile.T

    return call(
        body,
        (pl.cdiv(ops, LANES),),
        1,
        [pl.BlockSpec(memory_space=pl.ANY)]
        + [pl.BlockSpec((tiles, LANES, LANES), lambda i, s: (0, i, 0))] * full
        + [pl.BlockSpec((tiles, ops - wide, LANES), lambda i, s: (0, 0, i))]
        + [whole(code)] * (2 * full),
        pl.BlockSpec((1, LANES, tiles, ops), lambda i, s: (0, i, 0, 0)),
        f32(*out.shape),
        after,
        {1: 0},
    )(place_in, out, *owned, *[c for pair in came for c in pair])


def finish(place_in, out, straight, across, states):
    _, ops, tiles, _ = out.shape
    rest, half = straight.shape[0] - 1, states // 2

    def body(s_ref, out_in, straight_ref, across_ref, out_ref, rows_ref, sem):
        x = s_ref[0]

        @pl.when(s_ref[1] == 0)
        def _():
            for a in range(half):
                for v in range(states):
                    one = a * half + v % half
                    block = jnp.where(v // half == x, straight_ref[:, one], across_ref[:, one])
                    rows_ref[:, a * states + v] = decoded(block[:rest], block[rest:])
            copy = pltpu.make_async_copy(rows_ref, out_ref.at[0, pl.ds(ops - rest, rest)], sem)
            copy.start()
            copy.wait()

    return pl.pallas_call(
        body,
        in_specs=[
            pl.BlockSpec(memory_space=pltpu.SMEM),
            pl.BlockSpec(memory_space=pl.ANY),
            pl.BlockSpec(memory_space=pltpu.VMEM),
            pl.BlockSpec(memory_space=pltpu.VMEM),
        ],
        out_specs=pl.BlockSpec(memory_space=pl.ANY),
        out_shape=f32(*out.shape),
        input_output_aliases={1: 0},
        scratch_shapes=[pltpu.VMEM((rest, tiles, ops), jnp.float32), pltpu.SemaphoreType.DMA],
    )(place_in, out, straight, across)


def paired(amplitudes):
    blocks = lax.axis_size("state")
    far = blocks.bit_length() - 2
    states, depth, ops = amplitudes.shape
    full = ops // LANES
    wide = full * LANES
    both = ("state", "det")
    senders = [s for s in range(blocks) if (s & 1) == (s >> far & 1)]
    receivers = [s for s in range(blocks) if s not in senders]
    over = [(2 * s + x, 2 * (s ^ 1 << far) + x) for s in senders for x in range(2)]
    straight = [(b, a) for a, b in over]
    diagonal = [(b, a ^ 1) for a, b in over]
    across = [(2 * s + x, 2 * s + 1 - x) for s in receivers for x in range(2)]
    first_across = [(2 * s + x, 2 * s + 1 - x) for s in range(0, blocks, 2) for x in range(2)]
    to_second = [(2 * s + x, 2 * (s + 1) + x) for s in range(0, blocks, 2) for x in range(2)]

    state = lax.axis_index("state")
    x = lax.axis_index("det").astype(jnp.int32)
    det = x[None]
    receiver = ((state & 1) ^ (state >> far & 1)).astype(jnp.int32)
    core = (state & 1).astype(jnp.int32)

    partner = lax.ppermute(amplitudes, "state", [(s, s ^ 1) for s in range(blocks)])
    chunks = [amplitudes[:, :, :LANES].transpose(0, 2, 1)]
    chunks[0], later = lax.optimization_barrier((chunks[0], amplitudes))
    own = later.transpose(0, 2, 1)
    chunks += [own[:, k * LANES : (k + 1) * LANES] for k in range(1, full)]
    chunks.append(own[:, wide:].reshape(states * (ops - wide), depth))
    got = [lax.ppermute(c, both, over) for c in chunks]

    partner, own = lax.optimization_barrier((partner, own))
    partner = partner.transpose(0, 2, 1)
    crossed = near_send(det, own, partner, False, tuple(chunks[1:]))
    doubled = near_send(det, own, partner, True, (crossed,))
    keep = near_keep(det, own, partner, (doubled,))
    crossed = lax.ppermute(crossed, "det", [(0, 1), (1, 0)])
    doubled = lax.ppermute(doubled, both, first_across)

    def partials(k, done):
        send = far_terms(det, own, got[k], k < full, False, done)
        return send, far_terms(det, own, got[k], k < full, True, (send,))

    def finished(k, kept, came, done):
        rows = ops if k < full else ops - wide
        mine, *pair = far_sum(det, kept, came, states, rows, k < full, done)
        return mine, [v.astype(jnp.float16) for v in pair]

    def returned(pair):
        return [lax.ppermute(v, both, to) for v, to in zip(pair, (straight, diagonal))]

    owned, codes, done = [], [], keep
    for k in range(full):
        send, kept = partials(k, (done,))
        came = lax.ppermute(send, both, across)
        done = kept
        if k == 1:
            done = share = near_share(det, keep, doubled, states, (kept, crossed))
            given = lax.ppermute(share, both, to_second)
        done, pair = finished(k, kept, came, (done,))
        owned.append(done)
        codes.append(pair)
    codes[0] = [v.astype(jnp.float32) for v in returned(codes[0])]
    send, kept = partials(full, (done, *codes[0]))
    came = lax.ppermute(send, both, across)
    out = near_sum(jnp.stack([x, core]), keep, crossed, share, given, states, (kept,))
    mine, pair = finished(full, kept, came, (out,))
    owned.append(mine)
    codes[1:] = [returned(c) for c in codes[1:] + [pair]]

    at = jnp.stack([x, receiver])
    codes[1:full] = [[v.astype(jnp.float32) for v in c] for c in codes[1:full]]
    out = place(at, out, owned, codes[:full], states)
    *last, out = lax.optimization_barrier((*codes[full], out))
    return finish(at, out, *[v.astype(jnp.float32) for v in last], states).transpose(0, 2, 1, 3)


def partner_2(value, axis, stride):
    mask = 2**stride
    pairs = [(source, source ^ mask) for source in range(lax.axis_size(axis))]
    return lax.ppermute(value, axis, pairs)


def pair_terms(own_block, partner, count):
    operators = own_block.shape[2]
    terms = jnp.einsum("adp,bdq->abpq", own_block, partner, preferred_element_type=jnp.float32)
    return terms.reshape(count, operators, operators)


def exchanged(amplitudes):
    blocks = lax.axis_size("state")
    far_bit = blocks.bit_length() - 2
    states = amplitudes.shape[0]
    gathered = []
    for bit in (far_bit, 0):
        partner = partner_2(amplitudes, "state", bit)
        terms = pair_terms(amplitudes, partner, states * states)
        gathered.append(lax.psum_scatter(terms, "det", scatter_dimension=0, tiled=True))
    return jnp.stack(gathered)


def on_device(amplitudes):
    states, _, ops = amplitudes.shape
    two = lax.axis_size("det") == 2 and lax.axis_size("state") >= 4
    if two and states % 2 == 0 and ops > LANES and ops % LANES % 8:
        return paired(amplitudes)
    return exchanged(amplitudes)


def solution(mesh):
    return jax.shard_map(
        on_device,
        mesh=mesh,
        in_specs=(P("state", "det", None),),
        out_specs=P(None, ("state", "det"), None, None),
        check_vma=False,
    )
```

time: 483 us -> 231 us (0.48)
  the two profiles are of different devices: /device:TPU:0 before, /device:TPU:24 now
where the time goes in v3:
time: 231 us; the launch traced here: 230 us
  waiting for transfers between devices  99.6 us (43%)
  Pallas kernels  54.5 us (24%)
  starting transfers between devices  35.3 us (15%)
  local copies, waits for them, and re-layouts  33.4 us (14%)
  other arithmetic  6.68 us (3%)
    ppermute x3, waiting for transfers between devices, paired(): got = [lax.ppermute(c, both, over) for c in chunks]  66.1 us
    pallas_call x15, Pallas kernels, call(): return lambda *operands: kernel(*operands, *after)  53.4 us
    ppermute x3, waiting for transfers between devices, paired(): came = lax.ppermute(send, both, across)  26.4 us
    unnamed x53, local copies, waits for them, and re-layouts  14.7 us
    ppermute x6, starting transfers between devices, returned(): lax.ppermute(v, both, to)  14.4 us
    ppermute x3, starting transfers between devices, paired(): came = lax.ppermute(send, both, across)  10.2 us
    optimization_barrier x1, local copies, waits for them, and re-layouts, paired(): partner, own = lax.optimization_barrier((partner, own))  7.95 us
    ppermute x6, waiting for transfers between devices, returned(): lax.ppermute(v, both, to)  7.08 us
  transfers between devices with their start and end apart: 16, of which 5 were waited for; matrix products, arithmetic and copies ran while one was open for 11% of the time, Pallas kernels for 23%

profile of v3, /device:TPU:24, one launch (start us, length us, event | category | flops | bytes accessed | tf_op | source)
XLA Modules:
  0.0 230.1 jit_solution(8200640882813574143)
XLA Ops:
  0.0 2.8 %slice.9 = bf16[4,2048,128]{1,0,2:T(4,128)(2,1)S(1)} slice(bf16[4,2048,324]{1,0,2:T(4,128)(2,1)} %param.1), slice={[0:4], [0:2048], [0:128]} | slice | bytes 4194304 | tf_op jit(solution)/shard_map/slice | solution.py:359
  2.8 2.5 %copy.19 = bf16[4,2048,128]{1,2,0:T(8,128)(2,1)} copy(bf16[4,2048,128]{1,0,2:T(4,128)(2,1)S(1)} %slice.9) | data formatting | bytes 4194304
  5.2 1.3 collective-permute-start.3
  6.5 2.9 %copy.18 = bf16[4,2048,324]{1,2,0:T(8,128)(2,1)S(1)} copy(bf16[4,2048,324]{1,0,2:T(4,128)(2,1)S(1)} %copy-done.23) | data formatting | bytes 10616832 | tf_op jit(solution)/shard_map/optimization_barrier | solution.py:360
  9.4 1.7 slice.13.refs_3_
  11.1 1.3 collective-permute-start.2
  12.4 1.2 slice.12
  13.6 2.4 %copy-done = bf16[4,2048,324]{1,2,0:T(8,128)(2,1)} copy-done((bf16[4,2048,324]{1,2,0:T(8,128)(2,1)}, bf16[4,2048,324]{1,2,0:T(8,128)(2,1)S(1)}, u32[]{:S(2)}) %copy-start) | copy-done | bytes 5308440
  16.0 2.3 %reshape.3.refs_4_ = bf16[272,2048]{1,0:T(8,128)(2,1)} reshape(bf16[4,68,2048]{2,1,0:T(8,128)(2,1)} %slice.12) | data formatting | bytes 2228224 | tf_op jit(solution)/shard_map/reshape | solution.py:363
  18.3 0.0 collective-permute-done
  18.3 7.9 %copy.17 = bf16[4,2048,324]{1,2,0:T(8,128)(2,1)} copy(bf16[4,2048,324]{1,0,2:T(4,128)(2,1)} %collective-permute-done) | data formatting | bytes 10616832 | tf_op jit(solution)/shard_map/optimization_barrier | solution.py:366
  26.2 7.1 %shard_map.17.refs_3_ = f32[1744,256]{1,0:T(8,128)} custom-call(s32[1]{0:T(128)} %bitcast.refs_0_, bf16[4,324,2048]{2,1,0:T(8,128)(2,1)S(1)} %bitcast.17, bf16[4,324,2048]{2,1,0:T(8,128)(2,1)} %bitcast.26, bf16[4,128,2048]{2,1,0:T(8,128)(2,1)} %slice.13.refs_3_, bf16[272,2048]{1,0:T(8,128)(2,1)S(1)} %copy-done.16), custom_call_target="tpu_custom_call" | custom-call | tf_op jit(solution)/shard_map/pallas_call | solution.py:39
  33.3 5.1 %shard_map.18.refs_3_ = f32[1744,256]{1,0:T(8,128)} custom-call(s32[1]{0:T(128)} %bitcast.refs_0_, bf16[4,324,2048]{2,1,0:T(8,128)(2,1)S(1)} %bitcast.18, bf16[4,324,2048]{2,1,0:T(8,128)(2,1)S(1)} %bitcast.28, f32[1744,256]{1,0:T(8,128)} %shard_map.17.refs_3_), custom_call_target="tpu_custom_call" | custom-call | tf_op jit(solution)/shard_map/pallas_call | solution.py:39
  38.4 3.6 %collective-permute-start.6 = (f32[1744,256]{1,0:T(8,128)}, f32[1744,256]{1,0:T(8,128)}, u32[]{:S(2)}, u32[]{:S(2)}) collective-permute-start(f32[1744,256]{1,0:T(8,128)} %shard_map.18.refs_3_), channel_id=1, source_target_pairs={{0,1},{1,0},{4,5},{5,4},{8,9},{9,8},{12,13},{13,12},{16,17},{17,16... | collective-permute-start | bytes 5357576 | tf_op jit(solution)/shard_map/ppermute | solution.py:372
  42.0 0.6 collective-permute-start.7
  42.6 10.1 %shard_map.19.refs_3_.refs_1_ = f32[8,324,324]{2,1,0:T(8,128)S(1)} custom-call(s32[1]{0:T(128)} %bitcast.refs_0_, bf16[4,324,2048]{2,1,0:T(8,128)(2,1)S(1)} %bitcast.19, bf16[4,324,2048]{2,1,0:T(8,128)(2,1)} %bitcast.27, f32[1744,256]{1,0:T(8,128)} %shard_map.18.refs_3_), custom_call_target="tpu_custom_call" | custom-call | tf_op jit(solution)/shard_map/pallas_call | solution.py:39
  52.7 26.5 %collective-permute-done.3.refs_2_ = bf16[4,128,2048]{2,1,0:T(8,128)(2,1)} collective-permute-done((bf16[4,128,2048]{2,1,0:T(8,128)(2,1)}, bf16[4,128,2048]{2,1,0:T(8,128)(2,1)}, u32[]{:S(2)}, u32[]{:S(2)}) %collective-permute-start.3) | collective-permute-done | bytes 2097184 | tf_op jit(solution)/shard_map/ppermute | solution.py:364
  79.2 3.4 %shard_map.20.refs_3_ = f32[8,328,128]{2,1,0:T(8,128)S(1)} custom-call(s32[1]{0:T(128)} %bitcast.refs_0_, bf16[4,324,2048]{2,1,0:T(8,128)(2,1)S(1)} %bitcast.20, bf16[4,128,2048]{2,1,0:T(8,128)(2,1)} %collective-permute-done.3.refs_2_, f32[8,324,324]{2,1,0:T(8,128)S(1)} %shard_map.19.refs_3_.refs_1_), custom_call_target="tpu_custom_call" | custom-call | tf_op jit(solution)/shard_map/pallas_call | solution.py:39
  82.6 3.4 %collective-permute-start.4 = (f32[8,328,128]{2,1,0:T(8,128)S(1)}, f32[8,328,128]{2,1,0:T(8,128)S(1)}, u32[]{:S(2)}, u32[]{:S(2)}) collective-permute-start(f32[8,328,128]{2,1,0:T(8,128)S(1)} %shard_map.20.refs_3_), channel_id=1, source_target_pairs={{2,3},{3,2},{6,7},{7,6},{10,11},{11,10},{14,15},{15,14},{16,17},{1... | collective-permute-start | bytes 4030472 | tf_op jit(solution)/shard_map/ppermute | solution.py:389
  86.0 3.4 %shard_map.21.refs_1_.refs_3_ = f32[8,328,128]{2,1,0:T(8,128)S(1)} custom-call(s32[1]{0:T(128)} %bitcast.refs_0_, bf16[4,324,2048]{2,1,0:T(8,128)(2,1)S(1)} %bitcast.21, bf16[4,128,2048]{2,1,0:T(8,128)(2,1)} %collective-permute-done.3.refs_2_, f32[8,328,128]{2,1,0:T(8,128)S(1)} %shard_map.20.refs_3_), custom_call_target="tpu_custom_call" | custom-call | tf_op jit(solution)/shard_map/pallas_call | solution.py:39
  89.5 26.4 %collective-permute-done.4.refs_2_ = f32[8,328,128]{2,1,0:T(8,128)S(1)} collective-permute-done((f32[8,328,128]{2,1,0:T(8,128)S(1)}, f32[8,328,128]{2,1,0:T(8,128)S(1)}, u32[]{:S(2)}, u32[]{:S(2)}) %collective-permute-start.4) | collective-permute-done | bytes 1343520 | tf_op jit(solution)/shard_map/ppermute | solution.py:389
  115.9 0.7 shard_map.22
  116.6 1.8 shard_map.23.refs_3_
  118.5 3.4 %collective-permute-start.5 = (f32[8,328,128]{2,1,0:T(8,128)S(1)}, f32[8,328,128]{2,1,0:T(8,128)S(1)}, u32[]{:S(2)}, u32[]{:S(2)}) collective-permute-start(f32[8,328,128]{2,1,0:T(8,128)S(1)} %shard_map.23.refs_3_), channel_id=1, source_target_pairs={{2,3},{3,2},{6,7},{7,6},{10,11},{11,10},{14,15},{15,14},{16,17},{1... | collective-permute-start | bytes 4030472 | tf_op jit(solution)/shard_map/ppermute | solution.py:389
  121.9 1.8 shard_map.24.refs_3_.refs_1_
  123.8 0.0 collective-permute-done.6.refs_2_
  123.8 2.0 shard_map.25.refs_3_
  125.8 2.6 %collective-permute-start.11 = (f32[4,328,384]{2,1,0:T(8,128)S(1)}, f32[4,328,384]{2,1,0:T(8,128)}, u32[]{:S(2)}, u32[]{:S(2)}) collective-permute-start(f32[4,328,384]{2,1,0:T(8,128)S(1)} %shard_map.25.refs_3_), channel_id=1, source_target_pairs={{0,2},{1,3},{4,6},{5,7},{8,10},{9,11},{12,14},{13,15},{16,18},{17,... | collective-permute-start | bytes 6045704 | tf_op jit(solution)/shard_map/ppermute | solution.py:393
  128.4 1.3 collective-permute-start.1
  129.8 5.5 %collective-permute-start.9 = (f16[4,336,128]{2,1,0:T(8,128)(2,1)S(1)}, f16[4,336,128]{2,1,0:T(8,128)(2,1)S(1)}, u32[]{:S(2)}, u32[]{:S(2)}) collective-permute-start(f16[4,336,128]{2,1,0:T(8,128)(2,1)S(1)} %convert_element_type.38), channel_id=1, source_target_pairs={{16,1},{17,0},{20,5},{21,4},{24,9},{25,8},{28,13},{29,12},{2,19},{... | collective-permute-start | bytes 1032200 | tf_op jit(solution)/shard_map/ppermute | solution.py:384
  135.4 1.3 collective-permute-start.8
  136.7 3.4 %collective-permute-done.9 = f16[4,336,128]{2,1,0:T(8,128)(2,1)S(1)} collective-permute-done((f16[4,336,128]{2,1,0:T(8,128)(2,1)S(1)}, f16[4,336,128]{2,1,0:T(8,128)(2,1)S(1)}, u32[]{:S(2)}, u32[]{:S(2)}) %collective-permute-start.9) | collective-permute-done | bytes 344096 | tf_op jit(solution)/shard_map/ppermute | solution.py:384
  140.2 3.6 %collective-permute-done.8 = f16[4,336,128]{2,1,0:T(8,128)(2,1)S(1)} collective-permute-done((f16[4,336,128]{2,1,0:T(8,128)(2,1)S(1)}, f16[4,336,128]{2,1,0:T(8,128)(2,1)S(1)}, u32[]{:S(2)}, u32[]{:S(2)}) %collective-permute-start.8) | collective-permute-done | bytes 344096 | tf_op jit(solution)/shard_map/ppermute | solution.py:384
  143.9 0.7 shard_map.26
  144.7 39.6 %collective-permute-done.1.refs_2_ = bf16[272,2048]{1,0:T(8,128)(2,1)S(1)} collective-permute-done((bf16[272,2048]{1,0:T(8,128)(2,1)S(1)}, bf16[272,2048]{1,0:T(8,128)(2,1)S(1)}, u32[]{:S(2)}, u32[]{:S(2)}) %collective-permute-start.1) | collective-permute-done | bytes 1114144 | tf_op jit(solution)/shard_map/ppermute | solution.py:364
  184.2 2.3 %shard_map.27.refs_3_ = f32[8,72,324]{2,1,0:T(8,128)} custom-call(s32[1]{0:T(128)} %bitcast.refs_0_, bf16[4,324,2048]{2,1,0:T(8,128)(2,1)S(1)} %bitcast.24, bf16[272,2048]{1,0:T(8,128)(2,1)S(1)} %collective-permute-done.1.refs_2_, f32[8,324,128]{2,1,0:T(8,128)S(1)} %get-tuple-element.26.refs_3_, f32[4,336,128]{2,1,0:T(8,128)S(1)} %convert_element_type.37.refs_4_.refs_5_, ...), custom_call_target="tpu_custom_call" | custom-call | tf_op jit(solution)/shard_map/pallas_call | solution.py:39
  186.6 3.4 %collective-permute-start.10 = (f32[8,72,324]{2,1,0:T(8,128)}, f32[8,72,324]{2,1,0:T(8,128)}, u32[]{:S(2)}, u32[]{:S(2)}) collective-permute-start(f32[8,72,324]{2,1,0:T(8,128)} %shard_map.27.refs_3_), channel_id=1, source_target_pairs={{2,3},{3,2},{6,7},{7,6},{10,11},{11,10},{14,15},{15,14},{16,17},{1... | collective-permute-start | bytes 2239496 | tf_op jit(solution)/shard_map/ppermute | solution.py:399
  190.0 2.2 collective-permute-start.15
  192.2 0.8 convert_element_type.42
  193.0 2.0 collective-permute-start.14
  195.0 0.1 pad_add_fusion.1.refs_0_
  195.1 2.5 %copy-done.1 = bf16[4,2048,324]{1,2,0:T(8,128)(2,1)S(1)} copy-done((bf16[4,2048,324]{1,2,0:T(8,128)(2,1)S(1)}, bf16[4,2048,324]{1,2,0:T(8,128)(2,1)}, u32[]{:S(2)}) %copy-start.1) | copy-done | bytes 5308440
  197.6 1.5 shard_map.28.refs_5_.refs_1_
  199.1 0.0 collective-permute-done.11.refs_4_
  199.2 0.6 copy-done.5
  199.7 6.8 %shard_map.29.refs_3_.refs_1_ = f32[2,324,8,324]{3,2,1,0:T(8,128)} custom-call(s32[2]{0:T(128)S(1)} %pad_add_fusion.1.refs_0_, f32[8,324,324]{2,1,0:T(8,128)S(1)} %copy-done.5, f32[1744,256]{1,0:T(8,128)} %collective-permute-done.7.refs_4_.refs_2_, f32[4,328,384]{2,1,0:T(8,128)S(1)} %shard_map.25.refs_3_, f32[4,328,384]{2,1,0:T(8,128)} %collective-permute-done.11.refs_4_, ...), custom_call_target="tpu_custom_call" | custom-call | tf_op jit(solution)/shard_map/pallas_call | solution.py:39
  206.5 0.0 collective-permute-done.10.refs_2_
  206.5 3.3 %copy-done.2 = f32[2,324,8,324]{3,2,1,0:T(8,128)S(1)} copy-done((f32[2,324,8,324]{3,2,1,0:T(8,128)S(1)}, f32[2,324,8,324]{3,2,1,0:T(8,128)}, u32[]{:S(2)}) %copy-start.2) | copy-done | bytes 6718488
  209.8 1.8 shard_map.30
  211.6 0.9 copy-done.18
  212.5 0.1 convert_element_type.40
  212.6 0.8 convert_element_type.41
  213.3 1.4 collective-permute-start.13
  214.8 2.0 collective-permute-start.12
  216.8 0.1 pad_add_fusion.refs_0_.s_ref
  216.9 0.0 collective-permute-done.15
  216.9 1.0 convert_element_type.45.refs_8_
  217.9 1.0 convert_element_type.43.refs_7_
  219.0 1.3 copy-done.13
  220.3 1.2 copy-done.19
  221.4 4.7 %shard_map.31.out_in = f32[2,324,8,324]{3,2,1,0:T(8,128)} custom-call(s32[2]{0:T(128)S(1)} %pad_add_fusion.refs_0_.s_ref, f32[2,324,8,324]{3,2,1,0:T(8,128)} %shard_map.29.refs_3_.refs_1_, f32[8,324,128]{2,1,0:T(8,128)S(1)} %copy-done.11, f32[8,324,128]{2,1,0:T(8,128)S(1)} %copy-done.13, ...), custom_call_target="tpu_custom_call", output_to_operand_aliasing={{}: (1, {})} | custom-call | tf_op jit(solution)/shard_map/pallas_call | solution.py:39
  226.2 1.8 convert_element_type.46.straight_ref
  228.0 0.8 convert_element_type.47.across_ref
  228.8 1.2 shard_map.32
  (58 shorter events, 0.3 us)
Async XLA Ops:
  0.0 18.3 %collective-permute-start = (bf16[4,2048,324]{1,0,2:T(4,128)(2,1)}, bf16[4,2048,324]{1,0,2:T(4,128)(2,1)}, u32[]{:S(2)}, u32[]{:S(2)}) collective-permute-start(bf16[4,2048,324]{1,0,2:T(4,128)(2,1)} %param.1), channel_id=1, source_target_pairs={{0,2},{2,0},{4,6},{6,4},{8,10},{10,8},{12,14},{14,12},{16,18},{18,... | collective-permute-start | bytes 15925256 | tf_op jit(solution)/shard_map/ppermute | solution.py:358
  0.0 6.5 %copy-start.23 = (bf16[4,2048,324]{1,0,2:T(4,128)(2,1)S(1)}, bf16[4,2048,324]{1,0,2:T(4,128)(2,1)}, u32[]{:S(2)}) copy-start(bf16[4,2048,324]{1,0,2:T(4,128)(2,1)} %param.1) | copy-start | bytes 15925252
  5.2 74.0 %collective-permute-start.3 = (bf16[4,128,2048]{2,1,0:T(8,128)(2,1)}, bf16[4,128,2048]{2,1,0:T(8,128)(2,1)}, u32[]{:S(2)}, u32[]{:S(2)}) collective-permute-start(bf16[4,128,2048]{2,1,0:T(8,128)(2,1)} %bitcast.12), channel_id=1, source_target_pairs={{0,16},{1,17},{4,20},{5,21},{8,24},{9,25},{12,28},{13,29},{18,2},{... | collective-permute-start | bytes 6291464 | tf_op jit(solution)/shard_map/ppermute | solution.py:364
  11.1 105.5 %collective-permute-start.2 = (bf16[4,128,2048]{2,1,0:T(8,128)(2,1)}, bf16[4,128,2048]{2,1,0:T(8,128)(2,1)S(1)}, u32[]{:S(2)}, u32[]{:S(2)}) collective-permute-start(bf16[4,128,2048]{2,1,0:T(8,128)(2,1)} %slice.13.refs_3_), channel_id=1, source_target_pairs={{0,16},{1,17},{4,20},{5,21},{8,24},{9,25},{12,28},{13,29},{18,2},{... | collective-permute-start | bytes 6291464 | tf_op jit(solution)/shard_map/ppermute | solution.py:364
  13.5 2.4 %copy-start = (bf16[4,2048,324]{1,2,0:T(8,128)(2,1)}, bf16[4,2048,324]{1,2,0:T(8,128)(2,1)S(1)}, u32[]{:S(2)}) copy-start(bf16[4,2048,324]{1,2,0:T(8,128)(2,1)S(1)} %copy.18) | copy-start | bytes 15925252
  15.9 10.3 %slice-start = ((s8[5373952]{0:T(1024)(128)(4,1)}), s8[1179648]{0:T(1024)(128)(4,1)S(1)}, s32[]{:S(2)}) async-start(s8[5373952]{0:T(1024)(128)(4,1)} %bitcast.15), calls=%async_computation | async-start | bytes 2359296
  18.3 8.0 %slice-start.1 = ((s8[5373952]{0:T(1024)(128)(4,1)}), s8[4194304]{0:T(1024)(128)(4,1)S(1)}, s32[]{:S(2)}) async-start(s8[5373952]{0:T(1024)(128)(4,1)} %bitcast.15), calls=%async_computation.1 | async-start | bytes 8388608
  18.3 8.0 %copy-start.16 = (bf16[272,2048]{1,0:T(8,128)(2,1)S(1)}, bf16[272,2048]{1,0:T(8,128)(2,1)}, u32[]{:S(2)}) copy-start(bf16[272,2048]{1,0:T(8,128)(2,1)} %reshape.3.refs_4_) | copy-start | bytes 3342340
  26.2 7.1 %copy-start.3 = (bf16[4,2048,324]{1,2,0:T(8,128)(2,1)S(1)}, bf16[4,2048,324]{1,2,0:T(8,128)(2,1)}, u32[]{:S(2)}) copy-start(bf16[4,2048,324]{1,2,0:T(8,128)(2,1)} %copy.17) | copy-start | bytes 15925252
  38.4 85.4 %collective-permute-start.6 = (f32[1744,256]{1,0:T(8,128)}, f32[1744,256]{1,0:T(8,128)}, u32[]{:S(2)}, u32[]{:S(2)}) collective-permute-start(f32[1744,256]{1,0:T(8,128)} %shard_map.18.refs_3_), channel_id=1, source_target_pairs={{0,1},{1,0},{4,5},{5,4},{8,9},{9,8},{12,13},{13,12},{16,17},{17,16... | collective-permute-start | bytes 5357576 | tf_op jit(solution)/shard_map/ppermute | solution.py:372
  42.0 81.8 %collective-permute-start.7 = (f32[1744,256]{1,0:T(8,128)}, f32[1744,256]{1,0:T(8,128)}, u32[]{:S(2)}, u32[]{:S(2)}) collective-permute-start(f32[1744,256]{1,0:T(8,128)} %shard_map.17.refs_3_), channel_id=1, source_target_pairs={{0,1},{1,0},{2,3},{3,2},{4,5},{5,4},{6,7},{7,6},{8,9},{9,8},{10,11... | collective-permute-start | bytes 5357576 | tf_op jit(solution)/shard_map/ppermute | solution.py:371
  52.7 71.1 %copy-start.4 = (f32[8,324,324]{2,1,0:T(8,128)}, f32[8,324,324]{2,1,0:T(8,128)S(1)}, u32[]{:S(2)}) copy-start(f32[8,324,324]{2,1,0:T(8,128)S(1)} %shard_map.19.refs_3_.refs_1_) | copy-start | bytes 10077700
  82.6 33.2 %collective-permute-start.4 = (f32[8,328,128]{2,1,0:T(8,128)S(1)}, f32[8,328,128]{2,1,0:T(8,128)S(1)}, u32[]{:S(2)}, u32[]{:S(2)}) collective-permute-start(f32[8,328,128]{2,1,0:T(8,128)S(1)} %shard_map.20.refs_3_), channel_id=1, source_target_pairs={{2,3},{3,2},{6,7},{7,6},{10,11},{11,10},{14,15},{15,14},{16,17},{1... | collective-permute-start | bytes 4030472 | tf_op jit(solution)/shard_map/ppermute | solution.py:389
  116.6 1.9 copy-start.10
  116.6 1.9 copy-start.20
  118.5 25.4 %collective-permute-start.5 = (f32[8,328,128]{2,1,0:T(8,128)S(1)}, f32[8,328,128]{2,1,0:T(8,128)S(1)}, u32[]{:S(2)}, u32[]{:S(2)}) collective-permute-start(f32[8,328,128]{2,1,0:T(8,128)S(1)} %shard_map.23.refs_3_), channel_id=1, source_target_pairs={{2,3},{3,2},{6,7},{7,6},{10,11},{11,10},{14,15},{15,14},{16,17},{1... | collective-permute-start | bytes 4030472 | tf_op jit(solution)/shard_map/ppermute | solution.py:389
  123.8 4.7 %copy-start.17 = (bf16[272,2048]{1,0:T(8,128)(2,1)S(1)}, bf16[272,2048]{1,0:T(8,128)(2,1)}, u32[]{:S(2)}) copy-start(bf16[272,2048]{1,0:T(8,128)(2,1)} %reshape.3.refs_4_) | copy-start | bytes 3342340
  123.8 6.0 %copy-start.21 = (f32[4,336,128]{2,1,0:T(8,128)S(1)}, f32[4,336,128]{2,1,0:T(8,128)}, u32[]{:S(2)}) copy-start(f32[4,336,128]{2,1,0:T(8,128)} %copy-done.20) | copy-start | bytes 2064388
  125.8 73.4 %collective-permute-start.11 = (f32[4,328,384]{2,1,0:T(8,128)S(1)}, f32[4,328,384]{2,1,0:T(8,128)}, u32[]{:S(2)}, u32[]{:S(2)}) collective-permute-start(f32[4,328,384]{2,1,0:T(8,128)S(1)} %shard_map.25.refs_3_), channel_id=1, source_target_pairs={{0,2},{1,3},{4,6},{5,7},{8,10},{9,11},{12,14},{13,15},{16,18},{17,... | collective-permute-start | bytes 6045704 | tf_op jit(solution)/shard_map/ppermute | solution.py:393
  128.4 55.8 %collective-permute-start.1 = (bf16[272,2048]{1,0:T(8,128)(2,1)S(1)}, bf16[272,2048]{1,0:T(8,128)(2,1)S(1)}, u32[]{:S(2)}, u32[]{:S(2)}) collective-permute-start(bf16[272,2048]{1,0:T(8,128)(2,1)S(1)} %copy-done.17), channel_id=1, source_target_pairs={{0,16},{1,17},{4,20},{5,21},{8,24},{9,25},{12,28},{13,29},{18,2},{... | collective-permute-start | bytes 3342344 | tf_op jit(solution)/shard_map/ppermute | solution.py:364
  129.8 10.4 %collective-permute-start.9 = (f16[4,336,128]{2,1,0:T(8,128)(2,1)S(1)}, f16[4,336,128]{2,1,0:T(8,128)(2,1)S(1)}, u32[]{:S(2)}, u32[]{:S(2)}) collective-permute-start(f16[4,336,128]{2,1,0:T(8,128)(2,1)S(1)} %convert_element_type.38), channel_id=1, source_target_pairs={{16,1},{17,0},{20,5},{21,4},{24,9},{25,8},{28,13},{29,12},{2,19},{... | collective-permute-start | bytes 1032200 | tf_op jit(solution)/shard_map/ppermute | solution.py:384
  135.4 8.5 %collective-permute-start.8 = (f16[4,336,128]{2,1,0:T(8,128)(2,1)S(1)}, f16[4,336,128]{2,1,0:T(8,128)(2,1)S(1)}, u32[]{:S(2)}, u32[]{:S(2)}) collective-permute-start(f16[4,336,128]{2,1,0:T(8,128)(2,1)S(1)} %convert_element_type.36), channel_id=1, source_target_pairs={{16,0},{17,1},{20,4},{21,5},{24,8},{25,9},{28,12},{29,13},{2,18},{... | collective-permute-start | bytes 1032200 | tf_op jit(solution)/shard_map/ppermute | solution.py:384
  140.2 44.0 %copy-start.6 = (f32[4,336,128]{2,1,0:T(8,128)}, f32[4,336,128]{2,1,0:T(8,128)S(1)}, u32[]{:S(2)}) copy-start(f32[4,336,128]{2,1,0:T(8,128)S(1)} %convert_element_type.39.refs_5_.refs_6_) | copy-start | bytes 2064388
  143.9 40.3 %copy-start.8 = (f32[4,336,128]{2,1,0:T(8,128)}, f32[4,336,128]{2,1,0:T(8,128)S(1)}, u32[]{:S(2)}) copy-start(f32[4,336,128]{2,1,0:T(8,128)S(1)} %convert_element_type.37.refs_4_.refs_5_) | copy-start | bytes 2064388
  144.6 41.9 %copy-start.12 = (f32[8,324,128]{2,1,0:T(8,128)}, f32[8,324,128]{2,1,0:T(8,128)S(1)}, u32[]{:S(2)}) copy-start(f32[8,324,128]{2,1,0:T(8,128)S(1)} %get-tuple-element.26.refs_3_) | copy-start | bytes 3981316
  184.2 2.3 %copy-start.14 = (bf16[272,2048]{1,0:T(8,128)(2,1)}, bf16[272,2048]{1,0:T(8,128)(2,1)S(1)}, u32[]{:S(2)}) copy-start(bf16[272,2048]{1,0:T(8,128)(2,1)S(1)} %collective-permute-done.1.refs_2_) | copy-start | bytes 3342340
  186.6 19.9 %collective-permute-start.10 = (f32[8,72,324]{2,1,0:T(8,128)}, f32[8,72,324]{2,1,0:T(8,128)}, u32[]{:S(2)}, u32[]{:S(2)}) collective-permute-start(f32[8,72,324]{2,1,0:T(8,128)} %shard_map.27.refs_3_), channel_id=1, source_target_pairs={{2,3},{3,2},{6,7},{7,6},{10,11},{11,10},{14,15},{15,14},{16,17},{1... | collective-permute-start | bytes 2239496 | tf_op jit(solution)/shard_map/ppermute | solution.py:399
  190.0 5.1 %copy-start.15 = (bf16[272,2048]{1,0:T(8,128)(2,1)S(1)}, bf16[272,2048]{1,0:T(8,128)(2,1)}, u32[]{:S(2)}) copy-start(bf16[272,2048]{1,0:T(8,128)(2,1)} %copy-done.14) | copy-start | bytes 3342340
  190.0 26.8 %collective-permute-start.15 = (f16[4,336,128]{2,1,0:T(8,128)(2,1)S(1)}, f16[4,336,128]{2,1,0:T(8,128)(2,1)}, u32[]{:S(2)}, u32[]{:S(2)}) collective-permute-start(f16[4,336,128]{2,1,0:T(8,128)(2,1)S(1)} %convert_element_type.44), channel_id=1, source_target_pairs={{16,1},{17,0},{20,5},{21,4},{24,9},{25,8},{28,13},{29,12},{2,19},{... | collective-permute-start | bytes 1032200 | tf_op jit(solution)/shard_map/ppermute | solution.py:384
  193.0 24.9 %collective-permute-start.14 = (f16[4,336,128]{2,1,0:T(8,128)(2,1)}, f16[4,336,128]{2,1,0:T(8,128)(2,1)}, u32[]{:S(2)}, u32[]{:S(2)}) collective-permute-start(f16[4,336,128]{2,1,0:T(8,128)(2,1)} %convert_element_type.42), channel_id=1, source_target_pairs={{16,0},{17,1},{20,4},{21,5},{24,8},{25,9},{28,12},{29,13},{2,18},{... | collective-permute-start | bytes 1032200 | tf_op jit(solution)/shard_map/ppermute | solution.py:384
  195.1 2.5 %copy-start.1 = (bf16[4,2048,324]{1,2,0:T(8,128)(2,1)S(1)}, bf16[4,2048,324]{1,2,0:T(8,128)(2,1)}, u32[]{:S(2)}) copy-start(bf16[4,2048,324]{1,2,0:T(8,128)(2,1)} %copy-done) | copy-start | bytes 15925252
  197.6 2.1 copy-start.5
  206.5 3.3 %copy-start.2 = (f32[2,324,8,324]{3,2,1,0:T(8,128)S(1)}, f32[2,324,8,324]{3,2,1,0:T(8,128)}, u32[]{:S(2)}) copy-start(f32[2,324,8,324]{3,2,1,0:T(8,128)} %shard_map.29.refs_3_.refs_1_) | copy-start | bytes 20155396
  211.5 0.9 copy-start.18
  212.5 6.4 %copy-start.7 = (f32[4,336,128]{2,1,0:T(8,128)S(1)}, f32[4,336,128]{2,1,0:T(8,128)}, u32[]{:S(2)}) copy-start(f32[4,336,128]{2,1,0:T(8,128)} %copy-done.6) | copy-start | bytes 2064388
  212.5 6.4 %copy-start.9 = (f32[4,336,128]{2,1,0:T(8,128)S(1)}, f32[4,336,128]{2,1,0:T(8,128)}, u32[]{:S(2)}) copy-start(f32[4,336,128]{2,1,0:T(8,128)} %copy-done.8) | copy-start | bytes 2064388
  212.5 6.5 %copy-start.11 = (f32[8,324,128]{2,1,0:T(8,128)S(1)}, f32[8,324,128]{2,1,0:T(8,128)}, u32[]{:S(2)}) copy-start(f32[8,324,128]{2,1,0:T(8,128)} %copy-done.10) | copy-start | bytes 3981316
  213.3 12.8 %collective-permute-start.13 = (f16[69,4,324]{2,1,0:T(4,128)(2,1)}, f16[69,4,324]{2,1,0:T(4,128)(2,1)S(1)}, u32[]{:S(2)}, u32[]{:S(2)}) collective-permute-start(f16[69,4,324]{2,1,0:T(4,128)(2,1)} %convert_element_type.41), channel_id=1, source_target_pairs={{16,1},{17,0},{20,5},{21,4},{24,9},{25,8},{28,13},{29,12},{2,19},{... | collective-permute-start | bytes 536552 | tf_op jit(solution)/shard_map/ppermute | solution.py:384
  214.8 11.4 %collective-permute-start.12 = (f16[69,4,324]{2,1,0:T(4,128)(2,1)S(1)}, f16[69,4,324]{2,1,0:T(4,128)(2,1)}, u32[]{:S(2)}, u32[]{:S(2)}) collective-permute-start(f16[69,4,324]{2,1,0:T(4,128)(2,1)S(1)} %convert_element_type.40), channel_id=1, source_target_pairs={{16,0},{17,1},{20,4},{21,5},{24,8},{25,9},{28,12},{29,13},{2,18},{... | collective-permute-start | bytes 536552 | tf_op jit(solution)/shard_map/ppermute | solution.py:384
  216.8 9.3 %copy-start.22 = (s32[2]{0:T(128)}, s32[2]{0:T(128)S(1)}, u32[]{:S(2)}) copy-start(s32[2]{0:T(128)S(1)} %pad_add_fusion.refs_0_.s_ref) | copy-start | bytes 28
  219.0 1.3 copy-start.13
  220.3 1.2 copy-start.19

commit v4 on v3

--- a/solution.py
+++ b/solution.py
@@ -183,18 +183,15 @@
     )(place_in, keep, crossed, share, given)
 
 
-def far_terms(det, own, got, turned, mine, after=()):
+def far_terms(det, own, got, start, width, turned, mine, after=()):
     states, ops, depth = own.shape
     half = states // 2
-    width = got.size // (states * depth)
     rows = ops if turned else width
     tile = (up(ops, 8), width) if turned else (up(width, 8), ops)
 
     def body(x_ref, own_ref, got_ref, out_ref):
-        if turned:
-            every = contract_last(own_ref[0], got_ref[...].reshape(states * width, depth))
-        else:
-            every = contract_last(got_ref[...], own_ref[0])
+        rows_in = got_ref[start : start + states * width]
+        every = contract_last(own_ref[0], rows_in) if turned else contract_last(rows_in, own_ref[0])
         for u in range(states):
             part = slice(u * width, (u + 1) * width)
             out_ref[u, :rows] = every[:, part] if turned else every[part]
@@ -356,54 +353,54 @@
     core = (state & 1).astype(jnp.int32)
 
     partner = lax.ppermute(amplitudes, "state", [(s, s ^ 1) for s in range(blocks)])
-    chunks = [amplitudes[:, :, :LANES].transpose(0, 2, 1)]
-    chunks[0], later = lax.optimization_barrier((chunks[0], amplitudes))
+    first = amplitudes[:, :, :LANES].transpose(0, 2, 1)
+    first, later = lax.optimization_barrier((first, amplitudes))
     own = later.transpose(0, 2, 1)
-    chunks += [own[:, k * LANES : (k + 1) * LANES] for k in range(1, full)]
-    chunks.append(own[:, wide:].reshape(states * (ops - wide), depth))
-    got = [lax.ppermute(c, both, over) for c in chunks]
+    widths = [LANES] * full + [ops - wide]
+    later = [own[:, k * LANES : k * LANES + w].reshape(states * w, depth) for k, w in enumerate(widths) if k]
+    later = jnp.concatenate(later)
+    first = lax.ppermute(first.reshape(states * LANES, depth), both, over)
+    rest = lax.ppermute(later, both, over)
 
     partner, own = lax.optimization_barrier((partner, own))
     partner = partner.transpose(0, 2, 1)
-    crossed = near_send(det, own, partner, False, tuple(chunks[1:]))
+    crossed = near_send(det, own, partner, False, (later,))
     doubled = near_send(det, own, partner, True, (crossed,))
     keep = near_keep(det, own, partner, (doubled,))
     crossed = lax.ppermute(crossed, "det", [(0, 1), (1, 0)])
     doubled = lax.ppermute(doubled, both, first_across)
 
     def partials(k, done):
-        send = far_terms(det, own, got[k], k < full, False, done)
-        return send, far_terms(det, own, got[k], k < full, True, (send,))
-
-    def finished(k, kept, came, done):
-        rows = ops if k < full else ops - wide
-        mine, *pair = far_sum(det, kept, came, states, rows, k < full, done)
+        got, start = (rest, states * LANES * (k - 1)) if k else (first, 0)
+        what = det, own, got, start, widths[k], k < full
+        send = far_terms(*what, False, done)
+        return lax.ppermute(send, both, across), send, far_terms(*what, True, (send,))
+
+    def finished(k, came, kept, done):
+        mine, *pair = far_sum(det, kept, came, states, ops if k < full else widths[k], k < full, done)
         return mine, [v.astype(jnp.float16) for v in pair]
 
     def returned(pair):
         return [lax.ppermute(v, both, to) for v, to in zip(pair, (straight, diagonal))]
 
-    owned, codes, done = [], [], keep
-    for k in range(full):
-        send, kept = partials(k, (done,))
-        came = lax.ppermute(send, both, across)
+    came, _, kept = partials(0, (keep,))
+    mine, pair = finished(0, came, kept, ())
+    owned, codes = [mine], [returned(pair)]
+    share = near_share(det, keep, doubled, states, (mine, crossed))
+    given = lax.ppermute(share, both, to_second)
+    pending, done = [], share
+    for k in range(1, full + 1):
+        came, _, kept = partials(k, (done,))
+        pending.append((came, kept))
         done = kept
-        if k == 1:
-            done = share = near_share(det, keep, doubled, states, (kept, crossed))
-            given = lax.ppermute(share, both, to_second)
-        done, pair = finished(k, kept, came, (done,))
+    done = out = near_sum(jnp.stack([x, core]), keep, crossed, share, given, states, (done,))
+    for k, (came, kept) in enumerate(pending, 1):
+        done, pair = finished(k, came, kept, (done,))
         owned.append(done)
-        codes.append(pair)
-    codes[0] = [v.astype(jnp.float32) for v in returned(codes[0])]
-    send, kept = partials(full, (done, *codes[0]))
-    came = lax.ppermute(send, both, across)
-    out = near_sum(jnp.stack([x, core]), keep, crossed, share, given, states, (kept,))
-    mine, pair = finished(full, kept, came, (out,))
-    owned.append(mine)
-    codes[1:] = [returned(c) for c in codes[1:] + [pair]]
+        codes.append(returned(pair))
 
     at = jnp.stack([x, receiver])
-    codes[1:full] = [[v.astype(jnp.float32) for v in c] for c in codes[1:full]]
+    codes[:full] = [[v.astype(jnp.float32) for v in c] for c in codes[:full]]
     out = place(at, out, owned, codes[:full], states)
     *last, out = lax.optimization_barrier((*codes[full], out))
     return finish(at, out, *[v.astype(jnp.float32) for v in last], states).transpose(0, 2, 1, 3)

time: 231 us -> 209 us (0.905)
  the two profiles are of different devices: /device:TPU:24 before, /device:TPU:0 now
where the time goes in v4:
time: 209 us; the launch traced here: 208 us
  Pallas kernels  61.9 us (30%)
  waiting for transfers between devices  57.4 us (27%)
  starting transfers between devices  40.5 us (19%)
  local copies, waits for them, and re-layouts  31.6 us (15%)
  other arithmetic  16 us (8%)
    pallas_call x15, Pallas kernels, call(): return lambda *operands: kernel(*operands, *after)  58.4 us
    ppermute x1, waiting for transfers between devices, paired(): crossed = lax.ppermute(crossed, 'det', [(0, 1), (1, 0)])  23.1 us
    ppermute x6, waiting for transfers between devices, returned(): lax.ppermute(v, both, to)  17.3 us
    ppermute x1, waiting for transfers between devices, paired(): doubled = lax.ppermute(doubled, both, first_across)  17 us
    ppermute x1, starting transfers between devices, paired(): given = lax.ppermute(share, both, to_second)  15.1 us
    unnamed x38, local copies, waits for them, and re-layouts  12.7 us
    ppermute x6, starting transfers between devices, returned(): lax.ppermute(v, both, to)  8.05 us
    optimization_barrier x1, local copies, waits for them, and re-layouts, paired(): partner, own = lax.optimization_barrier((partner, own))  7.94 us
  transfers between devices with their start and end apart: 15, of which 4 were waited for; matrix products, arithmetic and copies ran while one was open for 15% of the time, Pallas kernels for 28%

profile of v4, /device:TPU:0, one launch (start us, length us, event | category | flops | bytes accessed | tf_op | source)
XLA Modules:
  0.0 208.0 jit_solution(5266049810171081704)
XLA Ops:
  0.0 0.5 collective-permute-start
  0.5 2.8 %slice_bitcast_fusion = bf16[4,128,2048]{2,0,1:T(4,128)(2,1)S(1)} fusion(bf16[4,2048,324]{1,0,2:T(4,128)(2,1)} %param.1), kind=kLoop, calls=%fused_computation.3 | loop fusion | bytes 4194304 | tf_op jit(solution)/shard_map/transpose | solution.py:356
  3.2 2.5 %copy.12 = bf16[4,128,2048]{2,1,0:T(8,128)(2,1)} copy(bf16[4,128,2048]{2,0,1:T(4,128)(2,1)S(1)} %slice_bitcast_fusion) | data formatting | bytes 4194304 | tf_op jit(solution)/shard_map/optimization_barrier | solution.py:357
  5.7 5.6 %collective-permute-start.3 = (bf16[512,2048]{1,0:T(8,128)(2,1)}, bf16[512,2048]{1,0:T(8,128)(2,1)S(1)}, u32[]{:S(2)}, u32[]{:S(2)}) collective-permute-start(bf16[512,2048]{1,0:T(8,128)(2,1)} %bitcast.6), channel_id=1, source_target_pairs={{0,16},{1,17},{4,20},{5,21},{8,24},{9,25},{12,28},{13,29},{18,2},{... | collective-permute-start | bytes 6291464 | tf_op jit(solution)/shard_map/ppermute | solution.py:362
  11.3 2.9 %copy.16 = bf16[4,2048,324]{1,2,0:T(8,128)(2,1)S(1)} copy(bf16[4,2048,324]{1,0,2:T(4,128)(2,1)S(1)} %copy-done.16) | data formatting | bytes 10616832 | tf_op jit(solution)/shard_map/optimization_barrier | solution.py:357
  14.3 0.1 slice.13
  14.3 1.7 slice.12
  16.0 2.4 %copy-done = bf16[4,2048,324]{1,2,0:T(8,128)(2,1)} copy-done((bf16[4,2048,324]{1,2,0:T(8,128)(2,1)}, bf16[4,2048,324]{1,2,0:T(8,128)(2,1)S(1)}, u32[]{:S(2)}) %copy-start) | copy-done | bytes 5308440
  18.4 1.1 reshape.10
  19.5 4.1 %pad_maximum_fusion.refs_3_ = bf16[784,2048]{1,0:T(8,128)(2,1)} fusion(bf16[272,2048]{1,0:T(8,128)(2,1)} %reshape.10, bf16[512,2048]{1,0:T(8,128)(2,1)} %bitcast.30), kind=kLoop, calls=%fused_computation.2 | loop fusion | flops 6422528 | bytes 6422528 | tf_op jit(solution)/shard_map/concatenate | solution.py:361
  23.6 3.0 %collective-permute-start.1 = (bf16[784,2048]{1,0:T(8,128)(2,1)}, bf16[784,2048]{1,0:T(8,128)(2,1)}, u32[]{:S(2)}, u32[]{:S(2)}) collective-permute-start(bf16[784,2048]{1,0:T(8,128)(2,1)} %pad_maximum_fusion.refs_3_), channel_id=1, source_target_pairs={{0,16},{1,17},{4,20},{5,21},{8,24},{9,25},{12,28},{13,29},{18,2},{... | collective-permute-start | bytes 9633800 | tf_op jit(solution)/shard_map/ppermute | solution.py:363
  26.7 0.0 collective-permute-done
  26.7 7.9 %copy.15 = bf16[4,2048,324]{1,2,0:T(8,128)(2,1)} copy(bf16[4,2048,324]{1,0,2:T(4,128)(2,1)} %collective-permute-done) | data formatting | bytes 10616832 | tf_op jit(solution)/shard_map/optimization_barrier | solution.py:365
  34.6 7.1 %shard_map.17.refs_3_ = f32[1744,256]{1,0:T(8,128)} custom-call(s32[1]{0:T(128)} %bitcast.refs_0_, bf16[4,324,2048]{2,1,0:T(8,128)(2,1)S(1)} %bitcast.18, bf16[4,324,2048]{2,1,0:T(8,128)(2,1)} %bitcast.27, bf16[784,2048]{1,0:T(8,128)(2,1)} %pad_maximum_fusion.refs_3_), custom_call_target="tpu_custom_call" | custom-call | tf_op jit(solution)/shard_map/pallas_call | solution.py:39
  41.7 5.1 %shard_map.18.refs_3_ = f32[1744,256]{1,0:T(8,128)} custom-call(s32[1]{0:T(128)} %bitcast.refs_0_, bf16[4,324,2048]{2,1,0:T(8,128)(2,1)S(1)} %bitcast.19, bf16[4,324,2048]{2,1,0:T(8,128)(2,1)S(1)} %bitcast.29, f32[1744,256]{1,0:T(8,128)} %shard_map.17.refs_3_), custom_call_target="tpu_custom_call" | custom-call | tf_op jit(solution)/shard_map/pallas_call | solution.py:39
  46.8 3.6 %collective-permute-start.2 = (f32[1744,256]{1,0:T(8,128)}, f32[1744,256]{1,0:T(8,128)S(1)}, u32[]{:S(2)}, u32[]{:S(2)}) collective-permute-start(f32[1744,256]{1,0:T(8,128)} %shard_map.18.refs_3_), channel_id=1, source_target_pairs={{0,1},{1,0},{4,5},{5,4},{8,9},{9,8},{12,13},{13,12},{16,17},{17,16... | collective-permute-start | bytes 5357576 | tf_op jit(solution)/shard_map/ppermute | solution.py:371
  50.4 0.6 collective-permute-start.5
  51.0 10.1 %shard_map.19.refs_3_.refs_1_ = f32[8,324,324]{2,1,0:T(8,128)S(1)} custom-call(s32[1]{0:T(128)} %bitcast.refs_0_, bf16[4,324,2048]{2,1,0:T(8,128)(2,1)S(1)} %bitcast.20, bf16[4,324,2048]{2,1,0:T(8,128)(2,1)} %bitcast.28, f32[1744,256]{1,0:T(8,128)} %shard_map.18.refs_3_), custom_call_target="tpu_custom_call" | custom-call | tf_op jit(solution)/shard_map/pallas_call | solution.py:39
  61.1 1.8 shard_map.20.refs_3_
  62.9 0.7 collective-permute-start.4
  63.7 1.8 shard_map.21.refs_1_
  65.5 0.7 shard_map.22
  66.3 0.8 copy-done.14
  67.1 17.0 %collective-permute-done.2.refs_2_ = f32[1744,256]{1,0:T(8,128)S(1)} collective-permute-done((f32[1744,256]{1,0:T(8,128)}, f32[1744,256]{1,0:T(8,128)S(1)}, u32[]{:S(2)}, u32[]{:S(2)}) %collective-permute-start.2) | collective-permute-done | bytes 1785888 | tf_op jit(solution)/shard_map/ppermute | solution.py:371
  84.1 1.2 copy-done.10
  85.3 23.1 %collective-permute-done.5.refs_4_.refs_2_ = f32[1744,256]{1,0:T(8,128)} collective-permute-done((f32[1744,256]{1,0:T(8,128)}, f32[1744,256]{1,0:T(8,128)}, u32[]{:S(2)}, u32[]{:S(2)}) %collective-permute-start.5) | collective-permute-done | bytes 1785888 | tf_op jit(solution)/shard_map/ppermute | solution.py:370
  108.4 1.5 copy-done.11
  109.9 0.3 shard_map.23.refs_3_
  110.2 15.1 %collective-permute-start.8 = (f32[4,328,384]{2,1,0:T(8,128)S(1)}, f32[4,328,384]{2,1,0:T(8,128)}, u32[]{:S(2)}, u32[]{:S(2)}) collective-permute-start(f32[4,328,384]{2,1,0:T(8,128)S(1)} %shard_map.23.refs_3_), channel_id=1, source_target_pairs={{0,2},{1,3},{4,6},{5,7},{8,10},{9,11},{12,14},{13,15},{16,18},{17,... | collective-permute-start | bytes 6045704 | tf_op jit(solution)/shard_map/ppermute | solution.py:390
  125.3 4.6 %shard_map.24.refs_3_ = f32[8,328,128]{2,1,0:T(8,128)} custom-call(s32[1]{0:T(128)} %bitcast.refs_0_, bf16[4,324,2048]{2,1,0:T(8,128)(2,1)S(1)} %bitcast.23, bf16[784,2048]{1,0:T(8,128)(2,1)} %collective-permute-done.1.refs_2_, f32[4,328,384]{2,1,0:T(8,128)S(1)} %shard_map.23.refs_3_), custom_call_target="tpu_custom_call" | custom-call | tf_op jit(solution)/shard_map/pallas_call | solution.py:39
  129.9 1.8 collective-permute-start.7
  131.7 3.7 %shard_map.25.refs_3_.refs_1_ = f32[8,328,128]{2,1,0:T(8,128)S(1)} custom-call(s32[1]{0:T(128)} %bitcast.refs_0_, bf16[4,324,2048]{2,1,0:T(8,128)(2,1)S(1)} %bitcast.24, bf16[784,2048]{1,0:T(8,128)(2,1)} %collective-permute-done.1.refs_2_, f32[8,328,128]{2,1,0:T(8,128)} %shard_map.24.refs_3_), custom_call_target="tpu_custom_call" | custom-call | tf_op jit(solution)/shard_map/pallas_call | solution.py:39
  135.5 4.7 %shard_map.26.refs_3_ = f32[8,72,324]{2,1,0:T(8,128)} custom-call(s32[1]{0:T(128)} %bitcast.refs_0_, bf16[4,324,2048]{2,1,0:T(8,128)(2,1)S(1)} %bitcast.25, bf16[784,2048]{1,0:T(8,128)(2,1)} %collective-permute-done.1.refs_2_, f32[8,328,128]{2,1,0:T(8,128)S(1)} %shard_map.25.refs_3_.refs_1_), custom_call_target="tpu_custom_call" | custom-call | tf_op jit(solution)/shard_map/pallas_call | solution.py:39
  140.2 1.6 collective-permute-start.6
  141.8 0.8 convert_element_type.38
  142.6 1.3 collective-permute-start.11
  143.9 0.1 pad_add_fusion.1.refs_0_
  143.9 1.9 convert_element_type.40
  145.8 1.3 collective-permute-start.12
  147.1 0.0 copy-start.1
  147.1 2.5 %copy-done.1 = bf16[4,2048,324]{1,2,0:T(8,128)(2,1)S(1)} copy-done((bf16[4,2048,324]{1,2,0:T(8,128)(2,1)S(1)}, bf16[4,2048,324]{1,2,0:T(8,128)(2,1)}, u32[]{:S(2)}) %copy-start.1) | copy-done | bytes 5308440
  149.6 3.6 %shard_map.27.refs_5_.refs_1_ = f32[8,72,324]{2,1,0:T(8,128)S(1)} custom-call(s32[1]{0:T(128)} %bitcast.refs_0_, bf16[4,324,2048]{2,1,0:T(8,128)(2,1)S(1)} %bitcast.26, bf16[784,2048]{1,0:T(8,128)(2,1)} %collective-permute-done.1.refs_2_, f32[8,72,324]{2,1,0:T(8,128)} %shard_map.26.refs_3_), custom_call_target="tpu_custom_call" | custom-call | tf_op jit(solution)/shard_map/pallas_call | solution.py:39
  153.3 6.5 %shard_map.28.refs_3_.refs_1_ = f32[2,324,8,324]{3,2,1,0:T(8,128)} custom-call(s32[2]{0:T(128)S(1)} %pad_add_fusion.1.refs_0_, f32[8,324,324]{2,1,0:T(8,128)S(1)} %copy-done.5, f32[1744,256]{1,0:T(8,128)} %collective-permute-done.5.refs_4_.refs_2_, f32[4,328,384]{2,1,0:T(8,128)S(1)} %shard_map.23.refs_3_, f32[4,328,384]{2,1,0:T(8,128)} %collective-permute-done.8.refs_4_, ...), custom_call_target="tpu_custom_call" | custom-call | tf_op jit(solution)/shard_map/pallas_call | solution.py:39
  159.8 3.3 %copy-done.2 = f32[2,324,8,324]{3,2,1,0:T(8,128)S(1)} copy-done((f32[2,324,8,324]{3,2,1,0:T(8,128)S(1)}, f32[2,324,8,324]{3,2,1,0:T(8,128)}, u32[]{:S(2)}) %copy-start.2) | copy-done | bytes 6718488
  163.1 2.0 shard_map.29
  165.2 1.3 collective-permute-start.13
  166.5 0.8 convert_element_type.44
  167.3 1.5 collective-permute-start.14
  168.8 1.8 shard_map.30
  170.6 0.9 copy-done.12
  171.5 0.8 convert_element_type.36
  172.3 1.3 collective-permute-start.9
  173.6 0.8 convert_element_type.37
  174.3 1.4 collective-permute-start.10
  175.8 0.1 pad_add_fusion.refs_0_.s_ref
  175.9 1.1 convert_element_type.41.refs_6_
  177.0 13.7 %collective-permute-done.13 = f16[4,336,128]{2,1,0:T(8,128)(2,1)} collective-permute-done((f16[4,336,128]{2,1,0:T(8,128)(2,1)S(1)}, f16[4,336,128]{2,1,0:T(8,128)(2,1)}, u32[]{:S(2)}, u32[]{:S(2)}) %collective-permute-start.13) | collective-permute-done | bytes 344096 | tf_op jit(solution)/shard_map/ppermute | solution.py:384
  190.7 1.0 convert_element_type.43.refs_7_
  191.7 3.6 %collective-permute-done.14 = f16[4,336,128]{2,1,0:T(8,128)(2,1)} collective-permute-done((f16[4,336,128]{2,1,0:T(8,128)(2,1)}, f16[4,336,128]{2,1,0:T(8,128)(2,1)}, u32[]{:S(2)}, u32[]{:S(2)}) %collective-permute-start.14) | collective-permute-done | bytes 344096 | tf_op jit(solution)/shard_map/ppermute | solution.py:384
  195.3 1.0 convert_element_type.45.refs_8_
  196.4 4.3 %shard_map.31.out_in = f32[2,324,8,324]{3,2,1,0:T(8,128)} custom-call(s32[2]{0:T(128)S(1)} %pad_add_fusion.refs_0_.s_ref, f32[2,324,8,324]{3,2,1,0:T(8,128)} %shard_map.28.refs_3_.refs_1_, f32[8,324,128]{2,1,0:T(8,128)S(1)} %copy-done.9, f32[8,324,128]{2,1,0:T(8,128)S(1)} %get-tuple-element.26.refs_3_, ...), custom_call_target="tpu_custom_call", output_to_operand_aliasing={{}: (1, {})} | custom-call | tf_op jit(solution)/shard_map/pallas_call | solution.py:39
  200.7 1.8 convert_element_type.46.straight_ref
  202.5 1.8 convert_element_type.47.across_ref
  204.3 3.5 %shard_map.32 = f32[2,324,8,324]{3,2,1,0:T(8,128)} custom-call(s32[2]{0:T(128)} %copy-done.15, f32[2,324,8,324]{3,2,1,0:T(8,128)} %shard_map.31.out_in, f32[69,4,324]{2,1,0:T(4,128)} %convert_element_type.46.straight_ref, f32[69,4,324]{2,1,0:T(4,128)} %convert_element_type.47.across_ref), custom_call_target="tpu_custom_call", output_to_operand_aliasing={{}: (1, {})} | custom-call | tf_op jit(solution)/shard_map/pallas_call | solution.py:318
  (43 shorter events, 0.2 us)
Async XLA Ops:
  0.0 26.7 %collective-permute-start = (bf16[4,2048,324]{1,0,2:T(4,128)(2,1)}, bf16[4,2048,324]{1,0,2:T(4,128)(2,1)}, u32[]{:S(2)}, u32[]{:S(2)}) collective-permute-start(bf16[4,2048,324]{1,0,2:T(4,128)(2,1)} %param.1), channel_id=1, source_target_pairs={{0,2},{2,0},{4,6},{6,4},{8,10},{10,8},{12,14},{14,12},{16,18},{18,... | collective-permute-start | bytes 15925256 | tf_op jit(solution)/shard_map/ppermute | solution.py:355
  0.5 10.9 %copy-start.16 = (bf16[4,2048,324]{1,0,2:T(4,128)(2,1)S(1)}, bf16[4,2048,324]{1,0,2:T(4,128)(2,1)}, u32[]{:S(2)}) copy-start(bf16[4,2048,324]{1,0,2:T(4,128)(2,1)} %param.1) | copy-start | bytes 15925252
  5.7 55.3 %collective-permute-start.3 = (bf16[512,2048]{1,0:T(8,128)(2,1)}, bf16[512,2048]{1,0:T(8,128)(2,1)S(1)}, u32[]{:S(2)}, u32[]{:S(2)}) collective-permute-start(bf16[512,2048]{1,0:T(8,128)(2,1)} %bitcast.6), channel_id=1, source_target_pairs={{0,16},{1,17},{4,20},{5,21},{8,24},{9,25},{12,28},{13,29},{18,2},{... | collective-permute-start | bytes 6291464 | tf_op jit(solution)/shard_map/ppermute | solution.py:362
  16.0 2.4 %copy-start = (bf16[4,2048,324]{1,2,0:T(8,128)(2,1)}, bf16[4,2048,324]{1,2,0:T(8,128)(2,1)S(1)}, u32[]{:S(2)}) copy-start(bf16[4,2048,324]{1,2,0:T(8,128)(2,1)S(1)} %copy.16) | copy-start | bytes 15925252
  19.5 15.1 %slice-start = ((s8[5373952]{0:T(1024)(128)(4,1)}), s8[1179648]{0:T(1024)(128)(4,1)S(1)}, s32[]{:S(2)}) async-start(s8[5373952]{0:T(1024)(128)(4,1)} %bitcast.16), calls=%async_computation | async-start | bytes 2359296
  23.6 101.7 %collective-permute-start.1 = (bf16[784,2048]{1,0:T(8,128)(2,1)}, bf16[784,2048]{1,0:T(8,128)(2,1)}, u32[]{:S(2)}, u32[]{:S(2)}) collective-permute-start(bf16[784,2048]{1,0:T(8,128)(2,1)} %pad_maximum_fusion.refs_3_), channel_id=1, source_target_pairs={{0,16},{1,17},{4,20},{5,21},{8,24},{9,25},{12,28},{13,29},{18,2},{... | collective-permute-start | bytes 9633800 | tf_op jit(solution)/shard_map/ppermute | solution.py:363
  26.7 8.0 %slice-start.1 = ((s8[5373952]{0:T(1024)(128)(4,1)}), s8[4194304]{0:T(1024)(128)(4,1)S(1)}, s32[]{:S(2)}) async-start(s8[5373952]{0:T(1024)(128)(4,1)} %bitcast.16), calls=%async_computation.1 | async-start | bytes 8388608
  34.6 7.1 %copy-start.3 = (bf16[4,2048,324]{1,2,0:T(8,128)(2,1)S(1)}, bf16[4,2048,324]{1,2,0:T(8,128)(2,1)}, u32[]{:S(2)}) copy-start(bf16[4,2048,324]{1,2,0:T(8,128)(2,1)} %copy.15) | copy-start | bytes 15925252
  46.8 37.3 %collective-permute-start.2 = (f32[1744,256]{1,0:T(8,128)}, f32[1744,256]{1,0:T(8,128)S(1)}, u32[]{:S(2)}, u32[]{:S(2)}) collective-permute-start(f32[1744,256]{1,0:T(8,128)} %shard_map.18.refs_3_), channel_id=1, source_target_pairs={{0,1},{1,0},{4,5},{5,4},{8,9},{9,8},{12,13},{13,12},{16,17},{17,16... | collective-permute-start | bytes 5357576 | tf_op jit(solution)/shard_map/ppermute | solution.py:371
  50.4 58.0 %collective-permute-start.5 = (f32[1744,256]{1,0:T(8,128)}, f32[1744,256]{1,0:T(8,128)}, u32[]{:S(2)}, u32[]{:S(2)}) collective-permute-start(f32[1744,256]{1,0:T(8,128)} %shard_map.17.refs_3_), channel_id=1, source_target_pairs={{0,1},{1,0},{2,3},{3,2},{4,5},{5,4},{6,7},{7,6},{8,9},{9,8},{10,11... | collective-permute-start | bytes 5357576 | tf_op jit(solution)/shard_map/ppermute | solution.py:370
  61.0 47.3 %copy-start.4 = (f32[8,324,324]{2,1,0:T(8,128)}, f32[8,324,324]{2,1,0:T(8,128)S(1)}, u32[]{:S(2)}) copy-start(f32[8,324,324]{2,1,0:T(8,128)S(1)} %shard_map.19.refs_3_.refs_1_) | copy-start | bytes 10077700
  62.9 2.6 %collective-permute-start.4 = (f32[8,328,128]{2,1,0:T(8,128)S(1)}, f32[8,328,128]{2,1,0:T(8,128)S(1)}, u32[]{:S(2)}, u32[]{:S(2)}) collective-permute-start(f32[8,328,128]{2,1,0:T(8,128)S(1)} %shard_map.20.refs_3_), channel_id=1, source_target_pairs={{2,3},{3,2},{6,7},{7,6},{10,11},{11,10},{14,15},{15,14},{16,17},{1... | collective-permute-start | bytes 4030472 | tf_op jit(solution)/shard_map/ppermute | solution.py:377
  66.3 0.8 copy-start.14
  67.1 43.1 %copy-start.8 = (f32[8,324,128]{2,1,0:T(8,128)}, f32[8,324,128]{2,1,0:T(8,128)S(1)}, u32[]{:S(2)}) copy-start(f32[8,324,128]{2,1,0:T(8,128)S(1)} %get-tuple-element.25.refs_3_.refs_2_) | copy-start | bytes 3981316
  84.1 1.2 copy-start.10
  108.4 1.5 copy-start.11
  110.2 43.1 %collective-permute-start.8 = (f32[4,328,384]{2,1,0:T(8,128)S(1)}, f32[4,328,384]{2,1,0:T(8,128)}, u32[]{:S(2)}, u32[]{:S(2)}) collective-permute-start(f32[4,328,384]{2,1,0:T(8,128)S(1)} %shard_map.23.refs_3_), channel_id=1, source_target_pairs={{0,2},{1,3},{4,6},{5,7},{8,10},{9,11},{12,14},{13,15},{16,18},{17,... | collective-permute-start | bytes 6045704 | tf_op jit(solution)/shard_map/ppermute | solution.py:390
  129.9 29.9 %collective-permute-start.7 = (f32[8,328,128]{2,1,0:T(8,128)}, f32[8,328,128]{2,1,0:T(8,128)}, u32[]{:S(2)}, u32[]{:S(2)}) collective-permute-start(f32[8,328,128]{2,1,0:T(8,128)} %shard_map.24.refs_3_), channel_id=1, source_target_pairs={{2,3},{3,2},{6,7},{7,6},{10,11},{11,10},{14,15},{15,14},{16,17},{1... | collective-permute-start | bytes 4030472 | tf_op jit(solution)/shard_map/ppermute | solution.py:377
  135.5 4.7 %copy-start.6 = (f32[8,328,128]{2,1,0:T(8,128)}, f32[8,328,128]{2,1,0:T(8,128)S(1)}, u32[]{:S(2)}) copy-start(f32[8,328,128]{2,1,0:T(8,128)S(1)} %shard_map.25.refs_3_.refs_1_) | copy-start | bytes 4030468
  140.2 28.6 %collective-permute-start.6 = (f32[8,72,324]{2,1,0:T(8,128)}, f32[8,72,324]{2,1,0:T(8,128)}, u32[]{:S(2)}, u32[]{:S(2)}) collective-permute-start(f32[8,72,324]{2,1,0:T(8,128)} %shard_map.26.refs_3_), channel_id=1, source_target_pairs={{2,3},{3,2},{6,7},{7,6},{10,11},{11,10},{14,15},{15,14},{16,17},{1... | collective-permute-start | bytes 2239496 | tf_op jit(solution)/shard_map/ppermute | solution.py:377
  142.6 31.8 %collective-permute-start.11 = (f16[4,336,128]{2,1,0:T(8,128)(2,1)}, f16[4,336,128]{2,1,0:T(8,128)(2,1)S(1)}, u32[]{:S(2)}, u32[]{:S(2)}) collective-permute-start(f16[4,336,128]{2,1,0:T(8,128)(2,1)} %convert_element_type.38), channel_id=1, source_target_pairs={{16,0},{17,1},{20,4},{21,5},{24,8},{25,9},{28,12},{29,13},{2,18},{... | collective-permute-start | bytes 1032200 | tf_op jit(solution)/shard_map/ppermute | solution.py:384
  145.8 30.1 %collective-permute-start.12 = (f16[4,336,128]{2,1,0:T(8,128)(2,1)}, f16[4,336,128]{2,1,0:T(8,128)(2,1)}, u32[]{:S(2)}, u32[]{:S(2)}) collective-permute-start(f16[4,336,128]{2,1,0:T(8,128)(2,1)} %convert_element_type.40), channel_id=1, source_target_pairs={{16,1},{17,0},{20,5},{21,4},{24,9},{25,8},{28,13},{29,12},{2,19},{... | collective-permute-start | bytes 1032200 | tf_op jit(solution)/shard_map/ppermute | solution.py:384
  147.1 2.5 %copy-start.1 = (bf16[4,2048,324]{1,2,0:T(8,128)(2,1)S(1)}, bf16[4,2048,324]{1,2,0:T(8,128)(2,1)}, u32[]{:S(2)}) copy-start(bf16[4,2048,324]{1,2,0:T(8,128)(2,1)} %copy-done) | copy-start | bytes 15925252
  149.6 3.6 %copy-start.5 = (f32[8,324,324]{2,1,0:T(8,128)S(1)}, f32[8,324,324]{2,1,0:T(8,128)}, u32[]{:S(2)}) copy-start(f32[8,324,324]{2,1,0:T(8,128)} %copy-done.4) | copy-start | bytes 10077700
  153.3 6.6 %copy-start.7 = (f32[8,328,128]{2,1,0:T(8,128)S(1)}, f32[8,328,128]{2,1,0:T(8,128)}, u32[]{:S(2)}) copy-start(f32[8,328,128]{2,1,0:T(8,128)} %copy-done.6) | copy-start | bytes 4030468
  159.8 3.3 %copy-start.2 = (f32[2,324,8,324]{3,2,1,0:T(8,128)S(1)}, f32[2,324,8,324]{3,2,1,0:T(8,128)}, u32[]{:S(2)}) copy-start(f32[2,324,8,324]{3,2,1,0:T(8,128)} %shard_map.28.refs_3_.refs_1_) | copy-start | bytes 20155396
  165.2 25.5 %collective-permute-start.13 = (f16[4,336,128]{2,1,0:T(8,128)(2,1)S(1)}, f16[4,336,128]{2,1,0:T(8,128)(2,1)}, u32[]{:S(2)}, u32[]{:S(2)}) collective-permute-start(f16[4,336,128]{2,1,0:T(8,128)(2,1)S(1)} %convert_element_type.42), channel_id=1, source_target_pairs={{16,0},{17,1},{20,4},{21,5},{24,8},{25,9},{28,12},{29,13},{2,18},{... | collective-permute-start | bytes 1032200 | tf_op jit(solution)/shard_map/ppermute | solution.py:384
  167.3 28.1 %collective-permute-start.14 = (f16[4,336,128]{2,1,0:T(8,128)(2,1)}, f16[4,336,128]{2,1,0:T(8,128)(2,1)}, u32[]{:S(2)}, u32[]{:S(2)}) collective-permute-start(f16[4,336,128]{2,1,0:T(8,128)(2,1)} %convert_element_type.44), channel_id=1, source_target_pairs={{16,1},{17,0},{20,5},{21,4},{24,9},{25,8},{28,13},{29,12},{2,19},{... | collective-permute-start | bytes 1032200 | tf_op jit(solution)/shard_map/ppermute | solution.py:384
  170.6 0.9 copy-start.12
  172.3 28.5 %collective-permute-start.9 = (f16[69,4,324]{2,1,0:T(4,128)(2,1)}, f16[69,4,324]{2,1,0:T(4,128)(2,1)}, u32[]{:S(2)}, u32[]{:S(2)}) collective-permute-start(f16[69,4,324]{2,1,0:T(4,128)(2,1)} %convert_element_type.36), channel_id=1, source_target_pairs={{16,0},{17,1},{20,4},{21,5},{24,8},{25,9},{28,12},{29,13},{2,18},{... | collective-permute-start | bytes 536552 | tf_op jit(solution)/shard_map/ppermute | solution.py:384
  174.3 22.0 %copy-start.9 = (f32[8,324,128]{2,1,0:T(8,128)S(1)}, f32[8,324,128]{2,1,0:T(8,128)}, u32[]{:S(2)}) copy-start(f32[8,324,128]{2,1,0:T(8,128)} %copy-done.8) | copy-start | bytes 3981316
  174.3 26.4 %collective-permute-start.10 = (f16[69,4,324]{2,1,0:T(4,128)(2,1)}, f16[69,4,324]{2,1,0:T(4,128)(2,1)}, u32[]{:S(2)}, u32[]{:S(2)}) collective-permute-start(f16[69,4,324]{2,1,0:T(4,128)(2,1)} %convert_element_type.37), channel_id=1, source_target_pairs={{16,1},{17,0},{20,5},{21,4},{24,9},{25,8},{28,13},{29,12},{2,19},{... | collective-permute-start | bytes 536552 | tf_op jit(solution)/shard_map/ppermute | solution.py:384
  175.8 20.6 %copy-start.13 = (f32[8,68,324]{2,1,0:T(8,128)S(1)}, f32[8,68,324]{2,1,0:T(8,128)}, u32[]{:S(2)}) copy-start(f32[8,68,324]{2,1,0:T(8,128)} %copy-done.12) | copy-start | bytes 2115076
  175.8 24.9 %copy-start.15 = (s32[2]{0:T(128)}, s32[2]{0:T(128)S(1)}, u32[]{:S(2)}) copy-start(s32[2]{0:T(128)S(1)} %pad_add_fusion.refs_0_.s_ref) | copy-start | bytes 28

commit v5 on v4

--- a/solution.py
+++ b/solution.py
@@ -9,8 +9,8 @@
 
 LANES = 128
 VMEM_LIMIT = 40 * 2**20
-SQUARE_TOP = 2.0**13
-SMALLEST = 2.0**-120
+POWER, LIFT = 10, 11
+SMALLEST = 2.0**-110
 
 
 def contract_last(left, right):
@@ -183,15 +183,15 @@
     )(place_in, keep, crossed, share, given)
 
 
-def far_terms(det, own, got, start, width, turned, mine, after=()):
+def far_terms(det, own, got, width, turned, mine, after=()):
     states, ops, depth = own.shape
     half = states // 2
     rows = ops if turned else width
     tile = (up(ops, 8), width) if turned else (up(width, 8), ops)
 
     def body(x_ref, own_ref, got_ref, out_ref):
-        rows_in = got_ref[start : start + states * width]
-        every = contract_last(own_ref[0], rows_in) if turned else contract_last(rows_in, own_ref[0])
+        pair = (own_ref[0], got_ref[...]) if turned else (got_ref[...], own_ref[0])
+        every = contract_last(*pair)
         for u in range(states):
             part = slice(u * width, (u + 1) * width)
             out_ref[u, :rows] = every[:, part] if turned else every[part]
@@ -213,7 +213,7 @@
 def far_sum(det, keep, came, states, rows, turned, after=()):
     tiles, padded, lanes = keep.shape
     half = states // 2
-    shape = (half * half, up(rows + 1, 16), lanes) if turned else (rows + 1, half * half, lanes)
+    shape = (half * half, up(rows + 1, 8), lanes)
 
     def body(x_ref, keep_ref, came_ref, own_ref, straight_ref, across_ref):
         x = x_ref[0]
@@ -223,19 +223,14 @@
             own_ref[t] = tile
             top = jnp.maximum(top, jnp.abs(tile))
         exponent = jnp.floor(jnp.log2(jnp.maximum(jnp.max(top, keepdims=True), SMALLEST)))
-        scale = jnp.exp2(-exponent)
+        scale = jnp.exp2(LIFT - exponent)
+        below = jnp.broadcast_to(exponent, (shape[1] - rows, lanes))
         for to_ref, first in ((straight_ref, half * x), (across_ref, half * (1 - x))):
             for a in range(half):
                 for b in range(half):
-                    scaled = own_ref[b * states + first + a] * scale
-                    code = scaled * jnp.abs(scaled) * SQUARE_TOP
-                    if turned:
-                        to_ref[a * half + b, :rows] = code
-                        to_ref[a * half + b, rows:] = jnp.broadcast_to(exponent, (shape[1] - rows, lanes))
-                    else:
-                        to_ref[:rows, a * half + b] = code
-            if not turned:
-                to_ref[rows] = jnp.broadcast_to(exponent, (half * half, lanes))
+                    to_ref[a * half + b] = jnp.concatenate(
+                        [powered(own_ref[b * states + first + a] * scale), below]
+                    ).astype(jnp.bfloat16)
 
     return call(
         body,
@@ -243,14 +238,22 @@
         1,
         [whole((tiles, padded, lanes))] * 2,
         [whole((tiles, rows, lanes)), whole(shape), whole(shape)],
-        [f32(tiles, rows, lanes), f32(*shape), f32(*shape)],
+        [f32(tiles, rows, lanes)] + [jax.ShapeDtypeStruct(shape, jnp.bfloat16)] * 2,
         after,
     )(det, keep, came)
 
 
-def decoded(values, exponent):
-    root = jnp.sqrt(jnp.abs(values)) * (jnp.exp2(exponent) * SQUARE_TOP**-0.5)
-    return jnp.where(values < 0, -root, root)
+def powered(value):
+    square = value * value
+    fourth = square * square
+    return value * jnp.abs(value) * (fourth * fourth)
+
+
+def decoded(code, rows):
+    code = code.astype(jnp.float32)
+    value, exponent = code[:rows], code[rows : rows + 1]
+    root = jnp.exp2(jnp.log2(jnp.abs(value)) * (1 / POWER)) * jnp.exp2(exponent - LIFT)
+    return jnp.where(value < 0, -root, root)
 
 
 def place(place_in, out, owned, came, states, after=()):
@@ -279,8 +282,7 @@
                     for v in range(states):
                         one = a * half + v % half
                         block = jnp.where(v // half == x, straight[one], across[one])
-                        tile = decoded(block[:ops], block[ops : ops + 1])
-                        out_ref[0, :, a * states + v] = tile.T
+                        out_ref[0, :, a * states + v] = decoded(block, ops).T
 
     return call(
         body,
@@ -299,7 +301,7 @@
 
 def finish(place_in, out, straight, across, states):
     _, ops, tiles, _ = out.shape
-    rest, half = straight.shape[0] - 1, states // 2
+    rest, half = ops % LANES, states // 2
 
     def body(s_ref, out_in, straight_ref, across_ref, out_ref, rows_ref, sem):
         x = s_ref[0]
@@ -309,8 +311,8 @@
             for a in range(half):
                 for v in range(states):
                     one = a * half + v % half
-                    block = jnp.where(v // half == x, straight_ref[:, one], across_ref[:, one])
-                    rows_ref[:, a * states + v] = decoded(block[:rest], block[rest:])
+                    block = jnp.where(v // half == x, straight_ref[one], across_ref[one])
+                    rows_ref[:, a * states + v] = decoded(block, rest)
             copy = pltpu.make_async_copy(rows_ref, out_ref.at[0, pl.ds(ops - rest, rest)], sem)
             copy.start()
             copy.wait()
@@ -357,53 +359,48 @@
     first, later = lax.optimization_barrier((first, amplitudes))
     own = later.transpose(0, 2, 1)
     widths = [LANES] * full + [ops - wide]
-    later = [own[:, k * LANES : k * LANES + w].reshape(states * w, depth) for k, w in enumerate(widths) if k]
-    later = jnp.concatenate(later)
-    first = lax.ppermute(first.reshape(states * LANES, depth), both, over)
-    rest = lax.ppermute(later, both, over)
+    chunks = [own[:, k * LANES : k * LANES + w].reshape(states * w, depth) for k, w in enumerate(widths)]
+    chunks[0] = first.reshape(states * LANES, depth)
+    got = [lax.ppermute(c, both, over) for c in chunks]
 
     partner, own = lax.optimization_barrier((partner, own))
     partner = partner.transpose(0, 2, 1)
-    crossed = near_send(det, own, partner, False, (later,))
+    crossed = near_send(det, own, partner, False, tuple(chunks[1:]))
     doubled = near_send(det, own, partner, True, (crossed,))
     keep = near_keep(det, own, partner, (doubled,))
     crossed = lax.ppermute(crossed, "det", [(0, 1), (1, 0)])
     doubled = lax.ppermute(doubled, both, first_across)
 
-    def partials(k, done):
-        got, start = (rest, states * LANES * (k - 1)) if k else (first, 0)
-        what = det, own, got, start, widths[k], k < full
-        send = far_terms(*what, False, done)
-        return lax.ppermute(send, both, across), send, far_terms(*what, True, (send,))
-
-    def finished(k, came, kept, done):
+    def terms(k, mine, done):
+        return far_terms(det, own, got[k], widths[k], k < full, mine, done)
+
+    def finished(k, send, kept, done):
+        came = lax.ppermute(send, both, across)
         mine, *pair = far_sum(det, kept, came, states, ops if k < full else widths[k], k < full, done)
-        return mine, [v.astype(jnp.float16) for v in pair]
-
-    def returned(pair):
-        return [lax.ppermute(v, both, to) for v, to in zip(pair, (straight, diagonal))]
-
-    came, _, kept = partials(0, (keep,))
-    mine, pair = finished(0, came, kept, ())
-    owned, codes = [mine], [returned(pair)]
+        codes.append([lax.ppermute(v, both, to) for v, to in zip(pair, (straight, diagonal))])
+        owned.append(mine)
+        return mine
+
+    owned, codes = [], []
+    send = terms(0, False, (keep,))
+    mine = finished(0, send, terms(0, True, (send,)), ())
     share = near_share(det, keep, doubled, states, (mine, crossed))
     given = lax.ppermute(share, both, to_second)
-    pending, done = [], share
+    sends, kepts, done = [], [], share
     for k in range(1, full + 1):
-        came, _, kept = partials(k, (done,))
-        pending.append((came, kept))
-        done = kept
+        done = terms(k, False, (done, *got[1:]))
+        sends.append(done)
+    for k in range(1, full + 1):
+        done = terms(k, True, (done,))
+        kepts.append(done)
     done = out = near_sum(jnp.stack([x, core]), keep, crossed, share, given, states, (done,))
-    for k, (came, kept) in enumerate(pending, 1):
-        done, pair = finished(k, came, kept, (done,))
-        owned.append(done)
-        codes.append(returned(pair))
+    for k in range(1, full + 1):
+        done = finished(k, sends[k - 1], kepts[k - 1], (done,))
 
     at = jnp.stack([x, receiver])
-    codes[:full] = [[v.astype(jnp.float32) for v in c] for c in codes[:full]]
     out = place(at, out, owned, codes[:full], states)
     *last, out = lax.optimization_barrier((*codes[full], out))
-    return finish(at, out, *[v.astype(jnp.float32) for v in last], states).transpose(0, 2, 1, 3)
+    return finish(at, out, *last, states).transpose(0, 2, 1, 3)
 
 
 def partner_2(value, axis, stride):

time: 209 us -> 193 us (0.923)
  other arithmetic: 16 us -> 0.15 us
  waiting for transfers between devices: 57.4 us -> 47.9 us
  starting transfers between devices: 40.5 us -> 47.9 us
  Pallas kernels: 61.9 us -> 64 us
    convert_element_type x12 -> x0, other arithmetic: 11.7 us -> none  [the longest x6 5 us: finished(): return (mine, [v.astype(jnp.float16) for v in pair])]
    ppermute x1, waiting for transfers between devices: 17 us -> 9.96 us  [paired(): doubled = lax.ppermute(doubled, both, first_across)]
    ppermute x1, starting transfers between devices: 15.1 us -> 20.5 us  [paired(): given = lax.ppermute(share, both, to_second)]
    concatenate x1 -> x0, other arithmetic: 4.08 us -> none  [paired(): later = jnp.concatenate(later)]
    ppermute x1, waiting for transfers between devices: 23.1 us -> 19.1 us  [paired(): crossed = lax.ppermute(crossed, 'det', [(0, 1), (1, 0)])]
    pallas_call x15, Pallas kernels: 58.4 us -> 61.5 us  [call(): return lambda *operands: kernel(*operands, *after)]
    ppermute x11 -> x12, starting transfers between devices: 20.8 us -> 22.9 us  [the longest x3 11 us: paired(): got = [lax.ppermute(c, both, over) for c in chunks]]
    ppermute x11 -> x12, waiting for transfers between devices: 17.3 us -> 18.8 us  [the longest x6 18.8 us: finished(): lax.ppermute(v, both, to)]
  transfers between devices with their start and end apart: 15 -> 16, of which waited for: 4 -> 6; matrix products, arithmetic and copies ran while one was open for 15% -> 10% of each run, Pallas kernels for 28% -> 32%
where the time goes in v5:
time: 193 us; the launch traced here: 192 us
  Pallas kernels  64 us (33%)
  starting transfers between devices  47.9 us (25%)
  waiting for transfers between devices  47.9 us (25%)
  local copies, waits for them, and re-layouts  32 us (17%)
    pallas_call x15, Pallas kernels, call(): return lambda *operands: kernel(*operands, *after)  61.5 us
    ppermute x1, starting transfers between devices, paired(): given = lax.ppermute(share, both, to_second)  20.5 us
    ppermute x1, waiting for transfers between devices, paired(): crossed = lax.ppermute(crossed, 'det', [(0, 1), (1, 0)])  19.1 us
    ppermute x6, waiting for transfers between devices, finished(): lax.ppermute(v, both, to)  18.8 us
    unnamed x36, local copies, waits for them, and re-layouts  13.1 us
    ppermute x3, starting transfers between devices, paired(): got = [lax.ppermute(c, both, over) for c in chunks]  11 us
    ppermute x1, waiting for transfers between devices, paired(): doubled = lax.ppermute(doubled, both, first_across)  9.96 us
    optimization_barrier x1, local copies, waits for them, and re-layouts, paired(): partner, own = lax.optimization_barrier((partner, own))  7.94 us
  transfers between devices with their start and end apart: 16, of which 6 were waited for; matrix products, arithmetic and copies ran while one was open for 10% of the time, Pallas kernels for 32%

profile of v5, /device:TPU:0, one launch (start us, length us, event | category | flops | bytes accessed | tf_op | source)
XLA Modules:
  0.0 192.4 jit_solution(15537373819477922105)
XLA Ops:
  0.0 0.5 collective-permute-start
  0.5 2.8 %slice_bitcast_fusion = bf16[4,128,2048]{2,0,1:T(4,128)(2,1)S(1)} fusion(bf16[4,2048,324]{1,0,2:T(4,128)(2,1)} %param.1), kind=kLoop, calls=%fused_computation.2 | loop fusion | bytes 4194304 | tf_op jit(solution)/shard_map/transpose | solution.py:358
  3.2 2.5 %copy.12 = bf16[4,128,2048]{2,1,0:T(8,128)(2,1)} copy(bf16[4,128,2048]{2,0,1:T(4,128)(2,1)S(1)} %slice_bitcast_fusion) | data formatting | bytes 4194304 | tf_op jit(solution)/shard_map/optimization_barrier | solution.py:359
  5.7 6.8 %collective-permute-start.4 = (bf16[512,2048]{1,0:T(8,128)(2,1)}, bf16[512,2048]{1,0:T(8,128)(2,1)}, u32[]{:S(2)}, u32[]{:S(2)}) collective-permute-start(bf16[512,2048]{1,0:T(8,128)(2,1)} %bitcast.6), channel_id=1, source_target_pairs={{0,16},{1,17},{4,20},{5,21},{8,24},{9,25},{12,28},{13,29},{18,2},{... | collective-permute-start | bytes 6291464 | tf_op jit(solution)/shard_map/ppermute | solution.py:364
  12.5 2.9 %copy.16 = bf16[4,2048,324]{1,2,0:T(8,128)(2,1)S(1)} copy(bf16[4,2048,324]{1,0,2:T(4,128)(2,1)S(1)} %copy-done.15) | data formatting | bytes 10616832 | tf_op jit(solution)/shard_map/optimization_barrier | solution.py:359
  15.4 0.1 slice.12
  15.5 1.7 slice.13
  17.1 2.4 %copy-done = bf16[4,2048,324]{1,2,0:T(8,128)(2,1)} copy-done((bf16[4,2048,324]{1,2,0:T(8,128)(2,1)}, bf16[4,2048,324]{1,2,0:T(8,128)(2,1)S(1)}, u32[]{:S(2)}) %copy-start) | copy-done | bytes 5308440
  19.5 1.1 reshape.9.refs_4_
  20.7 0.0 collective-permute-done
  20.7 7.9 %copy.15 = bf16[4,2048,324]{1,2,0:T(8,128)(2,1)} copy(bf16[4,2048,324]{1,0,2:T(4,128)(2,1)} %collective-permute-done) | data formatting | bytes 10616832 | tf_op jit(solution)/shard_map/optimization_barrier | solution.py:366
  28.6 7.0 %shard_map.17.refs_3_ = f32[1744,256]{1,0:T(8,128)} custom-call(s32[1]{0:T(128)} %bitcast.refs_0_, bf16[4,324,2048]{2,1,0:T(8,128)(2,1)S(1)} %bitcast.18, bf16[4,324,2048]{2,1,0:T(8,128)(2,1)} %bitcast.27, bf16[512,2048]{1,0:T(8,128)(2,1)} %bitcast.4.refs_3_, bf16[272,2048]{1,0:T(8,128)(2,1)} %reshape.9.refs_4_), custom_call_target="tpu_custom_call" | custom-call | tf_op jit(solution)/shard_map/pallas_call | solution.py:39
  35.7 5.1 %shard_map.18.refs_3_ = f32[1744,256]{1,0:T(8,128)} custom-call(s32[1]{0:T(128)} %bitcast.refs_0_, bf16[4,324,2048]{2,1,0:T(8,128)(2,1)S(1)} %bitcast.19, bf16[4,324,2048]{2,1,0:T(8,128)(2,1)S(1)} %bitcast.29, f32[1744,256]{1,0:T(8,128)} %shard_map.17.refs_3_), custom_call_target="tpu_custom_call" | custom-call | tf_op jit(solution)/shard_map/pallas_call | solution.py:39
  40.7 3.4 %collective-permute-start.3 = (f32[1744,256]{1,0:T(8,128)}, f32[1744,256]{1,0:T(8,128)}, u32[]{:S(2)}, u32[]{:S(2)}) collective-permute-start(f32[1744,256]{1,0:T(8,128)} %shard_map.18.refs_3_), channel_id=1, source_target_pairs={{0,1},{1,0},{4,5},{5,4},{8,9},{9,8},{12,13},{13,12},{16,17},{17,16... | collective-permute-start | bytes 5357576 | tf_op jit(solution)/shard_map/ppermute | solution.py:372
  44.1 0.6 collective-permute-start.6
  44.7 1.6 collective-permute-start.2
  46.3 10.1 %shard_map.19.refs_3_.refs_1_ = f32[8,324,324]{2,1,0:T(8,128)S(1)} custom-call(s32[1]{0:T(128)} %bitcast.refs_0_, bf16[4,324,2048]{2,1,0:T(8,128)(2,1)S(1)} %bitcast.20, bf16[4,324,2048]{2,1,0:T(8,128)(2,1)} %bitcast.28, f32[1744,256]{1,0:T(8,128)} %shard_map.18.refs_3_), custom_call_target="tpu_custom_call" | custom-call | tf_op jit(solution)/shard_map/pallas_call | solution.py:39
  56.5 0.0 collective-permute-done.4.refs_2_
  56.5 4.9 %shard_map.20.refs_3_ = f32[8,328,128]{2,1,0:T(8,128)S(1)} custom-call(s32[1]{0:T(128)} %bitcast.refs_0_, bf16[4,324,2048]{2,1,0:T(8,128)(2,1)S(1)} %bitcast.21, bf16[512,2048]{1,0:T(8,128)(2,1)} %collective-permute-done.4.refs_2_, f32[8,324,324]{2,1,0:T(8,128)S(1)} %shard_map.19.refs_3_.refs_1_), custom_call_target="tpu_custom_call" | custom-call | tf_op jit(solution)/shard_map/pallas_call | solution.py:39
  61.4 0.7 collective-permute-start.5
  62.1 2.6 %collective-permute-start.1 = (bf16[272,2048]{1,0:T(8,128)(2,1)}, bf16[272,2048]{1,0:T(8,128)(2,1)S(1)}, u32[]{:S(2)}, u32[]{:S(2)}) collective-permute-start(bf16[272,2048]{1,0:T(8,128)(2,1)} %reshape.9.refs_4_), channel_id=1, source_target_pairs={{0,16},{1,17},{4,20},{5,21},{8,24},{9,25},{12,28},{13,29},{18,2},{... | collective-permute-start | bytes 3342344 | tf_op jit(solution)/shard_map/ppermute | solution.py:364
  64.7 3.4 %shard_map.21.refs_1_ = f32[8,328,128]{2,1,0:T(8,128)S(1)} custom-call(s32[1]{0:T(128)} %bitcast.refs_0_, bf16[4,324,2048]{2,1,0:T(8,128)(2,1)S(1)} %bitcast.22, bf16[512,2048]{1,0:T(8,128)(2,1)} %collective-permute-done.4.refs_2_, f32[8,328,128]{2,1,0:T(8,128)S(1)} %shard_map.20.refs_3_), custom_call_target="tpu_custom_call" | custom-call | tf_op jit(solution)/shard_map/pallas_call | solution.py:39
  68.2 0.0 collective-permute-done.5.refs_2_
  68.2 1.5 shard_map.22
  69.6 10.0 %collective-permute-done.3.refs_2_ = f32[1744,256]{1,0:T(8,128)} collective-permute-done((f32[1744,256]{1,0:T(8,128)}, f32[1744,256]{1,0:T(8,128)}, u32[]{:S(2)}, u32[]{:S(2)}) %collective-permute-start.3) | collective-permute-done | bytes 1785888 | tf_op jit(solution)/shard_map/ppermute | solution.py:372
  79.6 19.1 %collective-permute-done.6.refs_4_.refs_2_ = f32[1744,256]{1,0:T(8,128)} collective-permute-done((f32[1744,256]{1,0:T(8,128)}, f32[1744,256]{1,0:T(8,128)}, u32[]{:S(2)}, u32[]{:S(2)}) %collective-permute-start.6) | collective-permute-done | bytes 1785888 | tf_op jit(solution)/shard_map/ppermute | solution.py:371
  98.7 3.2 %shard_map.23.refs_3_ = f32[4,328,384]{2,1,0:T(8,128)} custom-call(s32[1]{0:T(128)} %bitcast.refs_0_, f32[8,324,324]{2,1,0:T(8,128)S(1)} %shard_map.19.refs_3_.refs_1_, f32[1744,256]{1,0:T(8,128)} %collective-permute-done.3.refs_2_, f32[8,324,128]{2,1,0:T(8,128)S(1)} %get-tuple-element.25.refs_3_.refs_2_, f32[1744,256]{1,0:T(8,128)} %collective-permute-done.6.refs_4_.refs_2_), custom_call_target="tpu_custom_call" | custom-call | tf_op jit(solution)/shard_map/pallas_call | solution.py:39
  101.9 20.5 %collective-permute-start.9 = (f32[4,328,384]{2,1,0:T(8,128)}, f32[4,328,384]{2,1,0:T(8,128)}, u32[]{:S(2)}, u32[]{:S(2)}) collective-permute-start(f32[4,328,384]{2,1,0:T(8,128)} %shard_map.23.refs_3_), channel_id=1, source_target_pairs={{0,2},{1,3},{4,6},{5,7},{8,10},{9,11},{12,14},{13,15},{16,18},{17,... | collective-permute-start | bytes 6045704 | tf_op jit(solution)/shard_map/ppermute | solution.py:388
  122.4 0.0 collective-permute-done.1.refs_5_.refs_2_
  122.4 1.0 copy-done.6
  123.4 0.0 collective-permute-done.2.refs_2_.refs_4_
  123.4 1.2 copy-done.7
  124.7 2.7 %shard_map.24.refs_3_ = f32[8,328,128]{2,1,0:T(8,128)} custom-call(s32[1]{0:T(128)} %bitcast.refs_0_, bf16[4,324,2048]{2,1,0:T(8,128)(2,1)S(1)} %bitcast.23, bf16[512,2048]{1,0:T(8,128)(2,1)S(1)} %collective-permute-done.2.refs_2_.refs_4_, f32[4,328,384]{2,1,0:T(8,128)} %shard_map.23.refs_3_, bf16[512,2048]{1,0:T(8,128)(2,1)S(1)} %collective-permute-done.2.refs_2_.refs_4_, ...), custom_call_target="tpu_custom_call" | custom-call | tf_op jit(solution)/shard_map/pallas_call | solution.py:39
  127.4 1.8 collective-permute-start.8
  129.1 2.3 %shard_map.25.refs_3_ = f32[8,72,324]{2,1,0:T(8,128)} custom-call(s32[1]{0:T(128)} %bitcast.refs_0_, bf16[4,324,2048]{2,1,0:T(8,128)(2,1)S(1)} %bitcast.24, bf16[272,2048]{1,0:T(8,128)(2,1)S(1)} %copy-done.7, f32[8,328,128]{2,1,0:T(8,128)} %shard_map.24.refs_3_, bf16[512,2048]{1,0:T(8,128)(2,1)S(1)} %collective-permute-done.2.refs_2_.refs_4_, ...), custom_call_target="tpu_custom_call" | custom-call | tf_op jit(solution)/shard_map/pallas_call | solution.py:39
  131.5 1.6 collective-permute-start.7
  133.1 1.3 collective-permute-start.12
  134.4 0.1 pad_add_fusion.1.refs_0_
  134.4 1.3 collective-permute-start.13
  135.7 0.0 copy-start.1
  135.7 2.5 %copy-done.1 = bf16[4,2048,324]{1,2,0:T(8,128)(2,1)S(1)} copy-done((bf16[4,2048,324]{1,2,0:T(8,128)(2,1)S(1)}, bf16[4,2048,324]{1,2,0:T(8,128)(2,1)}, u32[]{:S(2)}) %copy-start.1) | copy-done | bytes 5308440
  138.3 1.9 shard_map.26.refs_3_.refs_1_
  140.1 1.6 shard_map.27.refs_5_.refs_1_
  141.7 0.0 collective-permute-done.9.refs_4_
  141.7 0.5 copy-done.5
  142.3 7.4 %shard_map.28.refs_3_.refs_1_ = f32[2,324,8,324]{3,2,1,0:T(8,128)} custom-call(s32[2]{0:T(128)S(1)} %pad_add_fusion.1.refs_0_, f32[8,324,324]{2,1,0:T(8,128)S(1)} %copy-done.5, f32[1744,256]{1,0:T(8,128)} %collective-permute-done.6.refs_4_.refs_2_, f32[4,328,384]{2,1,0:T(8,128)} %shard_map.23.refs_3_, f32[4,328,384]{2,1,0:T(8,128)} %collective-permute-done.9.refs_4_, ...), custom_call_target="tpu_custom_call" | custom-call | tf_op jit(solution)/shard_map/pallas_call | solution.py:39
  149.7 3.3 %copy-done.2 = f32[2,324,8,324]{3,2,1,0:T(8,128)S(1)} copy-done((f32[2,324,8,324]{3,2,1,0:T(8,128)S(1)}, f32[2,324,8,324]{3,2,1,0:T(8,128)}, u32[]{:S(2)}) %copy-start.2) | copy-done | bytes 6718488
  153.0 3.0 %shard_map.29 = (f32[8,324,128]{2,1,0:T(8,128)S(1)}, bf16[4,328,128]{2,1,0:T(8,128)(2,1)}, bf16[4,328,128]{2,1,0:T(8,128)(2,1)}) custom-call(s32[1]{0:T(128)} %bitcast.refs_0_, f32[8,328,128]{2,1,0:T(8,128)S(1)} %shard_map.26.refs_3_.refs_1_, f32[8,328,128]{2,1,0:T(8,128)} %collective-permute-done.8.refs_2_, f32[2,324,8,324]{3,2,1,0:T(8,128)S(1)} %copy-done.2), custom_call_target="tpu_custom_call" | custom-call | tf_op jit(solution)/shard_map/pallas_call | solution.py:39
  156.0 1.4 collective-permute-start.14
  157.4 1.3 collective-permute-start.15
  158.7 2.4 %shard_map.30 = (f32[8,68,324]{2,1,0:T(8,128)S(1)}, bf16[4,72,324]{2,1,0:T(8,128)(2,1)}, bf16[4,72,324]{2,1,0:T(8,128)(2,1)}) custom-call(s32[1]{0:T(128)} %bitcast.refs_0_, f32[8,72,324]{2,1,0:T(8,128)S(1)} %shard_map.27.refs_5_.refs_1_, f32[8,72,324]{2,1,0:T(8,128)} %collective-permute-done.7.refs_2_, f32[8,324,128]{2,1,0:T(8,128)S(1)} %get-tuple-element.26.refs_3_), custom_call_target="tpu_custom_call" | custom-call | tf_op jit(solution)/shard_map/pallas_call | solution.py:39
  161.1 0.9 copy-done.11
  162.0 1.3 collective-permute-start.10
  163.3 0.0 collective-permute-done.12.refs_5_
  163.3 1.3 collective-permute-start.11
  164.6 0.1 pad_add_fusion.refs_0_.s_ref
  164.7 0.0 collective-permute-done.13.refs_6_
  164.7 3.7 %collective-permute-done.14.refs_7_ = bf16[4,328,128]{2,1,0:T(8,128)(2,1)S(1)} collective-permute-done((bf16[4,328,128]{2,1,0:T(8,128)(2,1)}, bf16[4,328,128]{2,1,0:T(8,128)(2,1)S(1)}, u32[]{:S(2)}, u32[]{:S(2)}) %collective-permute-start.14) | collective-permute-done | bytes 335904 | tf_op jit(solution)/shard_map/ppermute | solution.py:380
  168.4 4.5 %collective-permute-done.15.refs_8_ = bf16[4,328,128]{2,1,0:T(8,128)(2,1)S(1)} collective-permute-done((bf16[4,328,128]{2,1,0:T(8,128)(2,1)}, bf16[4,328,128]{2,1,0:T(8,128)(2,1)S(1)}, u32[]{:S(2)}, u32[]{:S(2)}) %collective-permute-start.15) | collective-permute-done | bytes 335904 | tf_op jit(solution)/shard_map/ppermute | solution.py:380
  172.9 1.2 copy-done.12
  174.1 5.0 %shard_map.31.out_in = f32[2,324,8,324]{3,2,1,0:T(8,128)} custom-call(s32[2]{0:T(128)S(1)} %pad_add_fusion.refs_0_.s_ref, f32[2,324,8,324]{3,2,1,0:T(8,128)} %shard_map.28.refs_3_.refs_1_, f32[8,324,128]{2,1,0:T(8,128)S(1)} %copy-done.10, f32[8,324,128]{2,1,0:T(8,128)S(1)} %get-tuple-element.26.refs_3_, ...), custom_call_target="tpu_custom_call", output_to_operand_aliasing={{}: (1, {})} | custom-call | tf_op jit(solution)/shard_map/pallas_call | solution.py:39
  179.2 7.3 %collective-permute-done.10.straight_ref = bf16[4,72,324]{2,1,0:T(8,128)(2,1)} collective-permute-done((bf16[4,72,324]{2,1,0:T(8,128)(2,1)}, bf16[4,72,324]{2,1,0:T(8,128)(2,1)}, u32[]{:S(2)}, u32[]{:S(2)}) %collective-permute-start.10) | collective-permute-done | bytes 186656 | tf_op jit(solution)/shard_map/ppermute | solution.py:380
  186.4 3.3 %collective-permute-done.11.across_ref = bf16[4,72,324]{2,1,0:T(8,128)(2,1)} collective-permute-done((bf16[4,72,324]{2,1,0:T(8,128)(2,1)}, bf16[4,72,324]{2,1,0:T(8,128)(2,1)}, u32[]{:S(2)}, u32[]{:S(2)}) %collective-permute-start.11) | collective-permute-done | bytes 186656 | tf_op jit(solution)/shard_map/ppermute | solution.py:380
  189.7 2.5 %shard_map.32 = f32[2,324,8,324]{3,2,1,0:T(8,128)} custom-call(s32[2]{0:T(128)} %copy-done.13, f32[2,324,8,324]{3,2,1,0:T(8,128)} %shard_map.31.out_in, bf16[4,72,324]{2,1,0:T(8,128)(2,1)} %collective-permute-done.10.straight_ref, bf16[4,72,324]{2,1,0:T(8,128)(2,1)} %collective-permute-done.11.across_ref), custom_call_target="tpu_custom_call", output_to_operand_aliasing={{}: (1, {})} | custom-call | tf_op jit(solution)/shard_map/pallas_call | solution.py:320
  (30 shorter events, 0.1 us)
Async XLA Ops:
  0.0 20.7 %collective-permute-start = (bf16[4,2048,324]{1,0,2:T(4,128)(2,1)}, bf16[4,2048,324]{1,0,2:T(4,128)(2,1)}, u32[]{:S(2)}, u32[]{:S(2)}) collective-permute-start(bf16[4,2048,324]{1,0,2:T(4,128)(2,1)} %param.1), channel_id=1, source_target_pairs={{0,2},{2,0},{4,6},{6,4},{8,10},{10,8},{12,14},{14,12},{16,18},{18,... | collective-permute-start | bytes 15925256 | tf_op jit(solution)/shard_map/ppermute | solution.py:357
  0.5 12.0 %copy-start.15 = (bf16[4,2048,324]{1,0,2:T(4,128)(2,1)S(1)}, bf16[4,2048,324]{1,0,2:T(4,128)(2,1)}, u32[]{:S(2)}) copy-start(bf16[4,2048,324]{1,0,2:T(4,128)(2,1)} %param.1) | copy-start | bytes 15925252
  5.7 50.8 %collective-permute-start.4 = (bf16[512,2048]{1,0:T(8,128)(2,1)}, bf16[512,2048]{1,0:T(8,128)(2,1)}, u32[]{:S(2)}, u32[]{:S(2)}) collective-permute-start(bf16[512,2048]{1,0:T(8,128)(2,1)} %bitcast.6), channel_id=1, source_target_pairs={{0,16},{1,17},{4,20},{5,21},{8,24},{9,25},{12,28},{13,29},{18,2},{... | collective-permute-start | bytes 6291464 | tf_op jit(solution)/shard_map/ppermute | solution.py:364
  17.1 2.4 %copy-start = (bf16[4,2048,324]{1,2,0:T(8,128)(2,1)}, bf16[4,2048,324]{1,2,0:T(8,128)(2,1)S(1)}, u32[]{:S(2)}) copy-start(bf16[4,2048,324]{1,2,0:T(8,128)(2,1)S(1)} %copy.16) | copy-start | bytes 15925252
  19.5 9.1 %slice-start = ((s8[5373952]{0:T(1024)(128)(4,1)}), s8[1179648]{0:T(1024)(128)(4,1)S(1)}, s32[]{:S(2)}) async-start(s8[5373952]{0:T(1024)(128)(4,1)} %bitcast.16), calls=%async_computation | async-start | bytes 2359296
  20.6 8.0 %slice-start.1 = ((s8[5373952]{0:T(1024)(128)(4,1)}), s8[4194304]{0:T(1024)(128)(4,1)S(1)}, s32[]{:S(2)}) async-start(s8[5373952]{0:T(1024)(128)(4,1)} %bitcast.16), calls=%async_computation.1 | async-start | bytes 8388608
  28.6 7.1 %copy-start.3 = (bf16[4,2048,324]{1,2,0:T(8,128)(2,1)S(1)}, bf16[4,2048,324]{1,2,0:T(8,128)(2,1)}, u32[]{:S(2)}) copy-start(bf16[4,2048,324]{1,2,0:T(8,128)(2,1)} %copy.15) | copy-start | bytes 15925252
  40.7 38.9 %collective-permute-start.3 = (f32[1744,256]{1,0:T(8,128)}, f32[1744,256]{1,0:T(8,128)}, u32[]{:S(2)}, u32[]{:S(2)}) collective-permute-start(f32[1744,256]{1,0:T(8,128)} %shard_map.18.refs_3_), channel_id=1, source_target_pairs={{0,1},{1,0},{4,5},{5,4},{8,9},{9,8},{12,13},{13,12},{16,17},{17,16... | collective-permute-start | bytes 5357576 | tf_op jit(solution)/shard_map/ppermute | solution.py:372
  44.1 54.6 %collective-permute-start.6 = (f32[1744,256]{1,0:T(8,128)}, f32[1744,256]{1,0:T(8,128)}, u32[]{:S(2)}, u32[]{:S(2)}) collective-permute-start(f32[1744,256]{1,0:T(8,128)} %shard_map.17.refs_3_), channel_id=1, source_target_pairs={{0,1},{1,0},{2,3},{3,2},{4,5},{5,4},{6,7},{7,6},{8,9},{9,8},{10,11... | collective-permute-start | bytes 5357576 | tf_op jit(solution)/shard_map/ppermute | solution.py:371
  44.7 78.7 %collective-permute-start.2 = (bf16[512,2048]{1,0:T(8,128)(2,1)}, bf16[512,2048]{1,0:T(8,128)(2,1)S(1)}, u32[]{:S(2)}, u32[]{:S(2)}) collective-permute-start(bf16[512,2048]{1,0:T(8,128)(2,1)} %bitcast.4.refs_3_), channel_id=1, source_target_pairs={{0,16},{1,17},{4,20},{5,21},{8,24},{9,25},{12,28},{13,29},{18,2},{... | collective-permute-start | bytes 6291464 | tf_op jit(solution)/shard_map/ppermute | solution.py:364
  56.4 42.3 %copy-start.4 = (f32[8,324,324]{2,1,0:T(8,128)}, f32[8,324,324]{2,1,0:T(8,128)S(1)}, u32[]{:S(2)}) copy-start(f32[8,324,324]{2,1,0:T(8,128)S(1)} %shard_map.19.refs_3_.refs_1_) | copy-start | bytes 10077700
  61.4 6.8 %collective-permute-start.5 = (f32[8,328,128]{2,1,0:T(8,128)S(1)}, f32[8,328,128]{2,1,0:T(8,128)S(1)}, u32[]{:S(2)}, u32[]{:S(2)}) collective-permute-start(f32[8,328,128]{2,1,0:T(8,128)S(1)} %shard_map.20.refs_3_), channel_id=1, source_target_pairs={{2,3},{3,2},{6,7},{7,6},{10,11},{11,10},{14,15},{15,14},{16,17},{1... | collective-permute-start | bytes 4030472 | tf_op jit(solution)/shard_map/ppermute | solution.py:378
  62.1 60.3 %collective-permute-start.1 = (bf16[272,2048]{1,0:T(8,128)(2,1)}, bf16[272,2048]{1,0:T(8,128)(2,1)S(1)}, u32[]{:S(2)}, u32[]{:S(2)}) collective-permute-start(bf16[272,2048]{1,0:T(8,128)(2,1)} %reshape.9.refs_4_), channel_id=1, source_target_pairs={{0,16},{1,17},{4,20},{5,21},{8,24},{9,25},{12,28},{13,29},{18,2},{... | collective-permute-start | bytes 3342344 | tf_op jit(solution)/shard_map/ppermute | solution.py:364
  69.6 32.3 %copy-start.9 = (f32[8,324,128]{2,1,0:T(8,128)}, f32[8,324,128]{2,1,0:T(8,128)S(1)}, u32[]{:S(2)}) copy-start(f32[8,324,128]{2,1,0:T(8,128)S(1)} %get-tuple-element.25.refs_3_.refs_2_) | copy-start | bytes 3981316
  69.6 57.7 %copy-start.14 = (bf16[4,328,128]{2,1,0:T(8,128)(2,1)}, bf16[4,328,128]{2,1,0:T(8,128)(2,1)S(1)}, u32[]{:S(2)}) copy-start(bf16[4,328,128]{2,1,0:T(8,128)(2,1)S(1)} %get-tuple-element.31) | copy-start | bytes 1007620
  101.9 39.8 %collective-permute-start.9 = (f32[4,328,384]{2,1,0:T(8,128)}, f32[4,328,384]{2,1,0:T(8,128)}, u32[]{:S(2)}, u32[]{:S(2)}) collective-permute-start(f32[4,328,384]{2,1,0:T(8,128)} %shard_map.23.refs_3_), channel_id=1, source_target_pairs={{0,2},{1,3},{4,6},{5,7},{8,10},{9,11},{12,14},{13,15},{16,18},{17,... | collective-permute-start | bytes 6045704 | tf_op jit(solution)/shard_map/ppermute | solution.py:388
  122.4 1.0 copy-start.6
  123.4 1.2 copy-start.7
  127.4 22.3 %collective-permute-start.8 = (f32[8,328,128]{2,1,0:T(8,128)}, f32[8,328,128]{2,1,0:T(8,128)}, u32[]{:S(2)}, u32[]{:S(2)}) collective-permute-start(f32[8,328,128]{2,1,0:T(8,128)} %shard_map.24.refs_3_), channel_id=1, source_target_pairs={{2,3},{3,2},{6,7},{7,6},{10,11},{11,10},{14,15},{15,14},{16,17},{1... | collective-permute-start | bytes 4030472 | tf_op jit(solution)/shard_map/ppermute | solution.py:378
  131.5 27.2 %collective-permute-start.7 = (f32[8,72,324]{2,1,0:T(8,128)}, f32[8,72,324]{2,1,0:T(8,128)}, u32[]{:S(2)}, u32[]{:S(2)}) collective-permute-start(f32[8,72,324]{2,1,0:T(8,128)} %shard_map.25.refs_3_), channel_id=1, source_target_pairs={{2,3},{3,2},{6,7},{7,6},{10,11},{11,10},{14,15},{15,14},{16,17},{1... | collective-permute-start | bytes 2239496 | tf_op jit(solution)/shard_map/ppermute | solution.py:378
  133.1 30.3 %collective-permute-start.12 = (bf16[4,328,128]{2,1,0:T(8,128)(2,1)}, bf16[4,328,128]{2,1,0:T(8,128)(2,1)}, u32[]{:S(2)}, u32[]{:S(2)}) collective-permute-start(bf16[4,328,128]{2,1,0:T(8,128)(2,1)} %get-tuple-element.30), channel_id=1, source_target_pairs={{16,0},{17,1},{20,4},{21,5},{24,8},{25,9},{28,12},{29,13},{2,18},{... | collective-permute-start | bytes 1007624 | tf_op jit(solution)/shard_map/ppermute | solution.py:380
  134.4 30.3 %collective-permute-start.13 = (bf16[4,328,128]{2,1,0:T(8,128)(2,1)}, bf16[4,328,128]{2,1,0:T(8,128)(2,1)}, u32[]{:S(2)}, u32[]{:S(2)}) collective-permute-start(bf16[4,328,128]{2,1,0:T(8,128)(2,1)} %copy-done.14), channel_id=1, source_target_pairs={{16,1},{17,0},{20,5},{21,4},{24,9},{25,8},{28,13},{29,12},{2,19},{... | collective-permute-start | bytes 1007624 | tf_op jit(solution)/shard_map/ppermute | solution.py:380
  135.7 2.5 %copy-start.1 = (bf16[4,2048,324]{1,2,0:T(8,128)(2,1)S(1)}, bf16[4,2048,324]{1,2,0:T(8,128)(2,1)}, u32[]{:S(2)}) copy-start(bf16[4,2048,324]{1,2,0:T(8,128)(2,1)} %copy-done) | copy-start | bytes 15925252
  138.2 1.9 copy-start.8
  140.1 2.1 %copy-start.5 = (f32[8,324,324]{2,1,0:T(8,128)S(1)}, f32[8,324,324]{2,1,0:T(8,128)}, u32[]{:S(2)}) copy-start(f32[8,324,324]{2,1,0:T(8,128)} %copy-done.4) | copy-start | bytes 10077700
  149.7 3.3 %copy-start.2 = (f32[2,324,8,324]{3,2,1,0:T(8,128)S(1)}, f32[2,324,8,324]{3,2,1,0:T(8,128)}, u32[]{:S(2)}) copy-start(f32[2,324,8,324]{3,2,1,0:T(8,128)} %shard_map.28.refs_3_.refs_1_) | copy-start | bytes 20155396
  156.0 17.0 %copy-start.10 = (f32[8,324,128]{2,1,0:T(8,128)S(1)}, f32[8,324,128]{2,1,0:T(8,128)}, u32[]{:S(2)}) copy-start(f32[8,324,128]{2,1,0:T(8,128)} %copy-done.9) | copy-start | bytes 3981316
  156.0 12.5 %collective-permute-start.14 = (bf16[4,328,128]{2,1,0:T(8,128)(2,1)}, bf16[4,328,128]{2,1,0:T(8,128)(2,1)S(1)}, u32[]{:S(2)}, u32[]{:S(2)}) collective-permute-start(bf16[4,328,128]{2,1,0:T(8,128)(2,1)} %get-tuple-element.32), channel_id=1, source_target_pairs={{16,0},{17,1},{20,4},{21,5},{24,8},{25,9},{28,12},{29,13},{2,18},{... | collective-permute-start | bytes 1007624 | tf_op jit(solution)/shard_map/ppermute | solution.py:380
  157.4 15.6 %collective-permute-start.15 = (bf16[4,328,128]{2,1,0:T(8,128)(2,1)}, bf16[4,328,128]{2,1,0:T(8,128)(2,1)S(1)}, u32[]{:S(2)}, u32[]{:S(2)}) collective-permute-start(bf16[4,328,128]{2,1,0:T(8,128)(2,1)} %get-tuple-element.33), channel_id=1, source_target_pairs={{16,1},{17,0},{20,5},{21,4},{24,9},{25,8},{28,13},{29,12},{2,19},{... | collective-permute-start | bytes 1007624 | tf_op jit(solution)/shard_map/ppermute | solution.py:380
  161.1 0.9 copy-start.11
  162.0 24.4 %collective-permute-start.10 = (bf16[4,72,324]{2,1,0:T(8,128)(2,1)}, bf16[4,72,324]{2,1,0:T(8,128)(2,1)}, u32[]{:S(2)}, u32[]{:S(2)}) collective-permute-start(bf16[4,72,324]{2,1,0:T(8,128)(2,1)} %get-tuple-element.27), channel_id=1, source_target_pairs={{16,0},{17,1},{20,4},{21,5},{24,8},{25,9},{28,12},{29,13},{2,18},{... | collective-permute-start | bytes 559880 | tf_op jit(solution)/shard_map/ppermute | solution.py:380
  163.3 26.4 %collective-permute-start.11 = (bf16[4,72,324]{2,1,0:T(8,128)(2,1)}, bf16[4,72,324]{2,1,0:T(8,128)(2,1)}, u32[]{:S(2)}, u32[]{:S(2)}) collective-permute-start(bf16[4,72,324]{2,1,0:T(8,128)(2,1)} %get-tuple-element.28), channel_id=1, source_target_pairs={{16,1},{17,0},{20,5},{21,4},{24,9},{25,8},{28,13},{29,12},{2,19},{... | collective-permute-start | bytes 559880 | tf_op jit(solution)/shard_map/ppermute | solution.py:380
  164.7 14.4 %copy-start.13 = (s32[2]{0:T(128)}, s32[2]{0:T(128)S(1)}, u32[]{:S(2)}) copy-start(s32[2]{0:T(128)S(1)} %pad_add_fusion.refs_0_.s_ref) | copy-start | bytes 28
  172.9 1.2 copy-start.12

commit v6 on v5

--- a/solution.py
+++ b/solution.py
@@ -8,7 +8,7 @@
 from jax.sharding import PartitionSpec as P
 
 LANES = 128
-VMEM_LIMIT = 40 * 2**20
+VMEM_LIMIT = 20 * 2**20
 POWER, LIFT = 10, 11
 SMALLEST = 2.0**-110
 
@@ -22,17 +22,19 @@
 
     def waiting(*refs):
         first = scalars + len(in_specs)
-        body(*refs[:first], *refs[first + idle :])
-
+        body(*refs[:first], *refs[first + idle : -1])
+        refs[-1][...] = jnp.zeros_like(refs[-1])
+
+    token = (8, LANES)
     kernel = pl.pallas_call(
         waiting,
         grid_spec=pltpu.PrefetchScalarGridSpec(
             num_scalar_prefetch=scalars,
             grid=grid,
             in_specs=in_specs + [pl.BlockSpec(memory_space=pl.ANY)] * idle,
-            out_specs=out_specs,
+            out_specs=[*out_specs, whole(token)],
         ),
-        out_shape=out_shape,
+        out_shape=[*out_shape, f32(*token)],
         input_output_aliases=aliases,
         compiler_params=pltpu.CompilerParams(vmem_limit_bytes=VMEM_LIMIT),
     )
@@ -48,7 +50,7 @@
 
 
 def whole(shape):
-    return pl.BlockSpec(shape, lambda *_: (0,) * len(shape))
+    return pl.BlockSpec(shape, lambda *_: (0,) * len(shape), pipeline_mode=pl.Buffered(1))
 
 
 class Packing:
@@ -104,8 +106,8 @@
             pl.BlockSpec((1, ops, depth), lambda t, x: (half * (1 - x[0]) + t // half, 0, 0)),
             pl.BlockSpec((1, ops, depth), lambda t, x: (second(x) + t % half, 0, 0)),
         ],
-        whole(packing.shape),
-        f32(*packing.shape),
+        [whole(packing.shape)],
+        [f32(*packing.shape)],
         after,
     )(det, own, partner)
 
@@ -125,8 +127,8 @@
             pl.BlockSpec((1, ops, depth), lambda a, b, x: (half * x[0] + a, 0, 0)),
             pl.BlockSpec((1, ops, depth), lambda a, b, x: (b, 0, 0)),
         ],
-        pl.BlockSpec((1, ops, ops), lambda a, b, x: (a * states + b, 0, 0)),
-        f32(half * states, ops, ops),
+        [pl.BlockSpec((1, ops, ops), lambda a, b, x: (a * states + b, 0, 0))],
+        [f32(half * states, ops, ops)],
         after,
     )(det, own, partner)
 
@@ -144,7 +146,7 @@
                 tile_ref[t, rows, columns] = keep_ref[kept, rows, columns] + values
 
     return call(
-        body, (1,), 1, [whole(keep.shape), whole(packing.shape)], whole(shape), f32(*shape), after
+        body, (1,), 1, [whole(keep.shape), whole(packing.shape)], [whole(shape)], [f32(*shape)], after
     )(det, keep, doubled)
 
 
@@ -177,8 +179,8 @@
         (1,),
         1,
         [whole(keep.shape), whole(packing.shape), whole(share.shape), whole(given.shape)],
-        pl.BlockSpec((1, ops, tiles, ops), lambda i, s: (1, 0, 0, 0)),
-        f32(2, ops, tiles, ops),
+        [pl.BlockSpec((1, ops, tiles, ops), lambda i, s: (1, 0, 0, 0), pipeline_mode=pl.Buffered(1))],
+        [f32(2, ops, tiles, ops)],
         after,
     )(place_in, keep, crossed, share, given)
 
@@ -204,8 +206,8 @@
         (half,),
         1,
         [pl.BlockSpec((1, ops, depth), state), whole(got.shape)],
-        pl.BlockSpec((states, *tile), lambda b, x: (b, 0, 0)),
-        f32(half * states, *tile),
+        [pl.BlockSpec((states, *tile), lambda b, x: (b, 0, 0))],
+        [f32(half * states, *tile)],
         after,
     )(det, own, got)
 
@@ -292,8 +294,8 @@
         + [pl.BlockSpec((tiles, LANES, LANES), lambda i, s: (0, i, 0))] * full
         + [pl.BlockSpec((tiles, ops - wide, LANES), lambda i, s: (0, 0, i))]
         + [whole(code)] * (2 * full),
-        pl.BlockSpec((1, LANES, tiles, ops), lambda i, s: (0, i, 0, 0)),
-        f32(*out.shape),
+        [pl.BlockSpec((1, LANES, tiles, ops), lambda i, s: (0, i, 0, 0))],
+        [f32(*out.shape)],
         after,
         {1: 0},
     )(place_in, out, *owned, *[c for pair in came for c in pair])
@@ -356,49 +358,53 @@
 
     partner = lax.ppermute(amplitudes, "state", [(s, s ^ 1) for s in range(blocks)])
     first = amplitudes[:, :, :LANES].transpose(0, 2, 1)
-    first, later = lax.optimization_barrier((first, amplitudes))
+    first, later = lax.optimization_barrier((first.reshape(states * LANES, depth), amplitudes))
+    got = [lax.ppermute(first, both, over)]
     own = later.transpose(0, 2, 1)
-    widths = [LANES] * full + [ops - wide]
-    chunks = [own[:, k * LANES : k * LANES + w].reshape(states * w, depth) for k, w in enumerate(widths)]
-    chunks[0] = first.reshape(states * LANES, depth)
-    got = [lax.ppermute(c, both, over) for c in chunks]
-
     partner, own = lax.optimization_barrier((partner, own))
     partner = partner.transpose(0, 2, 1)
-    crossed = near_send(det, own, partner, False, tuple(chunks[1:]))
-    doubled = near_send(det, own, partner, True, (crossed,))
-    keep = near_keep(det, own, partner, (doubled,))
+
+    crossed, token = near_send(det, own, partner, False, (first,))
     crossed = lax.ppermute(crossed, "det", [(0, 1), (1, 0)])
+    doubled, token = near_send(det, own, partner, True, (token,))
     doubled = lax.ppermute(doubled, both, first_across)
-
-    def terms(k, mine, done):
+    whole_own, token = lax.optimization_barrier((own, token))
+    widths = [LANES] * full + [ops - wide]
+    for k in range(1, full + 1):
+        chunk = whole_own[:, k * LANES : k * LANES + widths[k]].reshape(states * widths[k], depth)
+        chunk, token = lax.optimization_barrier((chunk, token))
+        got.append(lax.ppermute(chunk, both, over))
+    keep, token = near_keep(det, own, partner, (token,))
+    def terms(k, mine, *done):
         return far_terms(det, own, got[k], widths[k], k < full, mine, done)
 
-    def finished(k, send, kept, done):
+    def finished(k, send, kept, *done):
         came = lax.ppermute(send, both, across)
-        mine, *pair = far_sum(det, kept, came, states, ops if k < full else widths[k], k < full, done)
+        rows = ops if k < full else widths[k]
+        mine, *pair, token = far_sum(det, kept, came, states, rows, k < full, done)
         codes.append([lax.ppermute(v, both, to) for v, to in zip(pair, (straight, diagonal))])
         owned.append(mine)
-        return mine
+        return token
 
     owned, codes = [], []
-    send = terms(0, False, (keep,))
-    mine = finished(0, send, terms(0, True, (send,)), ())
-    share = near_share(det, keep, doubled, states, (mine, crossed))
+    kept, token = terms(0, True, token)
+    share, token = near_share(det, keep, doubled, states, (token, crossed))
     given = lax.ppermute(share, both, to_second)
-    sends, kepts, done = [], [], share
+    send, token = terms(0, False, token)
+    out, token = near_sum(jnp.stack([x, core]), keep, crossed, share, given, states, (token,))
+    token = finished(0, send, kept, token)
+    sends, kepts = [], []
     for k in range(1, full + 1):
-        done = terms(k, False, (done, *got[1:]))
-        sends.append(done)
+        send, token = terms(k, False, token)
+        sends.append(send)
     for k in range(1, full + 1):
-        done = terms(k, True, (done,))
-        kepts.append(done)
-    done = out = near_sum(jnp.stack([x, core]), keep, crossed, share, given, states, (done,))
+        kept, token = terms(k, True, token)
+        kepts.append(kept)
     for k in range(1, full + 1):
-        done = finished(k, sends[k - 1], kepts[k - 1], (done,))
+        token = finished(k, sends[k - 1], kepts[k - 1], token)
 
     at = jnp.stack([x, receiver])
-    out = place(at, out, owned, codes[:full], states)
+    out, token = place(at, out, owned, codes[:full], states, (token,))
     *last, out = lax.optimization_barrier((*codes[full], out))
     return finish(at, out, *last, states).transpose(0, 2, 1, 3)
 

time: 193 us -> 201 us (1.041)
  waiting for transfers between devices: 47.9 us -> 77.8 us
  starting transfers between devices: 47.9 us -> 33.5 us
  Pallas kernels: 64 us -> 57.5 us
    ppermute x6, waiting for transfers between devices: 18.8 us -> 46.6 us  [finished(): lax.ppermute(v, both, to)]
    ppermute x1, starting transfers between devices: 20.5 us -> 2.59 us  [paired(): given = lax.ppermute(share, both, to_second)]
    pallas_call x15, Pallas kernels: 61.5 us -> 55 us  [call(): return lambda *operands: kernel(*operands, *after)]
    ppermute x3, starting transfers between devices: 11 us -> 15.3 us  [the longest x2 8.53 us: paired(): got.append(lax.ppermute(chunk, both, over))]
    unnamed x36 -> x34, local copies, waits for them, and re-layouts: 13.1 us -> 10.6 us
    transpose x1 -> x2, local copies, waits for them, and re-layouts: 2.76 us -> 5.03 us  [paired(): first = amplitudes[:, :, :LANES].transpose(0, 2, 1)]
    ppermute x1, waiting for transfers between devices: 9.96 us -> 12 us  [paired(): doubled = lax.ppermute(doubled, both, first_across)]
    optimization_barrier x2 -> x1, local copies, waits for them, and re-layouts: 5.36 us -> 5.41 us  [paired(): lax.optimization_barrier((first.reshape(states * LANES, depth), amplitudes))]
  transfers between devices with their start and end apart: 16 -> 16, of which waited for: 6 -> 8; matrix products, arithmetic and copies ran while one was open for 10% -> 10% of each run, Pallas kernels for 32% -> 27%
where the time goes in v6:
time: 201 us
  waiting for transfers between devices  77.8 us (39%)
  Pallas kernels  57.5 us (29%)
  starting transfers between devices  33.5 us (17%)
  local copies, waits for them, and re-layouts  31.3 us (16%)
    pallas_call x15, Pallas kernels, call(): return lambda *operands: kernel(*operands, *after)  55 us
    ppermute x6, waiting for transfers between devices, finished(): lax.ppermute(v, both, to)  46.6 us
    ppermute x1, waiting for transfers between devices, paired(): crossed = lax.ppermute(crossed, 'det', [(0, 1), (1, 0)])  19.1 us
    ppermute x1, waiting for transfers between devices, paired(): doubled = lax.ppermute(doubled, both, first_across)  12 us
    unnamed x34, local copies, waits for them, and re-layouts  10.6 us
    ppermute x2, starting transfers between devices, paired(): got.append(lax.ppermute(chunk, both, over))  8.53 us
    ppermute x6, starting transfers between devices, finished(): lax.ppermute(v, both, to)  7.94 us
    optimization_barrier x1, local copies, waits for them, and re-layouts, paired(): partner, own = lax.optimization_barrier((partner, own))  7.35 us
  transfers between devices with their start and end apart: 16, of which 8 were waited for; matrix products, arithmetic and copies ran while one was open for 10% of the time, Pallas kernels for 27%

profile of v6, /device:TPU:0, one launch (start us, length us, event | category | flops | bytes accessed | tf_op | source)
XLA Modules:
  0.0 200.6 jit_solution(6979949861905250214)
XLA Ops:
  0.0 0.5 collective-permute-start
  0.5 2.6 %slice_bitcast_fusion = bf16[4,128,2048]{2,0,1:T(4,128)(2,1)S(1)} fusion(bf16[4,2048,324]{1,0,2:T(4,128)(2,1)} %param.1), kind=kLoop, calls=%fused_computation.2 | loop fusion | bytes 4194304 | tf_op jit(solution)/shard_map/transpose | solution.py:360
  3.1 2.4 %copy.10 = bf16[4,128,2048]{2,1,0:T(8,128)(2,1)} copy(bf16[4,128,2048]{2,0,1:T(4,128)(2,1)S(1)} %slice_bitcast_fusion) | data formatting | bytes 4194304 | tf_op jit(solution)/shard_map/transpose | solution.py:360
  5.5 6.8 %collective-permute-start.3 = (bf16[512,2048]{1,0:T(8,128)(2,1)}, bf16[512,2048]{1,0:T(8,128)(2,1)}, u32[]{:S(2)}, u32[]{:S(2)}) collective-permute-start(bf16[512,2048]{1,0:T(8,128)(2,1)} %bitcast.3.refs_3_), channel_id=1, source_target_pairs={{0,16},{1,17},{4,20},{5,21},{8,24},{9,25},{12,28},{13,29},{18,2},{... | collective-permute-start | bytes 6291464 | tf_op jit(solution)/shard_map/ppermute | solution.py:362
  12.3 5.4 %copy.16 = bf16[4,2048,324]{1,2,0:T(8,128)(2,1)S(1)} copy(bf16[4,2048,324]{1,0,2:T(4,128)(2,1)} %param.1) | data formatting | bytes 10616832 | tf_op jit(solution)/shard_map/optimization_barrier | solution.py:361
  17.7 0.0 collective-permute-done
  17.7 7.4 %copy.15 = bf16[4,2048,324]{1,2,0:T(8,128)(2,1)S(1)} copy(bf16[4,2048,324]{1,0,2:T(4,128)(2,1)} %collective-permute-done) | data formatting | bytes 10616832 | tf_op jit(solution)/shard_map/optimization_barrier | solution.py:364
  25.1 0.0 copy-start.2
  25.1 5.1 %shard_map.17 = (f32[1744,256]{1,0:T(8,128)}, f32[8,128]{1,0:T(8,128)S(1)}) custom-call(s32[1]{0:T(128)} %bitcast.refs_0_, bf16[4,324,2048]{2,1,0:T(8,128)(2,1)S(1)} %bitcast.14, bf16[4,324,2048]{2,1,0:T(8,128)(2,1)S(1)} %bitcast.29, bf16[512,2048]{1,0:T(8,128)(2,1)} %bitcast.3.refs_3_), custom_call_target="tpu_custom_call" | custom-call | tf_op jit(solution)/shard_map/pallas_call | solution.py:41
  30.2 5.1 %shard_map.18 = (f32[1744,256]{1,0:T(8,128)}, f32[8,128]{1,0:T(8,128)S(1)}) custom-call(s32[1]{0:T(128)} %bitcast.refs_0_, bf16[4,324,2048]{2,1,0:T(8,128)(2,1)S(1)} %bitcast.15, bf16[4,324,2048]{2,1,0:T(8,128)(2,1)S(1)} %bitcast.30, f32[8,128]{1,0:T(8,128)S(1)} %get-tuple-element.57.refs_3_), custom_call_target="tpu_custom_call" | custom-call | tf_op jit(solution)/shard_map/pallas_call | solution.py:41
  35.3 3.4 %collective-permute-start.4 = (f32[1744,256]{1,0:T(8,128)}, f32[1744,256]{1,0:T(8,128)}, u32[]{:S(2)}, u32[]{:S(2)}) collective-permute-start(f32[1744,256]{1,0:T(8,128)} %get-tuple-element.68), channel_id=1, source_target_pairs={{0,1},{1,0},{4,5},{5,4},{8,9},{9,8},{12,13},{13,12},{16,17},{17,16... | collective-permute-start | bytes 5357576 | tf_op jit(solution)/shard_map/ppermute | solution.py:370
  38.7 0.6 collective-permute-start.5
  39.3 1.6 slice.11
  40.9 1.6 collective-permute-start.2
  42.5 0.1 slice.10
  42.6 1.2 reshape.10
  43.7 2.5 %copy-done.1 = bf16[4,2048,324]{1,2,0:T(8,128)(2,1)S(1)} copy-done((bf16[4,2048,324]{1,2,0:T(8,128)(2,1)S(1)}, bf16[4,2048,324]{1,2,0:T(8,128)(2,1)}, u32[]{:S(2)}) %copy-start.1) | copy-done | bytes 5308440
  46.3 2.5 %copy-done.3 = bf16[4,2048,324]{1,2,0:T(8,128)(2,1)S(1)} copy-done((bf16[4,2048,324]{1,2,0:T(8,128)(2,1)S(1)}, bf16[4,2048,324]{1,2,0:T(8,128)(2,1)}, u32[]{:S(2)}) %copy-start.3) | copy-done | bytes 5308440
  48.8 7.2 %shard_map.19 = (f32[8,324,324]{2,1,0:T(8,128)S(1)}, f32[8,128]{1,0:T(8,128)S(1)}) custom-call(s32[1]{0:T(128)} %bitcast.refs_0_, bf16[4,324,2048]{2,1,0:T(8,128)(2,1)S(1)} %bitcast.18, bf16[4,324,2048]{2,1,0:T(8,128)(2,1)S(1)} %bitcast.31, f32[8,128]{1,0:T(8,128)S(1)} %get-tuple-element.64.refs_3_), custom_call_target="tpu_custom_call" | custom-call | tf_op jit(solution)/shard_map/pallas_call | solution.py:41
  56.0 0.0 copy-start.4
  56.0 0.0 collective-permute-done.3.refs_2_
  56.0 0.0 slice-start
  56.0 5.0 %shard_map.20 = (f32[8,328,128]{2,1,0:T(8,128)S(1)}, f32[8,128]{1,0:T(8,128)S(1)}) custom-call(s32[1]{0:T(128)} %bitcast.refs_0_, bf16[4,324,2048]{2,1,0:T(8,128)(2,1)S(1)} %bitcast.19, bf16[512,2048]{1,0:T(8,128)(2,1)} %collective-permute-done.3.refs_2_, f32[8,128]{1,0:T(8,128)S(1)} %get-tuple-element.65.refs_3_), custom_call_target="tpu_custom_call" | custom-call | tf_op jit(solution)/shard_map/pallas_call | solution.py:41
  61.0 1.1 copy-done.8
  62.1 12.0 %collective-permute-done.4.refs_2_ = f32[1744,256]{1,0:T(8,128)} collective-permute-done((f32[1744,256]{1,0:T(8,128)}, f32[1744,256]{1,0:T(8,128)}, u32[]{:S(2)}, u32[]{:S(2)}) %collective-permute-start.4) | collective-permute-done | bytes 1785888 | tf_op jit(solution)/shard_map/ppermute | solution.py:370
  74.1 19.1 %collective-permute-done.5.refs_4_.refs_2_ = f32[1744,256]{1,0:T(8,128)} collective-permute-done((f32[1744,256]{1,0:T(8,128)}, f32[1744,256]{1,0:T(8,128)}, u32[]{:S(2)}, u32[]{:S(2)}) %collective-permute-start.5) | collective-permute-done | bytes 1785888 | tf_op jit(solution)/shard_map/ppermute | solution.py:368
  93.2 3.2 %shard_map.21 = (f32[4,328,384]{2,1,0:T(8,128)}, f32[8,128]{1,0:T(8,128)S(1)}) custom-call(s32[1]{0:T(128)} %bitcast.refs_0_, f32[8,324,324]{2,1,0:T(8,128)S(1)} %get-tuple-element.67.refs_1_, f32[1744,256]{1,0:T(8,128)} %collective-permute-done.4.refs_2_, f32[8,128]{1,0:T(8,128)S(1)} %get-tuple-element.69.refs_3_, ...), custom_call_target="tpu_custom_call" | custom-call | tf_op jit(solution)/shard_map/pallas_call | solution.py:41
  96.5 2.6 %collective-permute-start.7 = (f32[4,328,384]{2,1,0:T(8,128)}, f32[4,328,384]{2,1,0:T(8,128)}, u32[]{:S(2)}, u32[]{:S(2)}) collective-permute-start(f32[4,328,384]{2,1,0:T(8,128)} %get-tuple-element.73.refs_3_), channel_id=1, source_target_pairs={{0,2},{1,3},{4,6},{5,7},{8,10},{9,11},{12,14},{13,15},{16,18},{17,... | collective-permute-start | bytes 6045704 | tf_op jit(solution)/shard_map/ppermute | solution.py:392
  99.1 4.3 %shard_map.22 = (f32[8,328,128]{2,1,0:T(8,128)}, f32[8,128]{1,0:T(8,128)S(1)}) custom-call(s32[1]{0:T(128)} %bitcast.refs_0_, bf16[4,324,2048]{2,1,0:T(8,128)(2,1)S(1)} %bitcast.22, bf16[512,2048]{1,0:T(8,128)(2,1)} %collective-permute-done.3.refs_2_, f32[8,128]{1,0:T(8,128)S(1)} %get-tuple-element.71.refs_3_), custom_call_target="tpu_custom_call" | custom-call | tf_op jit(solution)/shard_map/pallas_call | solution.py:41
  103.3 1.7 collective-permute-start.6
  105.1 6.9 %collective-permute-start.1 = (bf16[272,2048]{1,0:T(8,128)(2,1)}, bf16[272,2048]{1,0:T(8,128)(2,1)S(1)}, u32[]{:S(2)}, u32[]{:S(2)}) collective-permute-start(bf16[272,2048]{1,0:T(8,128)(2,1)} %reshape.10), channel_id=1, source_target_pairs={{0,16},{1,17},{4,20},{5,21},{8,24},{9,25},{12,28},{13,29},{18,2},{... | collective-permute-start | bytes 3342344 | tf_op jit(solution)/shard_map/ppermute | solution.py:376
  112.0 0.1 pad_add_fusion.1.refs_0_
  112.1 0.0 collective-permute-done.7.refs_4_
  112.1 2.3 %copy-done.5 = f32[8,324,324]{2,1,0:T(8,128)S(1)} copy-done((f32[8,324,324]{2,1,0:T(8,128)S(1)}, f32[8,324,324]{2,1,0:T(8,128)}, u32[]{:S(2)}) %copy-start.5) | copy-done | bytes 3359256
  114.4 7.2 %shard_map.23 = (f32[2,324,8,324]{3,2,1,0:T(8,128)}, f32[8,128]{1,0:T(8,128)S(1)}) custom-call(s32[2]{0:T(128)S(1)} %pad_add_fusion.1.refs_0_, f32[8,324,324]{2,1,0:T(8,128)S(1)} %copy-done.5, f32[1744,256]{1,0:T(8,128)} %collective-permute-done.5.refs_4_.refs_2_, f32[4,328,384]{2,1,0:T(8,128)} %get-tuple-element.73.refs_3_, ...), custom_call_target="tpu_custom_call" | custom-call | tf_op jit(solution)/shard_map/pallas_call | solution.py:41
  121.6 0.0 collective-permute-done.6.refs_2_
  121.6 3.0 %shard_map.24 = (f32[8,324,128]{2,1,0:T(8,128)S(1)}, bf16[4,328,128]{2,1,0:T(8,128)(2,1)S(1)}, bf16[4,328,128]{2,1,0:T(8,128)(2,1)}, f32[8,128]{1,0:T(8,128)S(1)}) custom-call(s32[1]{0:T(128)} %bitcast.refs_0_, f32[8,328,128]{2,1,0:T(8,128)S(1)} %copy-done.9, f32[8,328,128]{2,1,0:T(8,128)} %collective-permute-done.6.refs_2_, ...), custom_call_target="tpu_custom_call" | custom-call | tf_op jit(solution)/shard_map/pallas_call | solution.py:41
  124.7 1.8 shard_map.25
  126.6 0.7 collective-permute-start.9
  127.3 0.0 collective-permute-done.1.refs_2_
  127.3 1.6 shard_map.26
  128.9 0.7 collective-permute-start.8
  129.6 1.3 collective-permute-start.12
  130.9 1.5 collective-permute-start.13
  132.4 1.8 shard_map.27
  134.3 1.6 shard_map.28
  135.9 0.0 collective-permute-done.9.refs_2_
  135.9 1.7 shard_map.29
  137.7 1.3 collective-permute-start.14
  138.9 1.3 collective-permute-start.15
  140.3 1.3 shard_map.30
  141.5 1.0 copy-done.10
  142.5 1.3 collective-permute-start.10
  143.8 1.7 collective-permute-done.12.refs_5_
  145.5 1.3 collective-permute-start.11
  146.8 0.1 pad_add_fusion.refs_0_.s_ref
  146.9 3.3 %collective-permute-done.13.refs_6_ = bf16[4,328,128]{2,1,0:T(8,128)(2,1)} collective-permute-done((bf16[4,328,128]{2,1,0:T(8,128)(2,1)}, bf16[4,328,128]{2,1,0:T(8,128)(2,1)}, u32[]{:S(2)}, u32[]{:S(2)}) %collective-permute-start.13) | collective-permute-done | bytes 335904 | tf_op jit(solution)/shard_map/ppermute | solution.py:385
  150.2 16.9 %collective-permute-done.14.refs_7_ = bf16[4,328,128]{2,1,0:T(8,128)(2,1)S(1)} collective-permute-done((bf16[4,328,128]{2,1,0:T(8,128)(2,1)}, bf16[4,328,128]{2,1,0:T(8,128)(2,1)S(1)}, u32[]{:S(2)}, u32[]{:S(2)}) %collective-permute-start.14) | collective-permute-done | bytes 335904 | tf_op jit(solution)/shard_map/ppermute | solution.py:385
  167.1 14.2 %collective-permute-done.15.refs_8_ = bf16[4,328,128]{2,1,0:T(8,128)(2,1)} collective-permute-done((bf16[4,328,128]{2,1,0:T(8,128)(2,1)}, bf16[4,328,128]{2,1,0:T(8,128)(2,1)}, u32[]{:S(2)}, u32[]{:S(2)}) %collective-permute-start.15) | collective-permute-done | bytes 335904 | tf_op jit(solution)/shard_map/ppermute | solution.py:385
  181.3 1.2 copy-done.11
  182.5 5.0 %shard_map.31 = (f32[2,324,8,324]{3,2,1,0:T(8,128)}, f32[8,128]{1,0:T(8,128)}) custom-call(s32[2]{0:T(128)S(1)} %pad_add_fusion.refs_0_.s_ref, f32[2,324,8,324]{3,2,1,0:T(8,128)} %get-tuple-element.88.refs_1_, f32[8,324,128]{2,1,0:T(8,128)S(1)} %copy-done.7, f32[8,324,128]{2,1,0:T(8,128)S(1)} %get-tuple-element.90.refs_3_, ...), custom_call_target="tpu_custom_call", output_to_operand_aliasing={{0}: (1, {})} | custom-call | tf_op jit(solution)/shard_map/pallas_call | solution.py:41
  187.5 1.2 collective-permute-done.10.straight_ref
  188.8 9.2 %collective-permute-done.11.across_ref = bf16[4,72,324]{2,1,0:T(8,128)(2,1)} collective-permute-done((bf16[4,72,324]{2,1,0:T(8,128)(2,1)}, bf16[4,72,324]{2,1,0:T(8,128)(2,1)}, u32[]{:S(2)}, u32[]{:S(2)}) %collective-permute-start.11) | collective-permute-done | bytes 186656 | tf_op jit(solution)/shard_map/ppermute | solution.py:385
  198.0 2.5 %shard_map.32 = f32[2,324,8,324]{3,2,1,0:T(8,128)} custom-call(s32[2]{0:T(128)} %copy-done.12, f32[2,324,8,324]{3,2,1,0:T(8,128)} %get-tuple-element.98.out_in, bf16[4,72,324]{2,1,0:T(8,128)(2,1)} %collective-permute-done.10.straight_ref, bf16[4,72,324]{2,1,0:T(8,128)(2,1)} %collective-permute-done.11.across_ref), custom_call_target="tpu_custom_call", output_to_operand_aliasing={{}: (1, {})} | custom-call | tf_op jit(solution)/shard_map/pallas_call | solution.py:322
  (29 shorter events, 0.1 us)
Async XLA Ops:
  0.0 17.7 %collective-permute-start = (bf16[4,2048,324]{1,0,2:T(4,128)(2,1)}, bf16[4,2048,324]{1,0,2:T(4,128)(2,1)}, u32[]{:S(2)}, u32[]{:S(2)}) collective-permute-start(bf16[4,2048,324]{1,0,2:T(4,128)(2,1)} %param.1), channel_id=1, source_target_pairs={{0,2},{2,0},{4,6},{6,4},{8,10},{10,8},{12,14},{14,12},{16,18},{18,... | collective-permute-start | bytes 15925256 | tf_op jit(solution)/shard_map/ppermute | solution.py:359
  5.5 50.5 %collective-permute-start.3 = (bf16[512,2048]{1,0:T(8,128)(2,1)}, bf16[512,2048]{1,0:T(8,128)(2,1)}, u32[]{:S(2)}, u32[]{:S(2)}) collective-permute-start(bf16[512,2048]{1,0:T(8,128)(2,1)} %bitcast.3.refs_3_), channel_id=1, source_target_pairs={{0,16},{1,17},{4,20},{5,21},{8,24},{9,25},{12,28},{13,29},{18,2},{... | collective-permute-start | bytes 6291464 | tf_op jit(solution)/shard_map/ppermute | solution.py:362
  17.7 24.8 %copy-start = (bf16[4,2048,324]{1,2,0:T(8,128)(2,1)}, bf16[4,2048,324]{1,2,0:T(8,128)(2,1)S(1)}, u32[]{:S(2)}) copy-start(bf16[4,2048,324]{1,2,0:T(8,128)(2,1)S(1)} %copy.16) | copy-start | bytes 15925252
  25.1 5.1 %copy-start.2 = (bf16[4,2048,324]{1,2,0:T(8,128)(2,1)}, bf16[4,2048,324]{1,2,0:T(8,128)(2,1)S(1)}, u32[]{:S(2)}) copy-start(bf16[4,2048,324]{1,2,0:T(8,128)(2,1)S(1)} %copy.15) | copy-start | bytes 15925252
  35.3 38.8 %collective-permute-start.4 = (f32[1744,256]{1,0:T(8,128)}, f32[1744,256]{1,0:T(8,128)}, u32[]{:S(2)}, u32[]{:S(2)}) collective-permute-start(f32[1744,256]{1,0:T(8,128)} %get-tuple-element.68), channel_id=1, source_target_pairs={{0,1},{1,0},{4,5},{5,4},{8,9},{9,8},{12,13},{13,12},{16,17},{17,16... | collective-permute-start | bytes 5357576 | tf_op jit(solution)/shard_map/ppermute | solution.py:370
  38.7 54.6 %collective-permute-start.5 = (f32[1744,256]{1,0:T(8,128)}, f32[1744,256]{1,0:T(8,128)}, u32[]{:S(2)}, u32[]{:S(2)}) collective-permute-start(f32[1744,256]{1,0:T(8,128)} %get-tuple-element.70), channel_id=1, source_target_pairs={{0,1},{1,0},{2,3},{3,2},{4,5},{5,4},{6,7},{7,6},{8,9},{9,8},{10,11... | collective-permute-start | bytes 5357576 | tf_op jit(solution)/shard_map/ppermute | solution.py:368
  40.9 83.8 %collective-permute-start.2 = (bf16[512,2048]{1,0:T(8,128)(2,1)}, bf16[512,2048]{1,0:T(8,128)(2,1)S(1)}, u32[]{:S(2)}, u32[]{:S(2)}) collective-permute-start(bf16[512,2048]{1,0:T(8,128)(2,1)} %bitcast.6), channel_id=1, source_target_pairs={{0,16},{1,17},{4,20},{5,21},{8,24},{9,25},{12,28},{13,29},{18,2},{... | collective-permute-start | bytes 6291464 | tf_op jit(solution)/shard_map/ppermute | solution.py:376
  43.7 2.5 %copy-start.1 = (bf16[4,2048,324]{1,2,0:T(8,128)(2,1)S(1)}, bf16[4,2048,324]{1,2,0:T(8,128)(2,1)}, u32[]{:S(2)}) copy-start(bf16[4,2048,324]{1,2,0:T(8,128)(2,1)} %copy-done) | copy-start | bytes 15925252
  46.3 2.5 %copy-start.3 = (bf16[4,2048,324]{1,2,0:T(8,128)(2,1)S(1)}, bf16[4,2048,324]{1,2,0:T(8,128)(2,1)}, u32[]{:S(2)}) copy-start(bf16[4,2048,324]{1,2,0:T(8,128)(2,1)} %copy-done.2) | copy-start | bytes 15925252
  56.0 37.2 %copy-start.4 = (f32[8,324,324]{2,1,0:T(8,128)}, f32[8,324,324]{2,1,0:T(8,128)S(1)}, u32[]{:S(2)}) copy-start(f32[8,324,324]{2,1,0:T(8,128)S(1)} %get-tuple-element.67.refs_1_) | copy-start | bytes 10077700
  56.0 43.0 %slice-start = ((s8[5373952]{0:T(1024)(128)(4,1)}), s8[4194304]{0:T(1024)(128)(4,1)S(1)}, s32[]{:S(2)}) async-start(s8[5373952]{0:T(1024)(128)(4,1)} %bitcast.20), calls=%async_computation | async-start | bytes 8388608
  61.0 1.1 copy-start.8
  93.2 5.8 %slice-start.1 = ((s8[5373952]{0:T(1024)(128)(4,1)}), s8[1179648]{0:T(1024)(128)(4,1)S(1)}, s32[]{:S(2)}) async-start(s8[5373952]{0:T(1024)(128)(4,1)} %bitcast.20), calls=%async_computation.1 | async-start | bytes 2359296
  96.5 15.6 %collective-permute-start.7 = (f32[4,328,384]{2,1,0:T(8,128)}, f32[4,328,384]{2,1,0:T(8,128)}, u32[]{:S(2)}, u32[]{:S(2)}) collective-permute-start(f32[4,328,384]{2,1,0:T(8,128)} %get-tuple-element.73.refs_3_), channel_id=1, source_target_pairs={{0,2},{1,3},{4,6},{5,7},{8,10},{9,11},{12,14},{13,15},{16,18},{17,... | collective-permute-start | bytes 6045704 | tf_op jit(solution)/shard_map/ppermute | solution.py:392
  103.3 18.3 %collective-permute-start.6 = (f32[8,328,128]{2,1,0:T(8,128)}, f32[8,328,128]{2,1,0:T(8,128)}, u32[]{:S(2)}, u32[]{:S(2)}) collective-permute-start(f32[8,328,128]{2,1,0:T(8,128)} %get-tuple-element.72), channel_id=1, source_target_pairs={{2,3},{3,2},{6,7},{7,6},{10,11},{11,10},{14,15},{15,14},{16,17},{1... | collective-permute-start | bytes 4030472 | tf_op jit(solution)/shard_map/ppermute | solution.py:382
  105.1 22.3 %collective-permute-start.1 = (bf16[272,2048]{1,0:T(8,128)(2,1)}, bf16[272,2048]{1,0:T(8,128)(2,1)S(1)}, u32[]{:S(2)}, u32[]{:S(2)}) collective-permute-start(bf16[272,2048]{1,0:T(8,128)(2,1)} %reshape.10), channel_id=1, source_target_pairs={{0,16},{1,17},{4,20},{5,21},{8,24},{9,25},{12,28},{13,29},{18,2},{... | collective-permute-start | bytes 3342344 | tf_op jit(solution)/shard_map/ppermute | solution.py:376
  112.1 12.6 %slice-start.2 = ((s8[5373952]{0:T(1024)(128)(4,1)}), s8[4194304]{0:T(1024)(128)(4,1)S(1)}, s32[]{:S(2)}) async-start(s8[5373952]{0:T(1024)(128)(4,1)} %bitcast.23), calls=%async_computation.2 | async-start | bytes 8388608
  112.1 2.3 %copy-start.5 = (f32[8,324,324]{2,1,0:T(8,128)S(1)}, f32[8,324,324]{2,1,0:T(8,128)}, u32[]{:S(2)}) copy-start(f32[8,324,324]{2,1,0:T(8,128)} %copy-done.4) | copy-start | bytes 10077700
  114.4 7.3 %copy-start.9 = (f32[8,328,128]{2,1,0:T(8,128)S(1)}, f32[8,328,128]{2,1,0:T(8,128)}, u32[]{:S(2)}) copy-start(f32[8,328,128]{2,1,0:T(8,128)} %copy-done.8) | copy-start | bytes 4030468
  114.4 10.3 %slice-start.3 = ((s8[5373952]{0:T(1024)(128)(4,1)}), s8[1179648]{0:T(1024)(128)(4,1)S(1)}, s32[]{:S(2)}) async-start(s8[5373952]{0:T(1024)(128)(4,1)} %bitcast.23), calls=%async_computation.3 | async-start | bytes 2359296
  124.7 1.9 copy-start.6
  126.6 9.3 %collective-permute-start.9 = (f32[8,328,128]{2,1,0:T(8,128)S(1)}, f32[8,328,128]{2,1,0:T(8,128)S(1)}, u32[]{:S(2)}, u32[]{:S(2)}) collective-permute-start(f32[8,328,128]{2,1,0:T(8,128)S(1)} %get-tuple-element.83), channel_id=1, source_target_pairs={{2,3},{3,2},{6,7},{7,6},{10,11},{11,10},{14,15},{15,14},{16,17},{1... | collective-permute-start | bytes 4030472 | tf_op jit(solution)/shard_map/ppermute | solution.py:382
  128.9 11.3 %collective-permute-start.8 = (f32[8,72,324]{2,1,0:T(8,128)S(1)}, f32[8,72,324]{2,1,0:T(8,128)S(1)}, u32[]{:S(2)}, u32[]{:S(2)}) collective-permute-start(f32[8,72,324]{2,1,0:T(8,128)S(1)} %get-tuple-element.81), channel_id=1, source_target_pairs={{2,3},{3,2},{6,7},{7,6},{10,11},{11,10},{14,15},{15,14},{16,17},{1... | collective-permute-start | bytes 2239496 | tf_op jit(solution)/shard_map/ppermute | solution.py:382
  129.6 15.9 %collective-permute-start.12 = (bf16[4,328,128]{2,1,0:T(8,128)(2,1)S(1)}, bf16[4,328,128]{2,1,0:T(8,128)(2,1)S(1)}, u32[]{:S(2)}, u32[]{:S(2)}) collective-permute-start(bf16[4,328,128]{2,1,0:T(8,128)(2,1)S(1)} %get-tuple-element.92), channel_id=1, source_target_pairs={{16,0},{17,1},{20,4},{21,5},{24,8},{25,9},{28,12},{29,13},{2,18},{... | collective-permute-start | bytes 1007624 | tf_op jit(solution)/shard_map/ppermute | solution.py:385
  130.9 19.3 %collective-permute-start.13 = (bf16[4,328,128]{2,1,0:T(8,128)(2,1)}, bf16[4,328,128]{2,1,0:T(8,128)(2,1)}, u32[]{:S(2)}, u32[]{:S(2)}) collective-permute-start(bf16[4,328,128]{2,1,0:T(8,128)(2,1)} %get-tuple-element.93), channel_id=1, source_target_pairs={{16,1},{17,0},{20,5},{21,4},{24,9},{25,8},{28,13},{29,12},{2,19},{... | collective-permute-start | bytes 1007624 | tf_op jit(solution)/shard_map/ppermute | solution.py:385
  135.9 45.4 %copy-start.7 = (f32[8,324,128]{2,1,0:T(8,128)S(1)}, f32[8,324,128]{2,1,0:T(8,128)}, u32[]{:S(2)}) copy-start(f32[8,324,128]{2,1,0:T(8,128)} %copy-done.6) | copy-start | bytes 3981316
  137.7 29.4 %collective-permute-start.14 = (bf16[4,328,128]{2,1,0:T(8,128)(2,1)}, bf16[4,328,128]{2,1,0:T(8,128)(2,1)S(1)}, u32[]{:S(2)}, u32[]{:S(2)}) collective-permute-start(bf16[4,328,128]{2,1,0:T(8,128)(2,1)} %get-tuple-element.94), channel_id=1, source_target_pairs={{16,0},{17,1},{20,4},{21,5},{24,8},{25,9},{28,12},{29,13},{2,18},{... | collective-permute-start | bytes 1007624 | tf_op jit(solution)/shard_map/ppermute | solution.py:385
  138.9 42.4 %collective-permute-start.15 = (bf16[4,328,128]{2,1,0:T(8,128)(2,1)}, bf16[4,328,128]{2,1,0:T(8,128)(2,1)}, u32[]{:S(2)}, u32[]{:S(2)}) collective-permute-start(bf16[4,328,128]{2,1,0:T(8,128)(2,1)} %get-tuple-element.95), channel_id=1, source_target_pairs={{16,1},{17,0},{20,5},{21,4},{24,9},{25,8},{28,13},{29,12},{2,19},{... | collective-permute-start | bytes 1007624 | tf_op jit(solution)/shard_map/ppermute | solution.py:385
  141.5 1.0 copy-start.10
  142.5 46.2 %collective-permute-start.10 = (bf16[4,72,324]{2,1,0:T(8,128)(2,1)}, bf16[4,72,324]{2,1,0:T(8,128)(2,1)}, u32[]{:S(2)}, u32[]{:S(2)}) collective-permute-start(bf16[4,72,324]{2,1,0:T(8,128)(2,1)} %get-tuple-element.86), channel_id=1, source_target_pairs={{16,0},{17,1},{20,4},{21,5},{24,8},{25,9},{28,12},{29,13},{2,18},{... | collective-permute-start | bytes 559880 | tf_op jit(solution)/shard_map/ppermute | solution.py:385
  145.5 52.4 %collective-permute-start.11 = (bf16[4,72,324]{2,1,0:T(8,128)(2,1)}, bf16[4,72,324]{2,1,0:T(8,128)(2,1)}, u32[]{:S(2)}, u32[]{:S(2)}) collective-permute-start(bf16[4,72,324]{2,1,0:T(8,128)(2,1)} %get-tuple-element.87), channel_id=1, source_target_pairs={{16,1},{17,0},{20,5},{21,4},{24,9},{25,8},{28,13},{29,12},{2,19},{... | collective-permute-start | bytes 559880 | tf_op jit(solution)/shard_map/ppermute | solution.py:385
  146.9 40.6 %copy-start.12 = (s32[2]{0:T(128)}, s32[2]{0:T(128)S(1)}, u32[]{:S(2)}) copy-start(s32[2]{0:T(128)S(1)} %pad_add_fusion.refs_0_.s_ref) | copy-start | bytes 28
  181.3 1.2 copy-start.11

commit v7 on v6

--- a/solution.py
+++ b/solution.py
@@ -185,7 +185,7 @@
     )(place_in, keep, crossed, share, given)
 
 
-def far_terms(det, own, got, width, turned, mine, after=()):
+def far_terms(det, own, got, start, width, turned, mine, after=()):
     states, ops, depth = own.shape
     half = states // 2
     rows = ops if turned else width
@@ -205,7 +205,10 @@
         body,
         (half,),
         1,
-        [pl.BlockSpec((1, ops, depth), state), whole(got.shape)],
+        [
+            pl.BlockSpec((1, ops, depth), state),
+            pl.BlockSpec((pl.Element(states * width), pl.Element(depth)), lambda b, x: (start, 0), pipeline_mode=pl.Buffered(1)),
+        ],
         [pl.BlockSpec((states, *tile), lambda b, x: (b, 0, 0))],
         [f32(half * states, *tile)],
         after,
@@ -370,38 +373,39 @@
     doubled = lax.ppermute(doubled, both, first_across)
     whole_own, token = lax.optimization_barrier((own, token))
     widths = [LANES] * full + [ops - wide]
-    for k in range(1, full + 1):
-        chunk = whole_own[:, k * LANES : k * LANES + widths[k]].reshape(states * widths[k], depth)
-        chunk, token = lax.optimization_barrier((chunk, token))
-        got.append(lax.ppermute(chunk, both, over))
+    later = [
+        whole_own[:, k * LANES : k * LANES + w].reshape(states * w, depth) for k, w in enumerate(widths) if k
+    ]
+    later, token = lax.optimization_barrier((jnp.concatenate(later), token))
+    got.append(lax.ppermute(later, both, over))
     keep, token = near_keep(det, own, partner, (token,))
     def terms(k, mine, *done):
-        return far_terms(det, own, got[k], widths[k], k < full, mine, done)
-
-    def finished(k, send, kept, *done):
-        came = lax.ppermute(send, both, across)
+        start = states * LANES * (k - 1) if k else 0
+        return far_terms(det, own, got[min(k, 1)], start, widths[k], k < full, mine, done)
+
+    def finished(k, token):
         rows = ops if k < full else widths[k]
-        mine, *pair, token = far_sum(det, kept, came, states, rows, k < full, done)
+        mine, *pair, token = far_sum(det, kepts[k], came[k], states, rows, k < full, (token,))
         codes.append([lax.ppermute(v, both, to) for v, to in zip(pair, (straight, diagonal))])
         owned.append(mine)
         return token
 
-    owned, codes = [], []
+    owned, codes, kepts, came = [], [], [], []
     kept, token = terms(0, True, token)
+    kepts.append(kept)
     share, token = near_share(det, keep, doubled, states, (token, crossed))
     given = lax.ppermute(share, both, to_second)
-    send, token = terms(0, False, token)
-    out, token = near_sum(jnp.stack([x, core]), keep, crossed, share, given, states, (token,))
-    token = finished(0, send, kept, token)
-    sends, kepts = [], []
-    for k in range(1, full + 1):
+    for k in range(full + 1):
         send, token = terms(k, False, token)
-        sends.append(send)
+        came.append(lax.ppermute(send, both, across))
+        if k == 0:
+            out, token = near_sum(jnp.stack([x, core]), keep, crossed, share, given, states, (token,))
+    token = finished(0, token)
     for k in range(1, full + 1):
         kept, token = terms(k, True, token)
         kepts.append(kept)
     for k in range(1, full + 1):
-        token = finished(k, sends[k - 1], kepts[k - 1], token)
+        token = finished(k, token)
 
     at = jnp.stack([x, receiver])
     out, token = place(at, out, owned, codes[:full], states, (token,))

time: 201 us -> 181 us (0.900)
  waiting for transfers between devices: 77.8 us -> 61.7 us
  starting transfers between devices: 33.5 us -> 30.1 us
  local copies, waits for them, and re-layouts: 31.3 us -> 28.7 us
    ppermute x6, waiting for transfers between devices: 46.6 us -> 30.2 us  [finished(): lax.ppermute(v, both, to)]
    ppermute x5 -> x4, starting transfers between devices: 11.7 us -> 5.14 us  [the longest x3 3.21 us: paired(): came.append(lax.ppermute(send, both, across))]
    ppermute x1, starting transfers between devices: 2.59 us -> 5.78 us  [paired(): given = lax.ppermute(share, both, to_second)]
    unnamed x34 -> x30, local copies, waits for them, and re-layouts: 10.6 us -> 8.14 us
  transfers between devices with their start and end apart: 16 -> 15, of which waited for: 8 -> 7; matrix products, arithmetic and copies ran while one was open for 10% -> 13% of each run, Pallas kernels for 27% -> 30%
where the time goes in v7:
time: 181 us; the launch traced here: 180 us
  waiting for transfers between devices  61.7 us (34%)
  Pallas kernels  57.1 us (32%)
  starting transfers between devices  30.1 us (17%)
  local copies, waits for them, and re-layouts  28.7 us (16%)
  other arithmetic  2.05 us (1%)
    pallas_call x15, Pallas kernels, call(): return lambda *operands: kernel(*operands, *after)  54.7 us
    ppermute x6, waiting for transfers between devices, finished(): lax.ppermute(v, both, to)  30.2 us
    ppermute x1, waiting for transfers between devices, paired(): crossed = lax.ppermute(crossed, 'det', [(0, 1), (1, 0)])  19.1 us
    ppermute x1, waiting for transfers between devices, paired(): doubled = lax.ppermute(doubled, both, first_across)  12.3 us
    unnamed x30, local copies, waits for them, and re-layouts  8.14 us
    ppermute x6, starting transfers between devices, finished(): lax.ppermute(v, both, to)  7.94 us
    optimization_barrier x1, local copies, waits for them, and re-layouts, paired(): partner, own = lax.optimization_barrier((partner, own))  7.35 us
    ppermute x1, starting transfers between devices, paired(): got = [lax.ppermute(first, both, over)]  6.82 us
  transfers between devices with their start and end apart: 15, of which 7 were waited for; matrix products, arithmetic and copies ran while one was open for 13% of the time, Pallas kernels for 30%

profile of v7, /device:TPU:0, one launch (start us, length us, event | category | flops | bytes accessed | tf_op | source)
XLA Modules:
  0.0 180.2 jit_solution(5761899795254857071)
XLA Ops:
  0.0 0.5 collective-permute-start
  0.5 2.6 %slice_bitcast_fusion = bf16[4,128,2048]{2,0,1:T(4,128)(2,1)S(1)} fusion(bf16[4,2048,324]{1,0,2:T(4,128)(2,1)} %param.1), kind=kLoop, calls=%fused_computation.3 | loop fusion | bytes 4194304 | tf_op jit(solution)/shard_map/transpose | solution.py:363
  3.1 2.5 %copy.10 = bf16[4,128,2048]{2,1,0:T(8,128)(2,1)} copy(bf16[4,128,2048]{2,0,1:T(4,128)(2,1)S(1)} %slice_bitcast_fusion) | data formatting | bytes 4194304 | tf_op jit(solution)/shard_map/transpose | solution.py:363
  5.5 6.8 %collective-permute-start.2 = (bf16[512,2048]{1,0:T(8,128)(2,1)}, bf16[512,2048]{1,0:T(8,128)(2,1)}, u32[]{:S(2)}, u32[]{:S(2)}) collective-permute-start(bf16[512,2048]{1,0:T(8,128)(2,1)} %bitcast.3.refs_3_), channel_id=1, source_target_pairs={{0,16},{1,17},{4,20},{5,21},{8,24},{9,25},{12,28},{13,29},{18,2},{... | collective-permute-start | bytes 6291464 | tf_op jit(solution)/shard_map/ppermute | solution.py:365
  12.4 5.4 %copy.16 = bf16[4,2048,324]{1,2,0:T(8,128)(2,1)S(1)} copy(bf16[4,2048,324]{1,0,2:T(4,128)(2,1)} %param.1) | data formatting | bytes 10616832 | tf_op jit(solution)/shard_map/optimization_barrier | solution.py:364
  17.8 0.0 collective-permute-done
  17.8 7.4 %copy.15 = bf16[4,2048,324]{1,2,0:T(8,128)(2,1)S(1)} copy(bf16[4,2048,324]{1,0,2:T(4,128)(2,1)} %collective-permute-done) | data formatting | bytes 10616832 | tf_op jit(solution)/shard_map/optimization_barrier | solution.py:367
  25.2 0.0 copy-start.2
  25.2 5.1 %shard_map.17 = (f32[1744,256]{1,0:T(8,128)}, f32[8,128]{1,0:T(8,128)S(1)}) custom-call(s32[1]{0:T(128)} %bitcast.refs_0_, bf16[4,324,2048]{2,1,0:T(8,128)(2,1)S(1)} %bitcast.14, bf16[4,324,2048]{2,1,0:T(8,128)(2,1)S(1)} %bitcast.27, bf16[512,2048]{1,0:T(8,128)(2,1)} %bitcast.3.refs_3_), custom_call_target="tpu_custom_call" | custom-call | tf_op jit(solution)/shard_map/pallas_call | solution.py:41
  30.3 5.1 %shard_map.18 = (f32[1744,256]{1,0:T(8,128)}, f32[8,128]{1,0:T(8,128)S(1)}) custom-call(s32[1]{0:T(128)} %bitcast.refs_0_, bf16[4,324,2048]{2,1,0:T(8,128)(2,1)S(1)} %bitcast.15, bf16[4,324,2048]{2,1,0:T(8,128)(2,1)S(1)} %bitcast.28, f32[8,128]{1,0:T(8,128)S(1)} %get-tuple-element.55.refs_3_), custom_call_target="tpu_custom_call" | custom-call | tf_op jit(solution)/shard_map/pallas_call | solution.py:41
  35.4 3.4 %collective-permute-start.3 = (f32[1744,256]{1,0:T(8,128)}, f32[1744,256]{1,0:T(8,128)}, u32[]{:S(2)}, u32[]{:S(2)}) collective-permute-start(f32[1744,256]{1,0:T(8,128)} %get-tuple-element.64), channel_id=1, source_target_pairs={{0,1},{1,0},{4,5},{5,4},{8,9},{9,8},{12,13},{13,12},{16,17},{17,16... | collective-permute-start | bytes 5357576 | tf_op jit(solution)/shard_map/ppermute | solution.py:373
  38.8 0.6 collective-permute-start.4
  39.4 1.2 slice.11
  40.6 0.1 slice.10
  40.8 1.4 reshape.11
  42.2 1.9 %pad_maximum_fusion = bf16[784,2048]{1,0:T(8,128)(2,1)} fusion(bf16[272,2048]{1,0:T(8,128)(2,1)S(1)} %reshape.11, bf16[512,2048]{1,0:T(8,128)(2,1)S(1)} %bitcast.30), kind=kLoop, calls=%fused_computation.2 | loop fusion | flops 6422528 | bytes 6422528 | tf_op jit(solution)/shard_map/concatenate | solution.py:379
  44.1 1.9 %collective-permute-start.1 = (bf16[784,2048]{1,0:T(8,128)(2,1)}, bf16[784,2048]{1,0:T(8,128)(2,1)S(1)}, u32[]{:S(2)}, u32[]{:S(2)}) collective-permute-start(bf16[784,2048]{1,0:T(8,128)(2,1)} %pad_maximum_fusion), channel_id=1, source_target_pairs={{0,16},{1,17},{4,20},{5,21},{8,24},{9,25},{12,28},{13,29},{18,2},{... | collective-permute-start | bytes 9633800 | tf_op jit(solution)/shard_map/ppermute | solution.py:380
  46.0 0.0 copy-start.3
  46.0 2.5 %copy-done.3 = bf16[4,2048,324]{1,2,0:T(8,128)(2,1)S(1)} copy-done((bf16[4,2048,324]{1,2,0:T(8,128)(2,1)S(1)}, bf16[4,2048,324]{1,2,0:T(8,128)(2,1)}, u32[]{:S(2)}) %copy-start.3) | copy-done | bytes 5308440
  48.5 7.2 %shard_map.19 = (f32[8,324,324]{2,1,0:T(8,128)S(1)}, f32[8,128]{1,0:T(8,128)S(1)}) custom-call(s32[1]{0:T(128)} %bitcast.refs_0_, bf16[4,324,2048]{2,1,0:T(8,128)(2,1)S(1)} %bitcast.18, bf16[4,324,2048]{2,1,0:T(8,128)(2,1)S(1)} %bitcast.29, f32[8,128]{1,0:T(8,128)S(1)} %get-tuple-element.60.refs_3_), custom_call_target="tpu_custom_call" | custom-call | tf_op jit(solution)/shard_map/pallas_call | solution.py:41
  55.7 0.0 copy-start.4
  55.8 0.0 collective-permute-done.2.refs_2_
  55.8 4.9 %shard_map.20 = (f32[8,328,128]{2,1,0:T(8,128)S(1)}, f32[8,128]{1,0:T(8,128)S(1)}) custom-call(s32[1]{0:T(128)} %bitcast.refs_0_, bf16[4,324,2048]{2,1,0:T(8,128)(2,1)S(1)} %bitcast.19, bf16[512,2048]{1,0:T(8,128)(2,1)} %collective-permute-done.2.refs_2_, f32[8,128]{1,0:T(8,128)S(1)} %get-tuple-element.61.refs_3_), custom_call_target="tpu_custom_call" | custom-call | tf_op jit(solution)/shard_map/pallas_call | solution.py:41
  60.7 1.2 copy-done.8
  61.8 12.3 %collective-permute-done.3.refs_2_ = f32[1744,256]{1,0:T(8,128)} collective-permute-done((f32[1744,256]{1,0:T(8,128)}, f32[1744,256]{1,0:T(8,128)}, u32[]{:S(2)}, u32[]{:S(2)}) %collective-permute-start.3) | collective-permute-done | bytes 1785888 | tf_op jit(solution)/shard_map/ppermute | solution.py:373
  74.2 19.1 %collective-permute-done.4.refs_4_.refs_2_ = f32[1744,256]{1,0:T(8,128)} collective-permute-done((f32[1744,256]{1,0:T(8,128)}, f32[1744,256]{1,0:T(8,128)}, u32[]{:S(2)}, u32[]{:S(2)}) %collective-permute-start.4) | collective-permute-done | bytes 1785888 | tf_op jit(solution)/shard_map/ppermute | solution.py:371
  93.3 3.1 %shard_map.21 = (f32[4,328,384]{2,1,0:T(8,128)}, f32[8,128]{1,0:T(8,128)S(1)}) custom-call(s32[1]{0:T(128)} %bitcast.refs_0_, f32[8,324,324]{2,1,0:T(8,128)S(1)} %get-tuple-element.63.refs_1_, f32[1744,256]{1,0:T(8,128)} %collective-permute-done.3.refs_2_, f32[8,128]{1,0:T(8,128)S(1)} %get-tuple-element.65.refs_3_, ...), custom_call_target="tpu_custom_call" | custom-call | tf_op jit(solution)/shard_map/pallas_call | solution.py:41
  96.4 5.8 %collective-permute-start.6 = (f32[4,328,384]{2,1,0:T(8,128)}, f32[4,328,384]{2,1,0:T(8,128)}, u32[]{:S(2)}, u32[]{:S(2)}) collective-permute-start(f32[4,328,384]{2,1,0:T(8,128)} %get-tuple-element.69.refs_3_), channel_id=1, source_target_pairs={{0,2},{1,3},{4,6},{5,7},{8,10},{9,11},{12,14},{13,15},{16,18},{17,... | collective-permute-start | bytes 6045704 | tf_op jit(solution)/shard_map/ppermute | solution.py:397
  102.1 4.3 %shard_map.22 = (f32[8,328,128]{2,1,0:T(8,128)}, f32[8,128]{1,0:T(8,128)S(1)}) custom-call(s32[1]{0:T(128)} %bitcast.refs_0_, bf16[4,324,2048]{2,1,0:T(8,128)(2,1)S(1)} %bitcast.20, bf16[512,2048]{1,0:T(8,128)(2,1)} %collective-permute-done.2.refs_2_, f32[8,128]{1,0:T(8,128)S(1)} %get-tuple-element.67.refs_3_), custom_call_target="tpu_custom_call" | custom-call | tf_op jit(solution)/shard_map/pallas_call | solution.py:41
  106.4 1.7 collective-permute-start.5
  108.2 0.1 pad_add_fusion.1.refs_0_
  108.2 0.0 collective-permute-done.6.refs_4_
  108.3 2.3 %copy-done.5 = f32[8,324,324]{2,1,0:T(8,128)S(1)} copy-done((f32[8,324,324]{2,1,0:T(8,128)S(1)}, f32[8,324,324]{2,1,0:T(8,128)}, u32[]{:S(2)}) %copy-start.5) | copy-done | bytes 3359256
  110.5 7.2 %shard_map.23 = (f32[2,324,8,324]{3,2,1,0:T(8,128)}, f32[8,128]{1,0:T(8,128)S(1)}) custom-call(s32[2]{0:T(128)S(1)} %pad_add_fusion.1.refs_0_, f32[8,324,324]{2,1,0:T(8,128)S(1)} %copy-done.5, f32[1744,256]{1,0:T(8,128)} %collective-permute-done.4.refs_4_.refs_2_, f32[4,328,384]{2,1,0:T(8,128)} %get-tuple-element.69.refs_3_, ...), custom_call_target="tpu_custom_call" | custom-call | tf_op jit(solution)/shard_map/pallas_call | solution.py:41
  117.7 0.0 collective-permute-done.1.refs_2_
  117.7 1.8 %shard_map.24 = (f32[8,328,128]{2,1,0:T(8,128)S(1)}, f32[8,128]{1,0:T(8,128)S(1)}) custom-call(s32[1]{0:T(128)} %bitcast.refs_0_, bf16[4,324,2048]{2,1,0:T(8,128)(2,1)S(1)} %bitcast.23, bf16[784,2048]{1,0:T(8,128)(2,1)S(1)} %collective-permute-done.1.refs_2_, f32[8,128]{1,0:T(8,128)S(1)} %get-tuple-element.71.refs_3_), custom_call_target="tpu_custom_call" | custom-call | tf_op jit(solution)/shard_map/pallas_call | solution.py:41
  119.6 0.7 collective-permute-start.8
  120.4 1.6 shard_map.25
  121.9 0.7 collective-permute-start.7
  122.7 0.0 collective-permute-done.5.refs_2_
  122.7 3.0 %shard_map.26 = (f32[8,324,128]{2,1,0:T(8,128)S(1)}, bf16[4,328,128]{2,1,0:T(8,128)(2,1)S(1)}, bf16[4,328,128]{2,1,0:T(8,128)(2,1)}, f32[8,128]{1,0:T(8,128)S(1)}) custom-call(s32[1]{0:T(128)} %bitcast.refs_0_, f32[8,328,128]{2,1,0:T(8,128)S(1)} %copy-done.9, f32[8,328,128]{2,1,0:T(8,128)} %collective-permute-done.5.refs_2_, ...), custom_call_target="tpu_custom_call" | custom-call | tf_op jit(solution)/shard_map/pallas_call | solution.py:41
  125.7 1.3 collective-permute-start.11
  127.0 1.5 collective-permute-start.12
  128.5 1.8 %shard_map.27 = (f32[8,328,128]{2,1,0:T(8,128)S(1)}, f32[8,128]{1,0:T(8,128)S(1)}) custom-call(s32[1]{0:T(128)} %bitcast.refs_0_, bf16[4,324,2048]{2,1,0:T(8,128)(2,1)S(1)} %bitcast.25, bf16[784,2048]{1,0:T(8,128)(2,1)S(1)} %collective-permute-done.1.refs_2_, f32[8,128]{1,0:T(8,128)S(1)} %get-tuple-element.74.refs_3_), custom_call_target="tpu_custom_call" | custom-call | tf_op jit(solution)/shard_map/pallas_call | solution.py:41
  130.4 1.6 shard_map.28
  132.0 0.0 collective-permute-done.8.refs_2_
  132.0 1.7 shard_map.29
  133.6 1.3 collective-permute-start.13
  134.9 1.3 collective-permute-start.14
  136.2 0.0 collective-permute-done.7.refs_2_
  136.2 1.3 shard_map.30
  137.5 1.0 copy-done.10
  138.5 1.3 collective-permute-start.9
  139.8 0.0 collective-permute-done.11.refs_5_
  139.8 1.3 collective-permute-start.10
  141.1 0.1 pad_add_fusion.refs_0_.s_ref
  141.2 0.9 collective-permute-done.12.refs_6_
  142.1 14.2 %collective-permute-done.13.refs_7_ = bf16[4,328,128]{2,1,0:T(8,128)(2,1)S(1)} collective-permute-done((bf16[4,328,128]{2,1,0:T(8,128)(2,1)}, bf16[4,328,128]{2,1,0:T(8,128)(2,1)S(1)}, u32[]{:S(2)}, u32[]{:S(2)}) %collective-permute-start.13) | collective-permute-done | bytes 335904 | tf_op jit(solution)/shard_map/ppermute | solution.py:389
  156.3 4.7 %collective-permute-done.14.refs_8_ = bf16[4,328,128]{2,1,0:T(8,128)(2,1)} collective-permute-done((bf16[4,328,128]{2,1,0:T(8,128)(2,1)}, bf16[4,328,128]{2,1,0:T(8,128)(2,1)}, u32[]{:S(2)}, u32[]{:S(2)}) %collective-permute-start.14) | collective-permute-done | bytes 335904 | tf_op jit(solution)/shard_map/ppermute | solution.py:389
  161.0 1.2 copy-done.11
  162.2 5.0 %shard_map.31 = (f32[2,324,8,324]{3,2,1,0:T(8,128)}, f32[8,128]{1,0:T(8,128)}) custom-call(s32[2]{0:T(128)S(1)} %pad_add_fusion.refs_0_.s_ref, f32[2,324,8,324]{3,2,1,0:T(8,128)} %get-tuple-element.84.refs_1_, f32[8,324,128]{2,1,0:T(8,128)S(1)} %copy-done.7, f32[8,324,128]{2,1,0:T(8,128)S(1)} %get-tuple-element.86.refs_3_, ...), custom_call_target="tpu_custom_call", output_to_operand_aliasing={{0}: (1, {})} | custom-call | tf_op jit(solution)/shard_map/pallas_call | solution.py:41
  167.2 2.3 %collective-permute-done.9.straight_ref = bf16[4,72,324]{2,1,0:T(8,128)(2,1)} collective-permute-done((bf16[4,72,324]{2,1,0:T(8,128)(2,1)}, bf16[4,72,324]{2,1,0:T(8,128)(2,1)}, u32[]{:S(2)}, u32[]{:S(2)}) %collective-permute-start.9) | collective-permute-done | bytes 186656 | tf_op jit(solution)/shard_map/ppermute | solution.py:389
  169.6 8.0 %collective-permute-done.10.across_ref = bf16[4,72,324]{2,1,0:T(8,128)(2,1)} collective-permute-done((bf16[4,72,324]{2,1,0:T(8,128)(2,1)}, bf16[4,72,324]{2,1,0:T(8,128)(2,1)}, u32[]{:S(2)}, u32[]{:S(2)}) %collective-permute-start.10) | collective-permute-done | bytes 186656 | tf_op jit(solution)/shard_map/ppermute | solution.py:389
  177.6 2.5 %shard_map.32 = f32[2,324,8,324]{3,2,1,0:T(8,128)} custom-call(s32[2]{0:T(128)} %copy-done.12, f32[2,324,8,324]{3,2,1,0:T(8,128)} %get-tuple-element.94.out_in, bf16[4,72,324]{2,1,0:T(8,128)(2,1)} %collective-permute-done.9.straight_ref, bf16[4,72,324]{2,1,0:T(8,128)(2,1)} %collective-permute-done.10.across_ref), custom_call_target="tpu_custom_call", output_to_operand_aliasing={{}: (1, {})} | custom-call | tf_op jit(solution)/shard_map/pallas_call | solution.py:325
  (23 shorter events, 0.0 us)
Async XLA Ops:
  0.0 17.8 %collective-permute-start = (bf16[4,2048,324]{1,0,2:T(4,128)(2,1)}, bf16[4,2048,324]{1,0,2:T(4,128)(2,1)}, u32[]{:S(2)}, u32[]{:S(2)}) collective-permute-start(bf16[4,2048,324]{1,0,2:T(4,128)(2,1)} %param.1), channel_id=1, source_target_pairs={{0,2},{2,0},{4,6},{6,4},{8,10},{10,8},{12,14},{14,12},{16,18},{18,... | collective-permute-start | bytes 15925256 | tf_op jit(solution)/shard_map/ppermute | solution.py:362
  5.5 50.2 %collective-permute-start.2 = (bf16[512,2048]{1,0:T(8,128)(2,1)}, bf16[512,2048]{1,0:T(8,128)(2,1)}, u32[]{:S(2)}, u32[]{:S(2)}) collective-permute-start(bf16[512,2048]{1,0:T(8,128)(2,1)} %bitcast.3.refs_3_), channel_id=1, source_target_pairs={{0,16},{1,17},{4,20},{5,21},{8,24},{9,25},{12,28},{13,29},{18,2},{... | collective-permute-start | bytes 6291464 | tf_op jit(solution)/shard_map/ppermute | solution.py:365
  17.8 22.8 %copy-start = (bf16[4,2048,324]{1,2,0:T(8,128)(2,1)}, bf16[4,2048,324]{1,2,0:T(8,128)(2,1)S(1)}, u32[]{:S(2)}) copy-start(bf16[4,2048,324]{1,2,0:T(8,128)(2,1)S(1)} %copy.16) | copy-start | bytes 15925252
  25.2 5.1 %copy-start.2 = (bf16[4,2048,324]{1,2,0:T(8,128)(2,1)}, bf16[4,2048,324]{1,2,0:T(8,128)(2,1)S(1)}, u32[]{:S(2)}) copy-start(bf16[4,2048,324]{1,2,0:T(8,128)(2,1)S(1)} %copy.15) | copy-start | bytes 15925252
  35.4 38.8 %collective-permute-start.3 = (f32[1744,256]{1,0:T(8,128)}, f32[1744,256]{1,0:T(8,128)}, u32[]{:S(2)}, u32[]{:S(2)}) collective-permute-start(f32[1744,256]{1,0:T(8,128)} %get-tuple-element.64), channel_id=1, source_target_pairs={{0,1},{1,0},{4,5},{5,4},{8,9},{9,8},{12,13},{13,12},{16,17},{17,16... | collective-permute-start | bytes 5357576 | tf_op jit(solution)/shard_map/ppermute | solution.py:373
  38.8 54.5 %collective-permute-start.4 = (f32[1744,256]{1,0:T(8,128)}, f32[1744,256]{1,0:T(8,128)}, u32[]{:S(2)}, u32[]{:S(2)}) collective-permute-start(f32[1744,256]{1,0:T(8,128)} %get-tuple-element.66), channel_id=1, source_target_pairs={{0,1},{1,0},{2,3},{3,2},{4,5},{5,4},{6,7},{7,6},{8,9},{9,8},{10,11... | collective-permute-start | bytes 5357576 | tf_op jit(solution)/shard_map/ppermute | solution.py:371
  42.1 3.9 %copy-start.1 = (bf16[4,2048,324]{1,2,0:T(8,128)(2,1)S(1)}, bf16[4,2048,324]{1,2,0:T(8,128)(2,1)}, u32[]{:S(2)}) copy-start(bf16[4,2048,324]{1,2,0:T(8,128)(2,1)} %copy-done) | copy-start | bytes 15925252
  44.1 73.7 %collective-permute-start.1 = (bf16[784,2048]{1,0:T(8,128)(2,1)}, bf16[784,2048]{1,0:T(8,128)(2,1)S(1)}, u32[]{:S(2)}, u32[]{:S(2)}) collective-permute-start(bf16[784,2048]{1,0:T(8,128)(2,1)} %pad_maximum_fusion), channel_id=1, source_target_pairs={{0,16},{1,17},{4,20},{5,21},{8,24},{9,25},{12,28},{13,29},{18,2},{... | collective-permute-start | bytes 9633800 | tf_op jit(solution)/shard_map/ppermute | solution.py:380
  46.0 2.5 %copy-start.3 = (bf16[4,2048,324]{1,2,0:T(8,128)(2,1)S(1)}, bf16[4,2048,324]{1,2,0:T(8,128)(2,1)}, u32[]{:S(2)}) copy-start(bf16[4,2048,324]{1,2,0:T(8,128)(2,1)} %copy-done.2) | copy-start | bytes 15925252
  55.7 37.5 %copy-start.4 = (f32[8,324,324]{2,1,0:T(8,128)}, f32[8,324,324]{2,1,0:T(8,128)S(1)}, u32[]{:S(2)}) copy-start(f32[8,324,324]{2,1,0:T(8,128)S(1)} %get-tuple-element.63.refs_1_) | copy-start | bytes 10077700
  60.7 1.2 copy-start.8
  96.4 11.9 %collective-permute-start.6 = (f32[4,328,384]{2,1,0:T(8,128)}, f32[4,328,384]{2,1,0:T(8,128)}, u32[]{:S(2)}, u32[]{:S(2)}) collective-permute-start(f32[4,328,384]{2,1,0:T(8,128)} %get-tuple-element.69.refs_3_), channel_id=1, source_target_pairs={{0,2},{1,3},{4,6},{5,7},{8,10},{9,11},{12,14},{13,15},{16,18},{17,... | collective-permute-start | bytes 6045704 | tf_op jit(solution)/shard_map/ppermute | solution.py:397
  106.4 16.2 %collective-permute-start.5 = (f32[8,328,128]{2,1,0:T(8,128)}, f32[8,328,128]{2,1,0:T(8,128)}, u32[]{:S(2)}, u32[]{:S(2)}) collective-permute-start(f32[8,328,128]{2,1,0:T(8,128)} %get-tuple-element.68), channel_id=1, source_target_pairs={{2,3},{3,2},{6,7},{7,6},{10,11},{11,10},{14,15},{15,14},{16,17},{1... | collective-permute-start | bytes 4030472 | tf_op jit(solution)/shard_map/ppermute | solution.py:400
  108.2 9.5 %slice-start = ((s8[5373952]{0:T(1024)(128)(4,1)}), s8[4194304]{0:T(1024)(128)(4,1)S(1)}, s32[]{:S(2)}) async-start(s8[5373952]{0:T(1024)(128)(4,1)} %bitcast.21), calls=%async_computation | async-start | bytes 8388608
  108.3 2.3 %copy-start.5 = (f32[8,324,324]{2,1,0:T(8,128)S(1)}, f32[8,324,324]{2,1,0:T(8,128)}, u32[]{:S(2)}) copy-start(f32[8,324,324]{2,1,0:T(8,128)} %copy-done.4) | copy-start | bytes 10077700
  110.5 7.2 %slice-start.1 = ((s8[5373952]{0:T(1024)(128)(4,1)}), s8[1179648]{0:T(1024)(128)(4,1)S(1)}, s32[]{:S(2)}) async-start(s8[5373952]{0:T(1024)(128)(4,1)} %bitcast.21), calls=%async_computation.1 | async-start | bytes 2359296
  119.6 12.4 %collective-permute-start.8 = (f32[8,328,128]{2,1,0:T(8,128)S(1)}, f32[8,328,128]{2,1,0:T(8,128)S(1)}, u32[]{:S(2)}, u32[]{:S(2)}) collective-permute-start(f32[8,328,128]{2,1,0:T(8,128)S(1)} %get-tuple-element.79), channel_id=1, source_target_pairs={{2,3},{3,2},{6,7},{7,6},{10,11},{11,10},{14,15},{15,14},{16,17},{1... | collective-permute-start | bytes 4030472 | tf_op jit(solution)/shard_map/ppermute | solution.py:400
  120.3 2.3 %copy-start.9 = (f32[8,328,128]{2,1,0:T(8,128)S(1)}, f32[8,328,128]{2,1,0:T(8,128)}, u32[]{:S(2)}) copy-start(f32[8,328,128]{2,1,0:T(8,128)} %copy-done.8) | copy-start | bytes 4030468
  121.9 14.3 %collective-permute-start.7 = (f32[8,72,324]{2,1,0:T(8,128)S(1)}, f32[8,72,324]{2,1,0:T(8,128)S(1)}, u32[]{:S(2)}, u32[]{:S(2)}) collective-permute-start(f32[8,72,324]{2,1,0:T(8,128)S(1)} %get-tuple-element.77), channel_id=1, source_target_pairs={{2,3},{3,2},{6,7},{7,6},{10,11},{11,10},{14,15},{15,14},{16,17},{1... | collective-permute-start | bytes 2239496 | tf_op jit(solution)/shard_map/ppermute | solution.py:400
  125.7 4.7 %copy-start.6 = (f32[8,324,128]{2,1,0:T(8,128)}, f32[8,324,128]{2,1,0:T(8,128)S(1)}, u32[]{:S(2)}) copy-start(f32[8,324,128]{2,1,0:T(8,128)S(1)} %get-tuple-element.85.refs_2_) | copy-start | bytes 3981316
  125.7 14.1 %collective-permute-start.11 = (bf16[4,328,128]{2,1,0:T(8,128)(2,1)S(1)}, bf16[4,328,128]{2,1,0:T(8,128)(2,1)S(1)}, u32[]{:S(2)}, u32[]{:S(2)}) collective-permute-start(bf16[4,328,128]{2,1,0:T(8,128)(2,1)S(1)} %get-tuple-element.88), channel_id=1, source_target_pairs={{16,0},{17,1},{20,4},{21,5},{24,8},{25,9},{28,12},{29,13},{2,18},{... | collective-permute-start | bytes 1007624 | tf_op jit(solution)/shard_map/ppermute | solution.py:389
  127.0 15.1 %collective-permute-start.12 = (bf16[4,328,128]{2,1,0:T(8,128)(2,1)}, bf16[4,328,128]{2,1,0:T(8,128)(2,1)}, u32[]{:S(2)}, u32[]{:S(2)}) collective-permute-start(bf16[4,328,128]{2,1,0:T(8,128)(2,1)} %get-tuple-element.89), channel_id=1, source_target_pairs={{16,1},{17,0},{20,5},{21,4},{24,9},{25,8},{28,13},{29,12},{2,19},{... | collective-permute-start | bytes 1007624 | tf_op jit(solution)/shard_map/ppermute | solution.py:389
  132.0 29.1 %copy-start.7 = (f32[8,324,128]{2,1,0:T(8,128)S(1)}, f32[8,324,128]{2,1,0:T(8,128)}, u32[]{:S(2)}) copy-start(f32[8,324,128]{2,1,0:T(8,128)} %copy-done.6) | copy-start | bytes 3981316
  133.6 22.6 %collective-permute-start.13 = (bf16[4,328,128]{2,1,0:T(8,128)(2,1)}, bf16[4,328,128]{2,1,0:T(8,128)(2,1)S(1)}, u32[]{:S(2)}, u32[]{:S(2)}) collective-permute-start(bf16[4,328,128]{2,1,0:T(8,128)(2,1)} %get-tuple-element.90), channel_id=1, source_target_pairs={{16,0},{17,1},{20,4},{21,5},{24,8},{25,9},{28,12},{29,13},{2,18},{... | collective-permute-start | bytes 1007624 | tf_op jit(solution)/shard_map/ppermute | solution.py:389
  134.9 26.1 %collective-permute-start.14 = (bf16[4,328,128]{2,1,0:T(8,128)(2,1)}, bf16[4,328,128]{2,1,0:T(8,128)(2,1)}, u32[]{:S(2)}, u32[]{:S(2)}) collective-permute-start(bf16[4,328,128]{2,1,0:T(8,128)(2,1)} %get-tuple-element.91), channel_id=1, source_target_pairs={{16,1},{17,0},{20,5},{21,4},{24,9},{25,8},{28,13},{29,12},{2,19},{... | collective-permute-start | bytes 1007624 | tf_op jit(solution)/shard_map/ppermute | solution.py:389
  137.5 1.0 copy-start.10
  138.5 31.1 %collective-permute-start.9 = (bf16[4,72,324]{2,1,0:T(8,128)(2,1)}, bf16[4,72,324]{2,1,0:T(8,128)(2,1)}, u32[]{:S(2)}, u32[]{:S(2)}) collective-permute-start(bf16[4,72,324]{2,1,0:T(8,128)(2,1)} %get-tuple-element.82), channel_id=1, source_target_pairs={{16,0},{17,1},{20,4},{21,5},{24,8},{25,9},{28,12},{29,13},{2,18},{... | collective-permute-start | bytes 559880 | tf_op jit(solution)/shard_map/ppermute | solution.py:389
  139.8 37.8 %collective-permute-start.10 = (bf16[4,72,324]{2,1,0:T(8,128)(2,1)}, bf16[4,72,324]{2,1,0:T(8,128)(2,1)}, u32[]{:S(2)}, u32[]{:S(2)}) collective-permute-start(bf16[4,72,324]{2,1,0:T(8,128)(2,1)} %get-tuple-element.83), channel_id=1, source_target_pairs={{16,1},{17,0},{20,5},{21,4},{24,9},{25,8},{28,13},{29,12},{2,19},{... | collective-permute-start | bytes 559880 | tf_op jit(solution)/shard_map/ppermute | solution.py:389
  141.2 26.1 %copy-start.12 = (s32[2]{0:T(128)}, s32[2]{0:T(128)S(1)}, u32[]{:S(2)}) copy-start(s32[2]{0:T(128)S(1)} %pad_add_fusion.refs_0_.s_ref) | copy-start | bytes 28
  161.0 1.2 copy-start.11

commit v8 on v7

--- a/solution.py
+++ b/solution.py
@@ -191,61 +191,93 @@
     rows = ops if turned else width
     tile = (up(ops, 8), width) if turned else (up(width, 8), ops)
 
+    def first(x):
+        return half * x if mine else half * (1 - x)
+
     def body(x_ref, own_ref, got_ref, out_ref):
-        pair = (own_ref[0], got_ref[...]) if turned else (got_ref[...], own_ref[0])
-        every = contract_last(*pair)
-        for u in range(states):
-            part = slice(u * width, (u + 1) * width)
-            out_ref[u, :rows] = every[:, part] if turned else every[part]
-
-    def state(b, x):
-        return ((half * x[0] if mine else half * (1 - x[0])) + b, 0, 0)
-
-    return call(
-        body,
-        (half,),
+        if turned:
+            both = contract_last(own_ref[0], got_ref[...])
+            parts = [both[:, a * width : (a + 1) * width] for a in range(half)]
+        else:
+            every = contract_last(got_ref[...], own_ref[0])
+            parts = [every[u * width : (u + 1) * width] for u in range(states)]
+            parts = [jnp.where(first(x_ref[0]) == 0, parts[a], parts[half + a]) for a in range(half)]
+        for a in range(half):
+            out_ref[a, 0, :rows] = parts[a]
+
+    picked = half if turned else states
+
+    def rows_in(v, x):
+        return (start + first(x[0]) * width if turned else start, 0)
+
+    return call(
+        body,
+        (states,),
         1,
         [
-            pl.BlockSpec((1, ops, depth), state),
-            pl.BlockSpec((pl.Element(states * width), pl.Element(depth)), lambda b, x: (start, 0), pipeline_mode=pl.Buffered(1)),
+            pl.BlockSpec((1, ops, depth), lambda v, x: (v, 0, 0)),
+            pl.BlockSpec(
+                (pl.Element(picked * width), pl.Element(depth)), rows_in, pipeline_mode=pl.Buffered(1)
+            ),
         ],
-        [pl.BlockSpec((states, *tile), lambda b, x: (b, 0, 0))],
-        [f32(half * states, *tile)],
+        [pl.BlockSpec((half, 1, *tile), lambda v, x: (0, v, 0, 0))],
+        [f32(half, states, *tile)],
         after,
     )(det, own, got)
 
 
-def far_sum(det, keep, came, states, rows, turned, after=()):
-    tiles, padded, lanes = keep.shape
-    half = states // 2
-    shape = (half * half, up(rows + 1, 8), lanes)
-
-    def body(x_ref, keep_ref, came_ref, own_ref, straight_ref, across_ref):
+def far_sum(det, keep, came, rows, turned, others=None, after=()):
+    half, states, padded, lanes = keep.shape
+    earlier = len(others or ())
+    shape = (up(rows + 1, 8), lanes)
+
+    def body(x_ref, keep_ref, came_ref, *refs):
         x = x_ref[0]
+        other_refs, (tile_ref, code_ref), cross_refs = refs[:earlier], refs[earlier:][:2], refs[earlier + 2 :]
         top = jnp.zeros((rows, lanes), jnp.float32)
-        for t in range(tiles):
-            tile = keep_ref[t, :rows] + came_ref[t, :rows]
-            own_ref[t] = tile
-            top = jnp.maximum(top, jnp.abs(tile))
-        exponent = jnp.floor(jnp.log2(jnp.maximum(jnp.max(top, keepdims=True), SMALLEST)))
-        scale = jnp.exp2(LIFT - exponent)
-        below = jnp.broadcast_to(exponent, (shape[1] - rows, lanes))
-        for to_ref, first in ((straight_ref, half * x), (across_ref, half * (1 - x))):
+        for a in range(half):
+            for v in range(states):
+                tile = keep_ref[a, v, :rows] + came_ref[a, v, :rows]
+                tile_ref[a, v] = tile
+                top = jnp.maximum(top, jnp.abs(tile))
+
+        def coder(top):
+            exponent = jnp.floor(jnp.log2(jnp.maximum(jnp.max(top, keepdims=True), SMALLEST)))
+            scale = jnp.exp2(LIFT - exponent)
+            below = jnp.broadcast_to(exponent, (shape[0] - rows, lanes))
+            return lambda tile: jnp.concatenate([powered(tile * scale), below]).astype(jnp.bfloat16)
+
+        code = coder(top)
+        for a in range(half):
+            for v in range(states):
+                code_ref[a, v] = code(tile_ref[a, v])
+        for cross_ref in cross_refs:
             for a in range(half):
                 for b in range(half):
-                    to_ref[a * half + b] = jnp.concatenate(
-                        [powered(own_ref[b * states + first + a] * scale), below]
-                    ).astype(jnp.bfloat16)
-
+                    cross_ref[earlier, a, b] = code_ref[a, half * (1 - x) + b]
+            for k, other_ref in enumerate(other_refs):
+                top = jnp.zeros((rows, lanes), jnp.float32)
+                for a in range(half):
+                    for v in range(states):
+                        top = jnp.maximum(top, jnp.abs(other_ref[a, v]))
+                code = coder(top)
+                for a in range(half):
+                    for b in range(half):
+                        cross_ref[k, a, b] = code(other_ref[a, half * (1 - x) + b])
+
+    shapes = [(half, states, rows, lanes), (half, states, *shape)]
+    if others is not None:
+        shapes.append((earlier + 1, half, half, *shape))
+    kinds = [jnp.float32] + [jnp.bfloat16] * (len(shapes) - 1)
     return call(
         body,
         (1,),
         1,
-        [whole((tiles, padded, lanes))] * 2,
-        [whole((tiles, rows, lanes)), whole(shape), whole(shape)],
-        [f32(tiles, rows, lanes)] + [jax.ShapeDtypeStruct(shape, jnp.bfloat16)] * 2,
+        [whole(keep.shape)] * 2 + [whole(shapes[0])] * earlier,
+        [whole(s) for s in shapes],
+        [jax.ShapeDtypeStruct(s, kind) for s, kind in zip(shapes, kinds)],
         after,
-    )(det, keep, came)
+    )(det, keep, came, *(others or ()))
 
 
 def powered(value):
@@ -254,70 +286,86 @@
     return value * jnp.abs(value) * (fourth * fourth)
 
 
+def rooted(code, exponent):
+    code = code.astype(jnp.float32)
+    root = jnp.exp2(jnp.log2(jnp.abs(code)) * (1 / POWER)) * jnp.exp2(exponent - LIFT)
+    return jnp.where(code < 0, -root, root)
+
+
 def decoded(code, rows):
-    code = code.astype(jnp.float32)
-    value, exponent = code[:rows], code[rows : rows + 1]
-    root = jnp.exp2(jnp.log2(jnp.abs(value)) * (1 / POWER)) * jnp.exp2(exponent - LIFT)
-    return jnp.where(value < 0, -root, root)
-
-
-def place(place_in, out, owned, came, states, after=()):
+    return rooted(code[:rows], code[rows:].astype(jnp.float32)[:1])
+
+
+def place(place_in, out, finished, crossed, came, after=()):
     _, ops, tiles, _ = out.shape
-    full, half = len(came), states // 2
+    full = len(came)
+    half, states, _, _ = finished[0].shape
     wide = full * LANES
-    code = came[0][0].shape
+    turned, last = crossed
 
     def body(s_ref, out_in, *refs):
-        owned_refs, came_refs, out_ref = refs[: full + 1], refs[full + 1 : -1], refs[-1]
+        finished_refs, came_refs, out_ref = refs[: full + 1], refs[full + 4 : -1], refs[-1]
+        turned_ref, under_ref, last_ref = refs[full + 1 :][:3]
         x = s_ref[0]
 
         @pl.when(s_ref[1] == 1)
         def _():
-            for t in range(tiles):
-                for k in range(full):
-                    out_ref[0, :, t, k * LANES : (k + 1) * LANES] = owned_refs[k][t]
-                out_ref[0, :, t, wide:] = owned_refs[full][t].T
+            for b in range(half):
+                for u in range(states):
+                    a, t = u % half, b * states + u
+
+                    @pl.when(u // half == x)
+                    def _():
+                        for k in range(full):
+                            out_ref[0, :, t, k * LANES : (k + 1) * LANES] = finished_refs[k][a, half * x + b]
+                        out_ref[0, :, t, wide:] = finished_refs[full][a, half * x + b].T
+
+                    @pl.when(u // half != x)
+                    def _():
+                        for k in range(full):
+                            exponent = under_ref[k, a, b].astype(jnp.float32)[ops % 16 : ops % 16 + 1]
+                            out_ref[0, :, t, k * LANES : (k + 1) * LANES] = rooted(turned_ref[k, a, b], exponent)
+                        exponent = last_ref[a, b, ops - wide :, :1].astype(jnp.float32)[:1]
+                        out_ref[0, :, t, wide:] = rooted(last_ref[a, b, : ops - wide], exponent).T
 
         for k in range(full):
-            straight, across = came_refs[2 * k : 2 * k + 2]
 
             @pl.when((s_ref[1] == 0) & (pl.program_id(0) == k))
             def _():
                 for a in range(half):
                     for v in range(states):
-                        one = a * half + v % half
-                        block = jnp.where(v // half == x, straight[one], across[one])
-                        out_ref[0, :, a * states + v] = decoded(block, ops).T
-
-    return call(
-        body,
-        (pl.cdiv(ops, LANES),),
+                        out_ref[0, :, a * states + v] = decoded(came_refs[k][a, v], ops).T
+
+    steps = pl.cdiv(ops, LANES)
+    return call(
+        body,
+        (steps,),
         1,
         [pl.BlockSpec(memory_space=pl.ANY)]
-        + [pl.BlockSpec((tiles, LANES, LANES), lambda i, s: (0, i, 0))] * full
-        + [pl.BlockSpec((tiles, ops - wide, LANES), lambda i, s: (0, 0, i))]
-        + [whole(code)] * (2 * full),
+        + [pl.BlockSpec((half, states, LANES, LANES), lambda i, s: (0, 0, i, 0))] * full
+        + [pl.BlockSpec((half, states, ops - wide, LANES), lambda i, s: (0, 0, 0, i))]
+        + [pl.BlockSpec((full, half, half, LANES, LANES), lambda i, s: (0, 0, 0, i, 0))]
+        + [pl.BlockSpec((full, half, half, 16, LANES), lambda i, s: (0, 0, 0, ops // 16, 0))]
+        + [pl.BlockSpec((half, half, last.shape[2], LANES), lambda i, s: (0, 0, 0, i))]
+        + [whole(c.shape) for c in came],
         [pl.BlockSpec((1, LANES, tiles, ops), lambda i, s: (0, i, 0, 0))],
         [f32(*out.shape)],
         after,
         {1: 0},
-    )(place_in, out, *owned, *[c for pair in came for c in pair])
-
-
-def finish(place_in, out, straight, across, states):
+    )(place_in, out, *finished, turned, turned, last, *came)
+
+
+def finish(place_in, out, last):
     _, ops, tiles, _ = out.shape
-    rest, half = ops % LANES, states // 2
-
-    def body(s_ref, out_in, straight_ref, across_ref, out_ref, rows_ref, sem):
-        x = s_ref[0]
-
+    half, states, _, _ = last.shape
+    rest = ops % LANES
+
+    def body(s_ref, out_in, last_ref, out_ref, rows_ref, sem):
         @pl.when(s_ref[1] == 0)
         def _():
             for a in range(half):
                 for v in range(states):
-                    one = a * half + v % half
-                    block = jnp.where(v // half == x, straight_ref[one], across_ref[one])
-                    rows_ref[:, a * states + v] = decoded(block, rest)
+                    rows_ref[:, a * states + v] = decoded(last_ref[a, v], rest)
             copy = pltpu.make_async_copy(rows_ref, out_ref.at[0, pl.ds(ops - rest, rest)], sem)
             copy.start()
             copy.wait()
@@ -327,14 +375,13 @@
         in_specs=[
             pl.BlockSpec(memory_space=pltpu.SMEM),
             pl.BlockSpec(memory_space=pl.ANY),
-            pl.BlockSpec(memory_space=pltpu.VMEM),
             pl.BlockSpec(memory_space=pltpu.VMEM),
         ],
         out_specs=pl.BlockSpec(memory_space=pl.ANY),
         out_shape=f32(*out.shape),
         input_output_aliases={1: 0},
         scratch_shapes=[pltpu.VMEM((rest, tiles, ops), jnp.float32), pltpu.SemaphoreType.DMA],
-    )(place_in, out, straight, across)
+    )(place_in, out, last)
 
 
 def paired(amplitudes):
@@ -347,8 +394,7 @@
     senders = [s for s in range(blocks) if (s & 1) == (s >> far & 1)]
     receivers = [s for s in range(blocks) if s not in senders]
     over = [(2 * s + x, 2 * (s ^ 1 << far) + x) for s in senders for x in range(2)]
-    straight = [(b, a) for a, b in over]
-    diagonal = [(b, a ^ 1) for a, b in over]
+    back = [(b, a) for a, b in over]
     across = [(2 * s + x, 2 * s + 1 - x) for s in receivers for x in range(2)]
     first_across = [(2 * s + x, 2 * s + 1 - x) for s in range(0, blocks, 2) for x in range(2)]
     to_second = [(2 * s + x, 2 * (s + 1) + x) for s in range(0, blocks, 2) for x in range(2)]
@@ -383,14 +429,17 @@
         start = states * LANES * (k - 1) if k else 0
         return far_terms(det, own, got[min(k, 1)], start, widths[k], k < full, mine, done)
 
-    def finished(k, token):
+    finished, codes, crossing, kepts, came = [], [], [], [], []
+
+    def sum_up(k, token):
         rows = ops if k < full else widths[k]
-        mine, *pair, token = far_sum(det, kepts[k], came[k], states, rows, k < full, (token,))
-        codes.append([lax.ppermute(v, both, to) for v, to in zip(pair, (straight, diagonal))])
-        owned.append(mine)
+        others = finished[:k] if k == full - 1 else [] if k == full else None
+        tiles, code, *cross, token = far_sum(det, kepts[k], came[k], rows, k < full, others, (token,))
+        codes.append(lax.ppermute(code, both, back))
+        crossing.extend(lax.ppermute(c, both, across) for c in cross)
+        finished.append(tiles)
         return token
 
-    owned, codes, kepts, came = [], [], [], []
     kept, token = terms(0, True, token)
     kepts.append(kept)
     share, token = near_share(det, keep, doubled, states, (token, crossed))
@@ -400,17 +449,18 @@
         came.append(lax.ppermute(send, both, across))
         if k == 0:
             out, token = near_sum(jnp.stack([x, core]), keep, crossed, share, given, states, (token,))
-    token = finished(0, token)
+    token = sum_up(0, token)
     for k in range(1, full + 1):
         kept, token = terms(k, True, token)
         kepts.append(kept)
     for k in range(1, full + 1):
-        token = finished(k, token)
+        token = sum_up(k, token)
 
     at = jnp.stack([x, receiver])
-    out, token = place(at, out, owned, codes[:full], states, (token,))
-    *last, out = lax.optimization_barrier((*codes[full], out))
-    return finish(at, out, *last, states).transpose(0, 2, 1, 3)
+    crossing[1] = crossing[1].reshape(crossing[1].shape[1:])
+    out, token = place(at, out, finished, crossing, codes[:full], (token,))
+    last, out = lax.optimization_barrier((codes[full], out))
+    return finish(at, out, last).transpose(0, 2, 1, 3)
 
 
 def partner_2(value, axis, stride):

time: 181 us -> 181 us (level)
  starting transfers between devices: 30.1 us -> 27.3 us
  Pallas kernels: 57.1 us -> 59.9 us
    pallas_call x15, Pallas kernels: 54.7 us -> 57.5 us  [call(): return lambda *operands: kernel(*operands, *after)]
    ppermute x6 -> x5, starting transfers between devices: 7.94 us -> 6.26 us  [the longest x3 4.07 us: sum_up(): codes.append(lax.ppermute(code, both, back))]
    ppermute x6 -> x5, waiting for transfers between devices: 30.2 us -> 29.4 us  [the longest x3 29.4 us: sum_up(): codes.append(lax.ppermute(code, both, back))]
    unnamed x30 -> x32, local copies, waits for them, and re-layouts: 8.14 us -> 8.22 us
  transfers between devices with their start and end apart: 15 -> 14, of which waited for: 7 -> 5; matrix products, arithmetic and copies ran while one was open for 13% -> 13% of each run, Pallas kernels for 30% -> 32%
where the time goes in v8:
time: 181 us; the launch traced here: 180 us
  waiting for transfers between devices  61.6 us (34%)
  Pallas kernels  59.9 us (33%)
  local copies, waits for them, and re-layouts  28.8 us (16%)
  starting transfers between devices  27.3 us (15%)
  other arithmetic  2.17 us (1%)
    pallas_call x15, Pallas kernels, call(): return lambda *operands: kernel(*operands, *after)  57.5 us
    ppermute x3, waiting for transfers between devices, sum_up(): codes.append(lax.ppermute(code, both, back))  29.4 us
    ppermute x1, waiting for transfers between devices, paired(): crossed = lax.ppermute(crossed, 'det', [(0, 1), (1, 0)])  19.1 us
    ppermute x1, waiting for transfers between devices, paired(): doubled = lax.ppermute(doubled, both, first_across)  13 us
    unnamed x32, local copies, waits for them, and re-layouts  8.22 us
    optimization_barrier x1, local copies, waits for them, and re-layouts, paired(): partner, own = lax.optimization_barrier((partner, own))  7.35 us
    ppermute x1, starting transfers between devices, paired(): got = [lax.ppermute(first, both, over)]  6.81 us
    ppermute x1, starting transfers between devices, paired(): given = lax.ppermute(share, both, to_second)  5.83 us
  transfers between devices with their start and end apart: 14, of which 5 were waited for; matrix products, arithmetic and copies ran while one was open for 13% of the time, Pallas kernels for 32%

profile of v8, /device:TPU:0, one launch (start us, length us, event | category | flops | bytes accessed | tf_op | source)
XLA Modules:
  0.0 180.3 jit_solution(1714412195331279296)
XLA Ops:
  0.0 0.5 collective-permute-start
  0.5 2.6 %slice_bitcast_fusion = bf16[4,128,2048]{2,0,1:T(4,128)(2,1)S(1)} fusion(bf16[4,2048,324]{1,0,2:T(4,128)(2,1)} %param.1), kind=kLoop, calls=%fused_computation.3 | loop fusion | bytes 4194304 | tf_op jit(solution)/shard_map/transpose | solution.py:409
  3.1 2.5 %copy.10 = bf16[4,128,2048]{2,1,0:T(8,128)(2,1)} copy(bf16[4,128,2048]{2,0,1:T(4,128)(2,1)S(1)} %slice_bitcast_fusion) | data formatting | bytes 4194304 | tf_op jit(solution)/shard_map/transpose | solution.py:409
  5.5 6.8 %collective-permute-start.2 = (bf16[512,2048]{1,0:T(8,128)(2,1)}, bf16[512,2048]{1,0:T(8,128)(2,1)}, u32[]{:S(2)}, u32[]{:S(2)}) collective-permute-start(bf16[512,2048]{1,0:T(8,128)(2,1)} %bitcast.3.refs_3_), channel_id=1, source_target_pairs={{0,16},{1,17},{4,20},{5,21},{8,24},{9,25},{12,28},{13,29},{18,2},{... | collective-permute-start | bytes 6291464 | tf_op jit(solution)/shard_map/ppermute | solution.py:411
  12.3 5.4 %copy.16 = bf16[4,2048,324]{1,2,0:T(8,128)(2,1)S(1)} copy(bf16[4,2048,324]{1,0,2:T(4,128)(2,1)} %param.1) | data formatting | bytes 10616832 | tf_op jit(solution)/shard_map/optimization_barrier | solution.py:410
  17.8 0.0 collective-permute-done
  17.8 7.4 %copy.15 = bf16[4,2048,324]{1,2,0:T(8,128)(2,1)S(1)} copy(bf16[4,2048,324]{1,0,2:T(4,128)(2,1)} %collective-permute-done) | data formatting | bytes 10616832 | tf_op jit(solution)/shard_map/optimization_barrier | solution.py:413
  25.1 0.0 copy-start.3
  25.1 5.1 %shard_map.17 = (f32[1744,256]{1,0:T(8,128)}, f32[8,128]{1,0:T(8,128)S(1)}) custom-call(s32[1]{0:T(128)} %bitcast.refs_0_, bf16[4,324,2048]{2,1,0:T(8,128)(2,1)S(1)} %bitcast.15, bf16[4,324,2048]{2,1,0:T(8,128)(2,1)S(1)} %bitcast.28, bf16[512,2048]{1,0:T(8,128)(2,1)} %bitcast.3.refs_3_), custom_call_target="tpu_custom_call" | custom-call | tf_op jit(solution)/shard_map/pallas_call | solution.py:41
  30.2 5.1 %shard_map.18 = (f32[1744,256]{1,0:T(8,128)}, f32[8,128]{1,0:T(8,128)S(1)}) custom-call(s32[1]{0:T(128)} %bitcast.refs_0_, bf16[4,324,2048]{2,1,0:T(8,128)(2,1)S(1)} %bitcast.16, bf16[4,324,2048]{2,1,0:T(8,128)(2,1)S(1)} %bitcast.29, f32[8,128]{1,0:T(8,128)S(1)} %get-tuple-element.53.refs_3_), custom_call_target="tpu_custom_call" | custom-call | tf_op jit(solution)/shard_map/pallas_call | solution.py:41
  35.3 3.4 %collective-permute-start.3 = (f32[1744,256]{1,0:T(8,128)}, f32[1744,256]{1,0:T(8,128)}, u32[]{:S(2)}, u32[]{:S(2)}) collective-permute-start(f32[1744,256]{1,0:T(8,128)} %get-tuple-element.62), channel_id=1, source_target_pairs={{0,1},{1,0},{4,5},{5,4},{8,9},{9,8},{12,13},{13,12},{16,17},{17,16... | collective-permute-start | bytes 5357576 | tf_op jit(solution)/shard_map/ppermute | solution.py:419
  38.7 0.6 collective-permute-start.4
  39.3 1.2 slice.11
  40.5 0.1 slice.10
  40.7 1.4 reshape.14
  42.1 2.0 %pad_maximum_fusion = bf16[784,2048]{1,0:T(8,128)(2,1)} fusion(bf16[272,2048]{1,0:T(8,128)(2,1)S(1)} %reshape.14, bf16[512,2048]{1,0:T(8,128)(2,1)S(1)} %bitcast.31), kind=kLoop, calls=%fused_computation.2 | loop fusion | flops 6422528 | bytes 6422528 | tf_op jit(solution)/shard_map/concatenate | solution.py:425
  44.1 1.8 collective-permute-start.1
  45.9 0.0 copy-start.4
  45.9 2.5 %copy-done.4 = bf16[4,2048,324]{1,2,0:T(8,128)(2,1)S(1)} copy-done((bf16[4,2048,324]{1,2,0:T(8,128)(2,1)S(1)}, bf16[4,2048,324]{1,2,0:T(8,128)(2,1)}, u32[]{:S(2)}) %copy-start.4) | copy-done | bytes 5308440
  48.4 7.2 %shard_map.19 = (f32[8,324,324]{2,1,0:T(8,128)S(1)}, f32[8,128]{1,0:T(8,128)S(1)}) custom-call(s32[1]{0:T(128)} %bitcast.refs_0_, bf16[4,324,2048]{2,1,0:T(8,128)(2,1)S(1)} %bitcast.19, bf16[4,324,2048]{2,1,0:T(8,128)(2,1)S(1)} %bitcast.30, f32[8,128]{1,0:T(8,128)S(1)} %get-tuple-element.58.refs_3_), custom_call_target="tpu_custom_call" | custom-call | tf_op jit(solution)/shard_map/pallas_call | solution.py:41
  55.6 0.0 copy-start.5
  55.7 0.0 collective-permute-done.2.refs_2_
  55.7 4.4 %shard_map.20 = (f32[2,4,328,128]{3,2,1,0:T(8,128)S(1)}, f32[8,128]{1,0:T(8,128)S(1)}) custom-call(s32[1]{0:T(128)} %bitcast.refs_0_, bf16[4,324,2048]{2,1,0:T(8,128)(2,1)S(1)} %bitcast.20, bf16[512,2048]{1,0:T(8,128)(2,1)} %collective-permute-done.2.refs_2_, f32[8,128]{1,0:T(8,128)S(1)} %get-tuple-element.59.refs_3_), custom_call_target="tpu_custom_call" | custom-call | tf_op jit(solution)/shard_map/pallas_call | solution.py:41
  60.0 0.0 copy-start.9
  60.1 1.1 copy-done.9
  61.1 13.0 %collective-permute-done.3.refs_2_ = f32[1744,256]{1,0:T(8,128)} collective-permute-done((f32[1744,256]{1,0:T(8,128)}, f32[1744,256]{1,0:T(8,128)}, u32[]{:S(2)}, u32[]{:S(2)}) %collective-permute-start.3) | collective-permute-done | bytes 1785888 | tf_op jit(solution)/shard_map/ppermute | solution.py:419
  74.1 19.1 %collective-permute-done.4.refs_4_.refs_2_ = f32[1744,256]{1,0:T(8,128)} collective-permute-done((f32[1744,256]{1,0:T(8,128)}, f32[1744,256]{1,0:T(8,128)}, u32[]{:S(2)}, u32[]{:S(2)}) %collective-permute-start.4) | collective-permute-done | bytes 1785888 | tf_op jit(solution)/shard_map/ppermute | solution.py:417
  93.3 0.0 copy-done.5
  93.3 3.1 %shard_map.21 = (f32[4,328,384]{2,1,0:T(8,128)}, f32[8,128]{1,0:T(8,128)S(1)}) custom-call(s32[1]{0:T(128)} %bitcast.refs_0_, f32[8,324,324]{2,1,0:T(8,128)S(1)} %get-tuple-element.61.refs_1_, f32[1744,256]{1,0:T(8,128)} %collective-permute-done.3.refs_2_, f32[8,128]{1,0:T(8,128)S(1)} %get-tuple-element.63.refs_3_, ...), custom_call_target="tpu_custom_call" | custom-call | tf_op jit(solution)/shard_map/pallas_call | solution.py:41
  96.3 5.8 %collective-permute-start.6 = (f32[4,328,384]{2,1,0:T(8,128)}, f32[4,328,384]{2,1,0:T(8,128)}, u32[]{:S(2)}, u32[]{:S(2)}) collective-permute-start(f32[4,328,384]{2,1,0:T(8,128)} %get-tuple-element.67.refs_3_), channel_id=1, source_target_pairs={{0,2},{1,3},{4,6},{5,7},{8,10},{9,11},{12,14},{13,15},{16,18},{17,... | collective-permute-start | bytes 6045704 | tf_op jit(solution)/shard_map/ppermute | solution.py:446
  102.2 2.5 %copy-done.2 = bf16[4,2048,324]{1,2,0:T(8,128)(2,1)S(1)} copy-done((bf16[4,2048,324]{1,2,0:T(8,128)(2,1)S(1)}, bf16[4,2048,324]{1,2,0:T(8,128)(2,1)}, u32[]{:S(2)}) %copy-start.2) | copy-done | bytes 5308440
  104.7 3.7 %shard_map.22 = (f32[2,4,328,128]{3,2,1,0:T(8,128)S(1)}, f32[8,128]{1,0:T(8,128)S(1)}) custom-call(s32[1]{0:T(128)} %bitcast.refs_0_, bf16[4,324,2048]{2,1,0:T(8,128)(2,1)S(1)} %bitcast.21, bf16[512,2048]{1,0:T(8,128)(2,1)} %collective-permute-done.2.refs_2_, f32[8,128]{1,0:T(8,128)S(1)} %get-tuple-element.65.refs_3_), custom_call_target="tpu_custom_call" | custom-call | tf_op jit(solution)/shard_map/pallas_call | solution.py:41
  108.4 0.7 collective-permute-start.5
  109.1 0.1 pad_add_fusion.1.refs_0_
  109.2 0.0 collective-permute-done.6.refs_4_
  109.2 7.4 %shard_map.23 = (f32[2,324,8,324]{3,2,1,0:T(8,128)}, f32[8,128]{1,0:T(8,128)S(1)}) custom-call(s32[2]{0:T(128)S(1)} %pad_add_fusion.1.refs_0_, f32[8,324,324]{2,1,0:T(8,128)S(1)} %copy-done.6, f32[1744,256]{1,0:T(8,128)} %collective-permute-done.4.refs_4_.refs_2_, f32[4,328,384]{2,1,0:T(8,128)} %get-tuple-element.67.refs_3_, ...), custom_call_target="tpu_custom_call" | custom-call | tf_op jit(solution)/shard_map/pallas_call | solution.py:41
  116.7 0.0 collective-permute-done.1.refs_2_
  116.7 2.4 %shard_map.24 = (f32[2,4,328,128]{3,2,1,0:T(8,128)S(1)}, f32[8,128]{1,0:T(8,128)S(1)}) custom-call(s32[1]{0:T(128)} %bitcast.refs_0_, bf16[4,324,2048]{2,1,0:T(8,128)(2,1)S(1)} %bitcast.24, bf16[784,2048]{1,0:T(8,128)(2,1)S(1)} %collective-permute-done.1.refs_2_, f32[8,128]{1,0:T(8,128)S(1)} %get-tuple-element.69.refs_3_), custom_call_target="tpu_custom_call" | custom-call | tf_op jit(solution)/shard_map/pallas_call | solution.py:41
  119.0 0.7 collective-permute-start.8
  119.8 3.1 %shard_map.25 = (f32[2,4,72,324]{3,2,1,0:T(8,128)S(1)}, f32[8,128]{1,0:T(8,128)S(1)}) custom-call(s32[1]{0:T(128)} %bitcast.refs_0_, bf16[4,324,2048]{2,1,0:T(8,128)(2,1)S(1)} %bitcast.25, bf16[784,2048]{1,0:T(8,128)(2,1)S(1)} %collective-permute-done.1.refs_2_, f32[8,128]{1,0:T(8,128)S(1)} %get-tuple-element.70.refs_3_), custom_call_target="tpu_custom_call" | custom-call | tf_op jit(solution)/shard_map/pallas_call | solution.py:41
  123.0 0.7 collective-permute-start.7
  123.7 0.0 collective-permute-done.5.refs_2_
  123.7 1.8 shard_map.26
  125.5 1.3 collective-permute-start.12
  126.8 2.4 %shard_map.27 = (f32[2,4,328,128]{3,2,1,0:T(8,128)S(1)}, f32[8,128]{1,0:T(8,128)S(1)}) custom-call(s32[1]{0:T(128)} %bitcast.refs_0_, bf16[4,324,2048]{2,1,0:T(8,128)(2,1)S(1)} %bitcast.26, bf16[784,2048]{1,0:T(8,128)(2,1)S(1)} %collective-permute-done.1.refs_2_, f32[8,128]{1,0:T(8,128)S(1)} %get-tuple-element.72.refs_3_), custom_call_target="tpu_custom_call" | custom-call | tf_op jit(solution)/shard_map/pallas_call | solution.py:41
  129.1 3.2 %shard_map.28 = (f32[2,4,72,324]{3,2,1,0:T(8,128)S(1)}, f32[8,128]{1,0:T(8,128)S(1)}) custom-call(s32[1]{0:T(128)} %bitcast.refs_0_, bf16[4,324,2048]{2,1,0:T(8,128)(2,1)S(1)} %bitcast.27, bf16[784,2048]{1,0:T(8,128)(2,1)S(1)} %collective-permute-done.1.refs_2_, f32[8,128]{1,0:T(8,128)S(1)} %get-tuple-element.73.refs_3_), custom_call_target="tpu_custom_call" | custom-call | tf_op jit(solution)/shard_map/pallas_call | solution.py:41
  132.3 0.0 collective-permute-done.8.refs_2_
  132.3 2.0 %shard_map.29 = (f32[2,4,324,128]{3,2,1,0:T(8,128)S(1)}, bf16[2,4,328,128]{3,2,1,0:T(8,128)(2,1)}, bf16[2,2,2,328,128]{4,3,2,1,0:T(8,128)(2,1)}, f32[8,128]{1,0:T(8,128)S(1)}) custom-call(s32[1]{0:T(128)} %bitcast.refs_0_, f32[2,4,328,128]{3,2,1,0:T(8,128)S(1)} %get-tuple-element.76.refs_1_, f32[2,4,328,128]{3,2,1,0:T(8,128)S(1)} %collective-permute-done.8.refs_2_, ...), custom_call_target="tpu_custom_call" | custom-call | tf_op jit(solution)/shard_map/pallas_call | solution.py:41
  134.3 0.8 collective-permute-start.10
  135.2 1.5 collective-permute-start.13
  136.7 0.0 collective-permute-done.7.refs_2_
  136.7 1.4 shard_map.30
  138.1 0.9 copy-done.11
  139.0 1.3 collective-permute-start.9
  140.3 1.4 collective-permute-start.11
  141.6 0.1 pad_add_fusion.refs_0_.s_ref
  141.7 1.7 collective-permute-done.12.refs_8_
  143.4 0.0 collective-permute-done.11
  143.4 0.0 collective-permute-done.10.refs_5_.refs_6_
  143.4 17.6 %collective-permute-done.13.refs_9_ = bf16[2,4,328,128]{3,2,1,0:T(8,128)(2,1)} collective-permute-done((bf16[2,4,328,128]{3,2,1,0:T(8,128)(2,1)}, bf16[2,4,328,128]{3,2,1,0:T(8,128)(2,1)}, u32[]{:S(2)}, u32[]{:S(2)}) %collective-permute-start.13) | collective-permute-done | bytes 671776 | tf_op jit(solution)/shard_map/ppermute | solution.py:438
  161.0 1.2 copy-done.12
  162.2 5.4 %shard_map.31 = (f32[2,324,8,324]{3,2,1,0:T(8,128)}, f32[8,128]{1,0:T(8,128)}) custom-call(s32[2]{0:T(128)S(1)} %pad_add_fusion.refs_0_.s_ref, f32[2,324,8,324]{3,2,1,0:T(8,128)} %get-tuple-element.82.refs_1_, f32[2,4,324,128]{3,2,1,0:T(8,128)S(1)} %copy-done.8, f32[2,4,324,128]{3,2,1,0:T(8,128)S(1)} %get-tuple-element.83.refs_3_, ...), custom_call_target="tpu_custom_call", output_to_operand_aliasing={{0}: (1, {})} | custom-call | tf_op jit(solution)/shard_map/pallas_call | solution.py:41
  167.5 10.1 %collective-permute-done.9.last_ref = bf16[2,4,72,324]{3,2,1,0:T(8,128)(2,1)} collective-permute-done((bf16[2,4,72,324]{3,2,1,0:T(8,128)(2,1)}, bf16[2,4,72,324]{3,2,1,0:T(8,128)(2,1)}, u32[]{:S(2)}, u32[]{:S(2)}) %collective-permute-start.9) | collective-permute-done | bytes 373280 | tf_op jit(solution)/shard_map/ppermute | solution.py:438
  177.7 2.4 %shard_map.32 = f32[2,324,8,324]{3,2,1,0:T(8,128)} custom-call(s32[2]{0:T(128)} %copy-done.13, f32[2,324,8,324]{3,2,1,0:T(8,128)} %get-tuple-element.91.out_in, bf16[2,4,72,324]{3,2,1,0:T(8,128)(2,1)} %collective-permute-done.9.last_ref), custom_call_target="tpu_custom_call", output_to_operand_aliasing={{}: (1, {})} | custom-call | tf_op jit(solution)/shard_map/pallas_call | solution.py:373
  (23 shorter events, 0.0 us)
Async XLA Ops:
  0.0 17.8 %collective-permute-start = (bf16[4,2048,324]{1,0,2:T(4,128)(2,1)}, bf16[4,2048,324]{1,0,2:T(4,128)(2,1)}, u32[]{:S(2)}, u32[]{:S(2)}) collective-permute-start(bf16[4,2048,324]{1,0,2:T(4,128)(2,1)} %param.1), channel_id=1, source_target_pairs={{0,2},{2,0},{4,6},{6,4},{8,10},{10,8},{12,14},{14,12},{16,18},{18,... | collective-permute-start | bytes 15925256 | tf_op jit(solution)/shard_map/ppermute | solution.py:408
  5.5 50.1 %collective-permute-start.2 = (bf16[512,2048]{1,0:T(8,128)(2,1)}, bf16[512,2048]{1,0:T(8,128)(2,1)}, u32[]{:S(2)}, u32[]{:S(2)}) collective-permute-start(bf16[512,2048]{1,0:T(8,128)(2,1)} %bitcast.3.refs_3_), channel_id=1, source_target_pairs={{0,16},{1,17},{4,20},{5,21},{8,24},{9,25},{12,28},{13,29},{18,2},{... | collective-permute-start | bytes 6291464 | tf_op jit(solution)/shard_map/ppermute | solution.py:411
  17.7 22.8 %copy-start = (bf16[4,2048,324]{1,2,0:T(8,128)(2,1)}, bf16[4,2048,324]{1,2,0:T(8,128)(2,1)S(1)}, u32[]{:S(2)}) copy-start(bf16[4,2048,324]{1,2,0:T(8,128)(2,1)S(1)} %copy.16) | copy-start | bytes 15925252
  25.1 5.1 %copy-start.3 = (bf16[4,2048,324]{1,2,0:T(8,128)(2,1)}, bf16[4,2048,324]{1,2,0:T(8,128)(2,1)S(1)}, u32[]{:S(2)}) copy-start(bf16[4,2048,324]{1,2,0:T(8,128)(2,1)S(1)} %copy.15) | copy-start | bytes 15925252
  35.3 38.8 %collective-permute-start.3 = (f32[1744,256]{1,0:T(8,128)}, f32[1744,256]{1,0:T(8,128)}, u32[]{:S(2)}, u32[]{:S(2)}) collective-permute-start(f32[1744,256]{1,0:T(8,128)} %get-tuple-element.62), channel_id=1, source_target_pairs={{0,1},{1,0},{4,5},{5,4},{8,9},{9,8},{12,13},{13,12},{16,17},{17,16... | collective-permute-start | bytes 5357576 | tf_op jit(solution)/shard_map/ppermute | solution.py:419
  38.7 54.6 %collective-permute-start.4 = (f32[1744,256]{1,0:T(8,128)}, f32[1744,256]{1,0:T(8,128)}, u32[]{:S(2)}, u32[]{:S(2)}) collective-permute-start(f32[1744,256]{1,0:T(8,128)} %get-tuple-element.64), channel_id=1, source_target_pairs={{0,1},{1,0},{2,3},{3,2},{4,5},{5,4},{6,7},{7,6},{8,9},{9,8},{10,11... | collective-permute-start | bytes 5357576 | tf_op jit(solution)/shard_map/ppermute | solution.py:417
  42.1 3.8 %copy-start.1 = (bf16[4,2048,324]{1,2,0:T(8,128)(2,1)S(1)}, bf16[4,2048,324]{1,2,0:T(8,128)(2,1)}, u32[]{:S(2)}) copy-start(bf16[4,2048,324]{1,2,0:T(8,128)(2,1)} %copy-done) | copy-start | bytes 15925252
  44.1 72.6 %collective-permute-start.1 = (bf16[784,2048]{1,0:T(8,128)(2,1)}, bf16[784,2048]{1,0:T(8,128)(2,1)S(1)}, u32[]{:S(2)}, u32[]{:S(2)}) collective-permute-start(bf16[784,2048]{1,0:T(8,128)(2,1)} %pad_maximum_fusion), channel_id=1, source_target_pairs={{0,16},{1,17},{4,20},{5,21},{8,24},{9,25},{12,28},{13,29},{18,2},{... | collective-permute-start | bytes 9633800 | tf_op jit(solution)/shard_map/ppermute | solution.py:426
  45.9 2.5 %copy-start.4 = (bf16[4,2048,324]{1,2,0:T(8,128)(2,1)S(1)}, bf16[4,2048,324]{1,2,0:T(8,128)(2,1)}, u32[]{:S(2)}) copy-start(bf16[4,2048,324]{1,2,0:T(8,128)(2,1)} %copy-done.3) | copy-start | bytes 15925252
  55.6 37.6 %copy-start.5 = (f32[8,324,324]{2,1,0:T(8,128)}, f32[8,324,324]{2,1,0:T(8,128)S(1)}, u32[]{:S(2)}) copy-start(f32[8,324,324]{2,1,0:T(8,128)S(1)} %get-tuple-element.61.refs_1_) | copy-start | bytes 10077700
  60.0 1.1 copy-start.9
  96.3 12.9 %collective-permute-start.6 = (f32[4,328,384]{2,1,0:T(8,128)}, f32[4,328,384]{2,1,0:T(8,128)}, u32[]{:S(2)}, u32[]{:S(2)}) collective-permute-start(f32[4,328,384]{2,1,0:T(8,128)} %get-tuple-element.67.refs_3_), channel_id=1, source_target_pairs={{0,2},{1,3},{4,6},{5,7},{8,10},{9,11},{12,14},{13,15},{16,18},{17,... | collective-permute-start | bytes 6045704 | tf_op jit(solution)/shard_map/ppermute | solution.py:446
  102.2 2.5 %copy-start.2 = (bf16[4,2048,324]{1,2,0:T(8,128)(2,1)S(1)}, bf16[4,2048,324]{1,2,0:T(8,128)(2,1)}, u32[]{:S(2)}) copy-start(bf16[4,2048,324]{1,2,0:T(8,128)(2,1)} %copy-done) | copy-start | bytes 15925252
  104.7 4.5 %copy-start.6 = (f32[8,324,324]{2,1,0:T(8,128)S(1)}, f32[8,324,324]{2,1,0:T(8,128)}, u32[]{:S(2)}) copy-start(f32[8,324,324]{2,1,0:T(8,128)} %copy-done.5) | copy-start | bytes 10077700
  108.4 15.3 %collective-permute-start.5 = (f32[2,4,328,128]{3,2,1,0:T(8,128)S(1)}, f32[2,4,328,128]{3,2,1,0:T(8,128)S(1)}, u32[]{:S(2)}, u32[]{:S(2)}) collective-permute-start(f32[2,4,328,128]{3,2,1,0:T(8,128)S(1)} %get-tuple-element.66), channel_id=1, source_target_pairs={{2,3},{3,2},{6,7},{7,6},{10,11},{11,10},{14,15},{15,14},{16,17},{1... | collective-permute-start | bytes 4030472 | tf_op jit(solution)/shard_map/ppermute | solution.py:449
  109.2 7.4 %slice-start = ((s8[5373952]{0:T(1024)(128)(4,1)}), s8[4194304]{0:T(1024)(128)(4,1)S(1)}, s32[]{:S(2)}) async-start(s8[5373952]{0:T(1024)(128)(4,1)} %bitcast.22), calls=%async_computation | async-start | bytes 8388608
  109.2 7.4 %slice-start.1 = ((s8[5373952]{0:T(1024)(128)(4,1)}), s8[1179648]{0:T(1024)(128)(4,1)S(1)}, s32[]{:S(2)}) async-start(s8[5373952]{0:T(1024)(128)(4,1)} %bitcast.22), calls=%async_computation.1 | async-start | bytes 2359296
  119.0 13.3 %collective-permute-start.8 = (f32[2,4,328,128]{3,2,1,0:T(8,128)S(1)}, f32[2,4,328,128]{3,2,1,0:T(8,128)S(1)}, u32[]{:S(2)}, u32[]{:S(2)}) collective-permute-start(f32[2,4,328,128]{3,2,1,0:T(8,128)S(1)} %get-tuple-element.77), channel_id=1, source_target_pairs={{2,3},{3,2},{6,7},{7,6},{10,11},{11,10},{14,15},{15,14},{16,17},{1... | collective-permute-start | bytes 4030472 | tf_op jit(solution)/shard_map/ppermute | solution.py:449
  119.8 3.9 %copy-start.10 = (f32[2,4,328,128]{3,2,1,0:T(8,128)S(1)}, f32[2,4,328,128]{3,2,1,0:T(8,128)}, u32[]{:S(2)}) copy-start(f32[2,4,328,128]{3,2,1,0:T(8,128)} %copy-done.9) | copy-start | bytes 4030468
  123.0 13.7 %collective-permute-start.7 = (f32[2,4,72,324]{3,2,1,0:T(8,128)S(1)}, f32[2,4,72,324]{3,2,1,0:T(8,128)S(1)}, u32[]{:S(2)}, u32[]{:S(2)}) collective-permute-start(f32[2,4,72,324]{3,2,1,0:T(8,128)S(1)} %get-tuple-element.75), channel_id=1, source_target_pairs={{2,3},{3,2},{6,7},{7,6},{10,11},{11,10},{14,15},{15,14},{16,17},{1... | collective-permute-start | bytes 2239496 | tf_op jit(solution)/shard_map/ppermute | solution.py:449
  125.5 6.8 %copy-start.7 = (f32[2,4,324,128]{3,2,1,0:T(8,128)}, f32[2,4,324,128]{3,2,1,0:T(8,128)S(1)}, u32[]{:S(2)}) copy-start(f32[2,4,324,128]{3,2,1,0:T(8,128)S(1)} %get-tuple-element.78.refs_3_.refs_2_) | copy-start | bytes 3981316
  125.5 17.9 %collective-permute-start.12 = (bf16[2,4,328,128]{3,2,1,0:T(8,128)(2,1)}, bf16[2,4,328,128]{3,2,1,0:T(8,128)(2,1)}, u32[]{:S(2)}, u32[]{:S(2)}) collective-permute-start(bf16[2,4,328,128]{3,2,1,0:T(8,128)(2,1)} %get-tuple-element.87), channel_id=1, source_target_pairs={{16,0},{17,1},{20,4},{21,5},{24,8},{25,9},{28,12},{29,13},{2,18},{... | collective-permute-start | bytes 2015240 | tf_op jit(solution)/shard_map/ppermute | solution.py:438
  134.3 26.7 %copy-start.8 = (f32[2,4,324,128]{3,2,1,0:T(8,128)S(1)}, f32[2,4,324,128]{3,2,1,0:T(8,128)}, u32[]{:S(2)}) copy-start(f32[2,4,324,128]{3,2,1,0:T(8,128)} %copy-done.7) | copy-start | bytes 3981316
  134.3 9.0 %collective-permute-start.10 = (bf16[2,2,2,328,128]{4,3,2,1,0:T(8,128)(2,1)}, bf16[2,2,2,328,128]{4,3,2,1,0:T(8,128)(2,1)S(1)}, u32[]{:S(2)}, u32[]{:S(2)}) collective-permute-start(bf16[2,2,2,328,128]{4,3,2,1,0:T(8,128)(2,1)} %get-tuple-element.85), channel_id=1, source_target_pairs={{2,3},{3,2},{6,7},{7,6},{10,11},{11,10},{14,15},{15,14},{16,17},{1... | collective-permute-start | bytes 2015240 | tf_op jit(solution)/shard_map/ppermute | solution.py:439
  135.2 25.8 %collective-permute-start.13 = (bf16[2,4,328,128]{3,2,1,0:T(8,128)(2,1)}, bf16[2,4,328,128]{3,2,1,0:T(8,128)(2,1)}, u32[]{:S(2)}, u32[]{:S(2)}) collective-permute-start(bf16[2,4,328,128]{3,2,1,0:T(8,128)(2,1)} %get-tuple-element.88), channel_id=1, source_target_pairs={{16,0},{17,1},{20,4},{21,5},{24,8},{25,9},{28,12},{29,13},{2,18},{... | collective-permute-start | bytes 2015240 | tf_op jit(solution)/shard_map/ppermute | solution.py:438
  138.1 0.9 copy-start.11
  139.0 38.7 %collective-permute-start.9 = (bf16[2,4,72,324]{3,2,1,0:T(8,128)(2,1)}, bf16[2,4,72,324]{3,2,1,0:T(8,128)(2,1)}, u32[]{:S(2)}, u32[]{:S(2)}) collective-permute-start(bf16[2,4,72,324]{3,2,1,0:T(8,128)(2,1)} %get-tuple-element.81), channel_id=1, source_target_pairs={{16,0},{17,1},{20,4},{21,5},{24,8},{25,9},{28,12},{29,13},{2,18},{... | collective-permute-start | bytes 1119752 | tf_op jit(solution)/shard_map/ppermute | solution.py:438
  140.3 3.1 %collective-permute-start.11 = (bf16[1,2,2,72,324]{4,3,2,1,0:T(8,128)(2,1)}, bf16[1,2,2,72,324]{4,3,2,1,0:T(8,128)(2,1)}, u32[]{:S(2)}, u32[]{:S(2)}) collective-permute-start(bf16[1,2,2,72,324]{4,3,2,1,0:T(8,128)(2,1)} %get-tuple-element.86), channel_id=1, source_target_pairs={{2,3},{3,2},{6,7},{7,6},{10,11},{11,10},{14,15},{15,14},{16,17},{1... | collective-permute-start | bytes 559880 | tf_op jit(solution)/shard_map/ppermute | solution.py:439
  141.7 25.8 %copy-start.13 = (s32[2]{0:T(128)}, s32[2]{0:T(128)S(1)}, u32[]{:S(2)}) copy-start(s32[2]{0:T(128)S(1)} %pad_add_fusion.refs_0_.s_ref) | copy-start | bytes 28
  161.0 1.2 copy-start.12

commit v9 on v8

--- a/solution.py
+++ b/solution.py
@@ -17,13 +17,14 @@
     return lax.dot_general(left, right, (((1,), (1,)), ((), ())), preferred_element_type=jnp.float32)
 
 
-def call(body, grid, scalars, in_specs, out_specs, out_shape, after=(), aliases={}):
+def call(body, grid, scalars, in_specs, out_specs, out_shape, after=(), aliases={}, scratch=()):
     idle = len(after)
 
     def waiting(*refs):
         first = scalars + len(in_specs)
-        body(*refs[:first], *refs[first + idle : -1])
-        refs[-1][...] = jnp.zeros_like(refs[-1])
+        last = first + idle + len(out_specs)
+        body(*refs[:first], *refs[first + idle : last], *refs[last + 1 :])
+        refs[last][...] = jnp.zeros_like(refs[last])
 
     token = (8, LANES)
     kernel = pl.pallas_call(
@@ -33,6 +34,7 @@
             grid=grid,
             in_specs=in_specs + [pl.BlockSpec(memory_space=pl.ANY)] * idle,
             out_specs=[*out_specs, whole(token)],
+            scratch_shapes=scratch,
         ),
         out_shape=[*out_shape, f32(*token)],
         input_output_aliases=aliases,
@@ -226,58 +228,39 @@
     )(det, own, got)
 
 
-def far_sum(det, keep, came, rows, turned, others=None, after=()):
-    half, states, padded, lanes = keep.shape
-    earlier = len(others or ())
+def far_sum(det, keep, came, rows, turned, after=()):
+    half, states, _, lanes = keep.shape
     shape = (up(rows + 1, 8), lanes)
 
-    def body(x_ref, keep_ref, came_ref, *refs):
+    def body(x_ref, keep_ref, came_ref, tile_ref, code_ref, cross_ref):
         x = x_ref[0]
-        other_refs, (tile_ref, code_ref), cross_refs = refs[:earlier], refs[earlier:][:2], refs[earlier + 2 :]
         top = jnp.zeros((rows, lanes), jnp.float32)
         for a in range(half):
             for v in range(states):
-                tile = keep_ref[a, v, :rows] + came_ref[a, v, :rows]
-                tile_ref[a, v] = tile
-                top = jnp.maximum(top, jnp.abs(tile))
-
-        def coder(top):
-            exponent = jnp.floor(jnp.log2(jnp.maximum(jnp.max(top, keepdims=True), SMALLEST)))
-            scale = jnp.exp2(LIFT - exponent)
-            below = jnp.broadcast_to(exponent, (shape[0] - rows, lanes))
-            return lambda tile: jnp.concatenate([powered(tile * scale), below]).astype(jnp.bfloat16)
-
-        code = coder(top)
+                top = jnp.maximum(top, jnp.abs(keep_ref[a, v, :rows] + came_ref[a, v, :rows]))
+        exponent = jnp.floor(jnp.log2(jnp.maximum(jnp.max(top, keepdims=True), SMALLEST)))
+        scale = jnp.exp2(LIFT - exponent)
+        below = jnp.broadcast_to(exponent, (shape[0] - rows, lanes))
         for a in range(half):
             for v in range(states):
-                code_ref[a, v] = code(tile_ref[a, v])
-        for cross_ref in cross_refs:
-            for a in range(half):
-                for b in range(half):
-                    cross_ref[earlier, a, b] = code_ref[a, half * (1 - x) + b]
-            for k, other_ref in enumerate(other_refs):
-                top = jnp.zeros((rows, lanes), jnp.float32)
-                for a in range(half):
-                    for v in range(states):
-                        top = jnp.maximum(top, jnp.abs(other_ref[a, v]))
-                code = coder(top)
-                for a in range(half):
-                    for b in range(half):
-                        cross_ref[k, a, b] = code(other_ref[a, half * (1 - x) + b])
-
-    shapes = [(half, states, rows, lanes), (half, states, *shape)]
-    if others is not None:
-        shapes.append((earlier + 1, half, half, *shape))
-    kinds = [jnp.float32] + [jnp.bfloat16] * (len(shapes) - 1)
+                tile = keep_ref[a, v, :rows] + came_ref[a, v, :rows]
+                code_ref[a, v] = jnp.concatenate([powered(tile * scale), below]).astype(jnp.bfloat16)
+            for b in range(half):
+                v = half * x + b
+                tile_ref[a, b] = keep_ref[a, v, :rows] + came_ref[a, v, :rows]
+                cross_ref[a, b] = code_ref[a, half * (1 - x) + b]
+
+    shapes = [(half, half, rows, lanes), (half, states, *shape), (half, half, *shape)]
+    kinds = [jnp.float32, jnp.bfloat16, jnp.bfloat16]
     return call(
         body,
         (1,),
         1,
-        [whole(keep.shape)] * 2 + [whole(shapes[0])] * earlier,
+        [whole(keep.shape)] * 2,
         [whole(s) for s in shapes],
         [jax.ShapeDtypeStruct(s, kind) for s, kind in zip(shapes, kinds)],
         after,
-    )(det, keep, came, *(others or ()))
+    )(det, keep, came)
 
 
 def powered(value):
@@ -286,102 +269,85 @@
     return value * jnp.abs(value) * (fourth * fourth)
 
 
-def rooted(code, exponent):
+def decoded(code, rows):
     code = code.astype(jnp.float32)
-    root = jnp.exp2(jnp.log2(jnp.abs(code)) * (1 / POWER)) * jnp.exp2(exponent - LIFT)
-    return jnp.where(code < 0, -root, root)
-
-
-def decoded(code, rows):
-    return rooted(code[:rows], code[rows:].astype(jnp.float32)[:1])
-
-
-def place(place_in, out, finished, crossed, came, after=()):
-    _, ops, tiles, _ = out.shape
-    full = len(came)
-    half, states, _, _ = finished[0].shape
-    wide = full * LANES
-    turned, last = crossed
+    value, exponent = code[:rows], code[rows : rows + 1]
+    root = jnp.exp2(jnp.log2(jnp.abs(value)) * (1 / POWER)) * jnp.exp2(exponent - LIFT)
+    return jnp.where(value < 0, -root, root)
+
+
+def into_place(role, place_in, out, pieces, after=()):
+    tiles = out.shape[2]
+    sources = [v for piece in pieces for v in piece[2]]
+    count = len(sources)
 
     def body(s_ref, out_in, *refs):
-        finished_refs, came_refs, out_ref = refs[: full + 1], refs[full + 4 : -1], refs[-1]
-        turned_ref, under_ref, last_ref = refs[full + 1 :][:3]
-        x = s_ref[0]
-
-        @pl.when(s_ref[1] == 1)
+        out_ref, held, made, sems = refs[count], refs[count + 1 : 2 * count + 1], refs[2 * count + 1 : -1], refs[-1]
+
+        @pl.when(s_ref[1] == role)
         def _():
-            for b in range(half):
-                for u in range(states):
-                    a, t = u % half, b * states + u
-
-                    @pl.when(u // half == x)
-                    def _():
-                        for k in range(full):
-                            out_ref[0, :, t, k * LANES : (k + 1) * LANES] = finished_refs[k][a, half * x + b]
-                        out_ref[0, :, t, wide:] = finished_refs[full][a, half * x + b].T
-
-                    @pl.when(u // half != x)
-                    def _():
-                        for k in range(full):
-                            exponent = under_ref[k, a, b].astype(jnp.float32)[ops % 16 : ops % 16 + 1]
-                            out_ref[0, :, t, k * LANES : (k + 1) * LANES] = rooted(turned_ref[k, a, b], exponent)
-                        exponent = last_ref[a, b, ops - wide :, :1].astype(jnp.float32)[:1]
-                        out_ref[0, :, t, wide:] = rooted(last_ref[a, b, : ops - wide], exponent).T
-
-        for k in range(full):
-
-            @pl.when((s_ref[1] == 0) & (pl.program_id(0) == k))
-            def _():
-                for a in range(half):
-                    for v in range(states):
-                        out_ref[0, :, a * states + v] = decoded(came_refs[k][a, v], ops).T
-
-    steps = pl.cdiv(ops, LANES)
-    return call(
-        body,
-        (steps,),
-        1,
-        [pl.BlockSpec(memory_space=pl.ANY)]
-        + [pl.BlockSpec((half, states, LANES, LANES), lambda i, s: (0, 0, i, 0))] * full
-        + [pl.BlockSpec((half, states, ops - wide, LANES), lambda i, s: (0, 0, 0, i))]
-        + [pl.BlockSpec((full, half, half, LANES, LANES), lambda i, s: (0, 0, 0, i, 0))]
-        + [pl.BlockSpec((full, half, half, 16, LANES), lambda i, s: (0, 0, 0, ops // 16, 0))]
-        + [pl.BlockSpec((half, half, last.shape[2], LANES), lambda i, s: (0, 0, 0, i))]
-        + [whole(c.shape) for c in came],
-        [pl.BlockSpec((1, LANES, tiles, ops), lambda i, s: (0, i, 0, 0))],
+            loads = [pltpu.make_async_copy(refs[k], held[k], sems.at[k]) for k in range(count)]
+            for load in loads:
+                load.start()
+            stores, first = [], 0
+            for k, (rows, lanes, own, fill) in enumerate(pieces):
+                for load in loads[first : first + len(own)]:
+                    load.wait()
+                fill(s_ref[0], held[first : first + len(own)], made[k])
+                first += len(own)
+                target = out_ref.at[0, pl.ds(*rows), :, pl.ds(*lanes)]
+                stores.append(pltpu.make_async_copy(made[k], target, sems.at[count + k]))
+                stores[k].start()
+            for store in stores:
+                store.wait()
+
+    return call(
+        body,
+        (1,),
+        1,
+        [pl.BlockSpec(memory_space=pl.ANY)] * (1 + count),
+        [pl.BlockSpec(memory_space=pl.ANY)],
         [f32(*out.shape)],
         after,
         {1: 0},
-    )(place_in, out, *finished, turned, turned, last, *came)
-
-
-def finish(place_in, out, last):
-    _, ops, tiles, _ = out.shape
-    half, states, _, _ = last.shape
-    rest = ops % LANES
-
-    def body(s_ref, out_in, last_ref, out_ref, rows_ref, sem):
-        @pl.when(s_ref[1] == 0)
-        def _():
-            for a in range(half):
-                for v in range(states):
-                    rows_ref[:, a * states + v] = decoded(last_ref[a, v], rest)
-            copy = pltpu.make_async_copy(rows_ref, out_ref.at[0, pl.ds(ops - rest, rest)], sem)
-            copy.start()
-            copy.wait()
-
-    return pl.pallas_call(
-        body,
-        in_specs=[
-            pl.BlockSpec(memory_space=pltpu.SMEM),
-            pl.BlockSpec(memory_space=pl.ANY),
-            pl.BlockSpec(memory_space=pltpu.VMEM),
-        ],
-        out_specs=pl.BlockSpec(memory_space=pl.ANY),
-        out_shape=f32(*out.shape),
-        input_output_aliases={1: 0},
-        scratch_shapes=[pltpu.VMEM((rest, tiles, ops), jnp.float32), pltpu.SemaphoreType.DMA],
-    )(place_in, out, last)
+        [pltpu.VMEM(v.shape, v.dtype) for v in sources]
+        + [pltpu.VMEM((rows[1], tiles, lanes[1]), jnp.float32) for rows, lanes, *_ in pieces]
+        + [pltpu.SemaphoreType.DMA((count + len(pieces),))],
+    )(place_in, out, *sources)
+
+
+def returned_piece(code, start, width, ops):
+    half, states, _, _ = code.shape
+    turned = code.shape[3] == width
+
+    def fill(x, refs, ref):
+        for a in range(half):
+            for v in range(states):
+                one = refs[0][a, v]
+                ref[:, a * states + v] = decoded(one, ops).T if turned else decoded(one, width)
+
+    return (start, width), (0, ops), (code,), fill
+
+
+def finished_piece(tiles, cross, start, width, ops):
+    half, _, rows, _ = tiles.shape
+    turned = rows == ops
+
+    def fill(x, refs, ref):
+        for b in range(half):
+            for u in range(2 * half):
+                a, t = u % half, 2 * half * b + u
+
+                @pl.when(u // half == x)
+                def _():
+                    ref[:, t] = refs[0][a, b] if turned else refs[0][a, b].T
+
+                @pl.when(u // half != x)
+                def _():
+                    one = decoded(refs[1][a, b], rows)
+                    ref[:, t] = one if turned else one.T
+
+    return (0, ops), (start, width), (tiles, cross), fill
 
 
 def paired(amplitudes):
@@ -429,15 +395,14 @@
         start = states * LANES * (k - 1) if k else 0
         return far_terms(det, own, got[min(k, 1)], start, widths[k], k < full, mine, done)
 
-    finished, codes, crossing, kepts, came = [], [], [], [], []
+    codes, mine, kepts, came = [], [], [], []
 
     def sum_up(k, token):
         rows = ops if k < full else widths[k]
-        others = finished[:k] if k == full - 1 else [] if k == full else None
-        tiles, code, *cross, token = far_sum(det, kepts[k], came[k], rows, k < full, others, (token,))
-        codes.append(lax.ppermute(code, both, back))
-        crossing.extend(lax.ppermute(c, both, across) for c in cross)
-        finished.append(tiles)
+        tiles, code, cross, token = far_sum(det, kepts[k], came[k], rows, k < full, (token,))
+        place = k * LANES, widths[k], ops
+        codes.append(returned_piece(lax.ppermute(code, both, back), *place))
+        mine.append(finished_piece(tiles, lax.ppermute(cross, both, across), *place))
         return token
 
     kept, token = terms(0, True, token)
@@ -449,7 +414,8 @@
         came.append(lax.ppermute(send, both, across))
         if k == 0:
             out, token = near_sum(jnp.stack([x, core]), keep, crossed, share, given, states, (token,))
-    token = sum_up(0, token)
+        if k == 1:
+            token = sum_up(0, token)
     for k in range(1, full + 1):
         kept, token = terms(k, True, token)
         kepts.append(kept)
@@ -457,10 +423,9 @@
         token = sum_up(k, token)
 
     at = jnp.stack([x, receiver])
-    crossing[1] = crossing[1].reshape(crossing[1].shape[1:])
-    out, token = place(at, out, finished, crossing, codes[:full], (token,))
-    last, out = lax.optimization_barrier((codes[full], out))
-    return finish(at, out, last).transpose(0, 2, 1, 3)
+    for role, pieces in ((0, codes[:full]), (1, mine[:full]), (1, mine[full:]), (0, codes[full:])):
+        out, token = into_place(role, at, out, pieces, (token,))
+    return out.transpose(0, 2, 1, 3)
 
 
 def partner_2(value, axis, stride):

time: 181 us -> 183 us (1.011)
    pallas_call x15 -> x18, Pallas kernels: 57.5 us -> 61 us  [call(): return lambda *operands: kernel(*operands, *after)]
    pallas_call x1 -> x0, Pallas kernels: 2.41 us -> none  [finish(): pl.pallas_call(body, in_specs=[pl.BlockSpec(memory_space=pltpu.SMEM), pl....]
    ppermute x5 -> x6, waiting for transfers between devices: 29.4 us -> 29.9 us  [the longest x3 29.9 us: sum_up(): codes.append(returned_piece(lax.ppermute(code, both, back), *place))]
    unnamed x32 -> x28, local copies, waits for them, and re-layouts: 8.22 us -> 7.96 us
    ppermute x5 -> x6, starting transfers between devices: 6.26 us -> 6.1 us  [the longest x3 4.07 us: sum_up(): codes.append(returned_piece(lax.ppermute(code, both, back), *place))]
  transfers between devices with their start and end apart: 14 -> 15, of which waited for: 5 -> 4; matrix products, arithmetic and copies ran while one was open for 13% -> 12% of each run, Pallas kernels for 32% -> 32%
where the time goes in v9:
time: 183 us; the launch traced here: 182 us
  waiting for transfers between devices  61.9 us (34%)
  Pallas kernels  61 us (33%)
  local copies, waits for them, and re-layouts  28.6 us (16%)
  starting transfers between devices  28.4 us (16%)
  other arithmetic  2.04 us (1%)
    pallas_call x18, Pallas kernels, call(): return lambda *operands: kernel(*operands, *after)  61 us
    ppermute x3, waiting for transfers between devices, sum_up(): codes.append(returned_piece(lax.ppermute(code, both, back), *place))  29.9 us
    ppermute x1, waiting for transfers between devices, paired(): crossed = lax.ppermute(crossed, 'det', [(0, 1), (1, 0)])  19.1 us
    ppermute x1, waiting for transfers between devices, paired(): doubled = lax.ppermute(doubled, both, first_across)  12.8 us
    unnamed x28, local copies, waits for them, and re-layouts  7.96 us
    optimization_barrier x1, local copies, waits for them, and re-layouts, paired(): partner, own = lax.optimization_barrier((partner, own))  7.35 us
    ppermute x1, starting transfers between devices, paired(): got = [lax.ppermute(first, both, over)]  6.83 us
    ppermute x1, starting transfers between devices, paired(): given = lax.ppermute(share, both, to_second)  5.89 us
  transfers between devices with their start and end apart: 15, of which 4 were waited for; matrix products, arithmetic and copies ran while one was open for 12% of the time, Pallas kernels for 32%

profile of v9, /device:TPU:0, one launch (start us, length us, event | category | flops | bytes accessed | tf_op | source)
XLA Modules:
  0.0 182.5 jit_solution(13073109552972602752)
XLA Ops:
  0.0 0.5 collective-permute-start
  0.5 2.6 %slice_bitcast_fusion = bf16[4,128,2048]{2,0,1:T(4,128)(2,1)S(1)} fusion(bf16[4,2048,324]{1,0,2:T(4,128)(2,1)} %param.1), kind=kLoop, calls=%fused_computation.3 | loop fusion | bytes 4194304 | tf_op jit(solution)/shard_map/transpose | solution.py:375
  3.1 2.5 %copy.12 = bf16[4,128,2048]{2,1,0:T(8,128)(2,1)} copy(bf16[4,128,2048]{2,0,1:T(4,128)(2,1)S(1)} %slice_bitcast_fusion) | data formatting | bytes 4194304 | tf_op jit(solution)/shard_map/transpose | solution.py:375
  5.6 6.8 %collective-permute-start.3 = (bf16[512,2048]{1,0:T(8,128)(2,1)}, bf16[512,2048]{1,0:T(8,128)(2,1)}, u32[]{:S(2)}, u32[]{:S(2)}) collective-permute-start(bf16[512,2048]{1,0:T(8,128)(2,1)} %bitcast.4.refs_3_), channel_id=1, source_target_pairs={{0,16},{1,17},{4,20},{5,21},{8,24},{9,25},{12,28},{13,29},{18,2},{... | collective-permute-start | bytes 6291464 | tf_op jit(solution)/shard_map/ppermute | solution.py:377
  12.4 5.4 %copy.18 = bf16[4,2048,324]{1,2,0:T(8,128)(2,1)S(1)} copy(bf16[4,2048,324]{1,0,2:T(4,128)(2,1)} %param.1) | data formatting | bytes 10616832 | tf_op jit(solution)/shard_map/optimization_barrier | solution.py:376
  17.8 0.0 collective-permute-done
  17.8 7.4 %copy.17 = bf16[4,2048,324]{1,2,0:T(8,128)(2,1)S(1)} copy(bf16[4,2048,324]{1,0,2:T(4,128)(2,1)} %collective-permute-done) | data formatting | bytes 10616832 | tf_op jit(solution)/shard_map/optimization_barrier | solution.py:379
  25.2 0.0 copy-start.2
  25.2 5.1 %shard_map.17 = (f32[1744,256]{1,0:T(8,128)}, f32[8,128]{1,0:T(8,128)S(1)}) custom-call(s32[1]{0:T(128)} %bitcast.refs_0_, bf16[4,324,2048]{2,1,0:T(8,128)(2,1)S(1)} %bitcast.14, bf16[4,324,2048]{2,1,0:T(8,128)(2,1)S(1)} %bitcast.27, bf16[512,2048]{1,0:T(8,128)(2,1)} %bitcast.4.refs_3_), custom_call_target="tpu_custom_call" | custom-call | tf_op jit(solution)/shard_map/pallas_call | solution.py:43
  30.3 5.1 %shard_map.18 = (f32[1744,256]{1,0:T(8,128)}, f32[8,128]{1,0:T(8,128)S(1)}) custom-call(s32[1]{0:T(128)} %bitcast.refs_0_, bf16[4,324,2048]{2,1,0:T(8,128)(2,1)S(1)} %bitcast.15, bf16[4,324,2048]{2,1,0:T(8,128)(2,1)S(1)} %bitcast.28, f32[8,128]{1,0:T(8,128)S(1)} %get-tuple-element.58.refs_3_), custom_call_target="tpu_custom_call" | custom-call | tf_op jit(solution)/shard_map/pallas_call | solution.py:43
  35.4 3.4 %collective-permute-start.2 = (f32[1744,256]{1,0:T(8,128)}, f32[1744,256]{1,0:T(8,128)}, u32[]{:S(2)}, u32[]{:S(2)}) collective-permute-start(f32[1744,256]{1,0:T(8,128)} %get-tuple-element.65), channel_id=1, source_target_pairs={{0,1},{1,0},{4,5},{5,4},{8,9},{9,8},{12,13},{13,12},{16,17},{17,16... | collective-permute-start | bytes 5357576 | tf_op jit(solution)/shard_map/ppermute | solution.py:385
  38.8 0.6 collective-permute-start.1
  39.4 1.2 slice.11
  40.6 0.1 slice.10
  40.8 1.4 reshape.11
  42.2 1.9 %pad_maximum_fusion = bf16[784,2048]{1,0:T(8,128)(2,1)} fusion(bf16[272,2048]{1,0:T(8,128)(2,1)S(1)} %reshape.11, bf16[512,2048]{1,0:T(8,128)(2,1)S(1)} %bitcast.30), kind=kLoop, calls=%fused_computation.2 | loop fusion | flops 6422528 | bytes 6422528 | tf_op jit(solution)/shard_map/concatenate | solution.py:391
  44.0 1.9 %collective-permute-start.6 = (bf16[784,2048]{1,0:T(8,128)(2,1)}, bf16[784,2048]{1,0:T(8,128)(2,1)S(1)}, u32[]{:S(2)}, u32[]{:S(2)}) collective-permute-start(bf16[784,2048]{1,0:T(8,128)(2,1)} %pad_maximum_fusion), channel_id=1, source_target_pairs={{0,16},{1,17},{4,20},{5,21},{8,24},{9,25},{12,28},{13,29},{18,2},{... | collective-permute-start | bytes 9633800 | tf_op jit(solution)/shard_map/ppermute | solution.py:392
  46.0 0.0 copy-start.3
  46.0 2.5 %copy-done.3 = bf16[4,2048,324]{1,2,0:T(8,128)(2,1)S(1)} copy-done((bf16[4,2048,324]{1,2,0:T(8,128)(2,1)S(1)}, bf16[4,2048,324]{1,2,0:T(8,128)(2,1)}, u32[]{:S(2)}) %copy-start.3) | copy-done | bytes 5308440
  48.5 7.2 %shard_map.19 = (f32[8,324,324]{2,1,0:T(8,128)S(1)}, f32[8,128]{1,0:T(8,128)S(1)}) custom-call(s32[1]{0:T(128)} %bitcast.refs_0_, bf16[4,324,2048]{2,1,0:T(8,128)(2,1)S(1)} %bitcast.18, bf16[4,324,2048]{2,1,0:T(8,128)(2,1)S(1)} %bitcast.29, f32[8,128]{1,0:T(8,128)S(1)} %get-tuple-element.62.refs_3_), custom_call_target="tpu_custom_call" | custom-call | tf_op jit(solution)/shard_map/pallas_call | solution.py:43
  55.7 0.0 copy-start.4
  55.7 0.0 collective-permute-done.3.refs_2_
  55.8 4.4 %shard_map.20 = (f32[2,4,328,128]{3,2,1,0:T(8,128)S(1)}, f32[8,128]{1,0:T(8,128)S(1)}) custom-call(s32[1]{0:T(128)} %bitcast.refs_0_, bf16[4,324,2048]{2,1,0:T(8,128)(2,1)S(1)} %bitcast.19, bf16[512,2048]{1,0:T(8,128)(2,1)} %collective-permute-done.3.refs_2_, f32[8,128]{1,0:T(8,128)S(1)} %get-tuple-element.66.refs_3_), custom_call_target="tpu_custom_call" | custom-call | tf_op jit(solution)/shard_map/pallas_call | solution.py:43
  60.2 1.2 copy-done.6
  61.3 12.8 %collective-permute-done.2.refs_2_ = f32[1744,256]{1,0:T(8,128)} collective-permute-done((f32[1744,256]{1,0:T(8,128)}, f32[1744,256]{1,0:T(8,128)}, u32[]{:S(2)}, u32[]{:S(2)}) %collective-permute-start.2) | collective-permute-done | bytes 1785888 | tf_op jit(solution)/shard_map/ppermute | solution.py:385
  74.2 19.1 %collective-permute-done.1.refs_4_.refs_2_ = f32[1744,256]{1,0:T(8,128)} collective-permute-done((f32[1744,256]{1,0:T(8,128)}, f32[1744,256]{1,0:T(8,128)}, u32[]{:S(2)}, u32[]{:S(2)}) %collective-permute-start.1) | collective-permute-done | bytes 1785888 | tf_op jit(solution)/shard_map/ppermute | solution.py:383
  93.3 3.1 %shard_map.21 = (f32[4,328,384]{2,1,0:T(8,128)}, f32[8,128]{1,0:T(8,128)S(1)}) custom-call(s32[1]{0:T(128)} %bitcast.refs_0_, f32[8,324,324]{2,1,0:T(8,128)S(1)} %get-tuple-element.63.refs_1_, f32[1744,256]{1,0:T(8,128)} %collective-permute-done.2.refs_2_, f32[8,128]{1,0:T(8,128)S(1)} %get-tuple-element.67.refs_3_, ...), custom_call_target="tpu_custom_call" | custom-call | tf_op jit(solution)/shard_map/pallas_call | solution.py:43
  96.4 5.9 %collective-permute-start.4 = (f32[4,328,384]{2,1,0:T(8,128)}, f32[4,328,384]{2,1,0:T(8,128)}, u32[]{:S(2)}, u32[]{:S(2)}) collective-permute-start(f32[4,328,384]{2,1,0:T(8,128)} %get-tuple-element.68.refs_3_), channel_id=1, source_target_pairs={{0,2},{1,3},{4,6},{5,7},{8,10},{9,11},{12,14},{13,15},{16,18},{17,... | collective-permute-start | bytes 6045704 | tf_op jit(solution)/shard_map/ppermute | solution.py:411
  102.3 4.4 %shard_map.22 = (f32[2,4,328,128]{3,2,1,0:T(8,128)}, f32[8,128]{1,0:T(8,128)S(1)}) custom-call(s32[1]{0:T(128)} %bitcast.refs_0_, bf16[4,324,2048]{2,1,0:T(8,128)(2,1)S(1)} %bitcast.20, bf16[512,2048]{1,0:T(8,128)(2,1)} %collective-permute-done.3.refs_2_, f32[8,128]{1,0:T(8,128)S(1)} %get-tuple-element.69.refs_3_), custom_call_target="tpu_custom_call" | custom-call | tf_op jit(solution)/shard_map/pallas_call | solution.py:43
  106.7 1.7 collective-permute-start.5
  108.4 0.1 pad_add_fusion.1.refs_0_
  108.5 0.0 collective-permute-done.4.refs_4_
  108.5 2.3 %copy-done.5 = f32[8,324,324]{2,1,0:T(8,128)S(1)} copy-done((f32[8,324,324]{2,1,0:T(8,128)S(1)}, f32[8,324,324]{2,1,0:T(8,128)}, u32[]{:S(2)}) %copy-start.5) | copy-done | bytes 3359256
  110.8 7.1 %shard_map.23 = (f32[2,324,8,324]{3,2,1,0:T(8,128)}, f32[8,128]{1,0:T(8,128)S(1)}) custom-call(s32[2]{0:T(128)S(1)} %pad_add_fusion.1.refs_0_, f32[8,324,324]{2,1,0:T(8,128)S(1)} %copy-done.5, f32[1744,256]{1,0:T(8,128)} %collective-permute-done.1.refs_4_.refs_2_, f32[4,328,384]{2,1,0:T(8,128)} %get-tuple-element.68.refs_3_, ...), custom_call_target="tpu_custom_call" | custom-call | tf_op jit(solution)/shard_map/pallas_call | solution.py:43
  117.9 0.0 collective-permute-done.6.refs_2_
  118.0 2.4 %shard_map.24 = (f32[2,4,328,128]{3,2,1,0:T(8,128)S(1)}, f32[8,128]{1,0:T(8,128)S(1)}) custom-call(s32[1]{0:T(128)} %bitcast.refs_0_, bf16[4,324,2048]{2,1,0:T(8,128)(2,1)S(1)} %bitcast.23, bf16[784,2048]{1,0:T(8,128)(2,1)S(1)} %collective-permute-done.6.refs_2_, f32[8,128]{1,0:T(8,128)S(1)} %get-tuple-element.75.refs_3_), custom_call_target="tpu_custom_call" | custom-call | tf_op jit(solution)/shard_map/pallas_call | solution.py:43
  120.3 0.7 collective-permute-start.8
  121.1 0.0 collective-permute-done.5.refs_2_
  121.1 2.4 %shard_map.25 = (f32[2,2,324,128]{3,2,1,0:T(8,128)S(1)}, bf16[2,4,328,128]{3,2,1,0:T(8,128)(2,1)S(1)}, bf16[2,2,328,128]{3,2,1,0:T(8,128)(2,1)S(1)}, f32[8,128]{1,0:T(8,128)S(1)}) custom-call(s32[1]{0:T(128)} %bitcast.refs_0_, f32[2,4,328,128]{3,2,1,0:T(8,128)S(1)} %copy-done.7, f32[2,4,328,128]{3,2,1,0:T(8,128)} %collective-permute-done.5.refs_2_, ...), custom_call_target="tpu_custom_call" | custom-call | tf_op jit(solution)/shard_map/pallas_call | solution.py:43
  123.5 3.1 %shard_map.26 = (f32[2,4,72,324]{3,2,1,0:T(8,128)S(1)}, f32[8,128]{1,0:T(8,128)S(1)}) custom-call(s32[1]{0:T(128)} %bitcast.refs_0_, bf16[4,324,2048]{2,1,0:T(8,128)(2,1)S(1)} %bitcast.24, bf16[784,2048]{1,0:T(8,128)(2,1)S(1)} %collective-permute-done.6.refs_2_, f32[8,128]{1,0:T(8,128)S(1)} %get-tuple-element.78.refs_3_), custom_call_target="tpu_custom_call" | custom-call | tf_op jit(solution)/shard_map/pallas_call | solution.py:43
  126.7 0.7 collective-permute-start.10
  127.4 1.3 collective-permute-start.7
  128.7 2.4 %shard_map.27 = (f32[2,4,328,128]{3,2,1,0:T(8,128)S(1)}, f32[8,128]{1,0:T(8,128)S(1)}) custom-call(s32[1]{0:T(128)} %bitcast.refs_0_, bf16[4,324,2048]{2,1,0:T(8,128)(2,1)S(1)} %bitcast.25, bf16[784,2048]{1,0:T(8,128)(2,1)S(1)} %collective-permute-done.6.refs_2_, f32[8,128]{1,0:T(8,128)S(1)} %get-tuple-element.79.refs_3_), custom_call_target="tpu_custom_call" | custom-call | tf_op jit(solution)/shard_map/pallas_call | solution.py:43
  131.0 3.2 %shard_map.28 = (f32[2,4,72,324]{3,2,1,0:T(8,128)S(1)}, f32[8,128]{1,0:T(8,128)S(1)}) custom-call(s32[1]{0:T(128)} %bitcast.refs_0_, bf16[4,324,2048]{2,1,0:T(8,128)(2,1)S(1)} %bitcast.26, bf16[784,2048]{1,0:T(8,128)(2,1)S(1)} %collective-permute-done.6.refs_2_, f32[8,128]{1,0:T(8,128)S(1)} %get-tuple-element.82.refs_3_), custom_call_target="tpu_custom_call" | custom-call | tf_op jit(solution)/shard_map/pallas_call | solution.py:43
  134.2 0.0 collective-permute-done.8.refs_2_
  134.2 2.0 %shard_map.29 = (f32[2,2,324,128]{3,2,1,0:T(8,128)S(1)}, bf16[2,4,328,128]{3,2,1,0:T(8,128)(2,1)}, bf16[2,2,328,128]{3,2,1,0:T(8,128)(2,1)}, f32[8,128]{1,0:T(8,128)S(1)}) custom-call(s32[1]{0:T(128)} %bitcast.refs_0_, f32[2,4,328,128]{3,2,1,0:T(8,128)S(1)} %get-tuple-element.80.refs_1_, f32[2,4,328,128]{3,2,1,0:T(8,128)S(1)} %collective-permute-done.8.refs_2_, ...), custom_call_target="tpu_custom_call" | custom-call | tf_op jit(solution)/shard_map/pallas_call | solution.py:43
  136.2 1.5 collective-permute-start.9
  137.7 0.0 collective-permute-done.10.refs_2_
  137.7 1.4 shard_map.30
  139.2 1.3 collective-permute-start.14
  140.5 0.7 collective-permute-start.11
  141.1 0.7 collective-permute-start.12
  141.8 4.5 %collective-permute-done.7.refs_2_ = bf16[2,4,328,128]{3,2,1,0:T(8,128)(2,1)S(1)} collective-permute-done((bf16[2,4,328,128]{3,2,1,0:T(8,128)(2,1)S(1)}, bf16[2,4,328,128]{3,2,1,0:T(8,128)(2,1)S(1)}, u32[]{:S(2)}, u32[]{:S(2)}) %collective-permute-start.7) | collective-permute-done | bytes 671776 | tf_op jit(solution)/shard_map/ppermute | solution.py:404
  146.4 0.8 copy-done.10
  147.2 0.7 collective-permute-start.13
  147.9 0.1 pad_add_fusion.refs_0_
  148.0 25.3 %collective-permute-done.9.refs_3_ = bf16[2,4,328,128]{3,2,1,0:T(8,128)(2,1)S(1)} collective-permute-done((bf16[2,4,328,128]{3,2,1,0:T(8,128)(2,1)}, bf16[2,4,328,128]{3,2,1,0:T(8,128)(2,1)S(1)}, u32[]{:S(2)}, u32[]{:S(2)}) %collective-permute-start.9) | collective-permute-done | bytes 671776 | tf_op jit(solution)/shard_map/ppermute | solution.py:404
  173.3 1.1 copy-done.11
  174.4 3.8 %shard_map.31 = (f32[2,324,8,324]{3,2,1,0:T(8,128)}, f32[8,128]{1,0:T(8,128)S(1)}) custom-call(s32[2]{0:T(128)S(1)} %pad_add_fusion.refs_0_, f32[2,324,8,324]{3,2,1,0:T(8,128)} %get-tuple-element.71.refs_1_, bf16[2,4,328,128]{3,2,1,0:T(8,128)(2,1)S(1)} %copy-done.11, ...), custom_call_target="tpu_custom_call", output_to_operand_aliasing={{0}: (1, {})} | custom-call | tf_op jit(solution)/shard_map/pallas_call | solution.py:43
  178.3 0.0 collective-permute-done.11.refs_3_
  178.3 0.0 collective-permute-done.12.refs_5_
  178.3 0.6 shard_map.32
  178.9 0.6 shard_map.33
  179.5 2.8 %shard_map.34 = (f32[2,324,8,324]{3,2,1,0:T(8,128)}, f32[8,128]{1,0:T(8,128)}) custom-call(s32[2]{0:T(128)S(1)} %pad_add_fusion.refs_0_, f32[2,324,8,324]{3,2,1,0:T(8,128)} %get-tuple-element.99.refs_1_, bf16[2,4,72,324]{3,2,1,0:T(8,128)(2,1)S(1)} %collective-permute-done.14.refs_2_, ...), custom_call_target="tpu_custom_call", output_to_operand_aliasing={{0}: (1, {})} | custom-call | tf_op jit(solution)/shard_map/pallas_call | solution.py:43
  (23 shorter events, 0.0 us)
Async XLA Ops:
  0.0 17.8 %collective-permute-start = (bf16[4,2048,324]{1,0,2:T(4,128)(2,1)}, bf16[4,2048,324]{1,0,2:T(4,128)(2,1)}, u32[]{:S(2)}, u32[]{:S(2)}) collective-permute-start(bf16[4,2048,324]{1,0,2:T(4,128)(2,1)} %param.1), channel_id=1, source_target_pairs={{0,2},{2,0},{4,6},{6,4},{8,10},{10,8},{12,14},{14,12},{16,18},{18,... | collective-permute-start | bytes 15925256 | tf_op jit(solution)/shard_map/ppermute | solution.py:374
  5.6 50.2 %collective-permute-start.3 = (bf16[512,2048]{1,0:T(8,128)(2,1)}, bf16[512,2048]{1,0:T(8,128)(2,1)}, u32[]{:S(2)}, u32[]{:S(2)}) collective-permute-start(bf16[512,2048]{1,0:T(8,128)(2,1)} %bitcast.4.refs_3_), channel_id=1, source_target_pairs={{0,16},{1,17},{4,20},{5,21},{8,24},{9,25},{12,28},{13,29},{18,2},{... | collective-permute-start | bytes 6291464 | tf_op jit(solution)/shard_map/ppermute | solution.py:377
  17.8 22.8 %copy-start = (bf16[4,2048,324]{1,2,0:T(8,128)(2,1)}, bf16[4,2048,324]{1,2,0:T(8,128)(2,1)S(1)}, u32[]{:S(2)}) copy-start(bf16[4,2048,324]{1,2,0:T(8,128)(2,1)S(1)} %copy.18) | copy-start | bytes 15925252
  25.2 5.1 %copy-start.2 = (bf16[4,2048,324]{1,2,0:T(8,128)(2,1)}, bf16[4,2048,324]{1,2,0:T(8,128)(2,1)S(1)}, u32[]{:S(2)}) copy-start(bf16[4,2048,324]{1,2,0:T(8,128)(2,1)S(1)} %copy.17) | copy-start | bytes 15925252
  35.4 38.8 %collective-permute-start.2 = (f32[1744,256]{1,0:T(8,128)}, f32[1744,256]{1,0:T(8,128)}, u32[]{:S(2)}, u32[]{:S(2)}) collective-permute-start(f32[1744,256]{1,0:T(8,128)} %get-tuple-element.65), channel_id=1, source_target_pairs={{0,1},{1,0},{4,5},{5,4},{8,9},{9,8},{12,13},{13,12},{16,17},{17,16... | collective-permute-start | bytes 5357576 | tf_op jit(solution)/shard_map/ppermute | solution.py:385
  38.8 54.5 %collective-permute-start.1 = (f32[1744,256]{1,0:T(8,128)}, f32[1744,256]{1,0:T(8,128)}, u32[]{:S(2)}, u32[]{:S(2)}) collective-permute-start(f32[1744,256]{1,0:T(8,128)} %get-tuple-element.64), channel_id=1, source_target_pairs={{0,1},{1,0},{2,3},{3,2},{4,5},{5,4},{6,7},{7,6},{8,9},{9,8},{10,11... | collective-permute-start | bytes 5357576 | tf_op jit(solution)/shard_map/ppermute | solution.py:383
  42.1 3.8 %copy-start.1 = (bf16[4,2048,324]{1,2,0:T(8,128)(2,1)S(1)}, bf16[4,2048,324]{1,2,0:T(8,128)(2,1)}, u32[]{:S(2)}) copy-start(bf16[4,2048,324]{1,2,0:T(8,128)(2,1)} %copy-done) | copy-start | bytes 15925252
  44.0 73.9 %collective-permute-start.6 = (bf16[784,2048]{1,0:T(8,128)(2,1)}, bf16[784,2048]{1,0:T(8,128)(2,1)S(1)}, u32[]{:S(2)}, u32[]{:S(2)}) collective-permute-start(bf16[784,2048]{1,0:T(8,128)(2,1)} %pad_maximum_fusion), channel_id=1, source_target_pairs={{0,16},{1,17},{4,20},{5,21},{8,24},{9,25},{12,28},{13,29},{18,2},{... | collective-permute-start | bytes 9633800 | tf_op jit(solution)/shard_map/ppermute | solution.py:392
  46.0 2.5 %copy-start.3 = (bf16[4,2048,324]{1,2,0:T(8,128)(2,1)S(1)}, bf16[4,2048,324]{1,2,0:T(8,128)(2,1)}, u32[]{:S(2)}) copy-start(bf16[4,2048,324]{1,2,0:T(8,128)(2,1)} %copy-done.2) | copy-start | bytes 15925252
  55.7 37.6 %copy-start.4 = (f32[8,324,324]{2,1,0:T(8,128)}, f32[8,324,324]{2,1,0:T(8,128)S(1)}, u32[]{:S(2)}) copy-start(f32[8,324,324]{2,1,0:T(8,128)S(1)} %get-tuple-element.63.refs_1_) | copy-start | bytes 10077700
  60.1 1.2 copy-start.6
  96.4 12.1 %collective-permute-start.4 = (f32[4,328,384]{2,1,0:T(8,128)}, f32[4,328,384]{2,1,0:T(8,128)}, u32[]{:S(2)}, u32[]{:S(2)}) collective-permute-start(f32[4,328,384]{2,1,0:T(8,128)} %get-tuple-element.68.refs_3_), channel_id=1, source_target_pairs={{0,2},{1,3},{4,6},{5,7},{8,10},{9,11},{12,14},{13,15},{16,18},{17,... | collective-permute-start | bytes 6045704 | tf_op jit(solution)/shard_map/ppermute | solution.py:411
  106.7 14.4 %collective-permute-start.5 = (f32[2,4,328,128]{3,2,1,0:T(8,128)}, f32[2,4,328,128]{3,2,1,0:T(8,128)}, u32[]{:S(2)}, u32[]{:S(2)}) collective-permute-start(f32[2,4,328,128]{3,2,1,0:T(8,128)} %get-tuple-element.73), channel_id=1, source_target_pairs={{2,3},{3,2},{6,7},{7,6},{10,11},{11,10},{14,15},{15,14},{16,17},{1... | collective-permute-start | bytes 4030472 | tf_op jit(solution)/shard_map/ppermute | solution.py:414
  108.5 9.5 %slice-start = ((s8[5373952]{0:T(1024)(128)(4,1)}), s8[4194304]{0:T(1024)(128)(4,1)S(1)}, s32[]{:S(2)}) async-start(s8[5373952]{0:T(1024)(128)(4,1)} %bitcast.21), calls=%async_computation | async-start | bytes 8388608
  108.5 2.3 %copy-start.5 = (f32[8,324,324]{2,1,0:T(8,128)S(1)}, f32[8,324,324]{2,1,0:T(8,128)}, u32[]{:S(2)}) copy-start(f32[8,324,324]{2,1,0:T(8,128)} %copy-done.4) | copy-start | bytes 10077700
  110.8 7.2 %slice-start.1 = ((s8[5373952]{0:T(1024)(128)(4,1)}), s8[1179648]{0:T(1024)(128)(4,1)S(1)}, s32[]{:S(2)}) async-start(s8[5373952]{0:T(1024)(128)(4,1)} %bitcast.21), calls=%async_computation.1 | async-start | bytes 2359296
  117.9 3.1 %copy-start.7 = (f32[2,4,328,128]{3,2,1,0:T(8,128)S(1)}, f32[2,4,328,128]{3,2,1,0:T(8,128)}, u32[]{:S(2)}) copy-start(f32[2,4,328,128]{3,2,1,0:T(8,128)} %copy-done.6) | copy-start | bytes 4030468
  120.3 13.9 %collective-permute-start.8 = (f32[2,4,328,128]{3,2,1,0:T(8,128)S(1)}, f32[2,4,328,128]{3,2,1,0:T(8,128)S(1)}, u32[]{:S(2)}, u32[]{:S(2)}) collective-permute-start(f32[2,4,328,128]{3,2,1,0:T(8,128)S(1)} %get-tuple-element.81), channel_id=1, source_target_pairs={{2,3},{3,2},{6,7},{7,6},{10,11},{11,10},{14,15},{15,14},{16,17},{1... | collective-permute-start | bytes 4030472 | tf_op jit(solution)/shard_map/ppermute | solution.py:414
  123.5 3.2 %copy-start.8 = (f32[2,2,324,128]{3,2,1,0:T(8,128)}, f32[2,2,324,128]{3,2,1,0:T(8,128)S(1)}, u32[]{:S(2)}) copy-start(f32[2,2,324,128]{3,2,1,0:T(8,128)S(1)} %get-tuple-element.90.refs_2_) | copy-start | bytes 1990660
  126.7 11.1 %collective-permute-start.10 = (f32[2,4,72,324]{3,2,1,0:T(8,128)S(1)}, f32[2,4,72,324]{3,2,1,0:T(8,128)S(1)}, u32[]{:S(2)}, u32[]{:S(2)}) collective-permute-start(f32[2,4,72,324]{3,2,1,0:T(8,128)S(1)} %get-tuple-element.86), channel_id=1, source_target_pairs={{2,3},{3,2},{6,7},{7,6},{10,11},{11,10},{14,15},{15,14},{16,17},{1... | collective-permute-start | bytes 2239496 | tf_op jit(solution)/shard_map/ppermute | solution.py:414
  127.4 19.0 %collective-permute-start.7 = (bf16[2,4,328,128]{3,2,1,0:T(8,128)(2,1)S(1)}, bf16[2,4,328,128]{3,2,1,0:T(8,128)(2,1)S(1)}, u32[]{:S(2)}, u32[]{:S(2)}) collective-permute-start(bf16[2,4,328,128]{3,2,1,0:T(8,128)(2,1)S(1)} %get-tuple-element.77), channel_id=1, source_target_pairs={{16,0},{17,1},{20,4},{21,5},{24,8},{25,9},{28,12},{29,13},{2,18},{... | collective-permute-start | bytes 2015240 | tf_op jit(solution)/shard_map/ppermute | solution.py:404
  136.2 37.1 %collective-permute-start.9 = (bf16[2,4,328,128]{3,2,1,0:T(8,128)(2,1)}, bf16[2,4,328,128]{3,2,1,0:T(8,128)(2,1)S(1)}, u32[]{:S(2)}, u32[]{:S(2)}) collective-permute-start(bf16[2,4,328,128]{3,2,1,0:T(8,128)(2,1)} %get-tuple-element.84), channel_id=1, source_target_pairs={{16,0},{17,1},{20,4},{21,5},{24,8},{25,9},{28,12},{29,13},{2,18},{... | collective-permute-start | bytes 2015240 | tf_op jit(solution)/shard_map/ppermute | solution.py:404
  139.2 40.3 %collective-permute-start.14 = (bf16[2,4,72,324]{3,2,1,0:T(8,128)(2,1)}, bf16[2,4,72,324]{3,2,1,0:T(8,128)(2,1)S(1)}, u32[]{:S(2)}, u32[]{:S(2)}) collective-permute-start(bf16[2,4,72,324]{3,2,1,0:T(8,128)(2,1)} %get-tuple-element.100), channel_id=1, source_target_pairs={{16,0},{17,1},{20,4},{21,5},{24,8},{25,9},{28,12},{29,13},{2,18},{... | collective-permute-start | bytes 1119752 | tf_op jit(solution)/shard_map/ppermute | solution.py:404
  140.5 37.8 %collective-permute-start.11 = (bf16[2,2,328,128]{3,2,1,0:T(8,128)(2,1)S(1)}, bf16[2,2,328,128]{3,2,1,0:T(8,128)(2,1)S(1)}, u32[]{:S(2)}, u32[]{:S(2)}) collective-permute-start(bf16[2,2,328,128]{3,2,1,0:T(8,128)(2,1)S(1)} %get-tuple-element.91), channel_id=1, source_target_pairs={{2,3},{3,2},{6,7},{7,6},{10,11},{11,10},{14,15},{15,14},{16,17},{1... | collective-permute-start | bytes 1007624 | tf_op jit(solution)/shard_map/ppermute | solution.py:405
  141.1 37.1 %collective-permute-start.12 = (bf16[2,2,328,128]{3,2,1,0:T(8,128)(2,1)}, bf16[2,2,328,128]{3,2,1,0:T(8,128)(2,1)S(1)}, u32[]{:S(2)}, u32[]{:S(2)}) collective-permute-start(bf16[2,2,328,128]{3,2,1,0:T(8,128)(2,1)} %get-tuple-element.93), channel_id=1, source_target_pairs={{2,3},{3,2},{6,7},{7,6},{10,11},{11,10},{14,15},{15,14},{16,17},{1... | collective-permute-start | bytes 1007624 | tf_op jit(solution)/shard_map/ppermute | solution.py:405
  146.4 0.9 copy-start.10
  147.2 31.7 %collective-permute-start.13 = (bf16[2,2,72,324]{3,2,1,0:T(8,128)(2,1)}, bf16[2,2,72,324]{3,2,1,0:T(8,128)(2,1)S(1)}, u32[]{:S(2)}, u32[]{:S(2)}) collective-permute-start(bf16[2,2,72,324]{3,2,1,0:T(8,128)(2,1)} %get-tuple-element.97), channel_id=1, source_target_pairs={{2,3},{3,2},{6,7},{7,6},{10,11},{11,10},{14,15},{15,14},{16,17},{1... | collective-permute-start | bytes 559880 | tf_op jit(solution)/shard_map/ppermute | solution.py:405
  173.3 1.1 copy-start.11
  174.4 3.9 %copy-start.9 = (f32[2,2,324,128]{3,2,1,0:T(8,128)S(1)}, f32[2,2,324,128]{3,2,1,0:T(8,128)}, u32[]{:S(2)}) copy-start(f32[2,2,324,128]{3,2,1,0:T(8,128)} %copy-done.8) | copy-start | bytes 1990660

commit v10 on v9

--- a/solution.py
+++ b/solution.py
@@ -11,13 +11,14 @@
 VMEM_LIMIT = 20 * 2**20
 POWER, LIFT = 10, 11
 SMALLEST = 2.0**-110
+LONG = 10**10
 
 
 def contract_last(left, right):
     return lax.dot_general(left, right, (((1,), (1,)), ((), ())), preferred_element_type=jnp.float32)
 
 
-def call(body, grid, scalars, in_specs, out_specs, out_shape, after=(), aliases={}, scratch=()):
+def call(body, grid, scalars, in_specs, out_specs, out_shape, after=(), aliases={}, scratch=(), declared=0):
     idle = len(after)
 
     def waiting(*refs):
@@ -39,6 +40,7 @@
         out_shape=[*out_shape, f32(*token)],
         input_output_aliases=aliases,
         compiler_params=pltpu.CompilerParams(vmem_limit_bytes=VMEM_LIMIT),
+        cost_estimate=pl.CostEstimate(flops=declared, bytes_accessed=declared // 100, transcendentals=0),
     )
     return lambda *operands: kernel(*operands, *after)
 
@@ -228,11 +230,11 @@
     )(det, own, got)
 
 
-def far_sum(det, keep, came, rows, turned, after=()):
+def far_sum(det, keep, came, rows, turned, after=(), declared=0):
     half, states, _, lanes = keep.shape
     shape = (up(rows + 1, 8), lanes)
 
-    def body(x_ref, keep_ref, came_ref, tile_ref, code_ref, cross_ref):
+    def body(x_ref, keep_ref, came_ref, tile_ref, code_ref):
         x = x_ref[0]
         top = jnp.zeros((rows, lanes), jnp.float32)
         for a in range(half):
@@ -248,10 +250,9 @@
             for b in range(half):
                 v = half * x + b
                 tile_ref[a, b] = keep_ref[a, v, :rows] + came_ref[a, v, :rows]
-                cross_ref[a, b] = code_ref[a, half * (1 - x) + b]
-
-    shapes = [(half, half, rows, lanes), (half, states, *shape), (half, half, *shape)]
-    kinds = [jnp.float32, jnp.bfloat16, jnp.bfloat16]
+
+    shapes = [(half, half, rows, lanes), (half, states, *shape)]
+    kinds = [jnp.float32, jnp.bfloat16]
     return call(
         body,
         (1,),
@@ -260,7 +261,27 @@
         [whole(s) for s in shapes],
         [jax.ShapeDtypeStruct(s, kind) for s, kind in zip(shapes, kinds)],
         after,
+        declared=declared,
     )(det, keep, came)
+
+
+def crossing_codes(det, codes, after=()):
+    half, states, *tile = codes[0].shape
+    shape = (len(codes), half, half, *tile)
+
+    def body(x_ref, *refs):
+        for k in range(len(codes)):
+            refs[-1][k] = refs[k][...]
+
+    return call(
+        body,
+        (1,),
+        1,
+        [pl.BlockSpec((half, half, *tile), lambda i, x: (0, 1 - x[0], 0, 0))] * len(codes),
+        [whole(shape)],
+        [jax.ShapeDtypeStruct(shape, jnp.bfloat16)],
+        after,
+    )(det, *codes)
 
 
 def powered(value):
@@ -276,9 +297,10 @@
     return jnp.where(value < 0, -root, root)
 
 
-def into_place(role, place_in, out, pieces, after=()):
+def into_place(role, place_in, out, pieces, after=(), declared=0):
     tiles = out.shape[2]
-    sources = [v for piece in pieces for v in piece[2]]
+    sources = [v for piece in pieces for v, _ in piece[2]]
+    picks = [pick for piece in pieces for _, pick in piece[2]]
     count = len(sources)
 
     def body(s_ref, out_in, *refs):
@@ -286,7 +308,7 @@
 
         @pl.when(s_ref[1] == role)
         def _():
-            loads = [pltpu.make_async_copy(refs[k], held[k], sems.at[k]) for k in range(count)]
+            loads = [pltpu.make_async_copy(refs[k].at[picks[k]], held[k], sems.at[k]) for k in range(count)]
             for load in loads:
                 load.start()
             stores, first = [], 0
@@ -310,9 +332,10 @@
         [f32(*out.shape)],
         after,
         {1: 0},
-        [pltpu.VMEM(v.shape, v.dtype) for v in sources]
+        [pltpu.VMEM(v.shape[1:], v.dtype) for v in sources]
         + [pltpu.VMEM((rows[1], tiles, lanes[1]), jnp.float32) for rows, lanes, *_ in pieces]
         + [pltpu.SemaphoreType.DMA((count + len(pieces),))],
+        declared,
     )(place_in, out, *sources)
 
 
@@ -323,13 +346,13 @@
     def fill(x, refs, ref):
         for a in range(half):
             for v in range(states):
-                one = refs[0][a, v]
+                one = refs[a][v]
                 ref[:, a * states + v] = decoded(one, ops).T if turned else decoded(one, width)
 
-    return (start, width), (0, ops), (code,), fill
-
-
-def finished_piece(tiles, cross, start, width, ops):
+    return (start, width), (0, ops), [(code, a) for a in range(half)], fill
+
+
+def finished_piece(tiles, cross, chunk, start, width, ops):
     half, _, rows, _ = tiles.shape
     turned = rows == ops
 
@@ -340,14 +363,14 @@
 
                 @pl.when(u // half == x)
                 def _():
-                    ref[:, t] = refs[0][a, b] if turned else refs[0][a, b].T
+                    ref[:, t] = refs[a][b] if turned else refs[a][b].T
 
                 @pl.when(u // half != x)
                 def _():
-                    one = decoded(refs[1][a, b], rows)
+                    one = decoded(refs[half][a, b], rows)
                     ref[:, t] = one if turned else one.T
 
-    return (0, ops), (start, width), (tiles, cross), fill
+    return (0, ops), (start, width), [(tiles, a) for a in range(half)] + [(cross, chunk)], fill
 
 
 def paired(amplitudes):
@@ -385,46 +408,68 @@
     doubled = lax.ppermute(doubled, both, first_across)
     whole_own, token = lax.optimization_barrier((own, token))
     widths = [LANES] * full + [ops - wide]
-    later = [
-        whole_own[:, k * LANES : k * LANES + w].reshape(states * w, depth) for k, w in enumerate(widths) if k
-    ]
-    later, token = lax.optimization_barrier((jnp.concatenate(later), token))
+    chunk = [whole_own[:, k * LANES : k * LANES + w].reshape(states * w, depth) for k, w in enumerate(widths)]
+    last, token = lax.optimization_barrier((chunk[full], token))
+    got.append(lax.ppermute(last, both, over))
+    later, token = lax.optimization_barrier((jnp.concatenate(chunk[1:full]), token))
     got.append(lax.ppermute(later, both, over))
     keep, token = near_keep(det, own, partner, (token,))
     def terms(k, mine, *done):
-        start = states * LANES * (k - 1) if k else 0
-        return far_terms(det, own, got[min(k, 1)], start, widths[k], k < full, mine, done)
-
-    codes, mine, kepts, came = [], [], [], []
+        wire, start = (0, 0) if k == 0 else (1, 0) if k == full else (2, states * LANES * (k - 1))
+        return far_terms(det, own, got[wire], start, widths[k], k < full, mine, done)
+
+    kepts, came, tiles, codes, mine, theirs = {}, {}, {}, {}, {}, {}
+
+    def place_of(k):
+        return k * LANES, widths[k], ops
+
+    def keep_terms(k, token):
+        kepts[k], token = terms(k, True, token)
+        return token
+
+    def send_terms(k, token):
+        send, token = terms(k, False, token)
+        came[k] = lax.ppermute(send, both, across)
+        return token
 
     def sum_up(k, token):
         rows = ops if k < full else widths[k]
-        tiles, code, cross, token = far_sum(det, kepts[k], came[k], rows, k < full, (token,))
-        place = k * LANES, widths[k], ops
-        codes.append(returned_piece(lax.ppermute(code, both, back), *place))
-        mine.append(finished_piece(tiles, lax.ppermute(cross, both, across), *place))
+        declared = LONG if k == early[-1] else 0
+        tiles[k], codes[k], token = far_sum(det, kepts[k], came[k], rows, k < full, (token,), declared)
+        theirs[k] = returned_piece(lax.ppermute(codes[k], both, back), *place_of(k))
         return token
 
-    kept, token = terms(0, True, token)
-    kepts.append(kept)
+    def cross(ks, token):
+        wire, token = crossing_codes(det, [codes[k] for k in ks], (token,))
+        wire = lax.ppermute(wire, both, across)
+        for n, k in enumerate(ks):
+            mine[k] = finished_piece(tiles[k], wire, n, *place_of(k))
+        return token
+
+    early, late = [0, full], list(range(1, full))
+    for k in early:
+        token = keep_terms(k, token)
     share, token = near_share(det, keep, doubled, states, (token, crossed))
     given = lax.ppermute(share, both, to_second)
-    for k in range(full + 1):
-        send, token = terms(k, False, token)
-        came.append(lax.ppermute(send, both, across))
-        if k == 0:
-            out, token = near_sum(jnp.stack([x, core]), keep, crossed, share, given, states, (token,))
-        if k == 1:
-            token = sum_up(0, token)
-    for k in range(1, full + 1):
-        kept, token = terms(k, True, token)
-        kepts.append(kept)
-    for k in range(1, full + 1):
+    for k in early:
+        token = send_terms(k, token)
+    out, token = near_sum(jnp.stack([x, core]), keep, crossed, share, given, states, (token,))
+    for k in late:
+        token = send_terms(k, token)
+    for k in early:
         token = sum_up(k, token)
+    token = cross([full], token)
+    for k in late:
+        token = keep_terms(k, token)
+    for k in late:
+        token = sum_up(k, token)
+    turned = list(range(full))
+    token = cross(turned, token)
 
     at = jnp.stack([x, receiver])
-    for role, pieces in ((0, codes[:full]), (1, mine[:full]), (1, mine[full:]), (0, codes[full:])):
-        out, token = into_place(role, at, out, pieces, (token,))
+    for role, kind, ks in ((0, theirs, early), (1, mine, [full]), (1, mine, turned), (0, theirs, late)):
+        declared = LONG if role == 1 else 0
+        out, token = into_place(role, at, out, [kind[k] for k in ks], (token,), declared)
     return out.transpose(0, 2, 1, 3)
 
 
@@ -455,7 +500,7 @@
 def on_device(amplitudes):
     states, _, ops = amplitudes.shape
     two = lax.axis_size("det") == 2 and lax.axis_size("state") >= 4
-    if two and states % 2 == 0 and ops > LANES and ops % LANES % 8:
+    if two and states % 2 == 0 and ops > 2 * LANES and ops % LANES % 8:
         return paired(amplitudes)
     return exchanged(amplitudes)
 

time: 183 us -> 194 us (1.060)
  starting transfers between devices: 28.4 us -> 42 us
  waiting for transfers between devices: 61.9 us -> 48.3 us
  Pallas kernels: 61 us -> 68.1 us
  local copies, waits for them, and re-layouts: 28.6 us -> 33.5 us
    ppermute x1, starting transfers between devices: 5.89 us -> 17 us  [paired(): given = lax.ppermute(share, both, to_second)]
    ppermute x9, waiting for transfers between devices: 29.9 us -> 22.6 us  [the longest x3 22.6 us: sum_up(): theirs[k] = returned_piece(lax.ppermute(codes[k], both, back), *place_of(k))]
    pallas_call x18 -> x20, Pallas kernels: 61 us -> 68.1 us  [call(): return lambda *operands: kernel(*operands, *after)]
    ppermute x1, waiting for transfers between devices: 12.8 us -> 6.57 us  [paired(): doubled = lax.ppermute(doubled, both, first_across)]
    unnamed x28 -> x32, local copies, waits for them, and re-layouts: 7.96 us -> 11.3 us
    ppermute x9, starting transfers between devices: 9.3 us -> 12 us  [the longest x3 5.25 us: send_terms(): came[k] = lax.ppermute(send, both, across)]
  transfers between devices with their start and end apart: 15 -> 15, of which waited for: 4 -> 4; matrix products, arithmetic and copies ran while one was open for 12% -> 12% of each run, Pallas kernels for 32% -> 34%
where the time goes in v10:
time: 194 us; the launch traced here: 193 us
  Pallas kernels  68.1 us (35%)
  waiting for transfers between devices  48.3 us (25%)
  starting transfers between devices  42 us (22%)
  local copies, waits for them, and re-layouts  33.5 us (17%)
    pallas_call x20, Pallas kernels, call(): return lambda *operands: kernel(*operands, *after)  68.1 us
    ppermute x3, waiting for transfers between devices, sum_up(): theirs[k] = returned_piece(lax.ppermute(codes[k], both, back), *place_of(k))  22.6 us
    ppermute x1, waiting for transfers between devices, paired(): crossed = lax.ppermute(crossed, 'det', [(0, 1), (1, 0)])  19.1 us
    ppermute x1, starting transfers between devices, paired(): given = lax.ppermute(share, both, to_second)  17 us
    unnamed x32, local copies, waits for them, and re-layouts  11.3 us
    optimization_barrier x1, local copies, waits for them, and re-layouts, paired(): partner, own = lax.optimization_barrier((partner, own))  7.35 us
    ppermute x1, starting transfers between devices, paired(): got = [lax.ppermute(first, both, over)]  6.9 us
    ppermute x1, waiting for transfers between devices, paired(): doubled = lax.ppermute(doubled, both, first_across)  6.57 us
  transfers between devices with their start and end apart: 15, of which 4 were waited for; matrix products, arithmetic and copies ran while one was open for 12% of the time, Pallas kernels for 34%

profile of v10, /device:TPU:0, one launch (start us, length us, event | category | flops | bytes accessed | tf_op | source)
XLA Modules:
  0.0 192.5 jit_solution(3273870283695706491)
XLA Ops:
  0.0 0.5 collective-permute-start
  0.5 2.6 %slice_bitcast_fusion = bf16[4,128,2048]{2,0,1:T(4,128)(2,1)S(1)} fusion(bf16[4,2048,324]{1,0,2:T(4,128)(2,1)} %param.1), kind=kLoop, calls=%fused_computation.2 | loop fusion | bytes 4194304 | tf_op jit(solution)/shard_map/transpose | solution.py:398
  3.1 2.5 %copy.12 = bf16[4,128,2048]{2,1,0:T(8,128)(2,1)} copy(bf16[4,128,2048]{2,0,1:T(4,128)(2,1)S(1)} %slice_bitcast_fusion) | data formatting | bytes 4194304 | tf_op jit(solution)/shard_map/transpose | solution.py:398
  5.5 6.9 %collective-permute-start.4 = (bf16[512,2048]{1,0:T(8,128)(2,1)}, bf16[512,2048]{1,0:T(8,128)(2,1)}, u32[]{:S(2)}, u32[]{:S(2)}) collective-permute-start(bf16[512,2048]{1,0:T(8,128)(2,1)} %bitcast.4.refs_3_), channel_id=1, source_target_pairs={{0,16},{1,17},{4,20},{5,21},{8,24},{9,25},{12,28},{13,29},{18,2},{... | collective-permute-start | bytes 6291464 | tf_op jit(solution)/shard_map/ppermute | solution.py:400
  12.4 5.4 %copy.18 = bf16[4,2048,324]{1,2,0:T(8,128)(2,1)S(1)} copy(bf16[4,2048,324]{1,0,2:T(4,128)(2,1)} %param.1) | data formatting | bytes 10616832 | tf_op jit(solution)/shard_map/optimization_barrier | solution.py:399
  17.8 0.0 collective-permute-done
  17.9 7.4 %copy.17 = bf16[4,2048,324]{1,2,0:T(8,128)(2,1)S(1)} copy(bf16[4,2048,324]{1,0,2:T(4,128)(2,1)} %collective-permute-done) | data formatting | bytes 10616832 | tf_op jit(solution)/shard_map/optimization_barrier | solution.py:402
  25.2 0.0 copy-start.4
  25.2 5.2 %shard_map.17 = (f32[1744,256]{1,0:T(8,128)}, f32[8,128]{1,0:T(8,128)S(1)}) custom-call(s32[1]{0:T(128)} %bitcast.refs_0_, bf16[4,324,2048]{2,1,0:T(8,128)(2,1)S(1)} %bitcast.14, bf16[4,324,2048]{2,1,0:T(8,128)(2,1)S(1)} %bitcast.27, bf16[512,2048]{1,0:T(8,128)(2,1)} %bitcast.4.refs_3_), custom_call_target="tpu_custom_call" | custom-call | tf_op jit(solution)/shard_map/pallas_call | solution.py:45
  30.4 5.1 %shard_map.18 = (f32[1744,256]{1,0:T(8,128)}, f32[8,128]{1,0:T(8,128)S(1)}) custom-call(s32[1]{0:T(128)} %bitcast.refs_0_, bf16[4,324,2048]{2,1,0:T(8,128)(2,1)S(1)} %bitcast.15, bf16[4,324,2048]{2,1,0:T(8,128)(2,1)S(1)} %bitcast.28, f32[8,128]{1,0:T(8,128)S(1)} %get-tuple-element.61.refs_3_), custom_call_target="tpu_custom_call" | custom-call | tf_op jit(solution)/shard_map/pallas_call | solution.py:45
  35.4 3.4 %collective-permute-start.2 = (f32[1744,256]{1,0:T(8,128)}, f32[1744,256]{1,0:T(8,128)}, u32[]{:S(2)}, u32[]{:S(2)}) collective-permute-start(f32[1744,256]{1,0:T(8,128)} %get-tuple-element.69), channel_id=1, source_target_pairs={{0,1},{1,0},{4,5},{5,4},{8,9},{9,8},{12,13},{13,12},{16,17},{17,16... | collective-permute-start | bytes 5357576 | tf_op jit(solution)/shard_map/ppermute | solution.py:408
  38.8 0.6 collective-permute-start.1
  39.4 0.1 slice.11
  39.6 1.1 reshape.11
  40.7 1.3 collective-permute-start.3
  42.0 3.2 %slice.10 = bf16[4,128,2048]{2,1,0:T(8,128)(2,1)} slice(bf16[4,324,2048]{2,1,0:T(8,128)(2,1)} %bitcast.17), slice={[0:4], [128:256], [0:2048]} | slice | bytes 4194304 | tf_op jit(solution)/shard_map/slice | solution.py:411
  45.2 1.6 collective-permute-start.7
  46.8 2.5 %copy-done.1 = bf16[4,2048,324]{1,2,0:T(8,128)(2,1)S(1)} copy-done((bf16[4,2048,324]{1,2,0:T(8,128)(2,1)S(1)}, bf16[4,2048,324]{1,2,0:T(8,128)(2,1)}, u32[]{:S(2)}) %copy-start.1) | copy-done | bytes 5308440
  49.4 2.5 %copy-done.5 = bf16[4,2048,324]{1,2,0:T(8,128)(2,1)S(1)} copy-done((bf16[4,2048,324]{1,2,0:T(8,128)(2,1)S(1)}, bf16[4,2048,324]{1,2,0:T(8,128)(2,1)}, u32[]{:S(2)}) %copy-start.5) | copy-done | bytes 5308440
  51.9 7.2 %shard_map.19 = (f32[8,324,324]{2,1,0:T(8,128)S(1)}, f32[8,128]{1,0:T(8,128)S(1)}) custom-call(s32[1]{0:T(128)} %bitcast.refs_0_, bf16[4,324,2048]{2,1,0:T(8,128)(2,1)S(1)} %bitcast.18, bf16[4,324,2048]{2,1,0:T(8,128)(2,1)S(1)} %bitcast.29, f32[8,128]{1,0:T(8,128)S(1)} %get-tuple-element.66.refs_3_), custom_call_target="tpu_custom_call" | custom-call | tf_op jit(solution)/shard_map/pallas_call | solution.py:45
  59.1 0.0 copy-start.6
  59.1 0.0 collective-permute-done.4.refs_2_
  59.1 4.4 %shard_map.20 = (f32[2,4,328,128]{3,2,1,0:T(8,128)S(1)}, f32[8,128]{1,0:T(8,128)S(1)}) custom-call(s32[1]{0:T(128)} %bitcast.refs_0_, bf16[4,324,2048]{2,1,0:T(8,128)(2,1)S(1)} %bitcast.19, bf16[512,2048]{1,0:T(8,128)(2,1)} %collective-permute-done.4.refs_2_, f32[8,128]{1,0:T(8,128)S(1)} %get-tuple-element.71.refs_3_), custom_call_target="tpu_custom_call" | custom-call | tf_op jit(solution)/shard_map/pallas_call | solution.py:45
  63.5 0.0 collective-permute-done.3.refs_2_
  63.5 3.1 %shard_map.21 = (f32[2,4,72,324]{3,2,1,0:T(8,128)S(1)}, f32[8,128]{1,0:T(8,128)S(1)}) custom-call(s32[1]{0:T(128)} %bitcast.refs_0_, bf16[4,324,2048]{2,1,0:T(8,128)(2,1)S(1)} %bitcast.20, bf16[272,2048]{1,0:T(8,128)(2,1)S(1)} %collective-permute-done.3.refs_2_, f32[8,128]{1,0:T(8,128)S(1)} %get-tuple-element.72.refs_3_), custom_call_target="tpu_custom_call" | custom-call | tf_op jit(solution)/shard_map/pallas_call | solution.py:45
  66.7 0.9 copy-done.8
  67.6 6.6 %collective-permute-done.2.refs_2_ = f32[1744,256]{1,0:T(8,128)} collective-permute-done((f32[1744,256]{1,0:T(8,128)}, f32[1744,256]{1,0:T(8,128)}, u32[]{:S(2)}, u32[]{:S(2)}) %collective-permute-start.2) | collective-permute-done | bytes 1785888 | tf_op jit(solution)/shard_map/ppermute | solution.py:408
  74.2 19.1 %collective-permute-done.1.refs_4_.refs_2_ = f32[1744,256]{1,0:T(8,128)} collective-permute-done((f32[1744,256]{1,0:T(8,128)}, f32[1744,256]{1,0:T(8,128)}, u32[]{:S(2)}, u32[]{:S(2)}) %collective-permute-start.1) | collective-permute-done | bytes 1785888 | tf_op jit(solution)/shard_map/ppermute | solution.py:406
  93.3 3.2 %shard_map.22 = (f32[4,328,384]{2,1,0:T(8,128)}, f32[8,128]{1,0:T(8,128)S(1)}) custom-call(s32[1]{0:T(128)} %bitcast.refs_0_, f32[8,324,324]{2,1,0:T(8,128)S(1)} %get-tuple-element.67.refs_1_, f32[1744,256]{1,0:T(8,128)} %collective-permute-done.2.refs_2_, f32[8,128]{1,0:T(8,128)S(1)} %get-tuple-element.73.refs_3_, ...), custom_call_target="tpu_custom_call" | custom-call | tf_op jit(solution)/shard_map/pallas_call | solution.py:45
  96.5 17.0 %collective-permute-start.5 = (f32[4,328,384]{2,1,0:T(8,128)}, f32[4,328,384]{2,1,0:T(8,128)}, u32[]{:S(2)}, u32[]{:S(2)}) collective-permute-start(f32[4,328,384]{2,1,0:T(8,128)} %get-tuple-element.74.refs_3_), channel_id=1, source_target_pairs={{0,2},{1,3},{4,6},{5,7},{8,10},{9,11},{12,14},{13,15},{16,18},{17,... | collective-permute-start | bytes 6045704 | tf_op jit(solution)/shard_map/ppermute | solution.py:453
  113.5 4.4 %shard_map.23 = (f32[2,4,328,128]{3,2,1,0:T(8,128)}, f32[8,128]{1,0:T(8,128)S(1)}) custom-call(s32[1]{0:T(128)} %bitcast.refs_0_, bf16[4,324,2048]{2,1,0:T(8,128)(2,1)S(1)} %bitcast.21, bf16[512,2048]{1,0:T(8,128)(2,1)} %collective-permute-done.4.refs_2_, f32[8,128]{1,0:T(8,128)S(1)} %get-tuple-element.75.refs_3_), custom_call_target="tpu_custom_call" | custom-call | tf_op jit(solution)/shard_map/pallas_call | solution.py:45
  117.9 1.7 collective-permute-start.6
  119.6 3.8 %shard_map.24 = (f32[2,4,72,324]{3,2,1,0:T(8,128)}, f32[8,128]{1,0:T(8,128)S(1)}) custom-call(s32[1]{0:T(128)} %bitcast.refs_0_, bf16[4,324,2048]{2,1,0:T(8,128)(2,1)S(1)} %bitcast.22, bf16[272,2048]{1,0:T(8,128)(2,1)S(1)} %collective-permute-done.3.refs_2_, f32[8,128]{1,0:T(8,128)S(1)} %get-tuple-element.76.refs_3_), custom_call_target="tpu_custom_call" | custom-call | tf_op jit(solution)/shard_map/pallas_call | solution.py:45
  123.5 1.6 collective-permute-start.9
  125.0 0.1 pad_add_fusion.1.refs_0_
  125.1 0.0 collective-permute-done.5.refs_4_
  125.1 2.3 %copy-done.7 = f32[8,324,324]{2,1,0:T(8,128)S(1)} copy-done((f32[8,324,324]{2,1,0:T(8,128)S(1)}, f32[8,324,324]{2,1,0:T(8,128)}, u32[]{:S(2)}) %copy-start.7) | copy-done | bytes 3359256
  127.4 7.2 %shard_map.25 = (f32[2,324,8,324]{3,2,1,0:T(8,128)}, f32[8,128]{1,0:T(8,128)S(1)}) custom-call(s32[2]{0:T(128)S(1)} %pad_add_fusion.1.refs_0_, f32[8,324,324]{2,1,0:T(8,128)S(1)} %copy-done.7, f32[1744,256]{1,0:T(8,128)} %collective-permute-done.1.refs_4_.refs_2_, f32[4,328,384]{2,1,0:T(8,128)} %get-tuple-element.74.refs_3_, ...), custom_call_target="tpu_custom_call" | custom-call | tf_op jit(solution)/shard_map/pallas_call | solution.py:45
  134.6 0.0 collective-permute-done.7.refs_2_
  134.6 3.3 %shard_map.26 = (f32[2,4,328,128]{3,2,1,0:T(8,128)}, f32[8,128]{1,0:T(8,128)S(1)}) custom-call(s32[1]{0:T(128)} %bitcast.refs_0_, bf16[4,324,2048]{2,1,0:T(8,128)(2,1)S(1)} %bitcast.25, bf16[512,2048]{1,0:T(8,128)(2,1)S(1)} %collective-permute-done.7.refs_2_, f32[8,128]{1,0:T(8,128)S(1)} %get-tuple-element.82.refs_3_), custom_call_target="tpu_custom_call" | custom-call | tf_op jit(solution)/shard_map/pallas_call | solution.py:45
  137.9 2.0 %collective-permute-start.11 = (f32[2,4,328,128]{3,2,1,0:T(8,128)}, f32[2,4,328,128]{3,2,1,0:T(8,128)}, u32[]{:S(2)}, u32[]{:S(2)}) collective-permute-start(f32[2,4,328,128]{3,2,1,0:T(8,128)} %get-tuple-element.92), channel_id=1, source_target_pairs={{2,3},{3,2},{6,7},{7,6},{10,11},{11,10},{14,15},{15,14},{16,17},{1... | collective-permute-start | bytes 4030472 | tf_op jit(solution)/shard_map/ppermute | solution.py:432
  139.8 0.0 collective-permute-done.6.refs_2_
  139.8 3.2 %shard_map.27 = (f32[2,2,324,128]{3,2,1,0:T(8,128)S(1)}, bf16[2,4,328,128]{3,2,1,0:T(8,128)(2,1)}, f32[8,128]{1,0:T(8,128)S(1)}) custom-call(s32[1]{0:T(128)} %bitcast.refs_0_, f32[2,4,328,128]{3,2,1,0:T(8,128)S(1)} %get-tuple-element.79.refs_1_, f32[2,4,328,128]{3,2,1,0:T(8,128)} %collective-permute-done.6.refs_2_, f32[8,128]{1,0:T(8,128)S(1)} %get-tuple-element.83.refs_3_), custom_call_target="tpu_custom_call" | custom-call | tf_op jit(solution)/shard_map/pallas_call | solution.py:45
  143.0 1.3 collective-permute-start.8
  144.3 0.0 collective-permute-done.9.refs_2_
  144.3 2.5 %shard_map.28 = (f32[2,2,68,324]{3,2,1,0:T(8,128)S(1)}, bf16[2,4,72,324]{3,2,1,0:T(8,128)(2,1)}, f32[8,128]{1,0:T(8,128)S(1)}) custom-call(s32[1]{0:T(128)} %bitcast.refs_0_, f32[2,4,72,324]{3,2,1,0:T(8,128)S(1)} %copy-done.9, f32[2,4,72,324]{3,2,1,0:T(8,128)} %collective-permute-done.9.refs_2_, f32[8,128]{1,0:T(8,128)S(1)} %get-tuple-element.87.refs_3_), custom_call_target="tpu_custom_call" | custom-call | flops 10000000000 | bytes 100000000 | tf_op jit(solution)/shard_map/pallas_call | solution.py:45
  146.8 1.3 collective-permute-start.10
  148.1 1.7 shard_map.29
  149.8 0.7 collective-permute-start.12
  150.5 0.1 pad_add_fusion.refs_0_
  150.5 2.5 %copy-done.3 = bf16[4,2048,324]{1,2,0:T(8,128)(2,1)S(1)} copy-done((bf16[4,2048,324]{1,2,0:T(8,128)(2,1)S(1)}, bf16[4,2048,324]{1,2,0:T(8,128)(2,1)}, u32[]{:S(2)}) %copy-start.3) | copy-done | bytes 5308440
  153.1 2.3 %shard_map.30 = (f32[2,4,328,128]{3,2,1,0:T(8,128)S(1)}, f32[8,128]{1,0:T(8,128)S(1)}) custom-call(s32[1]{0:T(128)} %bitcast.refs_0_, bf16[4,324,2048]{2,1,0:T(8,128)(2,1)S(1)} %bitcast.26, bf16[512,2048]{1,0:T(8,128)(2,1)S(1)} %collective-permute-done.7.refs_2_, f32[8,128]{1,0:T(8,128)S(1)} %get-tuple-element.90.refs_3_), custom_call_target="tpu_custom_call" | custom-call | tf_op jit(solution)/shard_map/pallas_call | solution.py:45
  155.4 2.4 %shard_map.31 = (f32[2,2,324,128]{3,2,1,0:T(8,128)S(1)}, bf16[2,4,328,128]{3,2,1,0:T(8,128)(2,1)S(1)}, f32[8,128]{1,0:T(8,128)S(1)}) custom-call(s32[1]{0:T(128)} %bitcast.refs_0_, f32[2,4,328,128]{3,2,1,0:T(8,128)S(1)} %get-tuple-element.91.refs_1_, f32[2,4,328,128]{3,2,1,0:T(8,128)} %collective-permute-done.11.refs_2_, f32[8,128]{1,0:T(8,128)S(1)} %get-tuple-element.93.refs_3_), custom_call_target="tpu_custom_call" | custom-call | tf_op jit(solution)/shard_map/pallas_call | solution.py:45
  157.8 1.5 collective-permute-start.14
  159.3 1.0 shard_map.32
  160.4 0.7 collective-permute-start.13
  161.1 20.8 %collective-permute-done.10.refs_4_.refs_5_ = bf16[2,4,72,324]{3,2,1,0:T(8,128)(2,1)S(1)} collective-permute-done((bf16[2,4,72,324]{3,2,1,0:T(8,128)(2,1)}, bf16[2,4,72,324]{3,2,1,0:T(8,128)(2,1)S(1)}, u32[]{:S(2)}, u32[]{:S(2)}) %collective-permute-start.10) | collective-permute-done | bytes 373280 | tf_op jit(solution)/shard_map/ppermute | solution.py:439
  181.8 0.0 collective-permute-done.8.refs_2_.refs_3_
  181.8 3.6 %shard_map.33 = (f32[2,324,8,324]{3,2,1,0:T(8,128)}, f32[8,128]{1,0:T(8,128)S(1)}) custom-call(s32[2]{0:T(128)S(1)} %pad_add_fusion.refs_0_, f32[2,324,8,324]{3,2,1,0:T(8,128)} %get-tuple-element.78.refs_1_, bf16[2,4,328,128]{3,2,1,0:T(8,128)(2,1)S(1)} %collective-permute-done.8.refs_2_.refs_3_, ...), custom_call_target="tpu_custom_call", output_to_operand_aliasing={{0}: (1, {})} | custom-call | tf_op jit(solution)/shard_map/pallas_call | solution.py:45
  185.5 0.6 shard_map.34
  186.1 0.5 copy-done.11
  186.6 0.6 shard_map.35
  187.2 1.8 collective-permute-done.14.refs_2_.refs_3_
  189.0 3.4 %shard_map.36 = (f32[2,324,8,324]{3,2,1,0:T(8,128)}, f32[8,128]{1,0:T(8,128)}) custom-call(s32[2]{0:T(128)S(1)} %pad_add_fusion.refs_0_, f32[2,324,8,324]{3,2,1,0:T(8,128)} %get-tuple-element.106.refs_1_, bf16[2,4,328,128]{3,2,1,0:T(8,128)(2,1)S(1)} %collective-permute-done.14.refs_2_.refs_3_, ...), custom_call_target="tpu_custom_call", output_to_operand_aliasing={{0}: (1, {})} | custom-call | tf_op jit(solution)/shard_map/pallas_call | solution.py:45
  (28 shorter events, 0.1 us)
Async XLA Ops:
  0.0 17.8 %collective-permute-start = (bf16[4,2048,324]{1,0,2:T(4,128)(2,1)}, bf16[4,2048,324]{1,0,2:T(4,128)(2,1)}, u32[]{:S(2)}, u32[]{:S(2)}) collective-permute-start(bf16[4,2048,324]{1,0,2:T(4,128)(2,1)} %param.1), channel_id=1, source_target_pairs={{0,2},{2,0},{4,6},{6,4},{8,10},{10,8},{12,14},{14,12},{16,18},{18,... | collective-permute-start | bytes 15925256 | tf_op jit(solution)/shard_map/ppermute | solution.py:397
  5.5 53.6 %collective-permute-start.4 = (bf16[512,2048]{1,0:T(8,128)(2,1)}, bf16[512,2048]{1,0:T(8,128)(2,1)}, u32[]{:S(2)}, u32[]{:S(2)}) collective-permute-start(bf16[512,2048]{1,0:T(8,128)(2,1)} %bitcast.4.refs_3_), channel_id=1, source_target_pairs={{0,16},{1,17},{4,20},{5,21},{8,24},{9,25},{12,28},{13,29},{18,2},{... | collective-permute-start | bytes 6291464 | tf_op jit(solution)/shard_map/ppermute | solution.py:400
  17.8 21.6 %copy-start = (bf16[4,2048,324]{1,2,0:T(8,128)(2,1)}, bf16[4,2048,324]{1,2,0:T(8,128)(2,1)S(1)}, u32[]{:S(2)}) copy-start(bf16[4,2048,324]{1,2,0:T(8,128)(2,1)S(1)} %copy.18) | copy-start | bytes 15925252
  25.2 5.2 %copy-start.4 = (bf16[4,2048,324]{1,2,0:T(8,128)(2,1)}, bf16[4,2048,324]{1,2,0:T(8,128)(2,1)S(1)}, u32[]{:S(2)}) copy-start(bf16[4,2048,324]{1,2,0:T(8,128)(2,1)S(1)} %copy.17) | copy-start | bytes 15925252
  35.4 38.7 %collective-permute-start.2 = (f32[1744,256]{1,0:T(8,128)}, f32[1744,256]{1,0:T(8,128)}, u32[]{:S(2)}, u32[]{:S(2)}) collective-permute-start(f32[1744,256]{1,0:T(8,128)} %get-tuple-element.69), channel_id=1, source_target_pairs={{0,1},{1,0},{4,5},{5,4},{8,9},{9,8},{12,13},{13,12},{16,17},{17,16... | collective-permute-start | bytes 5357576 | tf_op jit(solution)/shard_map/ppermute | solution.py:408
  38.8 54.5 %collective-permute-start.1 = (f32[1744,256]{1,0:T(8,128)}, f32[1744,256]{1,0:T(8,128)}, u32[]{:S(2)}, u32[]{:S(2)}) collective-permute-start(f32[1744,256]{1,0:T(8,128)} %get-tuple-element.68), channel_id=1, source_target_pairs={{0,1},{1,0},{2,3},{3,2},{4,5},{5,4},{6,7},{7,6},{8,9},{9,8},{10,11... | collective-permute-start | bytes 5357576 | tf_op jit(solution)/shard_map/ppermute | solution.py:406
  40.7 22.8 %collective-permute-start.3 = (bf16[272,2048]{1,0:T(8,128)(2,1)}, bf16[272,2048]{1,0:T(8,128)(2,1)S(1)}, u32[]{:S(2)}, u32[]{:S(2)}) collective-permute-start(bf16[272,2048]{1,0:T(8,128)(2,1)} %reshape.11), channel_id=1, source_target_pairs={{0,16},{1,17},{4,20},{5,21},{8,24},{9,25},{12,28},{13,29},{18,2},{... | collective-permute-start | bytes 3342344 | tf_op jit(solution)/shard_map/ppermute | solution.py:413
  45.2 89.4 %collective-permute-start.7 = (bf16[512,2048]{1,0:T(8,128)(2,1)}, bf16[512,2048]{1,0:T(8,128)(2,1)S(1)}, u32[]{:S(2)}, u32[]{:S(2)}) collective-permute-start(bf16[512,2048]{1,0:T(8,128)(2,1)} %bitcast.7), channel_id=1, source_target_pairs={{0,16},{1,17},{4,20},{5,21},{8,24},{9,25},{12,28},{13,29},{18,2},{... | collective-permute-start | bytes 6291464 | tf_op jit(solution)/shard_map/ppermute | solution.py:415
  46.8 2.5 %copy-start.1 = (bf16[4,2048,324]{1,2,0:T(8,128)(2,1)S(1)}, bf16[4,2048,324]{1,2,0:T(8,128)(2,1)}, u32[]{:S(2)}) copy-start(bf16[4,2048,324]{1,2,0:T(8,128)(2,1)} %copy-done) | copy-start | bytes 15925252
  49.4 2.5 %copy-start.5 = (bf16[4,2048,324]{1,2,0:T(8,128)(2,1)S(1)}, bf16[4,2048,324]{1,2,0:T(8,128)(2,1)}, u32[]{:S(2)}) copy-start(bf16[4,2048,324]{1,2,0:T(8,128)(2,1)} %copy-done.4) | copy-start | bytes 15925252
  51.9 7.2 %copy-start.2 = (bf16[4,2048,324]{1,2,0:T(8,128)(2,1)S(1)}, bf16[4,2048,324]{1,2,0:T(8,128)(2,1)}, u32[]{:S(2)}) copy-start(bf16[4,2048,324]{1,2,0:T(8,128)(2,1)} %copy-done) | copy-start | bytes 15925252
  59.1 34.2 %copy-start.6 = (f32[8,324,324]{2,1,0:T(8,128)}, f32[8,324,324]{2,1,0:T(8,128)S(1)}, u32[]{:S(2)}) copy-start(f32[8,324,324]{2,1,0:T(8,128)S(1)} %get-tuple-element.67.refs_1_) | copy-start | bytes 10077700
  66.7 0.9 copy-start.8
  96.5 28.6 %collective-permute-start.5 = (f32[4,328,384]{2,1,0:T(8,128)}, f32[4,328,384]{2,1,0:T(8,128)}, u32[]{:S(2)}, u32[]{:S(2)}) collective-permute-start(f32[4,328,384]{2,1,0:T(8,128)} %get-tuple-element.74.refs_3_), channel_id=1, source_target_pairs={{0,2},{1,3},{4,6},{5,7},{8,10},{9,11},{12,14},{13,15},{16,18},{17,... | collective-permute-start | bytes 6045704 | tf_op jit(solution)/shard_map/ppermute | solution.py:453
  117.9 21.9 %collective-permute-start.6 = (f32[2,4,328,128]{3,2,1,0:T(8,128)}, f32[2,4,328,128]{3,2,1,0:T(8,128)}, u32[]{:S(2)}, u32[]{:S(2)}) collective-permute-start(f32[2,4,328,128]{3,2,1,0:T(8,128)} %get-tuple-element.80), channel_id=1, source_target_pairs={{2,3},{3,2},{6,7},{7,6},{10,11},{11,10},{14,15},{15,14},{16,17},{1... | collective-permute-start | bytes 4030472 | tf_op jit(solution)/shard_map/ppermute | solution.py:432
  123.5 20.8 %collective-permute-start.9 = (f32[2,4,72,324]{3,2,1,0:T(8,128)}, f32[2,4,72,324]{3,2,1,0:T(8,128)}, u32[]{:S(2)}, u32[]{:S(2)}) collective-permute-start(f32[2,4,72,324]{3,2,1,0:T(8,128)} %get-tuple-element.86), channel_id=1, source_target_pairs={{2,3},{3,2},{6,7},{7,6},{10,11},{11,10},{14,15},{15,14},{16,17},{1... | collective-permute-start | bytes 2239496 | tf_op jit(solution)/shard_map/ppermute | solution.py:432
  125.1 9.5 %slice-start = ((s8[5373952]{0:T(1024)(128)(4,1)}), s8[4194304]{0:T(1024)(128)(4,1)S(1)}, s32[]{:S(2)}) async-start(s8[5373952]{0:T(1024)(128)(4,1)} %bitcast.23), calls=%async_computation | async-start | bytes 8388608
  125.1 2.3 %copy-start.7 = (f32[8,324,324]{2,1,0:T(8,128)S(1)}, f32[8,324,324]{2,1,0:T(8,128)}, u32[]{:S(2)}) copy-start(f32[8,324,324]{2,1,0:T(8,128)} %copy-done.6) | copy-start | bytes 10077700
  127.4 7.2 %slice-start.1 = ((s8[5373952]{0:T(1024)(128)(4,1)}), s8[1179648]{0:T(1024)(128)(4,1)S(1)}, s32[]{:S(2)}) async-start(s8[5373952]{0:T(1024)(128)(4,1)} %bitcast.23), calls=%async_computation.1 | async-start | bytes 2359296
  137.9 6.4 %copy-start.9 = (f32[2,4,72,324]{3,2,1,0:T(8,128)S(1)}, f32[2,4,72,324]{3,2,1,0:T(8,128)}, u32[]{:S(2)}) copy-start(f32[2,4,72,324]{3,2,1,0:T(8,128)} %copy-done.8) | copy-start | bytes 2239492
  137.9 17.5 %collective-permute-start.11 = (f32[2,4,328,128]{3,2,1,0:T(8,128)}, f32[2,4,328,128]{3,2,1,0:T(8,128)}, u32[]{:S(2)}, u32[]{:S(2)}) collective-permute-start(f32[2,4,328,128]{3,2,1,0:T(8,128)} %get-tuple-element.92), channel_id=1, source_target_pairs={{2,3},{3,2},{6,7},{7,6},{10,11},{11,10},{14,15},{15,14},{16,17},{1... | collective-permute-start | bytes 4030472 | tf_op jit(solution)/shard_map/ppermute | solution.py:432
  143.0 3.8 %copy-start.10 = (f32[2,2,324,128]{3,2,1,0:T(8,128)}, f32[2,2,324,128]{3,2,1,0:T(8,128)S(1)}, u32[]{:S(2)}) copy-start(f32[2,2,324,128]{3,2,1,0:T(8,128)S(1)} %get-tuple-element.102.refs_2_.refs_3_) | copy-start | bytes 1990660
  143.0 38.8 %collective-permute-start.8 = (bf16[2,4,328,128]{3,2,1,0:T(8,128)(2,1)}, bf16[2,4,328,128]{3,2,1,0:T(8,128)(2,1)S(1)}, u32[]{:S(2)}, u32[]{:S(2)}) collective-permute-start(bf16[2,4,328,128]{3,2,1,0:T(8,128)(2,1)} %get-tuple-element.84.refs_1_), channel_id=1, source_target_pairs={{16,0},{17,1},{20,4},{21,5},{24,8},{25,9},{28,12},{29,13},{2,18},{... | collective-permute-start | bytes 2015240 | tf_op jit(solution)/shard_map/ppermute | solution.py:439
  146.8 2.9 %copy-start.12 = (f32[2,2,68,324]{3,2,1,0:T(8,128)}, f32[2,2,68,324]{3,2,1,0:T(8,128)S(1)}, u32[]{:S(2)}) copy-start(f32[2,2,68,324]{3,2,1,0:T(8,128)S(1)} %get-tuple-element.98.refs_2_.refs_3_) | copy-start | bytes 1057540
  146.8 35.0 %collective-permute-start.10 = (bf16[2,4,72,324]{3,2,1,0:T(8,128)(2,1)}, bf16[2,4,72,324]{3,2,1,0:T(8,128)(2,1)S(1)}, u32[]{:S(2)}, u32[]{:S(2)}) collective-permute-start(bf16[2,4,72,324]{3,2,1,0:T(8,128)(2,1)} %get-tuple-element.88.refs_1_), channel_id=1, source_target_pairs={{16,0},{17,1},{20,4},{21,5},{24,8},{25,9},{28,12},{29,13},{2,18},{... | collective-permute-start | bytes 1119752 | tf_op jit(solution)/shard_map/ppermute | solution.py:439
  149.8 35.7 %collective-permute-start.12 = (bf16[1,2,2,72,324]{4,3,2,1,0:T(8,128)(2,1)}, bf16[1,2,2,72,324]{4,3,2,1,0:T(8,128)(2,1)S(1)}, u32[]{:S(2)}, u32[]{:S(2)}) collective-permute-start(bf16[1,2,2,72,324]{4,3,2,1,0:T(8,128)(2,1)} %get-tuple-element.99), channel_id=1, source_target_pairs={{2,3},{3,2},{6,7},{7,6},{10,11},{11,10},{14,15},{15,14},{16,17},{1... | collective-permute-start | bytes 559880 | tf_op jit(solution)/shard_map/ppermute | solution.py:444
  150.5 2.5 %copy-start.3 = (bf16[4,2048,324]{1,2,0:T(8,128)(2,1)S(1)}, bf16[4,2048,324]{1,2,0:T(8,128)(2,1)}, u32[]{:S(2)}) copy-start(bf16[4,2048,324]{1,2,0:T(8,128)(2,1)} %copy-done) | copy-start | bytes 15925252
  157.8 31.2 %collective-permute-start.14 = (bf16[2,4,328,128]{3,2,1,0:T(8,128)(2,1)S(1)}, bf16[2,4,328,128]{3,2,1,0:T(8,128)(2,1)S(1)}, u32[]{:S(2)}, u32[]{:S(2)}) collective-permute-start(bf16[2,4,328,128]{3,2,1,0:T(8,128)(2,1)S(1)} %get-tuple-element.94.refs_2_), channel_id=1, source_target_pairs={{16,0},{17,1},{20,4},{21,5},{24,8},{25,9},{28,12},{29,13},{2,18},{... | collective-permute-start | bytes 2015240 | tf_op jit(solution)/shard_map/ppermute | solution.py:439
  160.4 25.7 %collective-permute-start.13 = (bf16[2,2,2,328,128]{4,3,2,1,0:T(8,128)(2,1)S(1)}, bf16[2,2,2,328,128]{4,3,2,1,0:T(8,128)(2,1)S(1)}, u32[]{:S(2)}, u32[]{:S(2)}) collective-permute-start(bf16[2,2,2,328,128]{4,3,2,1,0:T(8,128)(2,1)S(1)} %get-tuple-element.103), channel_id=1, source_target_pairs={{2,3},{3,2},{6,7},{7,6},{10,11},{11,10},{14,15},{15,14},{16,17},{1... | collective-permute-start | bytes 2015240 | tf_op jit(solution)/shard_map/ppermute | solution.py:444
  181.8 3.7 %copy-start.13 = (f32[2,2,68,324]{3,2,1,0:T(8,128)S(1)}, f32[2,2,68,324]{3,2,1,0:T(8,128)}, u32[]{:S(2)}) copy-start(f32[2,2,68,324]{3,2,1,0:T(8,128)} %copy-done.12) | copy-start | bytes 1057540
  185.5 1.1 copy-start.11

commit v11 on v10

--- a/solution.py
+++ b/solution.py
@@ -75,6 +75,15 @@
         wire_ref[start : start + self.rest] = turned[:, : self.wide]
         wire_ref[row : row + self.rest, lane : lane + self.rest] = turned[:, self.wide :]
 
+    def rows(self, wire_ref, t, start, rows):
+        row, lane = self.corners[t]
+        under, padded = t * self.each + self.below, up(self.rest, 8)
+        if start < self.wide:
+            side = wire_ref[under : under + padded, start : start + rows].T[:, : self.rest]
+        else:
+            side = wire_ref[row : row + padded, lane : lane + LANES].T[:rows, : self.rest]
+        return jnp.concatenate([wire_ref[t * self.each + start : t * self.each + start + rows], side], axis=1)
+
     def parts(self, wire_ref, t):
         row, lane = self.corners[t]
         start, padded = t * self.each + self.below, up(self.rest, 8)
@@ -158,34 +167,67 @@
     tiles, ops, _ = keep.shape
     half = states // 2
     packing = Packing(half * half, ops)
-
-    def body(s_ref, keep_ref, wire_ref, share_ref, given_ref, out_ref):
+    blocks = [(p, min(LANES, ops - p)) for p in range(0, ops, LANES)]
+
+    def body(s_ref, keep_ref, wire_in, share_ref, given_ref, out_ref, kept, wire, mine, *rest):
+        made, sems = rest[:-1], rest[-1]
         x, core = s_ref[0], s_ref[1]
+        loads = [pltpu.make_async_copy(wire_in, wire, sems.at[0])]
         for a in range(half):
-            for b in range(states):
-                t, one, turned = a * states + b, a * half + b % half, b % half * half + a
-
-                @pl.when(b // half != x)
-                def _():
-                    for rows, columns, values in packing.parts(wire_ref, one):
-                        out_ref[0, rows, t, columns] = keep_ref[t, rows, columns] + values
-
-                @pl.when((b // half == x) & (core == 0))
-                def _():
-                    out_ref[0, :, t] = share_ref[one, :ops, :ops]
-
-                @pl.when((b // half == x) & (core == 1))
-                def _():
-                    out_ref[0, :, t] = given_ref[turned].T[:ops, :ops]
+            other = keep_ref.at[pl.ds(a * states + half * (1 - x), half)]
+            loads.append(pltpu.make_async_copy(other, kept.at[pl.ds(a * half, half)], sems.at[1 + a]))
+        for load in loads:
+            load.start()
+        for source, which in ((share_ref, 0), (given_ref, 1)):
+
+            @pl.when(core == which)
+            def _():
+                load = pltpu.make_async_copy(source, mine, sems.at[1 + half])
+                load.start()
+                load.wait()
+
+        for load in loads:
+            load.wait()
+        stores = []
+        for n, (start, rows) in enumerate(blocks):
+            ref = made[n]
+            for a in range(half):
+                for b in range(states):
+                    t, one, turned = a * states + b, a * half + b % half, b % half * half + a
+
+                    @pl.when(b // half != x)
+                    def _():
+                        ref[:, t] = kept[one, start : start + rows] + packing.rows(wire, one, start, rows)
+
+                    @pl.when((b // half == x) & (core == 0))
+                    def _():
+                        ref[:, t] = mine[one, start : start + rows, :ops]
+
+                    @pl.when((b // half == x) & (core == 1))
+                    def _():
+                        ref[:, t] = mine[turned, :, start : start + LANES].T[:rows, :ops]
+
+            target = out_ref.at[1, pl.ds(start, rows)]
+            stores.append(pltpu.make_async_copy(ref, target, sems.at[2 + half + n]))
+            stores[n].start()
+        for store in stores:
+            store.wait()
 
     return call(
         body,
         (1,),
         1,
-        [whole(keep.shape), whole(packing.shape), whole(share.shape), whole(given.shape)],
-        [pl.BlockSpec((1, ops, tiles, ops), lambda i, s: (1, 0, 0, 0), pipeline_mode=pl.Buffered(1))],
+        [pl.BlockSpec(memory_space=pl.ANY)] * 4,
+        [pl.BlockSpec(memory_space=pl.ANY)],
         [f32(2, ops, tiles, ops)],
         after,
+        scratch=[
+            pltpu.VMEM((half * half, ops, ops), jnp.float32),
+            pltpu.VMEM(packing.shape, jnp.float32),
+            pltpu.VMEM(share.shape, jnp.float32),
+            *[pltpu.VMEM((rows, tiles, ops), jnp.float32) for _, rows in blocks],
+            pltpu.SemaphoreType.DMA((2 + half + len(blocks),)),
+        ],
     )(place_in, keep, crossed, share, given)
 
 
@@ -409,13 +451,13 @@
     whole_own, token = lax.optimization_barrier((own, token))
     widths = [LANES] * full + [ops - wide]
     chunk = [whole_own[:, k * LANES : k * LANES + w].reshape(states * w, depth) for k, w in enumerate(widths)]
+    later, token = lax.optimization_barrier((jnp.concatenate(chunk[1:full]), token))
+    got.append(lax.ppermute(later, both, over))
     last, token = lax.optimization_barrier((chunk[full], token))
     got.append(lax.ppermute(last, both, over))
-    later, token = lax.optimization_barrier((jnp.concatenate(chunk[1:full]), token))
-    got.append(lax.ppermute(later, both, over))
     keep, token = near_keep(det, own, partner, (token,))
     def terms(k, mine, *done):
-        wire, start = (0, 0) if k == 0 else (1, 0) if k == full else (2, states * LANES * (k - 1))
+        wire, start = (0, 0) if k == 0 else (2, 0) if k == full else (1, states * LANES * (k - 1))
         return far_terms(det, own, got[wire], start, widths[k], k < full, mine, done)
 
     kepts, came, tiles, codes, mine, theirs = {}, {}, {}, {}, {}, {}
@@ -423,8 +465,8 @@
     def place_of(k):
         return k * LANES, widths[k], ops
 
-    def keep_terms(k, token):
-        kepts[k], token = terms(k, True, token)
+    def keep_terms(k, *token):
+        kepts[k], token = terms(k, True, *token)
         return token
 
     def send_terms(k, token):
@@ -432,10 +474,10 @@
         came[k] = lax.ppermute(send, both, across)
         return token
 
-    def sum_up(k, token):
+    def sum_up(k, *token):
         rows = ops if k < full else widths[k]
-        declared = LONG if k == early[-1] else 0
-        tiles[k], codes[k], token = far_sum(det, kepts[k], came[k], rows, k < full, (token,), declared)
+        declared = LONG if k in early else 0
+        tiles[k], codes[k], token = far_sum(det, kepts[k], came[k], rows, k < full, token, declared)
         theirs[k] = returned_piece(lax.ppermute(codes[k], both, back), *place_of(k))
         return token
 
@@ -446,28 +488,24 @@
             mine[k] = finished_piece(tiles[k], wire, n, *place_of(k))
         return token
 
-    early, late = [0, full], list(range(1, full))
+    early, late = list(range(full)), [full]
     for k in early:
-        token = keep_terms(k, token)
-    share, token = near_share(det, keep, doubled, states, (token, crossed))
-    given = lax.ppermute(share, both, to_second)
+        token = keep_terms(k, send_terms(k, token))
+        if k == 0:
+            share, token = near_share(det, keep, doubled, states, (token, crossed))
+            given = lax.ppermute(share, both, to_second)
+    token = send_terms(full, token)
     for k in early:
-        token = send_terms(k, token)
-    out, token = near_sum(jnp.stack([x, core]), keep, crossed, share, given, states, (token,))
-    for k in late:
-        token = send_terms(k, token)
-    for k in early:
-        token = sum_up(k, token)
-    token = cross([full], token)
-    for k in late:
-        token = keep_terms(k, token)
-    for k in late:
         token = sum_up(k, token)
     turned = list(range(full))
     token = cross(turned, token)
+    token = keep_terms(full, token, given)
+    token = sum_up(full, token)
+    token = cross([full], token)
+    out, token = near_sum(jnp.stack([x, core]), keep, crossed, share, given, states, (token,))
 
     at = jnp.stack([x, receiver])
-    for role, kind, ks in ((0, theirs, early), (1, mine, [full]), (1, mine, turned), (0, theirs, late)):
+    for role, kind, ks in ((0, theirs, early), (1, mine, early), (1, mine, late), (0, theirs, late)):
         declared = LONG if role == 1 else 0
         out, token = into_place(role, at, out, [kind[k] for k in ks], (token,), declared)
     return out.transpose(0, 2, 1, 3)

time: 194 us -> 200 us (1.031)
  the two profiles are of different devices: /device:TPU:0 before, /device:TPU:28 now
where the time goes in v11:
time: 200 us; the launch traced here: 199 us
  waiting for transfers between devices  73.3 us (37%)
  Pallas kernels  62.9 us (31%)
  local copies, waits for them, and re-layouts  31.6 us (16%)
  starting transfers between devices  30.7 us (15%)
    pallas_call x20, Pallas kernels, call(): return lambda *operands: kernel(*operands, *after)  62.9 us
    ppermute x1, waiting for transfers between devices, paired(): got = [lax.ppermute(first, both, over)]  39.2 us
    ppermute x1, waiting for transfers between devices, paired(): got.append(lax.ppermute(last, both, over))  20.1 us
    ppermute x1, waiting for transfers between devices, paired(): got.append(lax.ppermute(later, both, over))  14 us
    ppermute x3, starting transfers between devices, send_terms(): came[k] = lax.ppermute(send, both, across)  10.4 us
    unnamed x28, local copies, waits for them, and re-layouts  8.88 us
    optimization_barrier x1, local copies, waits for them, and re-layouts, paired(): partner, own = lax.optimization_barrier((partner, own))  7.35 us
    ppermute x2, starting transfers between devices, cross(): wire = lax.ppermute(wire, both, across)  5.83 us
  transfers between devices with their start and end apart: 15, of which 3 were waited for; matrix products, arithmetic and copies ran while one was open for 11% of the time, Pallas kernels for 31%

profile of v11, /device:TPU:28, one launch (start us, length us, event | category | flops | bytes accessed | tf_op | source)
XLA Modules:
  0.0 199.1 jit_solution(15778458388270317631)
XLA Ops:
  0.0 0.0 collective-permute-start
  0.0 2.6 %slice_bitcast_fusion = bf16[4,128,2048]{2,0,1:T(4,128)(2,1)S(1)} fusion(bf16[4,2048,324]{1,0,2:T(4,128)(2,1)} %param.1), kind=kLoop, calls=%fused_computation.2 | loop fusion | bytes 4194304 | tf_op jit(solution)/shard_map/transpose | solution.py:440
  2.6 2.5 %copy.12 = bf16[4,128,2048]{2,1,0:T(8,128)(2,1)} copy(bf16[4,128,2048]{2,0,1:T(4,128)(2,1)S(1)} %slice_bitcast_fusion) | data formatting | bytes 4194304 | tf_op jit(solution)/shard_map/transpose | solution.py:440
  5.1 1.3 collective-permute-start.3
  6.4 5.4 %copy.18 = bf16[4,2048,324]{1,2,0:T(8,128)(2,1)S(1)} copy(bf16[4,2048,324]{1,0,2:T(4,128)(2,1)} %param.1) | data formatting | bytes 10616832 | tf_op jit(solution)/shard_map/optimization_barrier | solution.py:441
  11.9 0.0 copy-start
  11.9 0.0 collective-permute-done
  11.9 7.4 %copy.17 = bf16[4,2048,324]{1,2,0:T(8,128)(2,1)S(1)} copy(bf16[4,2048,324]{1,0,2:T(4,128)(2,1)} %collective-permute-done) | data formatting | bytes 10616832 | tf_op jit(solution)/shard_map/optimization_barrier | solution.py:444
  19.2 5.1 %shard_map.17 = (f32[1744,256]{1,0:T(8,128)}, f32[8,128]{1,0:T(8,128)S(1)}) custom-call(s32[1]{0:T(128)} %bitcast.refs_0_, bf16[4,324,2048]{2,1,0:T(8,128)(2,1)S(1)} %bitcast.14, bf16[4,324,2048]{2,1,0:T(8,128)(2,1)S(1)} %bitcast.27, bf16[512,2048]{1,0:T(8,128)(2,1)} %bitcast.4.refs_3_), custom_call_target="tpu_custom_call" | custom-call | tf_op jit(solution)/shard_map/pallas_call | solution.py:45
  24.3 5.1 %shard_map.18 = (f32[1744,256]{1,0:T(8,128)}, f32[8,128]{1,0:T(8,128)S(1)}) custom-call(s32[1]{0:T(128)} %bitcast.refs_0_, bf16[4,324,2048]{2,1,0:T(8,128)(2,1)S(1)} %bitcast.15, bf16[4,324,2048]{2,1,0:T(8,128)(2,1)S(1)} %bitcast.28, f32[8,128]{1,0:T(8,128)S(1)} %get-tuple-element.61.refs_3_), custom_call_target="tpu_custom_call" | custom-call | tf_op jit(solution)/shard_map/pallas_call | solution.py:45
  29.4 1.5 slice.11
  31.0 1.3 collective-permute-start.7
  32.3 3.4 %collective-permute-start.2 = (f32[1744,256]{1,0:T(8,128)}, f32[1744,256]{1,0:T(8,128)}, u32[]{:S(2)}, u32[]{:S(2)}) collective-permute-start(f32[1744,256]{1,0:T(8,128)} %get-tuple-element.69), channel_id=1, source_target_pairs={{0,1},{1,0},{4,5},{5,4},{8,9},{9,8},{12,13},{13,12},{16,17},{17,16... | collective-permute-start | bytes 5357576 | tf_op jit(solution)/shard_map/ppermute | solution.py:450
  35.7 0.6 collective-permute-start.1
  36.3 1.1 slice.10
  37.4 2.2 %reshape.10 = bf16[272,2048]{1,0:T(8,128)(2,1)} reshape(bf16[4,68,2048]{2,1,0:T(8,128)(2,1)} %slice.10) | data formatting | bytes 2228224 | tf_op jit(solution)/shard_map/reshape | solution.py:453
  39.6 2.5 %copy-done.1 = bf16[4,2048,324]{1,2,0:T(8,128)(2,1)S(1)} copy-done((bf16[4,2048,324]{1,2,0:T(8,128)(2,1)S(1)}, bf16[4,2048,324]{1,2,0:T(8,128)(2,1)}, u32[]{:S(2)}) %copy-start.1) | copy-done | bytes 5308440
  42.1 2.5 %copy-done.4 = bf16[4,2048,324]{1,2,0:T(8,128)(2,1)S(1)} copy-done((bf16[4,2048,324]{1,2,0:T(8,128)(2,1)S(1)}, bf16[4,2048,324]{1,2,0:T(8,128)(2,1)}, u32[]{:S(2)}) %copy-start.4) | copy-done | bytes 5308440
  44.6 7.2 %shard_map.19 = (f32[8,324,324]{2,1,0:T(8,128)S(1)}, f32[8,128]{1,0:T(8,128)S(1)}) custom-call(s32[1]{0:T(128)} %bitcast.refs_0_, bf16[4,324,2048]{2,1,0:T(8,128)(2,1)S(1)} %bitcast.18, bf16[4,324,2048]{2,1,0:T(8,128)(2,1)S(1)} %bitcast.29, f32[8,128]{1,0:T(8,128)S(1)} %get-tuple-element.66.refs_3_), custom_call_target="tpu_custom_call" | custom-call | tf_op jit(solution)/shard_map/pallas_call | solution.py:45
  51.9 39.2 %collective-permute-done.3.refs_2_ = bf16[512,2048]{1,0:T(8,128)(2,1)} collective-permute-done((bf16[512,2048]{1,0:T(8,128)(2,1)}, bf16[512,2048]{1,0:T(8,128)(2,1)}, u32[]{:S(2)}, u32[]{:S(2)}) %collective-permute-start.3) | collective-permute-done | bytes 2097184 | tf_op jit(solution)/shard_map/ppermute | solution.py:442
  91.0 3.6 %shard_map.20 = (f32[2,4,328,128]{3,2,1,0:T(8,128)S(1)}, f32[8,128]{1,0:T(8,128)S(1)}) custom-call(s32[1]{0:T(128)} %bitcast.refs_0_, bf16[4,324,2048]{2,1,0:T(8,128)(2,1)S(1)} %bitcast.19, bf16[512,2048]{1,0:T(8,128)(2,1)} %collective-permute-done.3.refs_2_, f32[8,128]{1,0:T(8,128)S(1)} %get-tuple-element.70.refs_3_), custom_call_target="tpu_custom_call" | custom-call | tf_op jit(solution)/shard_map/pallas_call | solution.py:45
  94.7 3.6 %collective-permute-start.6 = (f32[2,4,328,128]{3,2,1,0:T(8,128)S(1)}, f32[2,4,328,128]{3,2,1,0:T(8,128)S(1)}, u32[]{:S(2)}, u32[]{:S(2)}) collective-permute-start(f32[2,4,328,128]{3,2,1,0:T(8,128)S(1)} %get-tuple-element.76), channel_id=1, source_target_pairs={{2,3},{3,2},{6,7},{7,6},{10,11},{11,10},{14,15},{15,14},{16,17},{1... | collective-permute-start | bytes 4030472 | tf_op jit(solution)/shard_map/ppermute | solution.py:474
  98.3 1.3 collective-permute-start.5
  99.6 0.0 slice-start
  99.6 3.7 %shard_map.21 = (f32[2,4,328,128]{3,2,1,0:T(8,128)S(1)}, f32[8,128]{1,0:T(8,128)S(1)}) custom-call(s32[1]{0:T(128)} %bitcast.refs_0_, bf16[4,324,2048]{2,1,0:T(8,128)(2,1)S(1)} %bitcast.20, bf16[512,2048]{1,0:T(8,128)(2,1)} %collective-permute-done.3.refs_2_, f32[8,128]{1,0:T(8,128)S(1)} %get-tuple-element.71.refs_3_), custom_call_target="tpu_custom_call" | custom-call | tf_op jit(solution)/shard_map/pallas_call | solution.py:45
  103.3 0.0 collective-permute-done.2.refs_2_
  103.3 0.0 collective-permute-done.1.refs_4_.refs_2_
  103.3 0.0 slice-start.1
  103.4 3.3 %shard_map.22 = (f32[4,328,384]{2,1,0:T(8,128)}, f32[8,128]{1,0:T(8,128)S(1)}) custom-call(s32[1]{0:T(128)} %bitcast.refs_0_, f32[8,324,324]{2,1,0:T(8,128)S(1)} %get-tuple-element.67.refs_1_, f32[1744,256]{1,0:T(8,128)} %collective-permute-done.2.refs_2_, f32[8,128]{1,0:T(8,128)S(1)} %get-tuple-element.72.refs_3_, ...), custom_call_target="tpu_custom_call" | custom-call | tf_op jit(solution)/shard_map/pallas_call | solution.py:45
  106.6 14.0 %collective-permute-done.7.refs_2_ = bf16[512,2048]{1,0:T(8,128)(2,1)S(1)} collective-permute-done((bf16[512,2048]{1,0:T(8,128)(2,1)}, bf16[512,2048]{1,0:T(8,128)(2,1)S(1)}, u32[]{:S(2)}, u32[]{:S(2)}) %collective-permute-start.7) | collective-permute-done | bytes 2097184 | tf_op jit(solution)/shard_map/ppermute | solution.py:455
  120.6 2.3 %shard_map.23 = (f32[2,4,328,128]{3,2,1,0:T(8,128)S(1)}, f32[8,128]{1,0:T(8,128)S(1)}) custom-call(s32[1]{0:T(128)} %bitcast.refs_0_, bf16[4,324,2048]{2,1,0:T(8,128)(2,1)S(1)} %bitcast.23, bf16[512,2048]{1,0:T(8,128)(2,1)S(1)} %collective-permute-done.7.refs_2_, f32[8,128]{1,0:T(8,128)S(1)} %get-tuple-element.78.refs_3_), custom_call_target="tpu_custom_call" | custom-call | tf_op jit(solution)/shard_map/pallas_call | solution.py:45
  122.9 3.4 %collective-permute-start.8 = (f32[2,4,328,128]{3,2,1,0:T(8,128)S(1)}, f32[2,4,328,128]{3,2,1,0:T(8,128)S(1)}, u32[]{:S(2)}, u32[]{:S(2)}) collective-permute-start(f32[2,4,328,128]{3,2,1,0:T(8,128)S(1)} %get-tuple-element.84), channel_id=1, source_target_pairs={{2,3},{3,2},{6,7},{7,6},{10,11},{11,10},{14,15},{15,14},{16,17},{1... | collective-permute-start | bytes 4030472 | tf_op jit(solution)/shard_map/ppermute | solution.py:474
  126.3 2.7 %collective-permute-start.4 = (f32[4,328,384]{2,1,0:T(8,128)}, f32[4,328,384]{2,1,0:T(8,128)}, u32[]{:S(2)}, u32[]{:S(2)}) collective-permute-start(f32[4,328,384]{2,1,0:T(8,128)} %get-tuple-element.73.refs_3_), channel_id=1, source_target_pairs={{0,2},{1,3},{4,6},{5,7},{8,10},{9,11},{12,14},{13,15},{16,18},{17,... | collective-permute-start | bytes 6045704 | tf_op jit(solution)/shard_map/ppermute | solution.py:496
  129.0 2.3 %shard_map.24 = (f32[2,4,328,128]{3,2,1,0:T(8,128)S(1)}, f32[8,128]{1,0:T(8,128)S(1)}) custom-call(s32[1]{0:T(128)} %bitcast.refs_0_, bf16[4,324,2048]{2,1,0:T(8,128)(2,1)S(1)} %bitcast.24, bf16[512,2048]{1,0:T(8,128)(2,1)S(1)} %collective-permute-done.7.refs_2_, f32[8,128]{1,0:T(8,128)S(1)} %get-tuple-element.79.refs_3_), custom_call_target="tpu_custom_call" | custom-call | tf_op jit(solution)/shard_map/pallas_call | solution.py:45
  131.3 20.1 %collective-permute-done.5.refs_2_ = bf16[272,2048]{1,0:T(8,128)(2,1)S(1)} collective-permute-done((bf16[272,2048]{1,0:T(8,128)(2,1)S(1)}, bf16[272,2048]{1,0:T(8,128)(2,1)S(1)}, u32[]{:S(2)}, u32[]{:S(2)}) %collective-permute-start.5) | collective-permute-done | bytes 1114144 | tf_op jit(solution)/shard_map/ppermute | solution.py:457
  151.4 3.8 %shard_map.25 = (f32[2,4,72,324]{3,2,1,0:T(8,128)}, f32[8,128]{1,0:T(8,128)S(1)}) custom-call(s32[1]{0:T(128)} %bitcast.refs_0_, bf16[4,324,2048]{2,1,0:T(8,128)(2,1)S(1)} %bitcast.25, bf16[272,2048]{1,0:T(8,128)(2,1)S(1)} %collective-permute-done.5.refs_2_, f32[8,128]{1,0:T(8,128)S(1)} %get-tuple-element.80.refs_3_), custom_call_target="tpu_custom_call" | custom-call | tf_op jit(solution)/shard_map/pallas_call | solution.py:45
  155.2 3.4 %collective-permute-start.9 = (f32[2,4,72,324]{3,2,1,0:T(8,128)}, f32[2,4,72,324]{3,2,1,0:T(8,128)}, u32[]{:S(2)}, u32[]{:S(2)}) collective-permute-start(f32[2,4,72,324]{3,2,1,0:T(8,128)} %get-tuple-element.90), channel_id=1, source_target_pairs={{2,3},{3,2},{6,7},{7,6},{10,11},{11,10},{14,15},{15,14},{16,17},{1... | collective-permute-start | bytes 2239496 | tf_op jit(solution)/shard_map/ppermute | solution.py:474
  158.6 0.0 collective-permute-done.6.refs_2_
  158.7 1.0 shard_map.26
  159.7 0.8 copy-done.7
  160.5 1.3 collective-permute-start.10
  161.9 0.0 collective-permute-done.8.refs_2_
  161.9 1.8 shard_map.27
  163.7 1.3 collective-permute-start.11
  165.0 1.9 shard_map.28
  167.0 2.4 %collective-permute-start.12 = (bf16[2,2,2,328,128]{4,3,2,1,0:T(8,128)(2,1)}, bf16[2,2,2,328,128]{4,3,2,1,0:T(8,128)(2,1)}, u32[]{:S(2)}, u32[]{:S(2)}) collective-permute-start(bf16[2,2,2,328,128]{4,3,2,1,0:T(8,128)(2,1)} %get-tuple-element.99), channel_id=1, source_target_pairs={{2,3},{3,2},{6,7},{7,6},{10,11},{11,10},{14,15},{15,14},{16,17},{1... | collective-permute-start | bytes 2015240 | tf_op jit(solution)/shard_map/ppermute | solution.py:486
  169.4 0.1 pad_add_fusion
  169.5 0.0 collective-permute-done.4.refs_4_
  169.5 2.5 %copy-done.2 = bf16[4,2048,324]{1,2,0:T(8,128)(2,1)S(1)} copy-done((bf16[4,2048,324]{1,2,0:T(8,128)(2,1)S(1)}, bf16[4,2048,324]{1,2,0:T(8,128)(2,1)}, u32[]{:S(2)}) %copy-start.2) | copy-done | bytes 5308440
  172.0 3.1 %shard_map.29 = (f32[2,4,72,324]{3,2,1,0:T(8,128)S(1)}, f32[8,128]{1,0:T(8,128)S(1)}) custom-call(s32[1]{0:T(128)} %bitcast.refs_0_, bf16[4,324,2048]{2,1,0:T(8,128)(2,1)S(1)} %bitcast.26, bf16[272,2048]{1,0:T(8,128)(2,1)S(1)} %collective-permute-done.5.refs_2_, f32[8,128]{1,0:T(8,128)S(1)} %get-tuple-element.88.refs_3_, ...), custom_call_target="tpu_custom_call" | custom-call | tf_op jit(solution)/shard_map/pallas_call | solution.py:45
  175.1 0.0 collective-permute-done.9.refs_2_
  175.2 1.8 shard_map.30
  177.0 1.3 collective-permute-start.14
  178.3 3.4 %collective-permute-start.13 = (bf16[1,2,2,72,324]{4,3,2,1,0:T(8,128)(2,1)S(1)}, bf16[1,2,2,72,324]{4,3,2,1,0:T(8,128)(2,1)S(1)}, u32[]{:S(2)}, u32[]{:S(2)}) collective-permute-start(bf16[1,2,2,72,324]{4,3,2,1,0:T(8,128)(2,1)S(1)} %get-tuple-element.104), channel_id=1, source_target_pairs={{2,3},{3,2},{6,7},{7,6},{10,11},{11,10},{14,15},{15,14},{16,17},{1... | collective-permute-start | bytes 559880 | tf_op jit(solution)/shard_map/ppermute | solution.py:486
  181.8 6.1 %shard_map.32 = (f32[2,324,8,324]{3,2,1,0:T(8,128)}, f32[8,128]{1,0:T(8,128)S(1)}) custom-call(s32[2]{0:T(128)S(1)} %get-tuple-element.110.refs_0_, f32[8,324,324]{2,1,0:T(8,128)S(1)} %copy-done.6, f32[1744,256]{1,0:T(8,128)} %collective-permute-done.1.refs_4_.refs_2_, f32[4,328,384]{2,1,0:T(8,128)} %get-tuple-element.73.refs_3_, ...), custom_call_target="tpu_custom_call" | custom-call | tf_op jit(solution)/shard_map/pallas_call | solution.py:45
  187.9 0.0 collective-permute-done.10.refs_2_.refs_3_
  187.9 0.0 collective-permute-done.11.refs_4_.refs_5_
  187.9 0.8 shard_map.33
  188.8 0.2 copy-done.8
  189.0 0.2 copy-done.10
  189.2 4.7 %shard_map.34 = (f32[2,324,8,324]{3,2,1,0:T(8,128)}, f32[8,128]{1,0:T(8,128)S(1)}) custom-call(s32[2]{0:T(128)S(1)} %get-tuple-element.109.refs_0_, f32[2,324,8,324]{3,2,1,0:T(8,128)} %get-tuple-element.97.refs_1_, f32[2,2,324,128]{3,2,1,0:T(8,128)S(1)} %copy-done.8, f32[2,2,324,128]{3,2,1,0:T(8,128)S(1)} %copy-done.8, ...), custom_call_target="tpu_custom_call", output_to_operand_aliasing={{0}: (1, {})} | custom-call | flops 10000000000 | bytes 100000000 | tf_op jit(solution)/shard_map/pallas_call | solution.py:45
  193.9 0.0 collective-permute-done.13.refs_4_
  193.9 3.9 %shard_map.35 = (f32[2,324,8,324]{3,2,1,0:T(8,128)}, f32[8,128]{1,0:T(8,128)S(1)}) custom-call(s32[2]{0:T(128)S(1)} %get-tuple-element.109.refs_0_, f32[2,324,8,324]{3,2,1,0:T(8,128)} %get-tuple-element.102.refs_1_, f32[2,2,68,324]{3,2,1,0:T(8,128)S(1)} %get-tuple-element.103.refs_2_.refs_3_, ...), custom_call_target="tpu_custom_call", output_to_operand_aliasing={{0}: (1, {})} | custom-call | flops 10000000000 | bytes 100000000 | tf_op jit(solution)/shard_map/pallas_call | solution.py:45
  197.8 1.2 shard_map.36
  (23 shorter events, 0.1 us)
Async XLA Ops:
  0.0 11.9 %collective-permute-start = (bf16[4,2048,324]{1,0,2:T(4,128)(2,1)}, bf16[4,2048,324]{1,0,2:T(4,128)(2,1)}, u32[]{:S(2)}, u32[]{:S(2)}) collective-permute-start(bf16[4,2048,324]{1,0,2:T(4,128)(2,1)} %param.1), channel_id=1, source_target_pairs={{0,2},{2,0},{4,6},{6,4},{8,10},{10,8},{12,14},{14,12},{16,18},{18,... | collective-permute-start | bytes 15925256 | tf_op jit(solution)/shard_map/ppermute | solution.py:439
  5.1 85.9 %collective-permute-start.3 = (bf16[512,2048]{1,0:T(8,128)(2,1)}, bf16[512,2048]{1,0:T(8,128)(2,1)}, u32[]{:S(2)}, u32[]{:S(2)}) collective-permute-start(bf16[512,2048]{1,0:T(8,128)(2,1)} %bitcast.4.refs_3_), channel_id=1, source_target_pairs={{0,16},{1,17},{4,20},{5,21},{8,24},{9,25},{12,28},{13,29},{18,2},{... | collective-permute-start | bytes 6291464 | tf_op jit(solution)/shard_map/ppermute | solution.py:442
  11.9 24.4 %copy-start = (bf16[4,2048,324]{1,2,0:T(8,128)(2,1)}, bf16[4,2048,324]{1,2,0:T(8,128)(2,1)S(1)}, u32[]{:S(2)}) copy-start(bf16[4,2048,324]{1,2,0:T(8,128)(2,1)S(1)} %copy.18) | copy-start | bytes 15925252
  19.2 5.1 %copy-start.3 = (bf16[4,2048,324]{1,2,0:T(8,128)(2,1)}, bf16[4,2048,324]{1,2,0:T(8,128)(2,1)S(1)}, u32[]{:S(2)}) copy-start(bf16[4,2048,324]{1,2,0:T(8,128)(2,1)S(1)} %copy.17) | copy-start | bytes 15925252
  31.0 89.6 %collective-permute-start.7 = (bf16[512,2048]{1,0:T(8,128)(2,1)}, bf16[512,2048]{1,0:T(8,128)(2,1)S(1)}, u32[]{:S(2)}, u32[]{:S(2)}) collective-permute-start(bf16[512,2048]{1,0:T(8,128)(2,1)} %bitcast.7), channel_id=1, source_target_pairs={{0,16},{1,17},{4,20},{5,21},{8,24},{9,25},{12,28},{13,29},{18,2},{... | collective-permute-start | bytes 6291464 | tf_op jit(solution)/shard_map/ppermute | solution.py:455
  32.3 71.1 %collective-permute-start.2 = (f32[1744,256]{1,0:T(8,128)}, f32[1744,256]{1,0:T(8,128)}, u32[]{:S(2)}, u32[]{:S(2)}) collective-permute-start(f32[1744,256]{1,0:T(8,128)} %get-tuple-element.69), channel_id=1, source_target_pairs={{0,1},{1,0},{4,5},{5,4},{8,9},{9,8},{12,13},{13,12},{16,17},{17,16... | collective-permute-start | bytes 5357576 | tf_op jit(solution)/shard_map/ppermute | solution.py:450
  35.7 67.7 %collective-permute-start.1 = (f32[1744,256]{1,0:T(8,128)}, f32[1744,256]{1,0:T(8,128)}, u32[]{:S(2)}, u32[]{:S(2)}) collective-permute-start(f32[1744,256]{1,0:T(8,128)} %get-tuple-element.68), channel_id=1, source_target_pairs={{0,1},{1,0},{2,3},{3,2},{4,5},{5,4},{6,7},{7,6},{8,9},{9,8},{10,11... | collective-permute-start | bytes 5357576 | tf_op jit(solution)/shard_map/ppermute | solution.py:448
  39.6 2.5 %copy-start.1 = (bf16[4,2048,324]{1,2,0:T(8,128)(2,1)S(1)}, bf16[4,2048,324]{1,2,0:T(8,128)(2,1)}, u32[]{:S(2)}) copy-start(bf16[4,2048,324]{1,2,0:T(8,128)(2,1)} %copy-done) | copy-start | bytes 15925252
  42.1 2.5 %copy-start.4 = (bf16[4,2048,324]{1,2,0:T(8,128)(2,1)S(1)}, bf16[4,2048,324]{1,2,0:T(8,128)(2,1)}, u32[]{:S(2)}) copy-start(bf16[4,2048,324]{1,2,0:T(8,128)(2,1)} %copy-done.3) | copy-start | bytes 15925252
  51.9 51.5 %copy-start.5 = (f32[8,324,324]{2,1,0:T(8,128)}, f32[8,324,324]{2,1,0:T(8,128)S(1)}, u32[]{:S(2)}) copy-start(f32[8,324,324]{2,1,0:T(8,128)S(1)} %get-tuple-element.67.refs_1_) | copy-start | bytes 10077700
  91.0 7.2 %copy-start.11 = (bf16[272,2048]{1,0:T(8,128)(2,1)S(1)}, bf16[272,2048]{1,0:T(8,128)(2,1)}, u32[]{:S(2)}) copy-start(bf16[272,2048]{1,0:T(8,128)(2,1)} %reshape.10) | copy-start | bytes 3342340
  94.7 64.0 %collective-permute-start.6 = (f32[2,4,328,128]{3,2,1,0:T(8,128)S(1)}, f32[2,4,328,128]{3,2,1,0:T(8,128)S(1)}, u32[]{:S(2)}, u32[]{:S(2)}) collective-permute-start(f32[2,4,328,128]{3,2,1,0:T(8,128)S(1)} %get-tuple-element.76), channel_id=1, source_target_pairs={{2,3},{3,2},{6,7},{7,6},{10,11},{11,10},{14,15},{15,14},{16,17},{1... | collective-permute-start | bytes 4030472 | tf_op jit(solution)/shard_map/ppermute | solution.py:474
  98.3 53.2 %collective-permute-start.5 = (bf16[272,2048]{1,0:T(8,128)(2,1)S(1)}, bf16[272,2048]{1,0:T(8,128)(2,1)S(1)}, u32[]{:S(2)}, u32[]{:S(2)}) collective-permute-start(bf16[272,2048]{1,0:T(8,128)(2,1)S(1)} %copy-done.11), channel_id=1, source_target_pairs={{0,16},{1,17},{4,20},{5,21},{8,24},{9,25},{12,28},{13,29},{18,2},{... | collective-permute-start | bytes 3342344 | tf_op jit(solution)/shard_map/ppermute | solution.py:457
  99.6 21.0 %slice-start = ((s8[5373952]{0:T(1024)(128)(4,1)}), s8[4194304]{0:T(1024)(128)(4,1)S(1)}, s32[]{:S(2)}) async-start(s8[5373952]{0:T(1024)(128)(4,1)} %bitcast.21), calls=%async_computation | async-start | bytes 8388608
  103.3 17.3 %slice-start.1 = ((s8[5373952]{0:T(1024)(128)(4,1)}), s8[1179648]{0:T(1024)(128)(4,1)S(1)}, s32[]{:S(2)}) async-start(s8[5373952]{0:T(1024)(128)(4,1)} %bitcast.21), calls=%async_computation.1 | async-start | bytes 2359296
  122.9 38.9 %collective-permute-start.8 = (f32[2,4,328,128]{3,2,1,0:T(8,128)S(1)}, f32[2,4,328,128]{3,2,1,0:T(8,128)S(1)}, u32[]{:S(2)}, u32[]{:S(2)}) collective-permute-start(f32[2,4,328,128]{3,2,1,0:T(8,128)S(1)} %get-tuple-element.84), channel_id=1, source_target_pairs={{2,3},{3,2},{6,7},{7,6},{10,11},{11,10},{14,15},{15,14},{16,17},{1... | collective-permute-start | bytes 4030472 | tf_op jit(solution)/shard_map/ppermute | solution.py:474
  126.3 43.1 %collective-permute-start.4 = (f32[4,328,384]{2,1,0:T(8,128)}, f32[4,328,384]{2,1,0:T(8,128)}, u32[]{:S(2)}, u32[]{:S(2)}) collective-permute-start(f32[4,328,384]{2,1,0:T(8,128)} %get-tuple-element.73.refs_3_), channel_id=1, source_target_pairs={{0,2},{1,3},{4,6},{5,7},{8,10},{9,11},{12,14},{13,15},{16,18},{17,... | collective-permute-start | bytes 6045704 | tf_op jit(solution)/shard_map/ppermute | solution.py:496
  155.2 19.9 %collective-permute-start.9 = (f32[2,4,72,324]{3,2,1,0:T(8,128)}, f32[2,4,72,324]{3,2,1,0:T(8,128)}, u32[]{:S(2)}, u32[]{:S(2)}) collective-permute-start(f32[2,4,72,324]{3,2,1,0:T(8,128)} %get-tuple-element.90), channel_id=1, source_target_pairs={{2,3},{3,2},{6,7},{7,6},{10,11},{11,10},{14,15},{15,14},{16,17},{1... | collective-permute-start | bytes 2239496 | tf_op jit(solution)/shard_map/ppermute | solution.py:474
  159.7 0.8 copy-start.7
  160.5 27.3 %collective-permute-start.10 = (bf16[2,4,328,128]{3,2,1,0:T(8,128)(2,1)S(1)}, bf16[2,4,328,128]{3,2,1,0:T(8,128)(2,1)S(1)}, u32[]{:S(2)}, u32[]{:S(2)}) collective-permute-start(bf16[2,4,328,128]{3,2,1,0:T(8,128)(2,1)S(1)} %get-tuple-element.82.refs_1_), channel_id=1, source_target_pairs={{16,0},{17,1},{20,4},{21,5},{24,8},{25,9},{28,12},{29,13},{2,18},{... | collective-permute-start | bytes 2015240 | tf_op jit(solution)/shard_map/ppermute | solution.py:481
  163.7 3.2 %copy-start.9 = (f32[2,2,324,128]{3,2,1,0:T(8,128)}, f32[2,2,324,128]{3,2,1,0:T(8,128)S(1)}, u32[]{:S(2)}) copy-start(f32[2,2,324,128]{3,2,1,0:T(8,128)S(1)} %get-tuple-element.100.refs_5_.refs_6_) | copy-start | bytes 1990660
  163.7 24.2 %collective-permute-start.11 = (bf16[2,4,328,128]{3,2,1,0:T(8,128)(2,1)}, bf16[2,4,328,128]{3,2,1,0:T(8,128)(2,1)S(1)}, u32[]{:S(2)}, u32[]{:S(2)}) collective-permute-start(bf16[2,4,328,128]{3,2,1,0:T(8,128)(2,1)} %get-tuple-element.86.refs_2_), channel_id=1, source_target_pairs={{16,0},{17,1},{20,4},{21,5},{24,8},{25,9},{28,12},{29,13},{2,18},{... | collective-permute-start | bytes 2015240 | tf_op jit(solution)/shard_map/ppermute | solution.py:481
  167.0 21.8 %collective-permute-start.12 = (bf16[2,2,2,328,128]{4,3,2,1,0:T(8,128)(2,1)}, bf16[2,2,2,328,128]{4,3,2,1,0:T(8,128)(2,1)}, u32[]{:S(2)}, u32[]{:S(2)}) collective-permute-start(bf16[2,2,2,328,128]{4,3,2,1,0:T(8,128)(2,1)} %get-tuple-element.99), channel_id=1, source_target_pairs={{2,3},{3,2},{6,7},{7,6},{10,11},{11,10},{14,15},{15,14},{16,17},{1... | collective-permute-start | bytes 2015240 | tf_op jit(solution)/shard_map/ppermute | solution.py:486
  169.5 2.5 %copy-start.2 = (bf16[4,2048,324]{1,2,0:T(8,128)(2,1)S(1)}, bf16[4,2048,324]{1,2,0:T(8,128)(2,1)}, u32[]{:S(2)}) copy-start(bf16[4,2048,324]{1,2,0:T(8,128)(2,1)} %copy-done) | copy-start | bytes 15925252
  172.0 9.8 %copy-start.6 = (f32[8,324,324]{2,1,0:T(8,128)S(1)}, f32[8,324,324]{2,1,0:T(8,128)}, u32[]{:S(2)}) copy-start(f32[8,324,324]{2,1,0:T(8,128)} %copy-done.5) | copy-start | bytes 10077700
  177.0 20.8 %collective-permute-start.14 = (bf16[2,4,72,324]{3,2,1,0:T(8,128)(2,1)S(1)}, bf16[2,4,72,324]{3,2,1,0:T(8,128)(2,1)S(1)}, u32[]{:S(2)}, u32[]{:S(2)}) collective-permute-start(bf16[2,4,72,324]{3,2,1,0:T(8,128)(2,1)S(1)} %get-tuple-element.92.refs_1_), channel_id=1, source_target_pairs={{16,0},{17,1},{20,4},{21,5},{24,8},{25,9},{28,12},{29,13},{2,18},{... | collective-permute-start | bytes 1119752 | tf_op jit(solution)/shard_map/ppermute | solution.py:481
  178.3 15.6 %collective-permute-start.13 = (bf16[1,2,2,72,324]{4,3,2,1,0:T(8,128)(2,1)S(1)}, bf16[1,2,2,72,324]{4,3,2,1,0:T(8,128)(2,1)S(1)}, u32[]{:S(2)}, u32[]{:S(2)}) collective-permute-start(bf16[1,2,2,72,324]{4,3,2,1,0:T(8,128)(2,1)S(1)} %get-tuple-element.104), channel_id=1, source_target_pairs={{2,3},{3,2},{6,7},{7,6},{10,11},{11,10},{14,15},{15,14},{16,17},{1... | collective-permute-start | bytes 559880 | tf_op jit(solution)/shard_map/ppermute | solution.py:486
  187.9 1.1 copy-start.8
  187.9 1.3 copy-start.10

commit v12 on v11

--- a/solution.py
+++ b/solution.py
@@ -231,7 +231,7 @@
     )(place_in, keep, crossed, share, given)
 
 
-def far_terms(det, own, got, start, width, turned, mine, after=()):
+def far_terms(det, own, got, start, width, turned, mine, after=(), declared=0):
     states, ops, depth = own.shape
     half = states // 2
     rows = ops if turned else width
@@ -269,6 +269,7 @@
         [pl.BlockSpec((half, 1, *tile), lambda v, x: (0, v, 0, 0))],
         [f32(half, states, *tile)],
         after,
+        declared=declared,
     )(det, own, got)
 
 
@@ -332,17 +333,18 @@
     return value * jnp.abs(value) * (fourth * fourth)
 
 
+def rooted(code, exponent):
+    code, exponent = code.astype(jnp.float32), exponent.astype(jnp.float32)
+    root = jnp.exp2(jnp.log2(jnp.abs(code)) * (1 / POWER)) * jnp.exp2(exponent - LIFT)
+    return jnp.where(code < 0, -root, root)
+
+
 def decoded(code, rows):
-    code = code.astype(jnp.float32)
-    value, exponent = code[:rows], code[rows : rows + 1]
-    root = jnp.exp2(jnp.log2(jnp.abs(value)) * (1 / POWER)) * jnp.exp2(exponent - LIFT)
-    return jnp.where(value < 0, -root, root)
-
-
-def into_place(role, place_in, out, pieces, after=(), declared=0):
-    tiles = out.shape[2]
-    sources = [v for piece in pieces for v, _ in piece[2]]
-    picks = [pick for piece in pieces for _, pick in piece[2]]
+    return rooted(code[:rows], code[rows : rows + 1])
+
+
+def into_place(role, place_in, out, sources, pieces, after=(), declared=0):
+    _, ops, tiles, _ = out.shape
     count = len(sources)
 
     def body(s_ref, out_in, *refs):
@@ -350,16 +352,15 @@
 
         @pl.when(s_ref[1] == role)
         def _():
-            loads = [pltpu.make_async_copy(refs[k].at[picks[k]], held[k], sems.at[k]) for k in range(count)]
+            loads = [pltpu.make_async_copy(refs[k], held[k], sems.at[k]) for k in range(count)]
             for load in loads:
                 load.start()
-            stores, first = [], 0
-            for k, (rows, lanes, own, fill) in enumerate(pieces):
-                for load in loads[first : first + len(own)]:
-                    load.wait()
-                fill(s_ref[0], held[first : first + len(own)], made[k])
-                first += len(own)
-                target = out_ref.at[0, pl.ds(*rows), :, pl.ds(*lanes)]
+            for load in loads:
+                load.wait()
+            stores = []
+            for k, (start, rows, fill) in enumerate(pieces):
+                fill(s_ref[0], held, made[k])
+                target = out_ref.at[0, pl.ds(start, rows)]
                 stores.append(pltpu.make_async_copy(made[k], target, sems.at[count + k]))
                 stores[k].start()
             for store in stores:
@@ -374,45 +375,58 @@
         [f32(*out.shape)],
         after,
         {1: 0},
-        [pltpu.VMEM(v.shape[1:], v.dtype) for v in sources]
-        + [pltpu.VMEM((rows[1], tiles, lanes[1]), jnp.float32) for rows, lanes, *_ in pieces]
+        [pltpu.VMEM(v.shape, v.dtype) for v in sources]
+        + [pltpu.VMEM((rows, tiles, ops), jnp.float32) for _, rows, _ in pieces]
         + [pltpu.SemaphoreType.DMA((count + len(pieces),))],
         declared,
     )(place_in, out, *sources)
 
 
-def returned_piece(code, start, width, ops):
-    half, states, _, _ = code.shape
-    turned = code.shape[3] == width
-
-    def fill(x, refs, ref):
-        for a in range(half):
-            for v in range(states):
-                one = refs[a][v]
-                ref[:, a * states + v] = decoded(one, ops).T if turned else decoded(one, width)
-
-    return (start, width), (0, ops), [(code, a) for a in range(half)], fill
-
-
-def finished_piece(tiles, cross, chunk, start, width, ops):
-    half, _, rows, _ = tiles.shape
-    turned = rows == ops
-
-    def fill(x, refs, ref):
-        for b in range(half):
-            for u in range(2 * half):
-                a, t = u % half, 2 * half * b + u
-
-                @pl.when(u // half == x)
-                def _():
-                    ref[:, t] = refs[a][b] if turned else refs[a][b].T
-
-                @pl.when(u // half != x)
-                def _():
-                    one = decoded(refs[half][a, b], rows)
-                    ref[:, t] = one if turned else one.T
-
-    return (0, ops), (start, width), [(tiles, a) for a in range(half)] + [(cross, chunk)], fill
+def returned(codes, chunks, widths, ops):
+    def piece(n, k):
+        half, states, _, _ = codes[n].shape
+
+        def fill(x, refs, ref):
+            for a in range(half):
+                for v in range(states):
+                    one = refs[n][a, v]
+                    last = widths[k] < LANES
+                    ref[:, a * states + v] = decoded(one, widths[k]) if last else decoded(one, ops).T
+
+        return k * LANES, widths[k], fill
+
+    return codes, [piece(n, k) for n, k in enumerate(chunks)]
+
+
+def completed(tiles, turned, last, widths, ops):
+    full = len(widths) - 1
+    half, _, rest, _ = tiles[full].shape
+
+    def piece(start, rows):
+        def fill(x, refs, ref):
+            for b in range(half):
+                for u in range(2 * half):
+                    a, t = u % half, 2 * half * b + u
+
+                    @pl.when(u // half == x)
+                    def _():
+                        for k in range(full):
+                            ref[:, t, k * LANES : (k + 1) * LANES] = refs[k][a, b, start : start + rows]
+                        block = refs[full][a, b, :, start : start + rows]
+                        ref[:, t, full * LANES :] = block.T
+
+                    @pl.when(u // half != x)
+                    def _():
+                        for k in range(full):
+                            code = refs[full + 1][k, a, b]
+                            value = rooted(code[start : start + rows], code[ops : ops + 1])
+                            ref[:, t, k * LANES : (k + 1) * LANES] = value
+                        code = refs[full + 2][0, a, b, :, start : start + rows]
+                        ref[:, t, full * LANES :] = decoded(code, rest).T
+
+        return start, rows, fill
+
+    return [*tiles, turned, last], [piece(p, min(LANES, ops - p)) for p in range(0, ops, LANES)]
 
 
 def paired(amplitudes):
@@ -456,20 +470,17 @@
     last, token = lax.optimization_barrier((chunk[full], token))
     got.append(lax.ppermute(last, both, over))
     keep, token = near_keep(det, own, partner, (token,))
-    def terms(k, mine, *done):
+    def terms(k, mine, done, declared=0):
         wire, start = (0, 0) if k == 0 else (2, 0) if k == full else (1, states * LANES * (k - 1))
-        return far_terms(det, own, got[wire], start, widths[k], k < full, mine, done)
-
-    kepts, came, tiles, codes, mine, theirs = {}, {}, {}, {}, {}, {}
-
-    def place_of(k):
-        return k * LANES, widths[k], ops
+        return far_terms(det, own, got[wire], start, widths[k], k < full, mine, done, declared)
+
+    kepts, came, tiles, codes, theirs = {}, {}, {}, {}, {}
 
     def keep_terms(k, *token):
-        kepts[k], token = terms(k, True, *token)
+        kepts[k], token = terms(k, True, token)
         return token
 
-    def send_terms(k, token):
+    def send_terms(k, *token):
         send, token = terms(k, False, token)
         came[k] = lax.ppermute(send, both, across)
         return token
@@ -478,36 +489,36 @@
         rows = ops if k < full else widths[k]
         declared = LONG if k in early else 0
         tiles[k], codes[k], token = far_sum(det, kepts[k], came[k], rows, k < full, token, declared)
-        theirs[k] = returned_piece(lax.ppermute(codes[k], both, back), *place_of(k))
+        theirs[k] = lax.ppermute(codes[k], both, back)
         return token
 
     def cross(ks, token):
         wire, token = crossing_codes(det, [codes[k] for k in ks], (token,))
-        wire = lax.ppermute(wire, both, across)
-        for n, k in enumerate(ks):
-            mine[k] = finished_piece(tiles[k], wire, n, *place_of(k))
-        return token
+        return lax.ppermute(wire, both, across), token
 
     early, late = list(range(full)), [full]
     for k in early:
-        token = keep_terms(k, send_terms(k, token))
+        token = send_terms(k, token)
+        if k == full - 1:
+            gate = lax.ppermute(token, "state", [(s, s ^ 1) for s in range(blocks)])
+        token = keep_terms(k, token)
         if k == 0:
             share, token = near_share(det, keep, doubled, states, (token, crossed))
             given = lax.ppermute(share, both, to_second)
-    token = send_terms(full, token)
+    token = send_terms(full, token, gate)
     for k in early:
         token = sum_up(k, token)
-    turned = list(range(full))
-    token = cross(turned, token)
+    turned, token = cross(early, token)
     token = keep_terms(full, token, given)
     token = sum_up(full, token)
-    token = cross([full], token)
+    last, token = cross(late, token)
     out, token = near_sum(jnp.stack([x, core]), keep, crossed, share, given, states, (token,))
 
     at = jnp.stack([x, receiver])
-    for role, kind, ks in ((0, theirs, early), (1, mine, early), (1, mine, late), (0, theirs, late)):
-        declared = LONG if role == 1 else 0
-        out, token = into_place(role, at, out, [kind[k] for k in ks], (token,), declared)
+    out, token = into_place(0, at, out, *returned([theirs[k] for k in early], early, widths, ops), (token,), LONG)
+    placed = completed([tiles[k] for k in early + late], turned, last, widths, ops)
+    out, token = into_place(1, at, out, *placed, (token,), LONG)
+    out, token = into_place(0, at, out, *returned([theirs[full]], late, widths, ops), (token,))
     return out.transpose(0, 2, 1, 3)
 
 

time: 200 us -> 181 us (0.905)
  the two profiles are of different devices: /device:TPU:28 before, /device:TPU:0 now
where the time goes in v12:
time: 181 us; the launch traced here: 180 us
  Pallas kernels  59.4 us (33%)
  waiting for transfers between devices  44.8 us (25%)
  starting transfers between devices  43.5 us (24%)
  local copies, waits for them, and re-layouts  32.1 us (18%)
    pallas_call x19, Pallas kernels, call(): return lambda *operands: kernel(*operands, *after)  59.4 us
    ppermute x1, waiting for transfers between devices, paired(): crossed = lax.ppermute(crossed, 'det', [(0, 1), (1, 0)])  19.1 us
    ppermute x3, waiting for transfers between devices, sum_up(): theirs[k] = lax.ppermute(codes[k], both, back)  18.4 us
    ppermute x1, starting transfers between devices, paired(): gate = lax.ppermute(token, 'state', [(s, s ^ 1) for s in range(blocks)])  17.3 us
    unnamed x28, local copies, waits for them, and re-layouts  9.33 us
    optimization_barrier x1, local copies, waits for them, and re-layouts, paired(): partner, own = lax.optimization_barrier((partner, own))  7.35 us
    ppermute x1, waiting for transfers between devices, paired(): doubled = lax.ppermute(doubled, both, first_across)  7.19 us
    ppermute x1, starting transfers between devices, paired(): got = [lax.ppermute(first, both, over)]  6.83 us
  transfers between devices with their start and end apart: 16, of which 3 were waited for; matrix products, arithmetic and copies ran while one was open for 13% of the time, Pallas kernels for 31%

profile of v12, /device:TPU:0, one launch (start us, length us, event | category | flops | bytes accessed | tf_op | source)
XLA Modules:
  0.0 180.4 jit_solution(12091645101392466072)
XLA Ops:
  0.0 0.5 collective-permute-start
  0.5 2.6 %slice_bitcast_fusion = bf16[4,128,2048]{2,0,1:T(4,128)(2,1)S(1)} fusion(bf16[4,2048,324]{1,0,2:T(4,128)(2,1)} %param.1), kind=kLoop, calls=%fused_computation.2 | loop fusion | bytes 4194304 | tf_op jit(solution)/shard_map/transpose | solution.py:454
  3.1 2.5 %copy.11 = bf16[4,128,2048]{2,1,0:T(8,128)(2,1)} copy(bf16[4,128,2048]{2,0,1:T(4,128)(2,1)S(1)} %slice_bitcast_fusion) | data formatting | bytes 4194304 | tf_op jit(solution)/shard_map/transpose | solution.py:454
  5.6 6.8 %collective-permute-start.3 = (bf16[512,2048]{1,0:T(8,128)(2,1)}, bf16[512,2048]{1,0:T(8,128)(2,1)}, u32[]{:S(2)}, u32[]{:S(2)}) collective-permute-start(bf16[512,2048]{1,0:T(8,128)(2,1)} %bitcast.4.refs_3_), channel_id=1, source_target_pairs={{0,16},{1,17},{4,20},{5,21},{8,24},{9,25},{12,28},{13,29},{18,2},{... | collective-permute-start | bytes 6291464 | tf_op jit(solution)/shard_map/ppermute | solution.py:456
  12.4 5.4 %copy.17 = bf16[4,2048,324]{1,2,0:T(8,128)(2,1)S(1)} copy(bf16[4,2048,324]{1,0,2:T(4,128)(2,1)} %param.1) | data formatting | bytes 10616832 | tf_op jit(solution)/shard_map/optimization_barrier | solution.py:455
  17.8 0.0 copy-start
  17.9 0.0 collective-permute-done
  17.9 7.4 %copy.16 = bf16[4,2048,324]{1,2,0:T(8,128)(2,1)S(1)} copy(bf16[4,2048,324]{1,0,2:T(4,128)(2,1)} %collective-permute-done) | data formatting | bytes 10616832 | tf_op jit(solution)/shard_map/optimization_barrier | solution.py:458
  25.2 5.1 %shard_map.17 = (f32[1744,256]{1,0:T(8,128)}, f32[8,128]{1,0:T(8,128)S(1)}) custom-call(s32[1]{0:T(128)} %bitcast.refs_0_, bf16[4,324,2048]{2,1,0:T(8,128)(2,1)S(1)} %bitcast.14, bf16[4,324,2048]{2,1,0:T(8,128)(2,1)S(1)} %bitcast.27, bf16[512,2048]{1,0:T(8,128)(2,1)} %bitcast.4.refs_3_), custom_call_target="tpu_custom_call" | custom-call | tf_op jit(solution)/shard_map/pallas_call | solution.py:45
  30.3 5.1 %shard_map.18 = (f32[1744,256]{1,0:T(8,128)}, f32[8,128]{1,0:T(8,128)S(1)}) custom-call(s32[1]{0:T(128)} %bitcast.refs_0_, bf16[4,324,2048]{2,1,0:T(8,128)(2,1)S(1)} %bitcast.15, bf16[4,324,2048]{2,1,0:T(8,128)(2,1)S(1)} %bitcast.28, f32[8,128]{1,0:T(8,128)S(1)} %get-tuple-element.59.refs_3_), custom_call_target="tpu_custom_call" | custom-call | tf_op jit(solution)/shard_map/pallas_call | solution.py:45
  35.4 1.5 slice.11
  37.0 1.4 collective-permute-start.7
  38.4 3.4 %collective-permute-start.2 = (f32[1744,256]{1,0:T(8,128)}, f32[1744,256]{1,0:T(8,128)}, u32[]{:S(2)}, u32[]{:S(2)}) collective-permute-start(f32[1744,256]{1,0:T(8,128)} %get-tuple-element.67), channel_id=1, source_target_pairs={{0,1},{1,0},{4,5},{5,4},{8,9},{9,8},{12,13},{13,12},{16,17},{17,16... | collective-permute-start | bytes 5357576 | tf_op jit(solution)/shard_map/ppermute | solution.py:464
  41.8 0.6 collective-permute-start.1
  42.4 1.1 slice.10
  43.5 2.2 %reshape.10 = bf16[272,2048]{1,0:T(8,128)(2,1)} reshape(bf16[4,68,2048]{2,1,0:T(8,128)(2,1)} %slice.10) | data formatting | bytes 2228224 | tf_op jit(solution)/shard_map/reshape | solution.py:467
  45.7 2.5 %copy-done.1 = bf16[4,2048,324]{1,2,0:T(8,128)(2,1)S(1)} copy-done((bf16[4,2048,324]{1,2,0:T(8,128)(2,1)S(1)}, bf16[4,2048,324]{1,2,0:T(8,128)(2,1)}, u32[]{:S(2)}) %copy-start.1) | copy-done | bytes 5308440
  48.2 2.5 %copy-done.4 = bf16[4,2048,324]{1,2,0:T(8,128)(2,1)S(1)} copy-done((bf16[4,2048,324]{1,2,0:T(8,128)(2,1)S(1)}, bf16[4,2048,324]{1,2,0:T(8,128)(2,1)}, u32[]{:S(2)}) %copy-start.4) | copy-done | bytes 5308440
  50.7 7.2 %shard_map.19 = (f32[8,324,324]{2,1,0:T(8,128)S(1)}, f32[8,128]{1,0:T(8,128)S(1)}) custom-call(s32[1]{0:T(128)} %bitcast.refs_0_, bf16[4,324,2048]{2,1,0:T(8,128)(2,1)S(1)} %bitcast.18, bf16[4,324,2048]{2,1,0:T(8,128)(2,1)S(1)} %bitcast.29, f32[8,128]{1,0:T(8,128)S(1)} %get-tuple-element.64.refs_3_), custom_call_target="tpu_custom_call" | custom-call | tf_op jit(solution)/shard_map/pallas_call | solution.py:45
  58.0 0.0 collective-permute-done.3.refs_2_
  58.0 4.6 %shard_map.20 = (f32[2,4,328,128]{3,2,1,0:T(8,128)S(1)}, f32[8,128]{1,0:T(8,128)S(1)}) custom-call(s32[1]{0:T(128)} %bitcast.refs_0_, bf16[4,324,2048]{2,1,0:T(8,128)(2,1)S(1)} %bitcast.19, bf16[512,2048]{1,0:T(8,128)(2,1)} %collective-permute-done.3.refs_2_, f32[8,128]{1,0:T(8,128)S(1)} %get-tuple-element.68.refs_3_), custom_call_target="tpu_custom_call" | custom-call | tf_op jit(solution)/shard_map/pallas_call | solution.py:45
  62.6 0.9 collective-permute-start.6
  63.5 2.6 %collective-permute-start.5 = (bf16[272,2048]{1,0:T(8,128)(2,1)S(1)}, bf16[272,2048]{1,0:T(8,128)(2,1)S(1)}, u32[]{:S(2)}, u32[]{:S(2)}) collective-permute-start(bf16[272,2048]{1,0:T(8,128)(2,1)S(1)} %copy-done.11), channel_id=1, source_target_pairs={{0,16},{1,17},{4,20},{5,21},{8,24},{9,25},{12,28},{13,29},{18,2},{... | collective-permute-start | bytes 3342344 | tf_op jit(solution)/shard_map/ppermute | solution.py:471
  66.1 0.0 slice-start
  66.1 3.7 %shard_map.21 = (f32[2,4,328,128]{3,2,1,0:T(8,128)S(1)}, f32[8,128]{1,0:T(8,128)S(1)}) custom-call(s32[1]{0:T(128)} %bitcast.refs_0_, bf16[4,324,2048]{2,1,0:T(8,128)(2,1)S(1)} %bitcast.20, bf16[512,2048]{1,0:T(8,128)(2,1)} %collective-permute-done.3.refs_2_, f32[8,128]{1,0:T(8,128)S(1)} %get-tuple-element.69.refs_3_), custom_call_target="tpu_custom_call" | custom-call | tf_op jit(solution)/shard_map/pallas_call | solution.py:45
  69.8 7.2 %collective-permute-done.2.refs_2_ = f32[1744,256]{1,0:T(8,128)} collective-permute-done((f32[1744,256]{1,0:T(8,128)}, f32[1744,256]{1,0:T(8,128)}, u32[]{:S(2)}, u32[]{:S(2)}) %collective-permute-start.2) | collective-permute-done | bytes 1785888 | tf_op jit(solution)/shard_map/ppermute | solution.py:464
  77.0 19.1 %collective-permute-done.1.refs_4_.refs_2_ = f32[1744,256]{1,0:T(8,128)} collective-permute-done((f32[1744,256]{1,0:T(8,128)}, f32[1744,256]{1,0:T(8,128)}, u32[]{:S(2)}, u32[]{:S(2)}) %collective-permute-start.1) | collective-permute-done | bytes 1785888 | tf_op jit(solution)/shard_map/ppermute | solution.py:462
  96.1 3.3 %shard_map.22 = (f32[4,328,384]{2,1,0:T(8,128)}, f32[8,128]{1,0:T(8,128)S(1)}) custom-call(s32[1]{0:T(128)} %bitcast.refs_0_, f32[8,324,324]{2,1,0:T(8,128)S(1)} %get-tuple-element.65.refs_1_, f32[1744,256]{1,0:T(8,128)} %collective-permute-done.2.refs_2_, f32[8,128]{1,0:T(8,128)S(1)} %get-tuple-element.70.refs_3_, ...), custom_call_target="tpu_custom_call" | custom-call | tf_op jit(solution)/shard_map/pallas_call | solution.py:45
  99.4 0.0 collective-permute-done.7.refs_2_
  99.4 2.4 %shard_map.23 = (f32[2,4,328,128]{3,2,1,0:T(8,128)S(1)}, f32[8,128]{1,0:T(8,128)S(1)}) custom-call(s32[1]{0:T(128)} %bitcast.refs_0_, bf16[4,324,2048]{2,1,0:T(8,128)(2,1)S(1)} %bitcast.23, bf16[512,2048]{1,0:T(8,128)(2,1)S(1)} %collective-permute-done.7.refs_2_, f32[8,128]{1,0:T(8,128)S(1)} %get-tuple-element.76.refs_3_), custom_call_target="tpu_custom_call" | custom-call | tf_op jit(solution)/shard_map/pallas_call | solution.py:45
  101.8 0.7 collective-permute-start.9
  102.5 17.3 %collective-permute-start.8 = (f32[8,128]{1,0:T(8,128)S(1)}, f32[8,128]{1,0:T(8,128)S(1)}, u32[]{:S(2)}, u32[]{:S(2)}) collective-permute-start(f32[8,128]{1,0:T(8,128)S(1)} %get-tuple-element.77.refs_3_), channel_id=1, source_target_pairs={{0,2},{2,0},{4,6},{6,4},{8,10},{10,8},{12,14},{14,12},{16,18},{18,... | collective-permute-start | bytes 12296 | tf_op jit(solution)/shard_map/ppermute | solution.py:503
  119.9 3.3 %collective-permute-start.4 = (f32[4,328,384]{2,1,0:T(8,128)}, f32[4,328,384]{2,1,0:T(8,128)}, u32[]{:S(2)}, u32[]{:S(2)}) collective-permute-start(f32[4,328,384]{2,1,0:T(8,128)} %get-tuple-element.71.refs_3_), channel_id=1, source_target_pairs={{0,2},{1,3},{4,6},{5,7},{8,10},{9,11},{12,14},{13,15},{16,18},{17,... | collective-permute-start | bytes 6045704 | tf_op jit(solution)/shard_map/ppermute | solution.py:507
  123.1 2.3 %shard_map.24 = (f32[2,4,328,128]{3,2,1,0:T(8,128)S(1)}, f32[8,128]{1,0:T(8,128)S(1)}) custom-call(s32[1]{0:T(128)} %bitcast.refs_0_, bf16[4,324,2048]{2,1,0:T(8,128)(2,1)S(1)} %bitcast.24, bf16[512,2048]{1,0:T(8,128)(2,1)S(1)} %collective-permute-done.7.refs_2_, f32[8,128]{1,0:T(8,128)S(1)} %get-tuple-element.77.refs_3_), custom_call_target="tpu_custom_call" | custom-call | tf_op jit(solution)/shard_map/pallas_call | solution.py:45
  125.5 0.0 collective-permute-done.5.refs_2_
  125.5 0.0 collective-permute-done.8.refs_4_
  125.5 3.8 %shard_map.25 = (f32[2,4,72,324]{3,2,1,0:T(8,128)}, f32[8,128]{1,0:T(8,128)S(1)}) custom-call(s32[1]{0:T(128)} %bitcast.refs_0_, bf16[4,324,2048]{2,1,0:T(8,128)(2,1)S(1)} %bitcast.25, bf16[272,2048]{1,0:T(8,128)(2,1)S(1)} %collective-permute-done.5.refs_2_, f32[8,128]{1,0:T(8,128)S(1)} %get-tuple-element.78.refs_3_, f32[8,128]{1,0:T(8,128)S(1)} %collective-permute-done.8.refs_4_), custom_call_target="tpu_custom_call" | custom-call | tf_op jit(solution)/shard_map/pallas_call | solution.py:45
  129.3 0.7 collective-permute-start.10
  130.0 1.0 shard_map.26
  131.1 0.8 copy-done.7
  131.9 1.3 collective-permute-start.11
  133.2 0.0 collective-permute-done.9.refs_2_
  133.2 1.8 %shard_map.27 = (f32[2,2,324,128]{3,2,1,0:T(8,128)S(1)}, bf16[2,4,328,128]{3,2,1,0:T(8,128)(2,1)}, f32[8,128]{1,0:T(8,128)S(1)}) custom-call(s32[1]{0:T(128)} %bitcast.refs_0_, f32[2,4,328,128]{3,2,1,0:T(8,128)S(1)} %get-tuple-element.81.refs_1_, f32[2,4,328,128]{3,2,1,0:T(8,128)S(1)} %collective-permute-done.9.refs_2_, f32[8,128]{1,0:T(8,128)S(1)} %get-tuple-element.83.refs_3_), custom_call_target="tpu_custom_call" | custom-call | flops 10000000000 | bytes 100000000 | tf_op jit(solution)/shard_map/pallas_call | solution.py:45
  135.1 0.9 copy-done.9
  135.9 1.3 collective-permute-start.12
  137.2 0.1 pad_add_fusion
  137.3 1.0 shard_map.28
  138.4 0.7 collective-permute-start.13
  139.1 0.0 collective-permute-done.4.refs_4_
  139.1 0.0 copy-start.2
  139.1 2.5 %copy-done.2 = bf16[4,2048,324]{1,2,0:T(8,128)(2,1)S(1)} copy-done((bf16[4,2048,324]{1,2,0:T(8,128)(2,1)S(1)}, bf16[4,2048,324]{1,2,0:T(8,128)(2,1)}, u32[]{:S(2)}) %copy-start.2) | copy-done | bytes 5308440
  141.6 3.1 %shard_map.29 = (f32[2,4,72,324]{3,2,1,0:T(8,128)S(1)}, f32[8,128]{1,0:T(8,128)S(1)}) custom-call(s32[1]{0:T(128)} %bitcast.refs_0_, bf16[4,324,2048]{2,1,0:T(8,128)(2,1)S(1)} %bitcast.26, bf16[272,2048]{1,0:T(8,128)(2,1)S(1)} %collective-permute-done.5.refs_2_, f32[8,128]{1,0:T(8,128)S(1)} %get-tuple-element.86.refs_3_, ...), custom_call_target="tpu_custom_call" | custom-call | tf_op jit(solution)/shard_map/pallas_call | solution.py:45
  144.8 0.6 shard_map.30
  145.3 1.3 collective-permute-start.15
  146.7 0.7 collective-permute-start.14
  147.4 6.1 %shard_map.32 = (f32[2,324,8,324]{3,2,1,0:T(8,128)}, f32[8,128]{1,0:T(8,128)S(1)}) custom-call(s32[2]{0:T(128)S(1)} %get-tuple-element.106.refs_0_, f32[8,324,324]{2,1,0:T(8,128)S(1)} %copy-done.6, f32[1744,256]{1,0:T(8,128)} %collective-permute-done.1.refs_4_.refs_2_, f32[4,328,384]{2,1,0:T(8,128)} %get-tuple-element.71.refs_3_, ...), custom_call_target="tpu_custom_call" | custom-call | tf_op jit(solution)/shard_map/pallas_call | solution.py:45
  153.5 0.0 collective-permute-done.11.refs_2_
  153.5 18.4 %collective-permute-done.12.refs_3_ = bf16[2,4,328,128]{3,2,1,0:T(8,128)(2,1)} collective-permute-done((bf16[2,4,328,128]{3,2,1,0:T(8,128)(2,1)}, bf16[2,4,328,128]{3,2,1,0:T(8,128)(2,1)}, u32[]{:S(2)}, u32[]{:S(2)}) %collective-permute-start.12) | collective-permute-done | bytes 671776 | tf_op jit(solution)/shard_map/ppermute | solution.py:492
  171.9 4.8 %shard_map.33 = (f32[2,324,8,324]{3,2,1,0:T(8,128)}, f32[8,128]{1,0:T(8,128)S(1)}) custom-call(s32[2]{0:T(128)S(1)} %get-tuple-element.105.refs_0_, f32[2,324,8,324]{3,2,1,0:T(8,128)} %get-tuple-element.93.refs_1_, bf16[2,4,328,128]{3,2,1,0:T(8,128)(2,1)} %collective-permute-done.11.refs_2_, ...), custom_call_target="tpu_custom_call", output_to_operand_aliasing={{0}: (1, {})} | custom-call | flops 10000000000 | bytes 100000000 | tf_op jit(solution)/shard_map/pallas_call | solution.py:45
  176.7 0.0 collective-permute-done.14.refs_6_
  176.7 0.0 collective-permute-done.13.refs_5_
  176.8 0.6 shard_map.34
  177.4 0.0 collective-permute-done.15.refs_2_
  177.4 2.8 %shard_map.35 = (f32[2,324,8,324]{3,2,1,0:T(8,128)}, f32[8,128]{1,0:T(8,128)}) custom-call(s32[2]{0:T(128)S(1)} %get-tuple-element.105.refs_0_, f32[2,324,8,324]{3,2,1,0:T(8,128)} %get-tuple-element.102.refs_1_, bf16[2,4,72,324]{3,2,1,0:T(8,128)(2,1)S(1)} %collective-permute-done.15.refs_2_, ...), custom_call_target="tpu_custom_call", output_to_operand_aliasing={{0}: (1, {})} | custom-call | tf_op jit(solution)/shard_map/pallas_call | solution.py:45
  (24 shorter events, 0.1 us)
Async XLA Ops:
  0.0 17.9 %collective-permute-start = (bf16[4,2048,324]{1,0,2:T(4,128)(2,1)}, bf16[4,2048,324]{1,0,2:T(4,128)(2,1)}, u32[]{:S(2)}, u32[]{:S(2)}) collective-permute-start(bf16[4,2048,324]{1,0,2:T(4,128)(2,1)} %param.1), channel_id=1, source_target_pairs={{0,2},{2,0},{4,6},{6,4},{8,10},{10,8},{12,14},{14,12},{16,18},{18,... | collective-permute-start | bytes 15925256 | tf_op jit(solution)/shard_map/ppermute | solution.py:453
  5.6 52.4 %collective-permute-start.3 = (bf16[512,2048]{1,0:T(8,128)(2,1)}, bf16[512,2048]{1,0:T(8,128)(2,1)}, u32[]{:S(2)}, u32[]{:S(2)}) collective-permute-start(bf16[512,2048]{1,0:T(8,128)(2,1)} %bitcast.4.refs_3_), channel_id=1, source_target_pairs={{0,16},{1,17},{4,20},{5,21},{8,24},{9,25},{12,28},{13,29},{18,2},{... | collective-permute-start | bytes 6291464 | tf_op jit(solution)/shard_map/ppermute | solution.py:456
  17.8 24.5 %copy-start = (bf16[4,2048,324]{1,2,0:T(8,128)(2,1)}, bf16[4,2048,324]{1,2,0:T(8,128)(2,1)S(1)}, u32[]{:S(2)}) copy-start(bf16[4,2048,324]{1,2,0:T(8,128)(2,1)S(1)} %copy.17) | copy-start | bytes 15925252
  25.2 5.1 %copy-start.3 = (bf16[4,2048,324]{1,2,0:T(8,128)(2,1)}, bf16[4,2048,324]{1,2,0:T(8,128)(2,1)S(1)}, u32[]{:S(2)}) copy-start(bf16[4,2048,324]{1,2,0:T(8,128)(2,1)S(1)} %copy.16) | copy-start | bytes 15925252
  37.0 62.5 %collective-permute-start.7 = (bf16[512,2048]{1,0:T(8,128)(2,1)}, bf16[512,2048]{1,0:T(8,128)(2,1)S(1)}, u32[]{:S(2)}, u32[]{:S(2)}) collective-permute-start(bf16[512,2048]{1,0:T(8,128)(2,1)} %bitcast.7), channel_id=1, source_target_pairs={{0,16},{1,17},{4,20},{5,21},{8,24},{9,25},{12,28},{13,29},{18,2},{... | collective-permute-start | bytes 6291464 | tf_op jit(solution)/shard_map/ppermute | solution.py:469
  38.4 38.6 %collective-permute-start.2 = (f32[1744,256]{1,0:T(8,128)}, f32[1744,256]{1,0:T(8,128)}, u32[]{:S(2)}, u32[]{:S(2)}) collective-permute-start(f32[1744,256]{1,0:T(8,128)} %get-tuple-element.67), channel_id=1, source_target_pairs={{0,1},{1,0},{4,5},{5,4},{8,9},{9,8},{12,13},{13,12},{16,17},{17,16... | collective-permute-start | bytes 5357576 | tf_op jit(solution)/shard_map/ppermute | solution.py:464
  41.8 54.4 %collective-permute-start.1 = (f32[1744,256]{1,0:T(8,128)}, f32[1744,256]{1,0:T(8,128)}, u32[]{:S(2)}, u32[]{:S(2)}) collective-permute-start(f32[1744,256]{1,0:T(8,128)} %get-tuple-element.66), channel_id=1, source_target_pairs={{0,1},{1,0},{2,3},{3,2},{4,5},{5,4},{6,7},{7,6},{8,9},{9,8},{10,11... | collective-permute-start | bytes 5357576 | tf_op jit(solution)/shard_map/ppermute | solution.py:462
  45.7 2.5 %copy-start.1 = (bf16[4,2048,324]{1,2,0:T(8,128)(2,1)S(1)}, bf16[4,2048,324]{1,2,0:T(8,128)(2,1)}, u32[]{:S(2)}) copy-start(bf16[4,2048,324]{1,2,0:T(8,128)(2,1)} %copy-done) | copy-start | bytes 15925252
  48.2 2.5 %copy-start.4 = (bf16[4,2048,324]{1,2,0:T(8,128)(2,1)S(1)}, bf16[4,2048,324]{1,2,0:T(8,128)(2,1)}, u32[]{:S(2)}) copy-start(bf16[4,2048,324]{1,2,0:T(8,128)(2,1)} %copy-done.3) | copy-start | bytes 15925252
  58.0 38.2 %copy-start.5 = (f32[8,324,324]{2,1,0:T(8,128)}, f32[8,324,324]{2,1,0:T(8,128)S(1)}, u32[]{:S(2)}) copy-start(f32[8,324,324]{2,1,0:T(8,128)S(1)} %get-tuple-element.65.refs_1_) | copy-start | bytes 10077700
  58.0 5.5 %copy-start.11 = (bf16[272,2048]{1,0:T(8,128)(2,1)S(1)}, bf16[272,2048]{1,0:T(8,128)(2,1)}, u32[]{:S(2)}) copy-start(bf16[272,2048]{1,0:T(8,128)(2,1)} %reshape.10) | copy-start | bytes 3342340
  62.6 67.5 %collective-permute-start.6 = (f32[2,4,328,128]{3,2,1,0:T(8,128)S(1)}, f32[2,4,328,128]{3,2,1,0:T(8,128)S(1)}, u32[]{:S(2)}, u32[]{:S(2)}) collective-permute-start(f32[2,4,328,128]{3,2,1,0:T(8,128)S(1)} %get-tuple-element.74), channel_id=1, source_target_pairs={{2,3},{3,2},{6,7},{7,6},{10,11},{11,10},{14,15},{15,14},{16,17},{1... | collective-permute-start | bytes 4030472 | tf_op jit(solution)/shard_map/ppermute | solution.py:485
  63.5 62.0 %collective-permute-start.5 = (bf16[272,2048]{1,0:T(8,128)(2,1)S(1)}, bf16[272,2048]{1,0:T(8,128)(2,1)S(1)}, u32[]{:S(2)}, u32[]{:S(2)}) collective-permute-start(bf16[272,2048]{1,0:T(8,128)(2,1)S(1)} %copy-done.11), channel_id=1, source_target_pairs={{0,16},{1,17},{4,20},{5,21},{8,24},{9,25},{12,28},{13,29},{18,2},{... | collective-permute-start | bytes 3342344 | tf_op jit(solution)/shard_map/ppermute | solution.py:471
  66.1 33.3 %slice-start = ((s8[5373952]{0:T(1024)(128)(4,1)}), s8[4194304]{0:T(1024)(128)(4,1)S(1)}, s32[]{:S(2)}) async-start(s8[5373952]{0:T(1024)(128)(4,1)} %bitcast.21), calls=%async_computation | async-start | bytes 8388608
  96.1 3.3 %slice-start.1 = ((s8[5373952]{0:T(1024)(128)(4,1)}), s8[1179648]{0:T(1024)(128)(4,1)S(1)}, s32[]{:S(2)}) async-start(s8[5373952]{0:T(1024)(128)(4,1)} %bitcast.21), calls=%async_computation.1 | async-start | bytes 2359296
  101.8 31.4 %collective-permute-start.9 = (f32[2,4,328,128]{3,2,1,0:T(8,128)S(1)}, f32[2,4,328,128]{3,2,1,0:T(8,128)S(1)}, u32[]{:S(2)}, u32[]{:S(2)}) collective-permute-start(f32[2,4,328,128]{3,2,1,0:T(8,128)S(1)} %get-tuple-element.82), channel_id=1, source_target_pairs={{2,3},{3,2},{6,7},{7,6},{10,11},{11,10},{14,15},{15,14},{16,17},{1... | collective-permute-start | bytes 4030472 | tf_op jit(solution)/shard_map/ppermute | solution.py:485
  102.5 22.9 %collective-permute-start.8 = (f32[8,128]{1,0:T(8,128)S(1)}, f32[8,128]{1,0:T(8,128)S(1)}, u32[]{:S(2)}, u32[]{:S(2)}) collective-permute-start(f32[8,128]{1,0:T(8,128)S(1)} %get-tuple-element.77.refs_3_), channel_id=1, source_target_pairs={{0,2},{2,0},{4,6},{6,4},{8,10},{10,8},{12,14},{14,12},{16,18},{18,... | collective-permute-start | bytes 12296 | tf_op jit(solution)/shard_map/ppermute | solution.py:503
  119.9 19.2 %collective-permute-start.4 = (f32[4,328,384]{2,1,0:T(8,128)}, f32[4,328,384]{2,1,0:T(8,128)}, u32[]{:S(2)}, u32[]{:S(2)}) collective-permute-start(f32[4,328,384]{2,1,0:T(8,128)} %get-tuple-element.71.refs_3_), channel_id=1, source_target_pairs={{0,2},{1,3},{4,6},{5,7},{8,10},{9,11},{12,14},{13,15},{16,18},{17,... | collective-permute-start | bytes 6045704 | tf_op jit(solution)/shard_map/ppermute | solution.py:507
  129.3 15.4 %collective-permute-start.10 = (f32[2,4,72,324]{3,2,1,0:T(8,128)}, f32[2,4,72,324]{3,2,1,0:T(8,128)S(1)}, u32[]{:S(2)}, u32[]{:S(2)}) collective-permute-start(f32[2,4,72,324]{3,2,1,0:T(8,128)} %get-tuple-element.88), channel_id=1, source_target_pairs={{2,3},{3,2},{6,7},{7,6},{10,11},{11,10},{14,15},{15,14},{16,17},{1... | collective-permute-start | bytes 2239496 | tf_op jit(solution)/shard_map/ppermute | solution.py:485
  131.1 0.9 copy-start.7
  131.9 21.6 %collective-permute-start.11 = (bf16[2,4,328,128]{3,2,1,0:T(8,128)(2,1)S(1)}, bf16[2,4,328,128]{3,2,1,0:T(8,128)(2,1)}, u32[]{:S(2)}, u32[]{:S(2)}) collective-permute-start(bf16[2,4,328,128]{3,2,1,0:T(8,128)(2,1)S(1)} %get-tuple-element.80.refs_1_), channel_id=1, source_target_pairs={{16,0},{17,1},{20,4},{21,5},{24,8},{25,9},{28,12},{29,13},{2,18},{... | collective-permute-start | bytes 2015240 | tf_op jit(solution)/shard_map/ppermute | solution.py:492
  135.1 0.9 copy-start.9
  135.9 36.0 %collective-permute-start.12 = (bf16[2,4,328,128]{3,2,1,0:T(8,128)(2,1)}, bf16[2,4,328,128]{3,2,1,0:T(8,128)(2,1)}, u32[]{:S(2)}, u32[]{:S(2)}) collective-permute-start(bf16[2,4,328,128]{3,2,1,0:T(8,128)(2,1)} %get-tuple-element.84.refs_2_), channel_id=1, source_target_pairs={{16,0},{17,1},{20,4},{21,5},{24,8},{25,9},{28,12},{29,13},{2,18},{... | collective-permute-start | bytes 2015240 | tf_op jit(solution)/shard_map/ppermute | solution.py:492
  138.4 38.4 %collective-permute-start.13 = (bf16[2,2,2,328,128]{4,3,2,1,0:T(8,128)(2,1)S(1)}, bf16[2,2,2,328,128]{4,3,2,1,0:T(8,128)(2,1)S(1)}, u32[]{:S(2)}, u32[]{:S(2)}) collective-permute-start(bf16[2,2,2,328,128]{4,3,2,1,0:T(8,128)(2,1)S(1)} %get-tuple-element.99), channel_id=1, source_target_pairs={{2,3},{3,2},{6,7},{7,6},{10,11},{11,10},{14,15},{15,14},{16,17},{1... | collective-permute-start | bytes 2015240 | tf_op jit(solution)/shard_map/ppermute | solution.py:497
  139.1 2.5 %copy-start.2 = (bf16[4,2048,324]{1,2,0:T(8,128)(2,1)S(1)}, bf16[4,2048,324]{1,2,0:T(8,128)(2,1)}, u32[]{:S(2)}) copy-start(bf16[4,2048,324]{1,2,0:T(8,128)(2,1)} %copy-done) | copy-start | bytes 15925252
  141.6 5.8 %copy-start.6 = (f32[8,324,324]{2,1,0:T(8,128)S(1)}, f32[8,324,324]{2,1,0:T(8,128)}, u32[]{:S(2)}) copy-start(f32[8,324,324]{2,1,0:T(8,128)} %copy-done.5) | copy-start | bytes 10077700
  145.3 32.1 %collective-permute-start.15 = (bf16[2,4,72,324]{3,2,1,0:T(8,128)(2,1)S(1)}, bf16[2,4,72,324]{3,2,1,0:T(8,128)(2,1)S(1)}, u32[]{:S(2)}, u32[]{:S(2)}) collective-permute-start(bf16[2,4,72,324]{3,2,1,0:T(8,128)(2,1)S(1)} %get-tuple-element.90.refs_1_), channel_id=1, source_target_pairs={{16,0},{17,1},{20,4},{21,5},{24,8},{25,9},{28,12},{29,13},{2,18},{... | collective-permute-start | bytes 1119752 | tf_op jit(solution)/shard_map/ppermute | solution.py:492
  146.7 30.0 %collective-permute-start.14 = (bf16[1,2,2,72,324]{4,3,2,1,0:T(8,128)(2,1)S(1)}, bf16[1,2,2,72,324]{4,3,2,1,0:T(8,128)(2,1)S(1)}, u32[]{:S(2)}, u32[]{:S(2)}) collective-permute-start(bf16[1,2,2,72,324]{4,3,2,1,0:T(8,128)(2,1)S(1)} %get-tuple-element.100), channel_id=1, source_target_pairs={{2,3},{3,2},{6,7},{7,6},{10,11},{11,10},{14,15},{15,14},{16,17},{1... | collective-permute-start | bytes 559880 | tf_op jit(solution)/shard_map/ppermute | solution.py:497
  171.9 4.8 %copy-start.8 = (f32[2,2,324,128]{3,2,1,0:T(8,128)S(1)}, f32[2,2,324,128]{3,2,1,0:T(8,128)}, u32[]{:S(2)}) copy-start(f32[2,2,324,128]{3,2,1,0:T(8,128)} %copy-done.7) | copy-start | bytes 1990660
  171.9 4.9 %copy-start.10 = (f32[2,2,324,128]{3,2,1,0:T(8,128)S(1)}, f32[2,2,324,128]{3,2,1,0:T(8,128)}, u32[]{:S(2)}) copy-start(f32[2,2,324,128]{3,2,1,0:T(8,128)} %copy-done.9) | copy-start | bytes 1990660

commit v13 on v12

--- a/solution.py
+++ b/solution.py
@@ -477,7 +477,7 @@
     kepts, came, tiles, codes, theirs = {}, {}, {}, {}, {}
 
     def keep_terms(k, *token):
-        kepts[k], token = terms(k, True, token)
+        kepts[k], token = terms(k, True, token, LONG if k == full - 1 else 0)
         return token
 
     def send_terms(k, *token):
@@ -501,21 +501,21 @@
         token = send_terms(k, token)
         if k == full - 1:
             gate = lax.ppermute(token, "state", [(s, s ^ 1) for s in range(blocks)])
-        token = keep_terms(k, token)
-        if k == 0:
             share, token = near_share(det, keep, doubled, states, (token, crossed))
             given = lax.ppermute(share, both, to_second)
+        token = keep_terms(k, token)
     token = send_terms(full, token, gate)
     for k in early:
         token = sum_up(k, token)
-    turned, token = cross(early, token)
     token = keep_terms(full, token, given)
     token = sum_up(full, token)
+    turned, token = cross(early, token)
     last, token = cross(late, token)
     out, token = near_sum(jnp.stack([x, core]), keep, crossed, share, given, states, (token,))
 
     at = jnp.stack([x, receiver])
-    out, token = into_place(0, at, out, *returned([theirs[k] for k in early], early, widths, ops), (token,), LONG)
+    for k in early:
+        out, token = into_place(0, at, out, *returned([theirs[k]], [k], widths, ops), (token,), LONG)
     placed = completed([tiles[k] for k in early + late], turned, last, widths, ops)
     out, token = into_place(1, at, out, *placed, (token,), LONG)
     out, token = into_place(0, at, out, *returned([theirs[full]], late, widths, ops), (token,))

time: 181 us -> 184 us (1.017)
  starting transfers between devices: 43.5 us -> 71.6 us
  waiting for transfers between devices: 44.8 us -> 22.7 us
    ppermute x1, starting transfers between devices: 17.3 us -> 43.6 us  [paired(): gate = lax.ppermute(token, 'state', [(s, s ^ 1) for s in range(blocks)])]
    ppermute x1, waiting for transfers between devices: 19.1 us -> 0.01 us  [paired(): crossed = lax.ppermute(crossed, 'det', [(0, 1), (1, 0)])]
    ppermute x1, waiting for transfers between devices: 7.19 us -> 0.01 us  [paired(): doubled = lax.ppermute(doubled, both, first_across)]
    ppermute x3, waiting for transfers between devices: 18.4 us -> 22.7 us  [sum_up(): theirs[k] = lax.ppermute(codes[k], both, back)]
    pallas_call x19 -> x20, Pallas kernels: 59.4 us -> 57.6 us  [call(): return lambda *operands: kernel(*operands, *after)]
    unnamed x28 -> x18, local copies, waits for them, and re-layouts: 9.33 us -> 7.6 us
  transfers between devices with their start and end apart: 16 -> 16, of which waited for: 3 -> 3; matrix products, arithmetic and copies ran while one was open for 13% -> 12% of each run, Pallas kernels for 31% -> 30%
where the time goes in v13:
time: 184 us; the launch traced here: 183 us
  starting transfers between devices  71.6 us (39%)
  Pallas kernels  57.6 us (31%)
  local copies, waits for them, and re-layouts  30.4 us (17%)
  waiting for transfers between devices  22.7 us (12%)
    pallas_call x20, Pallas kernels, call(): return lambda *operands: kernel(*operands, *after)  57.6 us
    ppermute x1, starting transfers between devices, paired(): gate = lax.ppermute(token, 'state', [(s, s ^ 1) for s in range(blocks)])  43.6 us
    ppermute x3, waiting for transfers between devices, sum_up(): theirs[k] = lax.ppermute(codes[k], both, back)  22.7 us
    unnamed x18, local copies, waits for them, and re-layouts  7.6 us
    optimization_barrier x1, local copies, waits for them, and re-layouts, paired(): partner, own = lax.optimization_barrier((partner, own))  7.35 us
    ppermute x1, starting transfers between devices, paired(): got = [lax.ppermute(first, both, over)]  5.61 us
    optimization_barrier x1, local copies, waits for them, and re-layouts, paired(): lax.optimization_barrier((first.reshape(states * LANES, depth), amplitudes))  5.41 us
    ppermute x1, starting transfers between devices, paired(): given = lax.ppermute(share, both, to_second)  5.1 us
  transfers between devices with their start and end apart: 16, of which 3 were waited for; matrix products, arithmetic and copies ran while one was open for 12% of the time, Pallas kernels for 30%

profile of v13, /device:TPU:0, one launch (start us, length us, event | category | flops | bytes accessed | tf_op | source)
XLA Modules:
  0.0 183.0 jit_solution(1422504593346919034)
XLA Ops:
  0.0 0.5 collective-permute-start
  0.5 2.6 %slice_bitcast_fusion = bf16[4,128,2048]{2,0,1:T(4,128)(2,1)S(1)} fusion(bf16[4,2048,324]{1,0,2:T(4,128)(2,1)} %param.1), kind=kLoop, calls=%fused_computation.2 | loop fusion | bytes 4194304 | tf_op jit(solution)/shard_map/transpose | solution.py:454
  3.1 2.5 %copy.12 = bf16[4,128,2048]{2,1,0:T(8,128)(2,1)} copy(bf16[4,128,2048]{2,0,1:T(4,128)(2,1)S(1)} %slice_bitcast_fusion) | data formatting | bytes 4194304 | tf_op jit(solution)/shard_map/transpose | solution.py:454
  5.5 5.6 %collective-permute-start.4 = (bf16[512,2048]{1,0:T(8,128)(2,1)}, bf16[512,2048]{1,0:T(8,128)(2,1)S(1)}, u32[]{:S(2)}, u32[]{:S(2)}) collective-permute-start(bf16[512,2048]{1,0:T(8,128)(2,1)} %bitcast.4.refs_3_), channel_id=1, source_target_pairs={{0,16},{1,17},{4,20},{5,21},{8,24},{9,25},{12,28},{13,29},{18,2},{... | collective-permute-start | bytes 6291464 | tf_op jit(solution)/shard_map/ppermute | solution.py:456
  11.1 5.4 %copy.18 = bf16[4,2048,324]{1,2,0:T(8,128)(2,1)S(1)} copy(bf16[4,2048,324]{1,0,2:T(4,128)(2,1)} %param.1) | data formatting | bytes 10616832 | tf_op jit(solution)/shard_map/optimization_barrier | solution.py:455
  16.5 0.0 copy-start
  16.6 0.0 collective-permute-done
  16.6 7.4 %copy.17 = bf16[4,2048,324]{1,2,0:T(8,128)(2,1)S(1)} copy(bf16[4,2048,324]{1,0,2:T(4,128)(2,1)} %collective-permute-done) | data formatting | bytes 10616832 | tf_op jit(solution)/shard_map/optimization_barrier | solution.py:458
  23.9 5.1 %shard_map.17 = (f32[1744,256]{1,0:T(8,128)}, f32[8,128]{1,0:T(8,128)S(1)}) custom-call(s32[1]{0:T(128)} %bitcast.refs_0_, bf16[4,324,2048]{2,1,0:T(8,128)(2,1)S(1)} %bitcast.14, bf16[4,324,2048]{2,1,0:T(8,128)(2,1)S(1)} %bitcast.27, bf16[512,2048]{1,0:T(8,128)(2,1)} %bitcast.4.refs_3_), custom_call_target="tpu_custom_call" | custom-call | tf_op jit(solution)/shard_map/pallas_call | solution.py:45
  29.0 5.1 %shard_map.18 = (f32[1744,256]{1,0:T(8,128)}, f32[8,128]{1,0:T(8,128)S(1)}) custom-call(s32[1]{0:T(128)} %bitcast.refs_0_, bf16[4,324,2048]{2,1,0:T(8,128)(2,1)S(1)} %bitcast.15, bf16[4,324,2048]{2,1,0:T(8,128)(2,1)S(1)} %bitcast.28, f32[8,128]{1,0:T(8,128)S(1)} %get-tuple-element.61.refs_3_), custom_call_target="tpu_custom_call" | custom-call | tf_op jit(solution)/shard_map/pallas_call | solution.py:45
  34.1 1.6 slice.11
  35.7 2.6 %collective-permute-start.3 = (bf16[512,2048]{1,0:T(8,128)(2,1)}, bf16[512,2048]{1,0:T(8,128)(2,1)}, u32[]{:S(2)}, u32[]{:S(2)}) collective-permute-start(bf16[512,2048]{1,0:T(8,128)(2,1)} %bitcast.7), channel_id=1, source_target_pairs={{0,16},{1,17},{4,20},{5,21},{8,24},{9,25},{12,28},{13,29},{18,2},{... | collective-permute-start | bytes 6291464 | tf_op jit(solution)/shard_map/ppermute | solution.py:469
  38.4 3.4 %collective-permute-start.2 = (f32[1744,256]{1,0:T(8,128)}, f32[1744,256]{1,0:T(8,128)}, u32[]{:S(2)}, u32[]{:S(2)}) collective-permute-start(f32[1744,256]{1,0:T(8,128)} %get-tuple-element.69), channel_id=1, source_target_pairs={{0,1},{1,0},{4,5},{5,4},{8,9},{9,8},{12,13},{13,12},{16,17},{17,16... | collective-permute-start | bytes 5357576 | tf_op jit(solution)/shard_map/ppermute | solution.py:464
  41.7 0.6 collective-permute-start.1
  42.4 1.1 slice.10
  43.5 2.2 %reshape.10 = bf16[272,2048]{1,0:T(8,128)(2,1)} reshape(bf16[4,68,2048]{2,1,0:T(8,128)(2,1)} %slice.10) | data formatting | bytes 2228224 | tf_op jit(solution)/shard_map/reshape | solution.py:467
  45.7 2.5 %copy-done.1 = bf16[4,2048,324]{1,2,0:T(8,128)(2,1)S(1)} copy-done((bf16[4,2048,324]{1,2,0:T(8,128)(2,1)S(1)}, bf16[4,2048,324]{1,2,0:T(8,128)(2,1)}, u32[]{:S(2)}) %copy-start.1) | copy-done | bytes 5308440
  48.2 2.5 %copy-done.4 = bf16[4,2048,324]{1,2,0:T(8,128)(2,1)S(1)} copy-done((bf16[4,2048,324]{1,2,0:T(8,128)(2,1)S(1)}, bf16[4,2048,324]{1,2,0:T(8,128)(2,1)}, u32[]{:S(2)}) %copy-start.4) | copy-done | bytes 5308440
  50.7 7.2 %shard_map.19 = (f32[8,324,324]{2,1,0:T(8,128)S(1)}, f32[8,128]{1,0:T(8,128)S(1)}) custom-call(s32[1]{0:T(128)} %bitcast.refs_0_, bf16[4,324,2048]{2,1,0:T(8,128)(2,1)S(1)} %bitcast.18, bf16[4,324,2048]{2,1,0:T(8,128)(2,1)S(1)} %bitcast.29, f32[8,128]{1,0:T(8,128)S(1)} %get-tuple-element.66.refs_3_), custom_call_target="tpu_custom_call" | custom-call | tf_op jit(solution)/shard_map/pallas_call | solution.py:45
  58.0 0.0 collective-permute-done.4.refs_2_
  58.0 3.6 %shard_map.20 = (f32[2,4,328,128]{3,2,1,0:T(8,128)}, f32[8,128]{1,0:T(8,128)S(1)}) custom-call(s32[1]{0:T(128)} %bitcast.refs_0_, bf16[4,324,2048]{2,1,0:T(8,128)(2,1)S(1)} %bitcast.19, bf16[512,2048]{1,0:T(8,128)(2,1)S(1)} %collective-permute-done.4.refs_2_, f32[8,128]{1,0:T(8,128)S(1)} %get-tuple-element.71.refs_3_), custom_call_target="tpu_custom_call" | custom-call | tf_op jit(solution)/shard_map/pallas_call | solution.py:45
  61.6 1.9 %collective-permute-start.8 = (f32[2,4,328,128]{3,2,1,0:T(8,128)}, f32[2,4,328,128]{3,2,1,0:T(8,128)}, u32[]{:S(2)}, u32[]{:S(2)}) collective-permute-start(f32[2,4,328,128]{3,2,1,0:T(8,128)} %get-tuple-element.81), channel_id=1, source_target_pairs={{2,3},{3,2},{6,7},{7,6},{10,11},{11,10},{14,15},{15,14},{16,17},{1... | collective-permute-start | bytes 4030472 | tf_op jit(solution)/shard_map/ppermute | solution.py:485
  63.5 1.6 collective-permute-start.6
  65.1 0.1 pad_add_fusion
  65.2 2.5 %copy-done.2 = bf16[4,2048,324]{1,2,0:T(8,128)(2,1)S(1)} copy-done((bf16[4,2048,324]{1,2,0:T(8,128)(2,1)S(1)}, bf16[4,2048,324]{1,2,0:T(8,128)(2,1)}, u32[]{:S(2)}) %copy-start.2) | copy-done | bytes 5308440
  67.7 2.4 %shard_map.21 = (f32[2,4,328,128]{3,2,1,0:T(8,128)S(1)}, f32[8,128]{1,0:T(8,128)S(1)}) custom-call(s32[1]{0:T(128)} %bitcast.refs_0_, bf16[4,324,2048]{2,1,0:T(8,128)(2,1)S(1)} %bitcast.20, bf16[512,2048]{1,0:T(8,128)(2,1)S(1)} %collective-permute-done.4.refs_2_, f32[8,128]{1,0:T(8,128)S(1)} %get-tuple-element.72.refs_3_), custom_call_target="tpu_custom_call" | custom-call | tf_op jit(solution)/shard_map/pallas_call | solution.py:45
  70.1 0.0 collective-permute-done.3.refs_2_
  70.1 0.0 slice-start
  70.1 3.8 %shard_map.22 = (f32[2,4,328,128]{3,2,1,0:T(8,128)S(1)}, f32[8,128]{1,0:T(8,128)S(1)}) custom-call(s32[1]{0:T(128)} %bitcast.refs_0_, bf16[4,324,2048]{2,1,0:T(8,128)(2,1)S(1)} %bitcast.21, bf16[512,2048]{1,0:T(8,128)(2,1)} %collective-permute-done.3.refs_2_, f32[8,128]{1,0:T(8,128)S(1)} %get-tuple-element.73.refs_3_), custom_call_target="tpu_custom_call" | custom-call | tf_op jit(solution)/shard_map/pallas_call | solution.py:45
  73.9 43.6 %collective-permute-start.9 = (f32[8,128]{1,0:T(8,128)S(1)}, f32[8,128]{1,0:T(8,128)S(1)}, u32[]{:S(2)}, u32[]{:S(2)}) collective-permute-start(f32[8,128]{1,0:T(8,128)S(1)} %get-tuple-element.74.refs_3_), channel_id=1, source_target_pairs={{0,2},{2,0},{4,6},{6,4},{8,10},{10,8},{12,14},{14,12},{16,18},{18,... | collective-permute-start | bytes 12296 | tf_op jit(solution)/shard_map/ppermute | solution.py:503
  117.5 0.0 collective-permute-done.2.refs_2_
  117.5 0.7 collective-permute-start.7
  118.3 0.0 collective-permute-done.1.refs_4_.refs_2_
  118.3 0.0 slice-start.1
  118.3 2.0 %shard_map.23 = (f32[4,328,384]{2,1,0:T(8,128)S(1)}, f32[8,128]{1,0:T(8,128)S(1)}) custom-call(s32[1]{0:T(128)} %bitcast.refs_0_, f32[8,324,324]{2,1,0:T(8,128)S(1)} %copy-done.6, f32[1744,256]{1,0:T(8,128)} %collective-permute-done.2.refs_2_, f32[8,128]{1,0:T(8,128)S(1)} %get-tuple-element.74.refs_3_, f32[1744,256]{1,0:T(8,128)} %collective-permute-done.1.refs_4_.refs_2_), custom_call_target="tpu_custom_call" | custom-call | tf_op jit(solution)/shard_map/pallas_call | solution.py:45
  120.3 5.1 %collective-permute-start.5 = (f32[4,328,384]{2,1,0:T(8,128)S(1)}, f32[4,328,384]{2,1,0:T(8,128)S(1)}, u32[]{:S(2)}, u32[]{:S(2)}) collective-permute-start(f32[4,328,384]{2,1,0:T(8,128)S(1)} %get-tuple-element.75.refs_3_), channel_id=1, source_target_pairs={{0,2},{1,3},{4,6},{5,7},{8,10},{9,11},{12,14},{13,15},{16,18},{17,... | collective-permute-start | bytes 6045704 | tf_op jit(solution)/shard_map/ppermute | solution.py:505
  125.4 3.6 %shard_map.24 = (f32[2,4,328,128]{3,2,1,0:T(8,128)S(1)}, f32[8,128]{1,0:T(8,128)S(1)}) custom-call(s32[1]{0:T(128)} %bitcast.refs_0_, bf16[4,324,2048]{2,1,0:T(8,128)(2,1)S(1)} %bitcast.24, bf16[512,2048]{1,0:T(8,128)(2,1)} %collective-permute-done.3.refs_2_, f32[8,128]{1,0:T(8,128)S(1)} %get-tuple-element.77.refs_3_), custom_call_target="tpu_custom_call" | custom-call | flops 10000000000 | bytes 100000000 | tf_op jit(solution)/shard_map/pallas_call | solution.py:45
  129.1 0.0 collective-permute-done.6.refs_2_
  129.1 0.0 collective-permute-done.9.refs_4_
  129.1 3.1 %shard_map.25 = (f32[2,4,72,324]{3,2,1,0:T(8,128)S(1)}, f32[8,128]{1,0:T(8,128)S(1)}) custom-call(s32[1]{0:T(128)} %bitcast.refs_0_, bf16[4,324,2048]{2,1,0:T(8,128)(2,1)S(1)} %bitcast.25, bf16[272,2048]{1,0:T(8,128)(2,1)S(1)} %collective-permute-done.6.refs_2_, f32[8,128]{1,0:T(8,128)S(1)} %get-tuple-element.82.refs_3_, ...), custom_call_target="tpu_custom_call" | custom-call | tf_op jit(solution)/shard_map/pallas_call | solution.py:45
  132.2 0.7 collective-permute-start.10
  133.0 0.0 collective-permute-done.8.refs_2_
  133.0 2.4 %shard_map.26 = (f32[2,2,324,128]{3,2,1,0:T(8,128)S(1)}, bf16[2,4,328,128]{3,2,1,0:T(8,128)(2,1)S(1)}, f32[8,128]{1,0:T(8,128)S(1)}) custom-call(s32[1]{0:T(128)} %bitcast.refs_0_, f32[2,4,328,128]{3,2,1,0:T(8,128)S(1)} %get-tuple-element.80.refs_1_, f32[2,4,328,128]{3,2,1,0:T(8,128)} %collective-permute-done.8.refs_2_, f32[8,128]{1,0:T(8,128)S(1)} %get-tuple-element.83.refs_3_), custom_call_target="tpu_custom_call" | custom-call | flops 10000000000 | bytes 100000000 | tf_op jit(solution)/shard_map/pallas_call | solution.py:45
  135.4 1.3 collective-permute-start.11
  136.7 0.0 collective-permute-done.7.refs_2_
  136.7 1.0 shard_map.27
  137.7 1.3 collective-permute-start.12
  139.0 0.0 collective-permute-done.5.refs_4_
  139.0 3.2 %shard_map.28 = (f32[2,4,72,324]{3,2,1,0:T(8,128)S(1)}, f32[8,128]{1,0:T(8,128)S(1)}) custom-call(s32[1]{0:T(128)} %bitcast.refs_0_, bf16[4,324,2048]{2,1,0:T(8,128)(2,1)S(1)} %bitcast.26, bf16[272,2048]{1,0:T(8,128)(2,1)S(1)} %collective-permute-done.6.refs_2_, f32[8,128]{1,0:T(8,128)S(1)} %get-tuple-element.85.refs_3_, ...), custom_call_target="tpu_custom_call" | custom-call | tf_op jit(solution)/shard_map/pallas_call | solution.py:45
  142.2 0.0 collective-permute-done.10.refs_2_
  142.2 0.6 shard_map.29
  142.9 0.1 shard_map.30
  143.0 1.3 collective-permute-start.15
  144.3 0.7 collective-permute-start.13
  145.0 0.7 collective-permute-start.14
  145.7 5.2 %shard_map.32 = (f32[2,324,8,324]{3,2,1,0:T(8,128)}, f32[8,128]{1,0:T(8,128)S(1)}) custom-call(s32[2]{0:T(128)S(1)} %get-tuple-element.110.refs_0_, f32[8,324,324]{2,1,0:T(8,128)S(1)} %copy-done.6, f32[1744,256]{1,0:T(8,128)} %collective-permute-done.1.refs_4_.refs_2_, f32[4,328,384]{2,1,0:T(8,128)S(1)} %get-tuple-element.75.refs_3_, ...), custom_call_target="tpu_custom_call" | custom-call | tf_op jit(solution)/shard_map/pallas_call | solution.py:45
  150.9 17.2 %collective-permute-done.11.refs_2_ = bf16[2,4,328,128]{3,2,1,0:T(8,128)(2,1)S(1)} collective-permute-done((bf16[2,4,328,128]{3,2,1,0:T(8,128)(2,1)S(1)}, bf16[2,4,328,128]{3,2,1,0:T(8,128)(2,1)S(1)}, u32[]{:S(2)}, u32[]{:S(2)}) %collective-permute-start.11) | collective-permute-done | bytes 671776 | tf_op jit(solution)/shard_map/ppermute | solution.py:492
  168.1 3.0 %shard_map.33 = (f32[2,324,8,324]{3,2,1,0:T(8,128)}, f32[8,128]{1,0:T(8,128)S(1)}) custom-call(s32[2]{0:T(128)S(1)} %get-tuple-element.109.refs_0_, f32[2,324,8,324]{3,2,1,0:T(8,128)} %get-tuple-element.95.refs_1_, bf16[2,4,328,128]{3,2,1,0:T(8,128)(2,1)S(1)} %collective-permute-done.11.refs_2_, ...), custom_call_target="tpu_custom_call", output_to_operand_aliasing={{0}: (1, {})} | custom-call | flops 10000000000 | bytes 100000000 | tf_op jit(solution)/shard_map/pallas_call | solution.py:45
  171.1 4.2 %collective-permute-done.12.refs_2_ = bf16[2,4,328,128]{3,2,1,0:T(8,128)(2,1)S(1)} collective-permute-done((bf16[2,4,328,128]{3,2,1,0:T(8,128)(2,1)S(1)}, bf16[2,4,328,128]{3,2,1,0:T(8,128)(2,1)S(1)}, u32[]{:S(2)}, u32[]{:S(2)}) %collective-permute-start.12) | collective-permute-done | bytes 671776 | tf_op jit(solution)/shard_map/ppermute | solution.py:492
  175.3 2.8 %shard_map.34 = (f32[2,324,8,324]{3,2,1,0:T(8,128)}, f32[8,128]{1,0:T(8,128)S(1)}) custom-call(s32[2]{0:T(128)S(1)} %get-tuple-element.109.refs_0_, f32[2,324,8,324]{3,2,1,0:T(8,128)} %get-tuple-element.97.refs_1_, bf16[2,4,328,128]{3,2,1,0:T(8,128)(2,1)S(1)} %collective-permute-done.12.refs_2_, ...), custom_call_target="tpu_custom_call", output_to_operand_aliasing={{0}: (1, {})} | custom-call | flops 10000000000 | bytes 100000000 | tf_op jit(solution)/shard_map/pallas_call | solution.py:45
  178.0 0.0 collective-permute-done.14.refs_6_
  178.1 0.6 shard_map.35
  178.7 1.3 collective-permute-done.15.refs_2_
  180.0 2.8 %shard_map.36 = (f32[2,324,8,324]{3,2,1,0:T(8,128)}, f32[8,128]{1,0:T(8,128)}) custom-call(s32[2]{0:T(128)S(1)} %get-tuple-element.109.refs_0_, f32[2,324,8,324]{3,2,1,0:T(8,128)} %get-tuple-element.106.refs_1_, bf16[2,4,72,324]{3,2,1,0:T(8,128)(2,1)S(1)} %collective-permute-done.15.refs_2_, ...), custom_call_target="tpu_custom_call", output_to_operand_aliasing={{0}: (1, {})} | custom-call | tf_op jit(solution)/shard_map/pallas_call | solution.py:45
  (15 shorter events, 0.1 us)
Async XLA Ops:
  0.0 16.6 %collective-permute-start = (bf16[4,2048,324]{1,0,2:T(4,128)(2,1)}, bf16[4,2048,324]{1,0,2:T(4,128)(2,1)}, u32[]{:S(2)}, u32[]{:S(2)}) collective-permute-start(bf16[4,2048,324]{1,0,2:T(4,128)(2,1)} %param.1), channel_id=1, source_target_pairs={{0,2},{2,0},{4,6},{6,4},{8,10},{10,8},{12,14},{14,12},{16,18},{18,... | collective-permute-start | bytes 15925256 | tf_op jit(solution)/shard_map/ppermute | solution.py:453
  5.5 52.5 %collective-permute-start.4 = (bf16[512,2048]{1,0:T(8,128)(2,1)}, bf16[512,2048]{1,0:T(8,128)(2,1)S(1)}, u32[]{:S(2)}, u32[]{:S(2)}) collective-permute-start(bf16[512,2048]{1,0:T(8,128)(2,1)} %bitcast.4.refs_3_), channel_id=1, source_target_pairs={{0,16},{1,17},{4,20},{5,21},{8,24},{9,25},{12,28},{13,29},{18,2},{... | collective-permute-start | bytes 6291464 | tf_op jit(solution)/shard_map/ppermute | solution.py:456
  16.5 25.8 %copy-start = (bf16[4,2048,324]{1,2,0:T(8,128)(2,1)}, bf16[4,2048,324]{1,2,0:T(8,128)(2,1)S(1)}, u32[]{:S(2)}) copy-start(bf16[4,2048,324]{1,2,0:T(8,128)(2,1)S(1)} %copy.18) | copy-start | bytes 15925252
  23.9 5.1 %copy-start.3 = (bf16[4,2048,324]{1,2,0:T(8,128)(2,1)}, bf16[4,2048,324]{1,2,0:T(8,128)(2,1)S(1)}, u32[]{:S(2)}) copy-start(bf16[4,2048,324]{1,2,0:T(8,128)(2,1)S(1)} %copy.17) | copy-start | bytes 15925252
  35.7 34.4 %collective-permute-start.3 = (bf16[512,2048]{1,0:T(8,128)(2,1)}, bf16[512,2048]{1,0:T(8,128)(2,1)}, u32[]{:S(2)}, u32[]{:S(2)}) collective-permute-start(bf16[512,2048]{1,0:T(8,128)(2,1)} %bitcast.7), channel_id=1, source_target_pairs={{0,16},{1,17},{4,20},{5,21},{8,24},{9,25},{12,28},{13,29},{18,2},{... | collective-permute-start | bytes 6291464 | tf_op jit(solution)/shard_map/ppermute | solution.py:469
  38.4 79.2 %collective-permute-start.2 = (f32[1744,256]{1,0:T(8,128)}, f32[1744,256]{1,0:T(8,128)}, u32[]{:S(2)}, u32[]{:S(2)}) collective-permute-start(f32[1744,256]{1,0:T(8,128)} %get-tuple-element.69), channel_id=1, source_target_pairs={{0,1},{1,0},{4,5},{5,4},{8,9},{9,8},{12,13},{13,12},{16,17},{17,16... | collective-permute-start | bytes 5357576 | tf_op jit(solution)/shard_map/ppermute | solution.py:464
  41.7 76.5 %collective-permute-start.1 = (f32[1744,256]{1,0:T(8,128)}, f32[1744,256]{1,0:T(8,128)}, u32[]{:S(2)}, u32[]{:S(2)}) collective-permute-start(f32[1744,256]{1,0:T(8,128)} %get-tuple-element.68), channel_id=1, source_target_pairs={{0,1},{1,0},{2,3},{3,2},{4,5},{5,4},{6,7},{7,6},{8,9},{9,8},{10,11... | collective-permute-start | bytes 5357576 | tf_op jit(solution)/shard_map/ppermute | solution.py:462
  45.7 2.5 %copy-start.1 = (bf16[4,2048,324]{1,2,0:T(8,128)(2,1)S(1)}, bf16[4,2048,324]{1,2,0:T(8,128)(2,1)}, u32[]{:S(2)}) copy-start(bf16[4,2048,324]{1,2,0:T(8,128)(2,1)} %copy-done) | copy-start | bytes 15925252
  48.2 2.5 %copy-start.4 = (bf16[4,2048,324]{1,2,0:T(8,128)(2,1)S(1)}, bf16[4,2048,324]{1,2,0:T(8,128)(2,1)}, u32[]{:S(2)}) copy-start(bf16[4,2048,324]{1,2,0:T(8,128)(2,1)} %copy-done.3) | copy-start | bytes 15925252
  58.0 3.6 %copy-start.5 = (f32[8,324,324]{2,1,0:T(8,128)}, f32[8,324,324]{2,1,0:T(8,128)S(1)}, u32[]{:S(2)}) copy-start(f32[8,324,324]{2,1,0:T(8,128)S(1)} %get-tuple-element.67.refs_1_) | copy-start | bytes 10077700
  61.6 71.4 %collective-permute-start.8 = (f32[2,4,328,128]{3,2,1,0:T(8,128)}, f32[2,4,328,128]{3,2,1,0:T(8,128)}, u32[]{:S(2)}, u32[]{:S(2)}) collective-permute-start(f32[2,4,328,128]{3,2,1,0:T(8,128)} %get-tuple-element.81), channel_id=1, source_target_pairs={{2,3},{3,2},{6,7},{7,6},{10,11},{11,10},{14,15},{15,14},{16,17},{1... | collective-permute-start | bytes 4030472 | tf_op jit(solution)/shard_map/ppermute | solution.py:485
  63.5 65.6 %collective-permute-start.6 = (bf16[272,2048]{1,0:T(8,128)(2,1)}, bf16[272,2048]{1,0:T(8,128)(2,1)S(1)}, u32[]{:S(2)}, u32[]{:S(2)}) collective-permute-start(bf16[272,2048]{1,0:T(8,128)(2,1)} %reshape.10), channel_id=1, source_target_pairs={{0,16},{1,17},{4,20},{5,21},{8,24},{9,25},{12,28},{13,29},{18,2},{... | collective-permute-start | bytes 3342344 | tf_op jit(solution)/shard_map/ppermute | solution.py:471
  65.2 2.5 %copy-start.2 = (bf16[4,2048,324]{1,2,0:T(8,128)(2,1)S(1)}, bf16[4,2048,324]{1,2,0:T(8,128)(2,1)}, u32[]{:S(2)}) copy-start(bf16[4,2048,324]{1,2,0:T(8,128)(2,1)} %copy-done) | copy-start | bytes 15925252
  70.1 48.2 %copy-start.6 = (f32[8,324,324]{2,1,0:T(8,128)S(1)}, f32[8,324,324]{2,1,0:T(8,128)}, u32[]{:S(2)}) copy-start(f32[8,324,324]{2,1,0:T(8,128)} %copy-done.5) | copy-start | bytes 10077700
  70.1 55.3 %slice-start = ((s8[5373952]{0:T(1024)(128)(4,1)}), s8[4194304]{0:T(1024)(128)(4,1)S(1)}, s32[]{:S(2)}) async-start(s8[5373952]{0:T(1024)(128)(4,1)} %bitcast.22), calls=%async_computation | async-start | bytes 8388608
  73.9 55.2 %collective-permute-start.9 = (f32[8,128]{1,0:T(8,128)S(1)}, f32[8,128]{1,0:T(8,128)S(1)}, u32[]{:S(2)}, u32[]{:S(2)}) collective-permute-start(f32[8,128]{1,0:T(8,128)S(1)} %get-tuple-element.74.refs_3_), channel_id=1, source_target_pairs={{0,2},{2,0},{4,6},{6,4},{8,10},{10,8},{12,14},{14,12},{16,18},{18,... | collective-permute-start | bytes 12296 | tf_op jit(solution)/shard_map/ppermute | solution.py:503
  117.5 19.2 %collective-permute-start.7 = (f32[2,4,328,128]{3,2,1,0:T(8,128)S(1)}, f32[2,4,328,128]{3,2,1,0:T(8,128)S(1)}, u32[]{:S(2)}, u32[]{:S(2)}) collective-permute-start(f32[2,4,328,128]{3,2,1,0:T(8,128)S(1)} %get-tuple-element.79), channel_id=1, source_target_pairs={{2,3},{3,2},{6,7},{7,6},{10,11},{11,10},{14,15},{15,14},{16,17},{1... | collective-permute-start | bytes 4030472 | tf_op jit(solution)/shard_map/ppermute | solution.py:485
  118.3 7.1 %slice-start.1 = ((s8[5373952]{0:T(1024)(128)(4,1)}), s8[1179648]{0:T(1024)(128)(4,1)S(1)}, s32[]{:S(2)}) async-start(s8[5373952]{0:T(1024)(128)(4,1)} %bitcast.22), calls=%async_computation.1 | async-start | bytes 2359296
  120.3 18.7 %collective-permute-start.5 = (f32[4,328,384]{2,1,0:T(8,128)S(1)}, f32[4,328,384]{2,1,0:T(8,128)S(1)}, u32[]{:S(2)}, u32[]{:S(2)}) collective-permute-start(f32[4,328,384]{2,1,0:T(8,128)S(1)} %get-tuple-element.75.refs_3_), channel_id=1, source_target_pairs={{0,2},{1,3},{4,6},{5,7},{8,10},{9,11},{12,14},{13,15},{16,18},{17,... | collective-permute-start | bytes 6045704 | tf_op jit(solution)/shard_map/ppermute | solution.py:505
  132.2 10.0 %collective-permute-start.10 = (f32[2,4,72,324]{3,2,1,0:T(8,128)S(1)}, f32[2,4,72,324]{3,2,1,0:T(8,128)S(1)}, u32[]{:S(2)}, u32[]{:S(2)}) collective-permute-start(f32[2,4,72,324]{3,2,1,0:T(8,128)S(1)} %get-tuple-element.87), channel_id=1, source_target_pairs={{2,3},{3,2},{6,7},{7,6},{10,11},{11,10},{14,15},{15,14},{16,17},{1... | collective-permute-start | bytes 2239496 | tf_op jit(solution)/shard_map/ppermute | solution.py:485
  135.4 32.7 %collective-permute-start.11 = (bf16[2,4,328,128]{3,2,1,0:T(8,128)(2,1)S(1)}, bf16[2,4,328,128]{3,2,1,0:T(8,128)(2,1)S(1)}, u32[]{:S(2)}, u32[]{:S(2)}) collective-permute-start(bf16[2,4,328,128]{3,2,1,0:T(8,128)(2,1)S(1)} %get-tuple-element.90.refs_1_), channel_id=1, source_target_pairs={{16,0},{17,1},{20,4},{21,5},{24,8},{25,9},{28,12},{29,13},{2,18},{... | collective-permute-start | bytes 2015240 | tf_op jit(solution)/shard_map/ppermute | solution.py:492
  137.7 37.5 %collective-permute-start.12 = (bf16[2,4,328,128]{3,2,1,0:T(8,128)(2,1)S(1)}, bf16[2,4,328,128]{3,2,1,0:T(8,128)(2,1)S(1)}, u32[]{:S(2)}, u32[]{:S(2)}) collective-permute-start(bf16[2,4,328,128]{3,2,1,0:T(8,128)(2,1)S(1)} %get-tuple-element.91.refs_2_), channel_id=1, source_target_pairs={{16,0},{17,1},{20,4},{21,5},{24,8},{25,9},{28,12},{29,13},{2,18},{... | collective-permute-start | bytes 2015240 | tf_op jit(solution)/shard_map/ppermute | solution.py:492
  143.0 37.1 %collective-permute-start.15 = (bf16[2,4,72,324]{3,2,1,0:T(8,128)(2,1)S(1)}, bf16[2,4,72,324]{3,2,1,0:T(8,128)(2,1)S(1)}, u32[]{:S(2)}, u32[]{:S(2)}) collective-permute-start(bf16[2,4,72,324]{3,2,1,0:T(8,128)(2,1)S(1)} %get-tuple-element.89.refs_1_), channel_id=1, source_target_pairs={{16,0},{17,1},{20,4},{21,5},{24,8},{25,9},{28,12},{29,13},{2,18},{... | collective-permute-start | bytes 1119752 | tf_op jit(solution)/shard_map/ppermute | solution.py:492
  144.3 33.7 %collective-permute-start.13 = (bf16[2,2,2,328,128]{4,3,2,1,0:T(8,128)(2,1)S(1)}, bf16[2,2,2,328,128]{4,3,2,1,0:T(8,128)(2,1)S(1)}, u32[]{:S(2)}, u32[]{:S(2)}) collective-permute-start(bf16[2,2,2,328,128]{4,3,2,1,0:T(8,128)(2,1)S(1)} %get-tuple-element.103), channel_id=1, source_target_pairs={{2,3},{3,2},{6,7},{7,6},{10,11},{11,10},{14,15},{15,14},{16,17},{1... | collective-permute-start | bytes 2015240 | tf_op jit(solution)/shard_map/ppermute | solution.py:497
  145.0 33.0 %collective-permute-start.14 = (bf16[1,2,2,72,324]{4,3,2,1,0:T(8,128)(2,1)S(1)}, bf16[1,2,2,72,324]{4,3,2,1,0:T(8,128)(2,1)S(1)}, u32[]{:S(2)}, u32[]{:S(2)}) collective-permute-start(bf16[1,2,2,72,324]{4,3,2,1,0:T(8,128)(2,1)S(1)} %get-tuple-element.104), channel_id=1, source_target_pairs={{2,3},{3,2},{6,7},{7,6},{10,11},{11,10},{14,15},{15,14},{16,17},{1... | collective-permute-start | bytes 559880 | tf_op jit(solution)/shard_map/ppermute | solution.py:497

commit v14 on v13

--- a/solution.py
+++ b/solution.py
@@ -171,7 +171,7 @@
 
     def body(s_ref, keep_ref, wire_in, share_ref, given_ref, out_ref, kept, wire, mine, *rest):
         made, sems = rest[:-1], rest[-1]
-        x, core = s_ref[0], s_ref[1]
+        x, second = s_ref[0], s_ref[1]
         loads = [pltpu.make_async_copy(wire_in, wire, sems.at[0])]
         for a in range(half):
             other = keep_ref.at[pl.ds(a * states + half * (1 - x), half)]
@@ -180,7 +180,7 @@
             load.start()
         for source, which in ((share_ref, 0), (given_ref, 1)):
 
-            @pl.when(core == which)
+            @pl.when(second == which)
             def _():
                 load = pltpu.make_async_copy(source, mine, sems.at[1 + half])
                 load.start()
@@ -199,11 +199,11 @@
                     def _():
                         ref[:, t] = kept[one, start : start + rows] + packing.rows(wire, one, start, rows)
 
-                    @pl.when((b // half == x) & (core == 0))
+                    @pl.when((b // half == x) & (second == 0))
                     def _():
                         ref[:, t] = mine[one, start : start + rows, :ops]
 
-                    @pl.when((b // half == x) & (core == 1))
+                    @pl.when((b // half == x) & (second == 1))
                     def _():
                         ref[:, t] = mine[turned, :, start : start + LANES].T[:rows, :ops]
 
@@ -231,7 +231,7 @@
     )(place_in, keep, crossed, share, given)
 
 
-def far_terms(det, own, got, start, width, turned, mine, after=(), declared=0):
+def far_terms(place_in, own, got, start, width, turned, mine, after=(), declared=0):
     states, ops, depth = own.shape
     half = states // 2
     rows = ops if turned else width
@@ -240,16 +240,18 @@
     def first(x):
         return half * x if mine else half * (1 - x)
 
-    def body(x_ref, own_ref, got_ref, out_ref):
-        if turned:
-            both = contract_last(own_ref[0], got_ref[...])
-            parts = [both[:, a * width : (a + 1) * width] for a in range(half)]
-        else:
-            every = contract_last(got_ref[...], own_ref[0])
-            parts = [every[u * width : (u + 1) * width] for u in range(states)]
-            parts = [jnp.where(first(x_ref[0]) == 0, parts[a], parts[half + a]) for a in range(half)]
-        for a in range(half):
-            out_ref[a, 0, :rows] = parts[a]
+    def body(s_ref, own_ref, got_ref, out_ref):
+        @pl.when(s_ref[1] == 1)
+        def _():
+            if turned:
+                both = contract_last(own_ref[0], got_ref[...])
+                parts = [both[:, a * width : (a + 1) * width] for a in range(half)]
+            else:
+                every = contract_last(got_ref[...], own_ref[0])
+                parts = [every[u * width : (u + 1) * width] for u in range(states)]
+                parts = [jnp.where(first(s_ref[0]) == 0, parts[a], parts[half + a]) for a in range(half)]
+            for a in range(half):
+                out_ref[a, 0, :rows] = parts[a]
 
     picked = half if turned else states
 
@@ -261,16 +263,16 @@
         (states,),
         1,
         [
-            pl.BlockSpec((1, ops, depth), lambda v, x: (v, 0, 0)),
+            pl.BlockSpec((1, ops, depth), lambda v, s: (v * s[1], 0, 0)),
             pl.BlockSpec(
                 (pl.Element(picked * width), pl.Element(depth)), rows_in, pipeline_mode=pl.Buffered(1)
             ),
         ],
-        [pl.BlockSpec((half, 1, *tile), lambda v, x: (0, v, 0, 0))],
+        [pl.BlockSpec((half, 1, *tile), lambda v, s: (0, v * s[1], 0, 0))],
         [f32(half, states, *tile)],
         after,
         declared=declared,
-    )(det, own, got)
+    )(place_in, own, got)
 
 
 def far_sum(det, keep, came, rows, turned, after=(), declared=0):
@@ -441,14 +443,15 @@
     over = [(2 * s + x, 2 * (s ^ 1 << far) + x) for s in senders for x in range(2)]
     back = [(b, a) for a, b in over]
     across = [(2 * s + x, 2 * s + 1 - x) for s in receivers for x in range(2)]
-    first_across = [(2 * s + x, 2 * s + 1 - x) for s in range(0, blocks, 2) for x in range(2)]
-    to_second = [(2 * s + x, 2 * (s + 1) + x) for s in range(0, blocks, 2) for x in range(2)]
+    first_across = [(2 * s + x, 2 * s + 1 - x) for s in senders for x in range(2)]
+    to_second = [(2 * s + x, 2 * (s ^ 1) + x) for s in senders for x in range(2)]
+    opens = [(s, s ^ 1) for s in senders if (s >> far ^ s >> far - 1) & 1]
 
     state = lax.axis_index("state")
     x = lax.axis_index("det").astype(jnp.int32)
     det = x[None]
     receiver = ((state & 1) ^ (state >> far & 1)).astype(jnp.int32)
-    core = (state & 1).astype(jnp.int32)
+    at = jnp.stack([x, receiver])
 
     partner = lax.ppermute(amplitudes, "state", [(s, s ^ 1) for s in range(blocks)])
     first = amplitudes[:, :, :LANES].transpose(0, 2, 1)
@@ -472,7 +475,7 @@
     keep, token = near_keep(det, own, partner, (token,))
     def terms(k, mine, done, declared=0):
         wire, start = (0, 0) if k == 0 else (2, 0) if k == full else (1, states * LANES * (k - 1))
-        return far_terms(det, own, got[wire], start, widths[k], k < full, mine, done, declared)
+        return far_terms(at, own, got[wire], start, widths[k], k < full, mine, done, declared)
 
     kepts, came, tiles, codes, theirs = {}, {}, {}, {}, {}
 
@@ -500,20 +503,19 @@
     for k in early:
         token = send_terms(k, token)
         if k == full - 1:
-            gate = lax.ppermute(token, "state", [(s, s ^ 1) for s in range(blocks)])
+            gate = lax.ppermute(token, "state", opens)
             share, token = near_share(det, keep, doubled, states, (token, crossed))
             given = lax.ppermute(share, both, to_second)
         token = keep_terms(k, token)
-    token = send_terms(full, token, gate)
+    token = send_terms(full, token)
     for k in early:
-        token = sum_up(k, token)
+        token = sum_up(k, token, *([gate] if k == 0 else []))
     token = keep_terms(full, token, given)
     token = sum_up(full, token)
     turned, token = cross(early, token)
     last, token = cross(late, token)
-    out, token = near_sum(jnp.stack([x, core]), keep, crossed, share, given, states, (token,))
-
-    at = jnp.stack([x, receiver])
+    out, token = near_sum(at, keep, crossed, share, given, states, (token,))
+
     for k in early:
         out, token = into_place(0, at, out, *returned([theirs[k]], [k], widths, ops), (token,), LONG)
     placed = completed([tiles[k] for k in early + late], turned, last, widths, ops)

time: 184 us -> 179 us (0.973)
  waiting for transfers between devices: 22.7 us -> 53.3 us
  starting transfers between devices: 71.6 us -> 52.3 us
  Pallas kernels: 57.6 us -> 42.8 us
    ppermute x1, starting transfers between devices: 43.6 us -> 0.66 us  [paired(): gate = lax.ppermute(token, 'state', opens)]
    ppermute x1, starting transfers between devices: 5.1 us -> 28.2 us  [paired(): given = lax.ppermute(share, both, to_second)]
    ppermute x1, waiting for transfers between devices: 0.01 us -> 18.4 us  [paired(): crossed = lax.ppermute(crossed, 'det', [(0, 1), (1, 0)])]
    pallas_call x20, Pallas kernels: 57.6 us -> 42.8 us  [call(): return lambda *operands: kernel(*operands, *after)]
    ppermute x1, waiting for transfers between devices: 0.01 us -> 9.63 us  [paired(): doubled = lax.ppermute(doubled, both, first_across)]
    unnamed x18 -> x14, local copies, waits for them, and re-layouts: 7.6 us -> 5.07 us
    ppermute x3, waiting for transfers between devices: 22.7 us -> 25.2 us  [sum_up(): theirs[k] = lax.ppermute(codes[k], both, back)]
  transfers between devices with their start and end apart: 16 -> 16, of which waited for: 3 -> 5; matrix products, arithmetic and copies ran while one was open for 12% -> 14% of each run, Pallas kernels for 30% -> 22%
where the time goes in v14:
time: 179 us; the launch traced here: 178 us
  waiting for transfers between devices  53.3 us (30%)
  starting transfers between devices  52.3 us (29%)
  Pallas kernels  42.8 us (24%)
  local copies, waits for them, and re-layouts  29.1 us (16%)
    pallas_call x20, Pallas kernels, call(): return lambda *operands: kernel(*operands, *after)  42.8 us
    ppermute x1, starting transfers between devices, paired(): given = lax.ppermute(share, both, to_second)  28.2 us
    ppermute x3, waiting for transfers between devices, sum_up(): theirs[k] = lax.ppermute(codes[k], both, back)  25.2 us
    ppermute x1, waiting for transfers between devices, paired(): crossed = lax.ppermute(crossed, 'det', [(0, 1), (1, 0)])  18.4 us
    ppermute x1, waiting for transfers between devices, paired(): doubled = lax.ppermute(doubled, both, first_across)  9.63 us
    optimization_barrier x1, local copies, waits for them, and re-layouts, paired(): partner, own = lax.optimization_barrier((partner, own))  7.35 us
    ppermute x1, starting transfers between devices, paired(): got = [lax.ppermute(first, both, over)]  5.61 us
    optimization_barrier x1, local copies, waits for them, and re-layouts, paired(): lax.optimization_barrier((first.reshape(states * LANES, depth), amplitudes))  5.41 us
  transfers between devices with their start and end apart: 16, of which 5 were waited for; matrix products, arithmetic and copies ran while one was open for 14% of the time, Pallas kernels for 22%

profile of v14, /device:TPU:0, one launch (start us, length us, event | category | flops | bytes accessed | tf_op | source)
XLA Modules:
  0.0 178.2 jit_solution(16238574108290404138)
XLA Ops:
  0.0 0.5 collective-permute-start
  0.5 2.6 %slice_bitcast_fusion = bf16[4,128,2048]{2,0,1:T(4,128)(2,1)S(1)} fusion(bf16[4,2048,324]{1,0,2:T(4,128)(2,1)} %param.1), kind=kLoop, calls=%fused_computation.2 | loop fusion | bytes 4194304 | tf_op jit(solution)/shard_map/transpose | solution.py:457
  3.1 2.5 %copy.12 = bf16[4,128,2048]{2,1,0:T(8,128)(2,1)} copy(bf16[4,128,2048]{2,0,1:T(4,128)(2,1)S(1)} %slice_bitcast_fusion) | data formatting | bytes 4194304 | tf_op jit(solution)/shard_map/transpose | solution.py:457
  5.5 5.6 %collective-permute-start.4 = (bf16[512,2048]{1,0:T(8,128)(2,1)}, bf16[512,2048]{1,0:T(8,128)(2,1)S(1)}, u32[]{:S(2)}, u32[]{:S(2)}) collective-permute-start(bf16[512,2048]{1,0:T(8,128)(2,1)} %bitcast.3.refs_3_), channel_id=1, source_target_pairs={{0,16},{1,17},{4,20},{5,21},{8,24},{9,25},{12,28},{13,29},{18,2},{... | collective-permute-start | bytes 6291464 | tf_op jit(solution)/shard_map/ppermute | solution.py:459
  11.1 5.4 %copy.18 = bf16[4,2048,324]{1,2,0:T(8,128)(2,1)S(1)} copy(bf16[4,2048,324]{1,0,2:T(4,128)(2,1)} %param.1) | data formatting | bytes 10616832 | tf_op jit(solution)/shard_map/optimization_barrier | solution.py:458
  16.6 0.0 copy-start
  16.6 0.0 collective-permute-done
  16.6 7.4 %copy.17 = bf16[4,2048,324]{1,2,0:T(8,128)(2,1)S(1)} copy(bf16[4,2048,324]{1,0,2:T(4,128)(2,1)} %collective-permute-done) | data formatting | bytes 10616832 | tf_op jit(solution)/shard_map/optimization_barrier | solution.py:461
  23.9 5.2 %shard_map.17 = (f32[1744,256]{1,0:T(8,128)}, f32[8,128]{1,0:T(8,128)S(1)}) custom-call(s32[1]{0:T(128)} %bitcast.refs_0_, bf16[4,324,2048]{2,1,0:T(8,128)(2,1)S(1)} %bitcast.13, bf16[4,324,2048]{2,1,0:T(8,128)(2,1)S(1)} %bitcast.26, bf16[512,2048]{1,0:T(8,128)(2,1)} %bitcast.3.refs_3_), custom_call_target="tpu_custom_call" | custom-call | tf_op jit(solution)/shard_map/pallas_call | solution.py:45
  29.1 5.0 %shard_map.18 = (f32[1744,256]{1,0:T(8,128)}, f32[8,128]{1,0:T(8,128)S(1)}) custom-call(s32[1]{0:T(128)} %bitcast.refs_0_, bf16[4,324,2048]{2,1,0:T(8,128)(2,1)S(1)} %bitcast.14, bf16[4,324,2048]{2,1,0:T(8,128)(2,1)S(1)} %bitcast.27, f32[8,128]{1,0:T(8,128)S(1)} %get-tuple-element.61.refs_3_), custom_call_target="tpu_custom_call" | custom-call | tf_op jit(solution)/shard_map/pallas_call | solution.py:45
  34.2 1.5 slice.11
  35.7 2.7 %collective-permute-start.3 = (bf16[512,2048]{1,0:T(8,128)(2,1)}, bf16[512,2048]{1,0:T(8,128)(2,1)}, u32[]{:S(2)}, u32[]{:S(2)}) collective-permute-start(bf16[512,2048]{1,0:T(8,128)(2,1)} %bitcast.6), channel_id=1, source_target_pairs={{0,16},{1,17},{4,20},{5,21},{8,24},{9,25},{12,28},{13,29},{18,2},{... | collective-permute-start | bytes 6291464 | tf_op jit(solution)/shard_map/ppermute | solution.py:472
  38.4 3.6 %collective-permute-start.2 = (f32[1744,256]{1,0:T(8,128)}, f32[1744,256]{1,0:T(8,128)}, u32[]{:S(2)}, u32[]{:S(2)}) collective-permute-start(f32[1744,256]{1,0:T(8,128)} %get-tuple-element.69), channel_id=1, source_target_pairs={{0,1},{1,0},{4,5},{5,4},{8,9},{9,8},{12,13},{13,12},{18,19},{19,18... | collective-permute-start | bytes 5357576 | tf_op jit(solution)/shard_map/ppermute | solution.py:467
  42.0 0.6 collective-permute-start.1
  42.6 0.1 pad_add_fusion.refs_0_
  42.6 2.4 %slice.10 = bf16[4,68,2048]{2,1,0:T(8,128)(2,1)} slice(bf16[4,324,2048]{2,1,0:T(8,128)(2,1)} %bitcast.16), slice={[0:4], [256:324], [0:2048]} | slice | bytes 2228224 | tf_op jit(solution)/shard_map/slice | solution.py:470
  45.1 2.3 %reshape.10 = bf16[272,2048]{1,0:T(8,128)(2,1)} reshape(bf16[4,68,2048]{2,1,0:T(8,128)(2,1)} %slice.10) | data formatting | bytes 2228224 | tf_op jit(solution)/shard_map/reshape | solution.py:470
  47.3 2.5 %copy-done.1 = bf16[4,2048,324]{1,2,0:T(8,128)(2,1)S(1)} copy-done((bf16[4,2048,324]{1,2,0:T(8,128)(2,1)S(1)}, bf16[4,2048,324]{1,2,0:T(8,128)(2,1)}, u32[]{:S(2)}) %copy-start.1) | copy-done | bytes 5308440
  49.9 2.5 %copy-done.3 = bf16[4,2048,324]{1,2,0:T(8,128)(2,1)S(1)} copy-done((bf16[4,2048,324]{1,2,0:T(8,128)(2,1)S(1)}, bf16[4,2048,324]{1,2,0:T(8,128)(2,1)}, u32[]{:S(2)}) %copy-start.3) | copy-done | bytes 5308440
  52.4 7.2 %shard_map.19 = (f32[8,324,324]{2,1,0:T(8,128)S(1)}, f32[8,128]{1,0:T(8,128)S(1)}) custom-call(s32[1]{0:T(128)} %bitcast.refs_0_, bf16[4,324,2048]{2,1,0:T(8,128)(2,1)S(1)} %bitcast.17, bf16[4,324,2048]{2,1,0:T(8,128)(2,1)S(1)} %bitcast.28, f32[8,128]{1,0:T(8,128)S(1)} %get-tuple-element.66.refs_3_), custom_call_target="tpu_custom_call" | custom-call | tf_op jit(solution)/shard_map/pallas_call | solution.py:45
  59.6 0.0 collective-permute-done.4.refs_2_
  59.6 0.0 slice-done
  59.6 0.0 slice-done.1
  59.7 0.7 shard_map.20
  60.3 0.7 collective-permute-start.8
  61.1 3.1 %collective-permute-start.6 = (bf16[272,2048]{1,0:T(8,128)(2,1)S(1)}, bf16[272,2048]{1,0:T(8,128)(2,1)S(1)}, u32[]{:S(2)}, u32[]{:S(2)}) collective-permute-start(bf16[272,2048]{1,0:T(8,128)(2,1)S(1)} %copy-done.4), channel_id=1, source_target_pairs={{0,16},{1,17},{4,20},{5,21},{8,24},{9,25},{12,28},{13,29},{18,2},{... | collective-permute-start | bytes 3342344 | tf_op jit(solution)/shard_map/ppermute | solution.py:474
  64.2 0.7 shard_map.21
  64.9 0.0 collective-permute-done.3.refs_2_
  64.9 1.8 %shard_map.22 = (f32[2,4,328,128]{3,2,1,0:T(8,128)S(1)}, f32[8,128]{1,0:T(8,128)S(1)}) custom-call(s32[2]{0:T(128)S(1)} %pad_add_fusion.refs_0_, bf16[4,324,2048]{2,1,0:T(8,128)(2,1)S(1)} %bitcast.22, bf16[512,2048]{1,0:T(8,128)(2,1)} %collective-permute-done.3.refs_2_, f32[8,128]{1,0:T(8,128)S(1)} %get-tuple-element.73.refs_3_), custom_call_target="tpu_custom_call" | custom-call | tf_op jit(solution)/shard_map/pallas_call | solution.py:45
  66.7 0.7 collective-permute-start.9
  67.4 9.6 %collective-permute-done.2.refs_2_ = f32[1744,256]{1,0:T(8,128)} collective-permute-done((f32[1744,256]{1,0:T(8,128)}, f32[1744,256]{1,0:T(8,128)}, u32[]{:S(2)}, u32[]{:S(2)}) %collective-permute-start.2) | collective-permute-done | bytes 1785888 | tf_op jit(solution)/shard_map/ppermute | solution.py:467
  77.0 0.7 collective-permute-start.7
  77.8 18.4 %collective-permute-done.1.refs_4_.refs_2_ = f32[1744,256]{1,0:T(8,128)} collective-permute-done((f32[1744,256]{1,0:T(8,128)}, f32[1744,256]{1,0:T(8,128)}, u32[]{:S(2)}, u32[]{:S(2)}) %collective-permute-start.1) | collective-permute-done | bytes 1785888 | tf_op jit(solution)/shard_map/ppermute | solution.py:465
  96.2 1.9 %shard_map.23 = (f32[4,328,384]{2,1,0:T(8,128)S(1)}, f32[8,128]{1,0:T(8,128)S(1)}) custom-call(s32[1]{0:T(128)} %bitcast.refs_0_, f32[8,324,324]{2,1,0:T(8,128)S(1)} %get-tuple-element.67.refs_1_, f32[1744,256]{1,0:T(8,128)} %collective-permute-done.2.refs_2_, f32[8,128]{1,0:T(8,128)S(1)} %get-tuple-element.74.refs_3_, ...), custom_call_target="tpu_custom_call" | custom-call | tf_op jit(solution)/shard_map/pallas_call | solution.py:45
  98.0 28.2 %collective-permute-start.5 = (f32[4,328,384]{2,1,0:T(8,128)S(1)}, f32[4,328,384]{2,1,0:T(8,128)S(1)}, u32[]{:S(2)}, u32[]{:S(2)}) collective-permute-start(f32[4,328,384]{2,1,0:T(8,128)S(1)} %get-tuple-element.75.refs_3_), channel_id=1, source_target_pairs={{0,2},{1,3},{4,6},{5,7},{8,10},{9,11},{12,14},{13,15},{18,16},{19,... | collective-permute-start | bytes 6045704 | tf_op jit(solution)/shard_map/ppermute | solution.py:508
  126.3 1.8 %shard_map.24 = (f32[2,4,328,128]{3,2,1,0:T(8,128)S(1)}, f32[8,128]{1,0:T(8,128)S(1)}) custom-call(s32[2]{0:T(128)S(1)} %pad_add_fusion.refs_0_, bf16[4,324,2048]{2,1,0:T(8,128)(2,1)S(1)} %bitcast.23, bf16[512,2048]{1,0:T(8,128)(2,1)} %collective-permute-done.3.refs_2_, f32[8,128]{1,0:T(8,128)S(1)} %get-tuple-element.77.refs_3_), custom_call_target="tpu_custom_call" | custom-call | flops 10000000000 | bytes 100000000 | tf_op jit(solution)/shard_map/pallas_call | solution.py:45
  128.1 0.0 collective-permute-done.6.refs_2_
  128.1 0.7 shard_map.25
  128.8 0.7 collective-permute-start.10
  129.5 0.0 collective-permute-done.8.refs_2_
  129.5 0.0 collective-permute-done.9.refs_4_
  129.6 1.0 shard_map.26
  130.6 1.3 collective-permute-start.11
  131.9 0.0 collective-permute-done.7.refs_2_
  131.9 1.0 shard_map.27
  132.9 1.3 collective-permute-start.12
  134.2 0.0 collective-permute-done.5.refs_4_
  134.2 0.7 shard_map.28
  134.9 0.0 collective-permute-done.10.refs_2_
  134.9 0.6 shard_map.29
  135.6 0.1 shard_map.30
  135.7 1.3 collective-permute-start.15
  137.0 0.7 collective-permute-start.14
  137.7 0.7 collective-permute-start.13
  138.4 5.4 %shard_map.32 = (f32[2,324,8,324]{3,2,1,0:T(8,128)}, f32[8,128]{1,0:T(8,128)S(1)}) custom-call(s32[2]{0:T(128)S(1)} %pad_add_fusion.refs_0_, f32[8,324,324]{2,1,0:T(8,128)S(1)} %get-tuple-element.67.refs_1_, f32[1744,256]{1,0:T(8,128)} %collective-permute-done.1.refs_4_.refs_2_, f32[4,328,384]{2,1,0:T(8,128)S(1)} %get-tuple-element.75.refs_3_, ...), custom_call_target="tpu_custom_call" | custom-call | tf_op jit(solution)/shard_map/pallas_call | solution.py:45
  143.8 0.3 collective-permute-done.11.refs_2_
  144.1 2.8 %shard_map.33 = (f32[2,324,8,324]{3,2,1,0:T(8,128)}, f32[8,128]{1,0:T(8,128)S(1)}) custom-call(s32[2]{0:T(128)S(1)} %pad_add_fusion.refs_0_, f32[2,324,8,324]{3,2,1,0:T(8,128)} %get-tuple-element.95.refs_1_, bf16[2,4,328,128]{3,2,1,0:T(8,128)(2,1)S(1)} %collective-permute-done.11.refs_2_, ...), custom_call_target="tpu_custom_call", output_to_operand_aliasing={{0}: (1, {})} | custom-call | flops 10000000000 | bytes 100000000 | tf_op jit(solution)/shard_map/pallas_call | solution.py:45
  146.9 23.6 %collective-permute-done.12.refs_2_ = bf16[2,4,328,128]{3,2,1,0:T(8,128)(2,1)S(1)} collective-permute-done((bf16[2,4,328,128]{3,2,1,0:T(8,128)(2,1)S(1)}, bf16[2,4,328,128]{3,2,1,0:T(8,128)(2,1)S(1)}, u32[]{:S(2)}, u32[]{:S(2)}) %collective-permute-start.12) | collective-permute-done | bytes 671776 | tf_op jit(solution)/shard_map/ppermute | solution.py:495
  170.5 2.8 %shard_map.34 = (f32[2,324,8,324]{3,2,1,0:T(8,128)}, f32[8,128]{1,0:T(8,128)S(1)}) custom-call(s32[2]{0:T(128)S(1)} %pad_add_fusion.refs_0_, f32[2,324,8,324]{3,2,1,0:T(8,128)} %get-tuple-element.97.refs_1_, bf16[2,4,328,128]{3,2,1,0:T(8,128)(2,1)S(1)} %collective-permute-done.12.refs_2_, ...), custom_call_target="tpu_custom_call", output_to_operand_aliasing={{0}: (1, {})} | custom-call | flops 10000000000 | bytes 100000000 | tf_op jit(solution)/shard_map/pallas_call | solution.py:45
  173.2 0.0 collective-permute-done.14.refs_6_
  173.2 0.0 collective-permute-done.13.refs_5_
  173.3 0.6 shard_map.35
  173.9 1.3 collective-permute-done.15.refs_2_
  175.2 2.8 %shard_map.36 = (f32[2,324,8,324]{3,2,1,0:T(8,128)}, f32[8,128]{1,0:T(8,128)}) custom-call(s32[2]{0:T(128)S(1)} %pad_add_fusion.refs_0_, f32[2,324,8,324]{3,2,1,0:T(8,128)} %get-tuple-element.106.refs_1_, bf16[2,4,72,324]{3,2,1,0:T(8,128)(2,1)S(1)} %collective-permute-done.15.refs_2_, ...), custom_call_target="tpu_custom_call", output_to_operand_aliasing={{0}: (1, {})} | custom-call | tf_op jit(solution)/shard_map/pallas_call | solution.py:45
  (11 shorter events, 0.1 us)
Async XLA Ops:
  0.0 16.6 %collective-permute-start = (bf16[4,2048,324]{1,0,2:T(4,128)(2,1)}, bf16[4,2048,324]{1,0,2:T(4,128)(2,1)}, u32[]{:S(2)}, u32[]{:S(2)}) collective-permute-start(bf16[4,2048,324]{1,0,2:T(4,128)(2,1)} %param.1), channel_id=1, source_target_pairs={{0,2},{2,0},{4,6},{6,4},{8,10},{10,8},{12,14},{14,12},{16,18},{18,... | collective-permute-start | bytes 15925256 | tf_op jit(solution)/shard_map/ppermute | solution.py:456
  5.5 54.1 %collective-permute-start.4 = (bf16[512,2048]{1,0:T(8,128)(2,1)}, bf16[512,2048]{1,0:T(8,128)(2,1)S(1)}, u32[]{:S(2)}, u32[]{:S(2)}) collective-permute-start(bf16[512,2048]{1,0:T(8,128)(2,1)} %bitcast.3.refs_3_), channel_id=1, source_target_pairs={{0,16},{1,17},{4,20},{5,21},{8,24},{9,25},{12,28},{13,29},{18,2},{... | collective-permute-start | bytes 6291464 | tf_op jit(solution)/shard_map/ppermute | solution.py:459
  16.6 17.6 %copy-start = (bf16[4,2048,324]{1,2,0:T(8,128)(2,1)}, bf16[4,2048,324]{1,2,0:T(8,128)(2,1)S(1)}, u32[]{:S(2)}) copy-start(bf16[4,2048,324]{1,2,0:T(8,128)(2,1)S(1)} %copy.18) | copy-start | bytes 15925252
  23.9 5.2 %copy-start.2 = (bf16[4,2048,324]{1,2,0:T(8,128)(2,1)}, bf16[4,2048,324]{1,2,0:T(8,128)(2,1)S(1)}, u32[]{:S(2)}) copy-start(bf16[4,2048,324]{1,2,0:T(8,128)(2,1)S(1)} %copy.17) | copy-start | bytes 15925252
  35.7 29.2 %collective-permute-start.3 = (bf16[512,2048]{1,0:T(8,128)(2,1)}, bf16[512,2048]{1,0:T(8,128)(2,1)}, u32[]{:S(2)}, u32[]{:S(2)}) collective-permute-start(bf16[512,2048]{1,0:T(8,128)(2,1)} %bitcast.6), channel_id=1, source_target_pairs={{0,16},{1,17},{4,20},{5,21},{8,24},{9,25},{12,28},{13,29},{18,2},{... | collective-permute-start | bytes 6291464 | tf_op jit(solution)/shard_map/ppermute | solution.py:472
  38.4 38.6 %collective-permute-start.2 = (f32[1744,256]{1,0:T(8,128)}, f32[1744,256]{1,0:T(8,128)}, u32[]{:S(2)}, u32[]{:S(2)}) collective-permute-start(f32[1744,256]{1,0:T(8,128)} %get-tuple-element.69), channel_id=1, source_target_pairs={{0,1},{1,0},{4,5},{5,4},{8,9},{9,8},{12,13},{13,12},{18,19},{19,18... | collective-permute-start | bytes 5357576 | tf_op jit(solution)/shard_map/ppermute | solution.py:467
  42.0 54.2 %collective-permute-start.1 = (f32[1744,256]{1,0:T(8,128)}, f32[1744,256]{1,0:T(8,128)}, u32[]{:S(2)}, u32[]{:S(2)}) collective-permute-start(f32[1744,256]{1,0:T(8,128)} %get-tuple-element.68), channel_id=1, source_target_pairs={{0,1},{1,0},{2,3},{3,2},{4,5},{5,4},{6,7},{7,6},{8,9},{9,8},{10,11... | collective-permute-start | bytes 5357576 | tf_op jit(solution)/shard_map/ppermute | solution.py:465
  45.1 14.6 %slice-start = ((s8[5373952]{0:T(1024)(128)(4,1)}), s8[1179648]{0:T(1024)(128)(4,1)S(1)}, s32[]{:S(2)}) async-start(s8[5373952]{0:T(1024)(128)(4,1)} %bitcast.18), calls=%async_computation | async-start | bytes 2359296
  47.3 2.5 %copy-start.1 = (bf16[4,2048,324]{1,2,0:T(8,128)(2,1)S(1)}, bf16[4,2048,324]{1,2,0:T(8,128)(2,1)}, u32[]{:S(2)}) copy-start(bf16[4,2048,324]{1,2,0:T(8,128)(2,1)} %copy-done) | copy-start | bytes 15925252
  49.9 2.5 %copy-start.3 = (bf16[4,2048,324]{1,2,0:T(8,128)(2,1)S(1)}, bf16[4,2048,324]{1,2,0:T(8,128)(2,1)}, u32[]{:S(2)}) copy-start(bf16[4,2048,324]{1,2,0:T(8,128)(2,1)} %copy-done.2) | copy-start | bytes 15925252
  52.4 7.2 %slice-start.1 = ((s8[5373952]{0:T(1024)(128)(4,1)}), s8[4194304]{0:T(1024)(128)(4,1)S(1)}, s32[]{:S(2)}) async-start(s8[5373952]{0:T(1024)(128)(4,1)} %bitcast.18), calls=%async_computation.1 | async-start | bytes 8388608
  59.6 1.5 copy-start.4
  60.3 69.2 %collective-permute-start.8 = (f32[2,4,328,128]{3,2,1,0:T(8,128)S(1)}, f32[2,4,328,128]{3,2,1,0:T(8,128)S(1)}, u32[]{:S(2)}, u32[]{:S(2)}) collective-permute-start(f32[2,4,328,128]{3,2,1,0:T(8,128)S(1)} %get-tuple-element.81), channel_id=1, source_target_pairs={{2,3},{3,2},{6,7},{7,6},{10,11},{11,10},{14,15},{15,14},{16,17},{1... | collective-permute-start | bytes 4030472 | tf_op jit(solution)/shard_map/ppermute | solution.py:488
  61.1 67.0 %collective-permute-start.6 = (bf16[272,2048]{1,0:T(8,128)(2,1)S(1)}, bf16[272,2048]{1,0:T(8,128)(2,1)S(1)}, u32[]{:S(2)}, u32[]{:S(2)}) collective-permute-start(bf16[272,2048]{1,0:T(8,128)(2,1)S(1)} %copy-done.4), channel_id=1, source_target_pairs={{0,16},{1,17},{4,20},{5,21},{8,24},{9,25},{12,28},{13,29},{18,2},{... | collective-permute-start | bytes 3342344 | tf_op jit(solution)/shard_map/ppermute | solution.py:474
  66.7 62.8 %collective-permute-start.9 = (f32[8,128]{1,0:T(8,128)S(1)}, f32[8,128]{1,0:T(8,128)S(1)}, u32[]{:S(2)}, u32[]{:S(2)}) collective-permute-start(f32[8,128]{1,0:T(8,128)S(1)} %get-tuple-element.74.refs_3_), channel_id=1, source_target_pairs={{8,10},{12,14},{18,16},{22,20},{9,11},{13,15},{19,17},{23,21}} | collective-permute-start | bytes 12296 | tf_op jit(solution)/shard_map/ppermute | solution.py:506
  77.0 54.9 %collective-permute-start.7 = (f32[2,4,328,128]{3,2,1,0:T(8,128)S(1)}, f32[2,4,328,128]{3,2,1,0:T(8,128)S(1)}, u32[]{:S(2)}, u32[]{:S(2)}) collective-permute-start(f32[2,4,328,128]{3,2,1,0:T(8,128)S(1)} %get-tuple-element.79), channel_id=1, source_target_pairs={{2,3},{3,2},{6,7},{7,6},{10,11},{11,10},{14,15},{15,14},{16,17},{1... | collective-permute-start | bytes 4030472 | tf_op jit(solution)/shard_map/ppermute | solution.py:488
  98.0 36.2 %collective-permute-start.5 = (f32[4,328,384]{2,1,0:T(8,128)S(1)}, f32[4,328,384]{2,1,0:T(8,128)S(1)}, u32[]{:S(2)}, u32[]{:S(2)}) collective-permute-start(f32[4,328,384]{2,1,0:T(8,128)S(1)} %get-tuple-element.75.refs_3_), channel_id=1, source_target_pairs={{0,2},{1,3},{4,6},{5,7},{8,10},{9,11},{12,14},{13,15},{18,16},{19,... | collective-permute-start | bytes 6045704 | tf_op jit(solution)/shard_map/ppermute | solution.py:508
  128.8 6.1 %collective-permute-start.10 = (f32[2,4,72,324]{3,2,1,0:T(8,128)S(1)}, f32[2,4,72,324]{3,2,1,0:T(8,128)S(1)}, u32[]{:S(2)}, u32[]{:S(2)}) collective-permute-start(f32[2,4,72,324]{3,2,1,0:T(8,128)S(1)} %get-tuple-element.87), channel_id=1, source_target_pairs={{2,3},{3,2},{6,7},{7,6},{10,11},{11,10},{14,15},{15,14},{16,17},{1... | collective-permute-start | bytes 2239496 | tf_op jit(solution)/shard_map/ppermute | solution.py:488
  130.6 13.6 %collective-permute-start.11 = (bf16[2,4,328,128]{3,2,1,0:T(8,128)(2,1)S(1)}, bf16[2,4,328,128]{3,2,1,0:T(8,128)(2,1)S(1)}, u32[]{:S(2)}, u32[]{:S(2)}) collective-permute-start(bf16[2,4,328,128]{3,2,1,0:T(8,128)(2,1)S(1)} %get-tuple-element.90.refs_1_), channel_id=1, source_target_pairs={{16,0},{17,1},{20,4},{21,5},{24,8},{25,9},{28,12},{29,13},{2,18},{... | collective-permute-start | bytes 2015240 | tf_op jit(solution)/shard_map/ppermute | solution.py:495
  132.9 37.5 %collective-permute-start.12 = (bf16[2,4,328,128]{3,2,1,0:T(8,128)(2,1)S(1)}, bf16[2,4,328,128]{3,2,1,0:T(8,128)(2,1)S(1)}, u32[]{:S(2)}, u32[]{:S(2)}) collective-permute-start(bf16[2,4,328,128]{3,2,1,0:T(8,128)(2,1)S(1)} %get-tuple-element.91.refs_2_), channel_id=1, source_target_pairs={{16,0},{17,1},{20,4},{21,5},{24,8},{25,9},{28,12},{29,13},{2,18},{... | collective-permute-start | bytes 2015240 | tf_op jit(solution)/shard_map/ppermute | solution.py:495
  135.7 39.6 %collective-permute-start.15 = (bf16[2,4,72,324]{3,2,1,0:T(8,128)(2,1)S(1)}, bf16[2,4,72,324]{3,2,1,0:T(8,128)(2,1)S(1)}, u32[]{:S(2)}, u32[]{:S(2)}) collective-permute-start(bf16[2,4,72,324]{3,2,1,0:T(8,128)(2,1)S(1)} %get-tuple-element.89.refs_1_), channel_id=1, source_target_pairs={{16,0},{17,1},{20,4},{21,5},{24,8},{25,9},{28,12},{29,13},{2,18},{... | collective-permute-start | bytes 1119752 | tf_op jit(solution)/shard_map/ppermute | solution.py:495
  137.0 36.2 %collective-permute-start.14 = (bf16[1,2,2,72,324]{4,3,2,1,0:T(8,128)(2,1)S(1)}, bf16[1,2,2,72,324]{4,3,2,1,0:T(8,128)(2,1)S(1)}, u32[]{:S(2)}, u32[]{:S(2)}) collective-permute-start(bf16[1,2,2,72,324]{4,3,2,1,0:T(8,128)(2,1)S(1)} %get-tuple-element.104), channel_id=1, source_target_pairs={{2,3},{3,2},{6,7},{7,6},{10,11},{11,10},{14,15},{15,14},{16,17},{1... | collective-permute-start | bytes 559880 | tf_op jit(solution)/shard_map/ppermute | solution.py:500
  137.7 35.6 %collective-permute-start.13 = (bf16[2,2,2,328,128]{4,3,2,1,0:T(8,128)(2,1)S(1)}, bf16[2,2,2,328,128]{4,3,2,1,0:T(8,128)(2,1)S(1)}, u32[]{:S(2)}, u32[]{:S(2)}) collective-permute-start(bf16[2,2,2,328,128]{4,3,2,1,0:T(8,128)(2,1)S(1)} %get-tuple-element.103), channel_id=1, source_target_pairs={{2,3},{3,2},{6,7},{7,6},{10,11},{11,10},{14,15},{15,14},{16,17},{1... | collective-permute-start | bytes 2015240 | tf_op jit(solution)/shard_map/ppermute | solution.py:500

commit v15 on v14

--- a/solution.py
+++ b/solution.py
@@ -146,21 +146,45 @@
     )(det, own, partner)
 
 
-def near_share(det, keep, doubled, states, after=()):
+def near_share(place_in, keep, doubled, states, after=()):
     _, ops, _ = keep.shape
     half, tiles = states // 2, (states // 2) ** 2
     packing = Packing(tiles, ops)
     shape = (tiles, up(ops, 8), up(ops, LANES))
 
-    def body(x_ref, keep_ref, wire_ref, tile_ref):
-        for t in range(tiles):
-            kept = t // half * states + half * x_ref[0] + t % half
-            for rows, columns, values in packing.parts(wire_ref, t):
-                tile_ref[t, rows, columns] = keep_ref[kept, rows, columns] + values
-
-    return call(
-        body, (1,), 1, [whole(keep.shape), whole(packing.shape)], [whole(shape)], [f32(*shape)], after
-    )(det, keep, doubled)
+    def body(s_ref, keep_ref, wire_in, out_ref, kept, wire, made, sems):
+        @pl.when(s_ref[1] == 0)
+        def _():
+            loads = [pltpu.make_async_copy(wire_in, wire, sems.at[0])]
+            for a in range(half):
+                mine = keep_ref.at[pl.ds(a * states + half * s_ref[0], half)]
+                loads.append(pltpu.make_async_copy(mine, kept.at[pl.ds(a * half, half)], sems.at[1 + a]))
+            for load in loads:
+                load.start()
+            for load in loads:
+                load.wait()
+            for t in range(tiles):
+                for rows, columns, values in packing.parts(wire, t):
+                    made[t, rows, columns] = kept[t, rows, columns] + values
+            store = pltpu.make_async_copy(made, out_ref, sems.at[0])
+            store.start()
+            store.wait()
+
+    return call(
+        body,
+        (1,),
+        1,
+        [pl.BlockSpec(memory_space=pl.ANY)] * 2,
+        [pl.BlockSpec(memory_space=pl.ANY)],
+        [f32(*shape)],
+        after,
+        scratch=[
+            pltpu.VMEM((tiles, ops, ops), jnp.float32),
+            pltpu.VMEM(packing.shape, jnp.float32),
+            pltpu.VMEM(shape, jnp.float32),
+            pltpu.SemaphoreType.DMA((1 + half,)),
+        ],
+    )(place_in, keep, doubled)
 
 
 def near_sum(place_in, keep, crossed, share, given, states, after=()):
@@ -310,7 +334,7 @@
     )(det, keep, came)
 
 
-def crossing_codes(det, codes, after=()):
+def crossing_codes(det, codes, after=(), declared=0):
     half, states, *tile = codes[0].shape
     shape = (len(codes), half, half, *tile)
 
@@ -326,6 +350,7 @@
         [whole(shape)],
         [jax.ShapeDtypeStruct(shape, jnp.bfloat16)],
         after,
+        declared=declared,
     )(det, *codes)
 
 
@@ -495,8 +520,8 @@
         theirs[k] = lax.ppermute(codes[k], both, back)
         return token
 
-    def cross(ks, token):
-        wire, token = crossing_codes(det, [codes[k] for k in ks], (token,))
+    def cross(ks, *token):
+        wire, token = crossing_codes(det, [codes[k] for k in ks], token, 3 * LONG if ks == early else 0)
         return lax.ppermute(wire, both, across), token
 
     early, late = list(range(full)), [full]
@@ -504,16 +529,16 @@
         token = send_terms(k, token)
         if k == full - 1:
             gate = lax.ppermute(token, "state", opens)
-            share, token = near_share(det, keep, doubled, states, (token, crossed))
-            given = lax.ppermute(share, both, to_second)
-        token = keep_terms(k, token)
+        token = keep_terms(k, token, *([crossed, doubled] if k == full - 1 else []))
     token = send_terms(full, token)
     for k in early:
         token = sum_up(k, token, *([gate] if k == 0 else []))
-    token = keep_terms(full, token, given)
+    token = keep_terms(full, token)
     token = sum_up(full, token)
+    share, token = near_share(at, keep, doubled, states, (token,))
+    given = lax.ppermute(share, both, to_second)
     turned, token = cross(early, token)
-    last, token = cross(late, token)
+    last, token = cross(late, token, given)
     out, token = near_sum(at, keep, crossed, share, given, states, (token,))
 
     for k in early:

time: 179 us -> 179 us (level)
  the two profiles are of different devices: /device:TPU:0 before, /device:TPU:11 now
where the time goes in v15:
time: 179 us; the launch traced here: 178 us
  Pallas kernels  57.3 us (32%)
  starting transfers between devices  45.9 us (26%)
  waiting for transfers between devices  45 us (25%)
  local copies, waits for them, and re-layouts  29.1 us (16%)
    pallas_call x20, Pallas kernels, call(): return lambda *operands: kernel(*operands, *after)  57.3 us
    ppermute x3, waiting for transfers between devices, send_terms(): came[k] = lax.ppermute(send, both, across)  25.7 us
    ppermute x3, starting transfers between devices, sum_up(): theirs[k] = lax.ppermute(codes[k], both, back)  23.9 us
    ppermute x1, waiting for transfers between devices, paired(): gate = lax.ppermute(token, 'state', opens)  17.4 us
    ppermute x3, starting transfers between devices, send_terms(): came[k] = lax.ppermute(send, both, across)  7.44 us
    optimization_barrier x1, local copies, waits for them, and re-layouts, paired(): partner, own = lax.optimization_barrier((partner, own))  7.35 us
    optimization_barrier x1, local copies, waits for them, and re-layouts, paired(): lax.optimization_barrier((first.reshape(states * LANES, depth), amplitudes))  5.41 us
    ppermute x2, starting transfers between devices, cross(): return (lax.ppermute(wire, both, across), token)  5.28 us
  transfers between devices with their start and end apart: 16, of which 7 were waited for; matrix products, arithmetic and copies ran while one was open for 14% of the time, Pallas kernels for 32%

profile of v15, /device:TPU:11, one launch (start us, length us, event | category | flops | bytes accessed | tf_op | source)
XLA Modules:
  0.0 178.0 jit_solution(15907417341379644513)
XLA Ops:
  0.0 0.7 collective-permute-start
  0.7 2.6 %slice_bitcast_fusion = bf16[4,128,2048]{2,0,1:T(4,128)(2,1)S(1)} fusion(bf16[4,2048,324]{1,0,2:T(4,128)(2,1)} %param.1), kind=kLoop, calls=%fused_computation.2 | loop fusion | bytes 4194304 | tf_op jit(solution)/shard_map/transpose | solution.py:482
  3.3 2.5 %copy.12 = bf16[4,128,2048]{2,1,0:T(8,128)(2,1)} copy(bf16[4,128,2048]{2,0,1:T(4,128)(2,1)S(1)} %slice_bitcast_fusion) | data formatting | bytes 4194304 | tf_op jit(solution)/shard_map/transpose | solution.py:482
  5.7 1.3 collective-permute-start.5
  7.0 5.4 %copy.18 = bf16[4,2048,324]{1,2,0:T(8,128)(2,1)S(1)} copy(bf16[4,2048,324]{1,0,2:T(4,128)(2,1)} %param.1) | data formatting | bytes 10616832 | tf_op jit(solution)/shard_map/optimization_barrier | solution.py:483
  12.4 0.0 copy-start
  12.5 0.0 collective-permute-done
  12.5 7.4 %copy.17 = bf16[4,2048,324]{1,2,0:T(8,128)(2,1)S(1)} copy(bf16[4,2048,324]{1,0,2:T(4,128)(2,1)} %collective-permute-done) | data formatting | bytes 10616832 | tf_op jit(solution)/shard_map/optimization_barrier | solution.py:486
  19.8 0.0 copy-start.2
  19.8 5.2 %shard_map.17 = (f32[1744,256]{1,0:T(8,128)}, f32[8,128]{1,0:T(8,128)S(1)}) custom-call(s32[1]{0:T(128)} %bitcast.refs_0_, bf16[4,324,2048]{2,1,0:T(8,128)(2,1)S(1)} %bitcast.13, bf16[4,324,2048]{2,1,0:T(8,128)(2,1)S(1)} %bitcast.26, bf16[512,2048]{1,0:T(8,128)(2,1)} %bitcast.3.refs_3_), custom_call_target="tpu_custom_call" | custom-call | tf_op jit(solution)/shard_map/pallas_call | solution.py:45
  25.0 5.0 %shard_map.18 = (f32[1744,256]{1,0:T(8,128)}, f32[8,128]{1,0:T(8,128)S(1)}) custom-call(s32[1]{0:T(128)} %bitcast.refs_0_, bf16[4,324,2048]{2,1,0:T(8,128)(2,1)S(1)} %bitcast.14, bf16[4,324,2048]{2,1,0:T(8,128)(2,1)S(1)} %bitcast.27, f32[8,128]{1,0:T(8,128)S(1)} %get-tuple-element.61.refs_3_), custom_call_target="tpu_custom_call" | custom-call | tf_op jit(solution)/shard_map/pallas_call | solution.py:45
  30.0 1.5 slice.11
  31.6 1.3 collective-permute-start.4
  32.9 1.9 %collective-permute-start.2 = (f32[1744,256]{1,0:T(8,128)}, f32[1744,256]{1,0:T(8,128)}, u32[]{:S(2)}, u32[]{:S(2)}) collective-permute-start(f32[1744,256]{1,0:T(8,128)} %get-tuple-element.69), channel_id=1, source_target_pairs={{0,1},{1,0},{4,5},{5,4},{8,9},{9,8},{12,13},{13,12},{18,19},{19,18... | collective-permute-start | bytes 5357576 | tf_op jit(solution)/shard_map/ppermute | solution.py:492
  34.8 0.2 collective-permute-start.1
  35.1 0.1 pad_add_fusion.refs_0_
  35.1 2.4 %slice.10 = bf16[4,68,2048]{2,1,0:T(8,128)(2,1)} slice(bf16[4,324,2048]{2,1,0:T(8,128)(2,1)} %bitcast.16), slice={[0:4], [256:324], [0:2048]} | slice | bytes 2228224 | tf_op jit(solution)/shard_map/slice | solution.py:495
  37.6 2.3 %reshape.10 = bf16[272,2048]{1,0:T(8,128)(2,1)} reshape(bf16[4,68,2048]{2,1,0:T(8,128)(2,1)} %slice.10) | data formatting | bytes 2228224 | tf_op jit(solution)/shard_map/reshape | solution.py:495
  39.8 2.5 %copy-done.1 = bf16[4,2048,324]{1,2,0:T(8,128)(2,1)S(1)} copy-done((bf16[4,2048,324]{1,2,0:T(8,128)(2,1)S(1)}, bf16[4,2048,324]{1,2,0:T(8,128)(2,1)}, u32[]{:S(2)}) %copy-start.1) | copy-done | bytes 5308440
  42.4 2.5 %copy-done.3 = bf16[4,2048,324]{1,2,0:T(8,128)(2,1)S(1)} copy-done((bf16[4,2048,324]{1,2,0:T(8,128)(2,1)S(1)}, bf16[4,2048,324]{1,2,0:T(8,128)(2,1)}, u32[]{:S(2)}) %copy-start.3) | copy-done | bytes 5308440
  44.9 7.2 %shard_map.19 = (f32[8,324,324]{2,1,0:T(8,128)S(1)}, f32[8,128]{1,0:T(8,128)S(1)}) custom-call(s32[1]{0:T(128)} %bitcast.refs_0_, bf16[4,324,2048]{2,1,0:T(8,128)(2,1)S(1)} %bitcast.17, bf16[4,324,2048]{2,1,0:T(8,128)(2,1)S(1)} %bitcast.28, f32[8,128]{1,0:T(8,128)S(1)} %get-tuple-element.66.refs_3_), custom_call_target="tpu_custom_call" | custom-call | tf_op jit(solution)/shard_map/pallas_call | solution.py:45
  52.1 0.0 collective-permute-done.5.refs_2_
  52.2 3.0 %shard_map.20 = (f32[2,4,328,128]{3,2,1,0:T(8,128)S(1)}, f32[8,128]{1,0:T(8,128)S(1)}) custom-call(s32[2]{0:T(128)S(1)} %pad_add_fusion.refs_0_, bf16[4,324,2048]{2,1,0:T(8,128)(2,1)S(1)} %bitcast.20, bf16[512,2048]{1,0:T(8,128)(2,1)S(1)} %collective-permute-done.5.refs_2_, f32[8,128]{1,0:T(8,128)S(1)} %get-tuple-element.72.refs_3_), custom_call_target="tpu_custom_call" | custom-call | tf_op jit(solution)/shard_map/pallas_call | solution.py:45
  55.1 3.1 %collective-permute-start.7 = (f32[2,4,328,128]{3,2,1,0:T(8,128)S(1)}, f32[2,4,328,128]{3,2,1,0:T(8,128)S(1)}, u32[]{:S(2)}, u32[]{:S(2)}) collective-permute-start(f32[2,4,328,128]{3,2,1,0:T(8,128)S(1)} %get-tuple-element.79), channel_id=1, source_target_pairs={{2,3},{3,2},{6,7},{7,6},{10,11},{11,10},{14,15},{15,14},{16,17},{1... | collective-permute-start | bytes 4030472 | tf_op jit(solution)/shard_map/ppermute | solution.py:513
  58.3 0.0 copy-done.4
  58.3 1.3 collective-permute-start.3
  59.6 3.0 %shard_map.21 = (f32[2,4,328,128]{3,2,1,0:T(8,128)S(1)}, f32[8,128]{1,0:T(8,128)S(1)}) custom-call(s32[2]{0:T(128)S(1)} %pad_add_fusion.refs_0_, bf16[4,324,2048]{2,1,0:T(8,128)(2,1)S(1)} %bitcast.21, bf16[512,2048]{1,0:T(8,128)(2,1)S(1)} %collective-permute-done.5.refs_2_, f32[8,128]{1,0:T(8,128)S(1)} %get-tuple-element.73.refs_3_), custom_call_target="tpu_custom_call" | custom-call | tf_op jit(solution)/shard_map/pallas_call | solution.py:45
  62.5 0.0 collective-permute-done.4.refs_2_
  62.5 4.2 %shard_map.22 = (f32[2,4,328,128]{3,2,1,0:T(8,128)S(1)}, f32[8,128]{1,0:T(8,128)S(1)}) custom-call(s32[2]{0:T(128)S(1)} %pad_add_fusion.refs_0_, bf16[4,324,2048]{2,1,0:T(8,128)(2,1)S(1)} %bitcast.22, bf16[512,2048]{1,0:T(8,128)(2,1)} %collective-permute-done.4.refs_2_, f32[8,128]{1,0:T(8,128)S(1)} %get-tuple-element.74.refs_3_), custom_call_target="tpu_custom_call" | custom-call | tf_op jit(solution)/shard_map/pallas_call | solution.py:45
  66.7 1.3 collective-permute-start.8
  68.0 0.0 collective-permute-done.2.refs_5_.refs_2_
  68.1 2.2 %collective-permute-start.6 = (f32[2,4,328,128]{3,2,1,0:T(8,128)S(1)}, f32[2,4,328,128]{3,2,1,0:T(8,128)S(1)}, u32[]{:S(2)}, u32[]{:S(2)}) collective-permute-start(f32[2,4,328,128]{3,2,1,0:T(8,128)S(1)} %get-tuple-element.77), channel_id=1, source_target_pairs={{2,3},{3,2},{6,7},{7,6},{10,11},{11,10},{14,15},{15,14},{16,17},{1... | collective-permute-start | bytes 4030472 | tf_op jit(solution)/shard_map/ppermute | solution.py:513
  70.2 0.7 collective-permute-done.1.refs_4_.refs_2_
  70.9 4.2 %shard_map.23 = (f32[2,4,328,128]{3,2,1,0:T(8,128)S(1)}, f32[8,128]{1,0:T(8,128)S(1)}) custom-call(s32[2]{0:T(128)S(1)} %pad_add_fusion.refs_0_, bf16[4,324,2048]{2,1,0:T(8,128)(2,1)S(1)} %bitcast.23, bf16[512,2048]{1,0:T(8,128)(2,1)} %collective-permute-done.4.refs_2_, f32[8,128]{1,0:T(8,128)S(1)} %get-tuple-element.75.refs_3_, ...), custom_call_target="tpu_custom_call" | custom-call | flops 10000000000 | bytes 100000000 | tf_op jit(solution)/shard_map/pallas_call | solution.py:45
  75.1 0.4 collective-permute-done.3.refs_2_
  75.5 3.7 %shard_map.24 = (f32[2,4,72,324]{3,2,1,0:T(8,128)S(1)}, f32[8,128]{1,0:T(8,128)S(1)}) custom-call(s32[2]{0:T(128)S(1)} %pad_add_fusion.refs_0_, bf16[4,324,2048]{2,1,0:T(8,128)(2,1)S(1)} %bitcast.24, bf16[272,2048]{1,0:T(8,128)(2,1)S(1)} %collective-permute-done.3.refs_2_, f32[8,128]{1,0:T(8,128)S(1)} %get-tuple-element.80.refs_3_), custom_call_target="tpu_custom_call" | custom-call | tf_op jit(solution)/shard_map/pallas_call | solution.py:45
  79.3 2.2 %collective-permute-start.9 = (f32[2,4,72,324]{3,2,1,0:T(8,128)S(1)}, f32[2,4,72,324]{3,2,1,0:T(8,128)S(1)}, u32[]{:S(2)}, u32[]{:S(2)}) collective-permute-start(f32[2,4,72,324]{3,2,1,0:T(8,128)S(1)} %get-tuple-element.85), channel_id=1, source_target_pairs={{2,3},{3,2},{6,7},{7,6},{10,11},{11,10},{14,15},{15,14},{16,17},{1... | collective-permute-start | bytes 2239496 | tf_op jit(solution)/shard_map/ppermute | solution.py:513
  81.4 18.3 %collective-permute-done.7.refs_2_ = f32[2,4,328,128]{3,2,1,0:T(8,128)S(1)} collective-permute-done((f32[2,4,328,128]{3,2,1,0:T(8,128)S(1)}, f32[2,4,328,128]{3,2,1,0:T(8,128)S(1)}, u32[]{:S(2)}, u32[]{:S(2)}) %collective-permute-start.7) | collective-permute-done | bytes 1343520 | tf_op jit(solution)/shard_map/ppermute | solution.py:513
  99.7 17.4 %collective-permute-done.8.refs_4_ = f32[8,128]{1,0:T(8,128)S(1)} collective-permute-done((f32[8,128]{1,0:T(8,128)S(1)}, f32[8,128]{1,0:T(8,128)S(1)}, u32[]{:S(2)}, u32[]{:S(2)}) %collective-permute-start.8) | collective-permute-done | bytes 4128 | tf_op jit(solution)/shard_map/ppermute | solution.py:531
  117.1 1.0 shard_map.25
  118.2 1.3 collective-permute-start.11
  119.5 4.1 %collective-permute-done.6.refs_2_ = f32[2,4,328,128]{3,2,1,0:T(8,128)S(1)} collective-permute-done((f32[2,4,328,128]{3,2,1,0:T(8,128)S(1)}, f32[2,4,328,128]{3,2,1,0:T(8,128)S(1)}, u32[]{:S(2)}, u32[]{:S(2)}) %collective-permute-start.6) | collective-permute-done | bytes 1343520 | tf_op jit(solution)/shard_map/ppermute | solution.py:513
  123.6 1.1 shard_map.26
  124.7 1.3 collective-permute-start.12
  126.0 3.7 %shard_map.27 = (f32[2,4,72,324]{3,2,1,0:T(8,128)S(1)}, f32[8,128]{1,0:T(8,128)S(1)}) custom-call(s32[2]{0:T(128)S(1)} %pad_add_fusion.refs_0_, bf16[4,324,2048]{2,1,0:T(8,128)(2,1)S(1)} %bitcast.25, bf16[272,2048]{1,0:T(8,128)(2,1)S(1)} %collective-permute-done.3.refs_2_, f32[8,128]{1,0:T(8,128)S(1)} %get-tuple-element.83.refs_3_), custom_call_target="tpu_custom_call" | custom-call | tf_op jit(solution)/shard_map/pallas_call | solution.py:45
  129.8 3.3 %collective-permute-done.9.refs_2_ = f32[2,4,72,324]{3,2,1,0:T(8,128)S(1)} collective-permute-done((f32[2,4,72,324]{3,2,1,0:T(8,128)S(1)}, f32[2,4,72,324]{3,2,1,0:T(8,128)S(1)}, u32[]{:S(2)}, u32[]{:S(2)}) %collective-permute-start.9) | collective-permute-done | bytes 746528 | tf_op jit(solution)/shard_map/ppermute | solution.py:513
  133.1 0.6 shard_map.28
  133.7 0.6 shard_map.29
  134.3 1.3 collective-permute-start.10
  135.6 0.1 shard_map.30
  135.7 21.2 %collective-permute-start.15 = (bf16[2,4,72,324]{3,2,1,0:T(8,128)(2,1)S(1)}, bf16[2,4,72,324]{3,2,1,0:T(8,128)(2,1)S(1)}, u32[]{:S(2)}, u32[]{:S(2)}) collective-permute-start(bf16[2,4,72,324]{3,2,1,0:T(8,128)(2,1)S(1)} %get-tuple-element.89.refs_1_), channel_id=1, source_target_pairs={{16,0},{17,1},{20,4},{21,5},{24,8},{25,9},{28,12},{29,13},{2,18},{... | collective-permute-start | bytes 1119752 | tf_op jit(solution)/shard_map/ppermute | solution.py:520
  156.9 2.2 %collective-permute-start.13 = (bf16[2,2,2,328,128]{4,3,2,1,0:T(8,128)(2,1)S(1)}, bf16[2,2,2,328,128]{4,3,2,1,0:T(8,128)(2,1)S(1)}, u32[]{:S(2)}, u32[]{:S(2)}) collective-permute-start(bf16[2,2,2,328,128]{4,3,2,1,0:T(8,128)(2,1)S(1)} %get-tuple-element.103), channel_id=1, source_target_pairs={{2,3},{3,2},{6,7},{7,6},{10,11},{11,10},{14,15},{15,14},{16,17},{1... | collective-permute-start | bytes 2015240 | tf_op jit(solution)/shard_map/ppermute | solution.py:525
  159.1 0.0 collective-permute-done.10.refs_3_.refs_4_
  159.2 3.1 %collective-permute-start.14 = (bf16[1,2,2,72,324]{4,3,2,1,0:T(8,128)(2,1)S(1)}, bf16[1,2,2,72,324]{4,3,2,1,0:T(8,128)(2,1)S(1)}, u32[]{:S(2)}, u32[]{:S(2)}) collective-permute-start(bf16[1,2,2,72,324]{4,3,2,1,0:T(8,128)(2,1)S(1)} %get-tuple-element.104), channel_id=1, source_target_pairs={{2,3},{3,2},{6,7},{7,6},{10,11},{11,10},{14,15},{15,14},{16,17},{1... | collective-permute-start | bytes 559880 | tf_op jit(solution)/shard_map/ppermute | solution.py:525
  162.3 6.6 %shard_map.32 = (f32[2,324,8,324]{3,2,1,0:T(8,128)}, f32[8,128]{1,0:T(8,128)S(1)}) custom-call(s32[2]{0:T(128)S(1)} %pad_add_fusion.refs_0_, f32[8,324,324]{2,1,0:T(8,128)S(1)} %get-tuple-element.67.refs_1_, f32[1744,256]{1,0:T(8,128)} %collective-permute-done.1.refs_4_.refs_2_, f32[4,328,384]{2,1,0:T(8,128)S(1)} %get-tuple-element.88.refs_3_, ...), custom_call_target="tpu_custom_call" | custom-call | tf_op jit(solution)/shard_map/pallas_call | solution.py:45
  168.9 0.0 collective-permute-done.11.refs_2_
  168.9 0.6 shard_map.33
  169.5 0.0 collective-permute-done.12.refs_2_
  169.5 0.6 shard_map.34
  170.1 0.0 collective-permute-done.13.refs_5_
  170.1 0.7 collective-permute-done.14.refs_6_
  170.8 5.8 %shard_map.35 = (f32[2,324,8,324]{3,2,1,0:T(8,128)}, f32[8,128]{1,0:T(8,128)S(1)}) custom-call(s32[2]{0:T(128)S(1)} %pad_add_fusion.refs_0_, f32[2,324,8,324]{3,2,1,0:T(8,128)} %get-tuple-element.99.refs_1_, f32[2,2,324,128]{3,2,1,0:T(8,128)S(1)} %get-tuple-element.100.refs_2_, ...), custom_call_target="tpu_custom_call", output_to_operand_aliasing={{0}: (1, {})} | custom-call | flops 10000000000 | bytes 100000000 | tf_op jit(solution)/shard_map/pallas_call | solution.py:45
  176.6 0.0 collective-permute-done.15.refs_2_
  176.6 1.2 shard_map.36
  (11 shorter events, 0.1 us)
Async XLA Ops:
  0.0 12.5 %collective-permute-start = (bf16[4,2048,324]{1,0,2:T(4,128)(2,1)}, bf16[4,2048,324]{1,0,2:T(4,128)(2,1)}, u32[]{:S(2)}, u32[]{:S(2)}) collective-permute-start(bf16[4,2048,324]{1,0,2:T(4,128)(2,1)} %param.1), channel_id=1, source_target_pairs={{0,2},{2,0},{4,6},{6,4},{8,10},{10,8},{12,14},{14,12},{16,18},{18,... | collective-permute-start | bytes 15925256 | tf_op jit(solution)/shard_map/ppermute | solution.py:481
  5.7 46.4 %collective-permute-start.5 = (bf16[512,2048]{1,0:T(8,128)(2,1)}, bf16[512,2048]{1,0:T(8,128)(2,1)S(1)}, u32[]{:S(2)}, u32[]{:S(2)}) collective-permute-start(bf16[512,2048]{1,0:T(8,128)(2,1)} %bitcast.3.refs_3_), channel_id=1, source_target_pairs={{0,16},{1,17},{4,20},{5,21},{8,24},{9,25},{12,28},{13,29},{18,2},{... | collective-permute-start | bytes 6291464 | tf_op jit(solution)/shard_map/ppermute | solution.py:484
  12.4 17.6 %copy-start = (bf16[4,2048,324]{1,2,0:T(8,128)(2,1)}, bf16[4,2048,324]{1,2,0:T(8,128)(2,1)S(1)}, u32[]{:S(2)}) copy-start(bf16[4,2048,324]{1,2,0:T(8,128)(2,1)S(1)} %copy.18) | copy-start | bytes 15925252
  19.8 5.2 %copy-start.2 = (bf16[4,2048,324]{1,2,0:T(8,128)(2,1)}, bf16[4,2048,324]{1,2,0:T(8,128)(2,1)S(1)}, u32[]{:S(2)}) copy-start(bf16[4,2048,324]{1,2,0:T(8,128)(2,1)S(1)} %copy.17) | copy-start | bytes 15925252
  31.6 30.9 %collective-permute-start.4 = (bf16[512,2048]{1,0:T(8,128)(2,1)}, bf16[512,2048]{1,0:T(8,128)(2,1)}, u32[]{:S(2)}, u32[]{:S(2)}) collective-permute-start(bf16[512,2048]{1,0:T(8,128)(2,1)} %bitcast.6), channel_id=1, source_target_pairs={{0,16},{1,17},{4,20},{5,21},{8,24},{9,25},{12,28},{13,29},{18,2},{... | collective-permute-start | bytes 6291464 | tf_op jit(solution)/shard_map/ppermute | solution.py:497
  32.9 35.2 %collective-permute-start.2 = (f32[1744,256]{1,0:T(8,128)}, f32[1744,256]{1,0:T(8,128)}, u32[]{:S(2)}, u32[]{:S(2)}) collective-permute-start(f32[1744,256]{1,0:T(8,128)} %get-tuple-element.69), channel_id=1, source_target_pairs={{0,1},{1,0},{4,5},{5,4},{8,9},{9,8},{12,13},{13,12},{18,19},{19,18... | collective-permute-start | bytes 5357576 | tf_op jit(solution)/shard_map/ppermute | solution.py:492
  34.8 36.1 %collective-permute-start.1 = (f32[1744,256]{1,0:T(8,128)}, f32[1744,256]{1,0:T(8,128)}, u32[]{:S(2)}, u32[]{:S(2)}) collective-permute-start(f32[1744,256]{1,0:T(8,128)} %get-tuple-element.68), channel_id=1, source_target_pairs={{0,1},{1,0},{2,3},{3,2},{4,5},{5,4},{6,7},{7,6},{8,9},{9,8},{10,11... | collective-permute-start | bytes 5357576 | tf_op jit(solution)/shard_map/ppermute | solution.py:490
  37.6 14.6 %slice-start = ((s8[5373952]{0:T(1024)(128)(4,1)}), s8[1179648]{0:T(1024)(128)(4,1)S(1)}, s32[]{:S(2)}) async-start(s8[5373952]{0:T(1024)(128)(4,1)} %bitcast.18), calls=%async_computation | async-start | bytes 2359296
  39.8 2.5 %copy-start.1 = (bf16[4,2048,324]{1,2,0:T(8,128)(2,1)S(1)}, bf16[4,2048,324]{1,2,0:T(8,128)(2,1)}, u32[]{:S(2)}) copy-start(bf16[4,2048,324]{1,2,0:T(8,128)(2,1)} %copy-done) | copy-start | bytes 15925252
  42.4 2.5 %copy-start.3 = (bf16[4,2048,324]{1,2,0:T(8,128)(2,1)S(1)}, bf16[4,2048,324]{1,2,0:T(8,128)(2,1)}, u32[]{:S(2)}) copy-start(bf16[4,2048,324]{1,2,0:T(8,128)(2,1)} %copy-done.2) | copy-start | bytes 15925252
  44.9 7.2 %slice-start.1 = ((s8[5373952]{0:T(1024)(128)(4,1)}), s8[4194304]{0:T(1024)(128)(4,1)S(1)}, s32[]{:S(2)}) async-start(s8[5373952]{0:T(1024)(128)(4,1)} %bitcast.18), calls=%async_computation.1 | async-start | bytes 8388608
  52.1 6.1 %copy-start.4 = (bf16[272,2048]{1,0:T(8,128)(2,1)S(1)}, bf16[272,2048]{1,0:T(8,128)(2,1)}, u32[]{:S(2)}) copy-start(bf16[272,2048]{1,0:T(8,128)(2,1)} %reshape.10) | copy-start | bytes 3342340
  55.1 44.6 %collective-permute-start.7 = (f32[2,4,328,128]{3,2,1,0:T(8,128)S(1)}, f32[2,4,328,128]{3,2,1,0:T(8,128)S(1)}, u32[]{:S(2)}, u32[]{:S(2)}) collective-permute-start(f32[2,4,328,128]{3,2,1,0:T(8,128)S(1)} %get-tuple-element.79), channel_id=1, source_target_pairs={{2,3},{3,2},{6,7},{7,6},{10,11},{11,10},{14,15},{15,14},{16,17},{1... | collective-permute-start | bytes 4030472 | tf_op jit(solution)/shard_map/ppermute | solution.py:513
  58.3 17.2 %collective-permute-start.3 = (bf16[272,2048]{1,0:T(8,128)(2,1)S(1)}, bf16[272,2048]{1,0:T(8,128)(2,1)S(1)}, u32[]{:S(2)}, u32[]{:S(2)}) collective-permute-start(bf16[272,2048]{1,0:T(8,128)(2,1)S(1)} %copy-done.4), channel_id=1, source_target_pairs={{0,16},{1,17},{4,20},{5,21},{8,24},{9,25},{12,28},{13,29},{18,2},{... | collective-permute-start | bytes 3342344 | tf_op jit(solution)/shard_map/ppermute | solution.py:499
  66.7 50.4 %collective-permute-start.8 = (f32[8,128]{1,0:T(8,128)S(1)}, f32[8,128]{1,0:T(8,128)S(1)}, u32[]{:S(2)}, u32[]{:S(2)}) collective-permute-start(f32[8,128]{1,0:T(8,128)S(1)} %get-tuple-element.75.refs_3_), channel_id=1, source_target_pairs={{8,10},{12,14},{18,16},{22,20},{9,11},{13,15},{19,17},{23,21}} | collective-permute-start | bytes 12296 | tf_op jit(solution)/shard_map/ppermute | solution.py:531
  68.1 55.6 %collective-permute-start.6 = (f32[2,4,328,128]{3,2,1,0:T(8,128)S(1)}, f32[2,4,328,128]{3,2,1,0:T(8,128)S(1)}, u32[]{:S(2)}, u32[]{:S(2)}) collective-permute-start(f32[2,4,328,128]{3,2,1,0:T(8,128)S(1)} %get-tuple-element.77), channel_id=1, source_target_pairs={{2,3},{3,2},{6,7},{7,6},{10,11},{11,10},{14,15},{15,14},{16,17},{1... | collective-permute-start | bytes 4030472 | tf_op jit(solution)/shard_map/ppermute | solution.py:513
  79.3 53.9 %collective-permute-start.9 = (f32[2,4,72,324]{3,2,1,0:T(8,128)S(1)}, f32[2,4,72,324]{3,2,1,0:T(8,128)S(1)}, u32[]{:S(2)}, u32[]{:S(2)}) collective-permute-start(f32[2,4,72,324]{3,2,1,0:T(8,128)S(1)} %get-tuple-element.85), channel_id=1, source_target_pairs={{2,3},{3,2},{6,7},{7,6},{10,11},{11,10},{14,15},{15,14},{16,17},{1... | collective-permute-start | bytes 2239496 | tf_op jit(solution)/shard_map/ppermute | solution.py:513
  118.2 50.7 %collective-permute-start.11 = (bf16[2,4,328,128]{3,2,1,0:T(8,128)(2,1)S(1)}, bf16[2,4,328,128]{3,2,1,0:T(8,128)(2,1)S(1)}, u32[]{:S(2)}, u32[]{:S(2)}) collective-permute-start(bf16[2,4,328,128]{3,2,1,0:T(8,128)(2,1)S(1)} %get-tuple-element.90.refs_1_), channel_id=1, source_target_pairs={{16,0},{17,1},{20,4},{21,5},{24,8},{25,9},{28,12},{29,13},{2,18},{... | collective-permute-start | bytes 2015240 | tf_op jit(solution)/shard_map/ppermute | solution.py:520
  124.7 44.8 %collective-permute-start.12 = (bf16[2,4,328,128]{3,2,1,0:T(8,128)(2,1)S(1)}, bf16[2,4,328,128]{3,2,1,0:T(8,128)(2,1)S(1)}, u32[]{:S(2)}, u32[]{:S(2)}) collective-permute-start(bf16[2,4,328,128]{3,2,1,0:T(8,128)(2,1)S(1)} %get-tuple-element.91.refs_2_), channel_id=1, source_target_pairs={{16,0},{17,1},{20,4},{21,5},{24,8},{25,9},{28,12},{29,13},{2,18},{... | collective-permute-start | bytes 2015240 | tf_op jit(solution)/shard_map/ppermute | solution.py:520
  134.3 24.8 %collective-permute-start.10 = (f32[4,328,384]{2,1,0:T(8,128)S(1)}, f32[4,328,384]{2,1,0:T(8,128)S(1)}, u32[]{:S(2)}, u32[]{:S(2)}) collective-permute-start(f32[4,328,384]{2,1,0:T(8,128)S(1)} %get-tuple-element.88.refs_3_), channel_id=1, source_target_pairs={{0,2},{1,3},{4,6},{5,7},{8,10},{9,11},{12,14},{13,15},{18,16},{19,... | collective-permute-start | bytes 6045704 | tf_op jit(solution)/shard_map/ppermute | solution.py:539
  135.7 40.9 %collective-permute-start.15 = (bf16[2,4,72,324]{3,2,1,0:T(8,128)(2,1)S(1)}, bf16[2,4,72,324]{3,2,1,0:T(8,128)(2,1)S(1)}, u32[]{:S(2)}, u32[]{:S(2)}) collective-permute-start(bf16[2,4,72,324]{3,2,1,0:T(8,128)(2,1)S(1)} %get-tuple-element.89.refs_1_), channel_id=1, source_target_pairs={{16,0},{17,1},{20,4},{21,5},{24,8},{25,9},{28,12},{29,13},{2,18},{... | collective-permute-start | bytes 1119752 | tf_op jit(solution)/shard_map/ppermute | solution.py:520
  156.9 13.1 %collective-permute-start.13 = (bf16[2,2,2,328,128]{4,3,2,1,0:T(8,128)(2,1)S(1)}, bf16[2,2,2,328,128]{4,3,2,1,0:T(8,128)(2,1)S(1)}, u32[]{:S(2)}, u32[]{:S(2)}) collective-permute-start(bf16[2,2,2,328,128]{4,3,2,1,0:T(8,128)(2,1)S(1)} %get-tuple-element.103), channel_id=1, source_target_pairs={{2,3},{3,2},{6,7},{7,6},{10,11},{11,10},{14,15},{15,14},{16,17},{1... | collective-permute-start | bytes 2015240 | tf_op jit(solution)/shard_map/ppermute | solution.py:525
  159.2 11.6 %collective-permute-start.14 = (bf16[1,2,2,72,324]{4,3,2,1,0:T(8,128)(2,1)S(1)}, bf16[1,2,2,72,324]{4,3,2,1,0:T(8,128)(2,1)S(1)}, u32[]{:S(2)}, u32[]{:S(2)}) collective-permute-start(bf16[1,2,2,72,324]{4,3,2,1,0:T(8,128)(2,1)S(1)} %get-tuple-element.104), channel_id=1, source_target_pairs={{2,3},{3,2},{6,7},{7,6},{10,11},{11,10},{14,15},{15,14},{16,17},{1... | collective-permute-start | bytes 559880 | tf_op jit(solution)/shard_map/ppermute | solution.py:525

commit v16 on v15

--- a/solution.py
+++ b/solution.py
@@ -533,10 +533,10 @@
     token = send_terms(full, token)
     for k in early:
         token = sum_up(k, token, *([gate] if k == 0 else []))
+    share, token = near_share(at, keep, doubled, states, (token,))
+    given = lax.ppermute(share, both, to_second)
     token = keep_terms(full, token)
     token = sum_up(full, token)
-    share, token = near_share(at, keep, doubled, states, (token,))
-    given = lax.ppermute(share, both, to_second)
     turned, token = cross(early, token)
     last, token = cross(late, token, given)
     out, token = near_sum(at, keep, crossed, share, given, states, (token,))

time: 179 us -> 174 us (0.972)
  the two profiles are of different devices: /device:TPU:11 before, /device:TPU:0 now
where the time goes in v16:
time: 174 us; the launch traced here: 173 us
  starting transfers between devices  62.3 us (36%)
  Pallas kernels  43.9 us (25%)
  waiting for transfers between devices  37 us (21%)
  local copies, waits for them, and re-layouts  29.1 us (17%)
    pallas_call x20, Pallas kernels, call(): return lambda *operands: kernel(*operands, *after)  43.9 us
    ppermute x1, starting transfers between devices, paired(): given = lax.ppermute(share, both, to_second)  38.2 us
    ppermute x1, waiting for transfers between devices, paired(): crossed = lax.ppermute(crossed, 'det', [(0, 1), (1, 0)])  18.4 us
    ppermute x1, waiting for transfers between devices, paired(): doubled = lax.ppermute(doubled, both, first_across)  9.63 us
    ppermute x3, waiting for transfers between devices, sum_up(): theirs[k] = lax.ppermute(codes[k], both, back)  8.84 us
    optimization_barrier x1, local copies, waits for them, and re-layouts, paired(): partner, own = lax.optimization_barrier((partner, own))  7.35 us
    ppermute x1, starting transfers between devices, paired(): got = [lax.ppermute(first, both, over)]  5.61 us
    optimization_barrier x1, local copies, waits for them, and re-layouts, paired(): lax.optimization_barrier((first.reshape(states * LANES, depth), amplitudes))  5.41 us
  transfers between devices with their start and end apart: 16, of which 4 were waited for; matrix products, arithmetic and copies ran while one was open for 14% of the time, Pallas kernels for 24%

profile of v16, /device:TPU:0, one launch (start us, length us, event | category | flops | bytes accessed | tf_op | source)
XLA Modules:
  0.0 172.9 jit_solution(3978573693425767047)
XLA Ops:
  0.0 0.5 collective-permute-start
  0.5 2.6 %slice_bitcast_fusion = bf16[4,128,2048]{2,0,1:T(4,128)(2,1)S(1)} fusion(bf16[4,2048,324]{1,0,2:T(4,128)(2,1)} %param.1), kind=kLoop, calls=%fused_computation.2 | loop fusion | bytes 4194304 | tf_op jit(solution)/shard_map/transpose | solution.py:482
  3.1 2.5 %copy.12 = bf16[4,128,2048]{2,1,0:T(8,128)(2,1)} copy(bf16[4,128,2048]{2,0,1:T(4,128)(2,1)S(1)} %slice_bitcast_fusion) | data formatting | bytes 4194304 | tf_op jit(solution)/shard_map/transpose | solution.py:482
  5.5 5.6 %collective-permute-start.4 = (bf16[512,2048]{1,0:T(8,128)(2,1)}, bf16[512,2048]{1,0:T(8,128)(2,1)S(1)}, u32[]{:S(2)}, u32[]{:S(2)}) collective-permute-start(bf16[512,2048]{1,0:T(8,128)(2,1)} %bitcast.3.refs_3_), channel_id=1, source_target_pairs={{0,16},{1,17},{4,20},{5,21},{8,24},{9,25},{12,28},{13,29},{18,2},{... | collective-permute-start | bytes 6291464 | tf_op jit(solution)/shard_map/ppermute | solution.py:484
  11.1 5.4 %copy.18 = bf16[4,2048,324]{1,2,0:T(8,128)(2,1)S(1)} copy(bf16[4,2048,324]{1,0,2:T(4,128)(2,1)} %param.1) | data formatting | bytes 10616832 | tf_op jit(solution)/shard_map/optimization_barrier | solution.py:483
  16.6 0.0 copy-start
  16.6 0.0 collective-permute-done
  16.6 7.4 %copy.17 = bf16[4,2048,324]{1,2,0:T(8,128)(2,1)S(1)} copy(bf16[4,2048,324]{1,0,2:T(4,128)(2,1)} %collective-permute-done) | data formatting | bytes 10616832 | tf_op jit(solution)/shard_map/optimization_barrier | solution.py:486
  23.9 0.0 copy-start.2
  23.9 5.2 %shard_map.17 = (f32[1744,256]{1,0:T(8,128)}, f32[8,128]{1,0:T(8,128)S(1)}) custom-call(s32[1]{0:T(128)} %bitcast.refs_0_, bf16[4,324,2048]{2,1,0:T(8,128)(2,1)S(1)} %bitcast.13, bf16[4,324,2048]{2,1,0:T(8,128)(2,1)S(1)} %bitcast.26, bf16[512,2048]{1,0:T(8,128)(2,1)} %bitcast.3.refs_3_), custom_call_target="tpu_custom_call" | custom-call | tf_op jit(solution)/shard_map/pallas_call | solution.py:45
  29.1 0.0 copy-done.2
  29.1 5.0 %shard_map.18 = (f32[1744,256]{1,0:T(8,128)}, f32[8,128]{1,0:T(8,128)S(1)}) custom-call(s32[1]{0:T(128)} %bitcast.refs_0_, bf16[4,324,2048]{2,1,0:T(8,128)(2,1)S(1)} %bitcast.14, bf16[4,324,2048]{2,1,0:T(8,128)(2,1)S(1)} %bitcast.27, f32[8,128]{1,0:T(8,128)S(1)} %get-tuple-element.61.refs_3_), custom_call_target="tpu_custom_call" | custom-call | tf_op jit(solution)/shard_map/pallas_call | solution.py:45
  34.2 1.5 slice.11
  35.7 2.7 %collective-permute-start.3 = (bf16[512,2048]{1,0:T(8,128)(2,1)}, bf16[512,2048]{1,0:T(8,128)(2,1)}, u32[]{:S(2)}, u32[]{:S(2)}) collective-permute-start(bf16[512,2048]{1,0:T(8,128)(2,1)} %bitcast.6), channel_id=1, source_target_pairs={{0,16},{1,17},{4,20},{5,21},{8,24},{9,25},{12,28},{13,29},{18,2},{... | collective-permute-start | bytes 6291464 | tf_op jit(solution)/shard_map/ppermute | solution.py:497
  38.4 3.6 %collective-permute-start.2 = (f32[1744,256]{1,0:T(8,128)}, f32[1744,256]{1,0:T(8,128)}, u32[]{:S(2)}, u32[]{:S(2)}) collective-permute-start(f32[1744,256]{1,0:T(8,128)} %get-tuple-element.69), channel_id=1, source_target_pairs={{0,1},{1,0},{4,5},{5,4},{8,9},{9,8},{12,13},{13,12},{18,19},{19,18... | collective-permute-start | bytes 5357576 | tf_op jit(solution)/shard_map/ppermute | solution.py:492
  42.0 0.6 collective-permute-start.1
  42.6 0.1 pad_add_fusion.refs_0_
  42.6 2.4 %slice.10 = bf16[4,68,2048]{2,1,0:T(8,128)(2,1)} slice(bf16[4,324,2048]{2,1,0:T(8,128)(2,1)} %bitcast.16), slice={[0:4], [256:324], [0:2048]} | slice | bytes 2228224 | tf_op jit(solution)/shard_map/slice | solution.py:495
  45.1 2.3 %reshape.10 = bf16[272,2048]{1,0:T(8,128)(2,1)} reshape(bf16[4,68,2048]{2,1,0:T(8,128)(2,1)} %slice.10) | data formatting | bytes 2228224 | tf_op jit(solution)/shard_map/reshape | solution.py:495
  47.3 2.5 %copy-done.1 = bf16[4,2048,324]{1,2,0:T(8,128)(2,1)S(1)} copy-done((bf16[4,2048,324]{1,2,0:T(8,128)(2,1)S(1)}, bf16[4,2048,324]{1,2,0:T(8,128)(2,1)}, u32[]{:S(2)}) %copy-start.1) | copy-done | bytes 5308440
  49.9 2.5 %copy-done.3 = bf16[4,2048,324]{1,2,0:T(8,128)(2,1)S(1)} copy-done((bf16[4,2048,324]{1,2,0:T(8,128)(2,1)S(1)}, bf16[4,2048,324]{1,2,0:T(8,128)(2,1)}, u32[]{:S(2)}) %copy-start.3) | copy-done | bytes 5308440
  52.4 7.2 %shard_map.19 = (f32[8,324,324]{2,1,0:T(8,128)S(1)}, f32[8,128]{1,0:T(8,128)S(1)}) custom-call(s32[1]{0:T(128)} %bitcast.refs_0_, bf16[4,324,2048]{2,1,0:T(8,128)(2,1)S(1)} %bitcast.17, bf16[4,324,2048]{2,1,0:T(8,128)(2,1)S(1)} %bitcast.28, f32[8,128]{1,0:T(8,128)S(1)} %get-tuple-element.66.refs_3_), custom_call_target="tpu_custom_call" | custom-call | tf_op jit(solution)/shard_map/pallas_call | solution.py:45
  59.6 0.0 collective-permute-done.4.refs_2_
  59.7 0.7 shard_map.20
  60.3 0.7 collective-permute-start.6
  61.1 3.1 %collective-permute-start.7 = (bf16[272,2048]{1,0:T(8,128)(2,1)S(1)}, bf16[272,2048]{1,0:T(8,128)(2,1)S(1)}, u32[]{:S(2)}, u32[]{:S(2)}) collective-permute-start(bf16[272,2048]{1,0:T(8,128)(2,1)S(1)} %copy-done.4), channel_id=1, source_target_pairs={{0,16},{1,17},{4,20},{5,21},{8,24},{9,25},{12,28},{13,29},{18,2},{... | collective-permute-start | bytes 3342344 | tf_op jit(solution)/shard_map/ppermute | solution.py:499
  64.2 0.7 shard_map.21
  64.9 0.0 collective-permute-done.3.refs_2_
  64.9 1.8 %shard_map.22 = (f32[2,4,328,128]{3,2,1,0:T(8,128)S(1)}, f32[8,128]{1,0:T(8,128)S(1)}) custom-call(s32[2]{0:T(128)S(1)} %pad_add_fusion.refs_0_, bf16[4,324,2048]{2,1,0:T(8,128)(2,1)S(1)} %bitcast.22, bf16[512,2048]{1,0:T(8,128)(2,1)} %collective-permute-done.3.refs_2_, f32[8,128]{1,0:T(8,128)S(1)} %get-tuple-element.73.refs_3_), custom_call_target="tpu_custom_call" | custom-call | tf_op jit(solution)/shard_map/pallas_call | solution.py:45
  66.7 0.7 collective-permute-start.8
  67.4 9.6 %collective-permute-done.2.refs_5_.refs_2_ = f32[1744,256]{1,0:T(8,128)} collective-permute-done((f32[1744,256]{1,0:T(8,128)}, f32[1744,256]{1,0:T(8,128)}, u32[]{:S(2)}, u32[]{:S(2)}) %collective-permute-start.2) | collective-permute-done | bytes 1785888 | tf_op jit(solution)/shard_map/ppermute | solution.py:492
  77.0 0.7 collective-permute-start.5
  77.8 18.4 %collective-permute-done.1.refs_4_.refs_2_ = f32[1744,256]{1,0:T(8,128)} collective-permute-done((f32[1744,256]{1,0:T(8,128)}, f32[1744,256]{1,0:T(8,128)}, u32[]{:S(2)}, u32[]{:S(2)}) %collective-permute-start.1) | collective-permute-done | bytes 1785888 | tf_op jit(solution)/shard_map/ppermute | solution.py:490
  96.2 1.8 %shard_map.23 = (f32[2,4,328,128]{3,2,1,0:T(8,128)S(1)}, f32[8,128]{1,0:T(8,128)S(1)}) custom-call(s32[2]{0:T(128)S(1)} %pad_add_fusion.refs_0_, bf16[4,324,2048]{2,1,0:T(8,128)(2,1)S(1)} %bitcast.23, bf16[512,2048]{1,0:T(8,128)(2,1)} %collective-permute-done.3.refs_2_, f32[8,128]{1,0:T(8,128)S(1)} %get-tuple-element.74.refs_3_, ...), custom_call_target="tpu_custom_call" | custom-call | flops 10000000000 | bytes 100000000 | tf_op jit(solution)/shard_map/pallas_call | solution.py:45
  98.0 0.0 collective-permute-done.7.refs_2_
  98.0 0.7 shard_map.24
  98.7 0.7 collective-permute-start.10
  99.4 0.0 collective-permute-done.6.refs_2_
  99.4 0.0 collective-permute-done.8.refs_4_
  99.4 1.1 shard_map.25
  100.5 1.3 collective-permute-start.11
  101.8 0.0 collective-permute-done.5.refs_2_
  101.8 1.1 shard_map.26
  102.9 1.3 collective-permute-start.12
  104.2 2.8 %shard_map.27 = (f32[4,328,384]{2,1,0:T(8,128)S(1)}, f32[8,128]{1,0:T(8,128)S(1)}) custom-call(s32[2]{0:T(128)S(1)} %pad_add_fusion.refs_0_, f32[8,324,324]{2,1,0:T(8,128)S(1)} %get-tuple-element.67.refs_1_, f32[1744,256]{1,0:T(8,128)} %collective-permute-done.2.refs_5_.refs_2_, f32[8,128]{1,0:T(8,128)S(1)} %get-tuple-element.83.refs_3_), custom_call_target="tpu_custom_call" | custom-call | tf_op jit(solution)/shard_map/pallas_call | solution.py:45
  107.0 38.2 %collective-permute-start.9 = (f32[4,328,384]{2,1,0:T(8,128)S(1)}, f32[4,328,384]{2,1,0:T(8,128)S(1)}, u32[]{:S(2)}, u32[]{:S(2)}) collective-permute-start(f32[4,328,384]{2,1,0:T(8,128)S(1)} %get-tuple-element.84.refs_3_), channel_id=1, source_target_pairs={{0,2},{1,3},{4,6},{5,7},{8,10},{9,11},{12,14},{13,15},{18,16},{19,... | collective-permute-start | bytes 6045704 | tf_op jit(solution)/shard_map/ppermute | solution.py:537
  145.3 0.7 shard_map.28
  145.9 0.0 collective-permute-done.10.refs_2_
  146.0 0.6 shard_map.29
  146.6 0.1 shard_map.30
  146.7 1.3 collective-permute-start.15
  148.0 0.7 collective-permute-start.13
  148.7 0.1 collective-permute-done.9.refs_3_.refs_4_
  148.8 0.7 collective-permute-start.14
  149.5 5.4 %shard_map.32 = (f32[2,324,8,324]{3,2,1,0:T(8,128)}, f32[8,128]{1,0:T(8,128)S(1)}) custom-call(s32[2]{0:T(128)S(1)} %pad_add_fusion.refs_0_, f32[8,324,324]{2,1,0:T(8,128)S(1)} %get-tuple-element.67.refs_1_, f32[1744,256]{1,0:T(8,128)} %collective-permute-done.1.refs_4_.refs_2_, f32[4,328,384]{2,1,0:T(8,128)S(1)} %get-tuple-element.84.refs_3_, ...), custom_call_target="tpu_custom_call" | custom-call | tf_op jit(solution)/shard_map/pallas_call | solution.py:45
  154.9 0.0 collective-permute-done.11.refs_2_
  154.9 2.8 %shard_map.33 = (f32[2,324,8,324]{3,2,1,0:T(8,128)}, f32[8,128]{1,0:T(8,128)S(1)}) custom-call(s32[2]{0:T(128)S(1)} %pad_add_fusion.refs_0_, f32[2,324,8,324]{3,2,1,0:T(8,128)} %get-tuple-element.95.refs_1_, bf16[2,4,328,128]{3,2,1,0:T(8,128)(2,1)S(1)} %collective-permute-done.11.refs_2_, ...), custom_call_target="tpu_custom_call", output_to_operand_aliasing={{0}: (1, {})} | custom-call | flops 10000000000 | bytes 100000000 | tf_op jit(solution)/shard_map/pallas_call | solution.py:45
  157.7 0.0 collective-permute-done.12.refs_2_
  157.7 2.8 %shard_map.34 = (f32[2,324,8,324]{3,2,1,0:T(8,128)}, f32[8,128]{1,0:T(8,128)S(1)}) custom-call(s32[2]{0:T(128)S(1)} %pad_add_fusion.refs_0_, f32[2,324,8,324]{3,2,1,0:T(8,128)} %get-tuple-element.97.refs_1_, bf16[2,4,328,128]{3,2,1,0:T(8,128)(2,1)S(1)} %collective-permute-done.12.refs_2_, ...), custom_call_target="tpu_custom_call", output_to_operand_aliasing={{0}: (1, {})} | custom-call | flops 10000000000 | bytes 100000000 | tf_op jit(solution)/shard_map/pallas_call | solution.py:45
  160.5 0.0 collective-permute-done.13.refs_5_
  160.5 0.0 collective-permute-done.14.refs_6_
  160.5 0.6 shard_map.35
  161.2 8.8 %collective-permute-done.15.refs_2_ = bf16[2,4,72,324]{3,2,1,0:T(8,128)(2,1)S(1)} collective-permute-done((bf16[2,4,72,324]{3,2,1,0:T(8,128)(2,1)S(1)}, bf16[2,4,72,324]{3,2,1,0:T(8,128)(2,1)S(1)}, u32[]{:S(2)}, u32[]{:S(2)}) %collective-permute-start.15) | collective-permute-done | bytes 373280 | tf_op jit(solution)/shard_map/ppermute | solution.py:520
  170.0 2.8 %shard_map.36 = (f32[2,324,8,324]{3,2,1,0:T(8,128)}, f32[8,128]{1,0:T(8,128)}) custom-call(s32[2]{0:T(128)S(1)} %pad_add_fusion.refs_0_, f32[2,324,8,324]{3,2,1,0:T(8,128)} %get-tuple-element.106.refs_1_, bf16[2,4,72,324]{3,2,1,0:T(8,128)(2,1)S(1)} %collective-permute-done.15.refs_2_, ...), custom_call_target="tpu_custom_call", output_to_operand_aliasing={{0}: (1, {})} | custom-call | tf_op jit(solution)/shard_map/pallas_call | solution.py:45
  (11 shorter events, 0.1 us)
Async XLA Ops:
  0.0 16.6 %collective-permute-start = (bf16[4,2048,324]{1,0,2:T(4,128)(2,1)}, bf16[4,2048,324]{1,0,2:T(4,128)(2,1)}, u32[]{:S(2)}, u32[]{:S(2)}) collective-permute-start(bf16[4,2048,324]{1,0,2:T(4,128)(2,1)} %param.1), channel_id=1, source_target_pairs={{0,2},{2,0},{4,6},{6,4},{8,10},{10,8},{12,14},{14,12},{16,18},{18,... | collective-permute-start | bytes 15925256 | tf_op jit(solution)/shard_map/ppermute | solution.py:481
  5.5 54.1 %collective-permute-start.4 = (bf16[512,2048]{1,0:T(8,128)(2,1)}, bf16[512,2048]{1,0:T(8,128)(2,1)S(1)}, u32[]{:S(2)}, u32[]{:S(2)}) collective-permute-start(bf16[512,2048]{1,0:T(8,128)(2,1)} %bitcast.3.refs_3_), channel_id=1, source_target_pairs={{0,16},{1,17},{4,20},{5,21},{8,24},{9,25},{12,28},{13,29},{18,2},{... | collective-permute-start | bytes 6291464 | tf_op jit(solution)/shard_map/ppermute | solution.py:484
  16.6 17.6 %copy-start = (bf16[4,2048,324]{1,2,0:T(8,128)(2,1)}, bf16[4,2048,324]{1,2,0:T(8,128)(2,1)S(1)}, u32[]{:S(2)}) copy-start(bf16[4,2048,324]{1,2,0:T(8,128)(2,1)S(1)} %copy.18) | copy-start | bytes 15925252
  23.9 5.2 %copy-start.2 = (bf16[4,2048,324]{1,2,0:T(8,128)(2,1)}, bf16[4,2048,324]{1,2,0:T(8,128)(2,1)S(1)}, u32[]{:S(2)}) copy-start(bf16[4,2048,324]{1,2,0:T(8,128)(2,1)S(1)} %copy.17) | copy-start | bytes 15925252
  35.7 29.2 %collective-permute-start.3 = (bf16[512,2048]{1,0:T(8,128)(2,1)}, bf16[512,2048]{1,0:T(8,128)(2,1)}, u32[]{:S(2)}, u32[]{:S(2)}) collective-permute-start(bf16[512,2048]{1,0:T(8,128)(2,1)} %bitcast.6), channel_id=1, source_target_pairs={{0,16},{1,17},{4,20},{5,21},{8,24},{9,25},{12,28},{13,29},{18,2},{... | collective-permute-start | bytes 6291464 | tf_op jit(solution)/shard_map/ppermute | solution.py:497
  38.4 38.6 %collective-permute-start.2 = (f32[1744,256]{1,0:T(8,128)}, f32[1744,256]{1,0:T(8,128)}, u32[]{:S(2)}, u32[]{:S(2)}) collective-permute-start(f32[1744,256]{1,0:T(8,128)} %get-tuple-element.69), channel_id=1, source_target_pairs={{0,1},{1,0},{4,5},{5,4},{8,9},{9,8},{12,13},{13,12},{18,19},{19,18... | collective-permute-start | bytes 5357576 | tf_op jit(solution)/shard_map/ppermute | solution.py:492
  42.0 54.2 %collective-permute-start.1 = (f32[1744,256]{1,0:T(8,128)}, f32[1744,256]{1,0:T(8,128)}, u32[]{:S(2)}, u32[]{:S(2)}) collective-permute-start(f32[1744,256]{1,0:T(8,128)} %get-tuple-element.68), channel_id=1, source_target_pairs={{0,1},{1,0},{2,3},{3,2},{4,5},{5,4},{6,7},{7,6},{8,9},{9,8},{10,11... | collective-permute-start | bytes 5357576 | tf_op jit(solution)/shard_map/ppermute | solution.py:490
  45.1 14.6 %slice-start = ((s8[5373952]{0:T(1024)(128)(4,1)}), s8[1179648]{0:T(1024)(128)(4,1)S(1)}, s32[]{:S(2)}) async-start(s8[5373952]{0:T(1024)(128)(4,1)} %bitcast.18), calls=%async_computation | async-start | bytes 2359296
  47.3 2.5 %copy-start.1 = (bf16[4,2048,324]{1,2,0:T(8,128)(2,1)S(1)}, bf16[4,2048,324]{1,2,0:T(8,128)(2,1)}, u32[]{:S(2)}) copy-start(bf16[4,2048,324]{1,2,0:T(8,128)(2,1)} %copy-done) | copy-start | bytes 15925252
  49.9 2.5 %copy-start.3 = (bf16[4,2048,324]{1,2,0:T(8,128)(2,1)S(1)}, bf16[4,2048,324]{1,2,0:T(8,128)(2,1)}, u32[]{:S(2)}) copy-start(bf16[4,2048,324]{1,2,0:T(8,128)(2,1)} %copy-done.2) | copy-start | bytes 15925252
  52.4 7.2 %slice-start.1 = ((s8[5373952]{0:T(1024)(128)(4,1)}), s8[4194304]{0:T(1024)(128)(4,1)S(1)}, s32[]{:S(2)}) async-start(s8[5373952]{0:T(1024)(128)(4,1)} %bitcast.18), calls=%async_computation.1 | async-start | bytes 8388608
  59.6 1.5 copy-start.4
  60.3 39.1 %collective-permute-start.6 = (f32[2,4,328,128]{3,2,1,0:T(8,128)S(1)}, f32[2,4,328,128]{3,2,1,0:T(8,128)S(1)}, u32[]{:S(2)}, u32[]{:S(2)}) collective-permute-start(f32[2,4,328,128]{3,2,1,0:T(8,128)S(1)} %get-tuple-element.78), channel_id=1, source_target_pairs={{2,3},{3,2},{6,7},{7,6},{10,11},{11,10},{14,15},{15,14},{16,17},{1... | collective-permute-start | bytes 4030472 | tf_op jit(solution)/shard_map/ppermute | solution.py:513
  61.1 36.9 %collective-permute-start.7 = (bf16[272,2048]{1,0:T(8,128)(2,1)S(1)}, bf16[272,2048]{1,0:T(8,128)(2,1)S(1)}, u32[]{:S(2)}, u32[]{:S(2)}) collective-permute-start(bf16[272,2048]{1,0:T(8,128)(2,1)S(1)} %copy-done.4), channel_id=1, source_target_pairs={{0,16},{1,17},{4,20},{5,21},{8,24},{9,25},{12,28},{13,29},{18,2},{... | collective-permute-start | bytes 3342344 | tf_op jit(solution)/shard_map/ppermute | solution.py:499
  66.7 32.7 %collective-permute-start.8 = (f32[8,128]{1,0:T(8,128)S(1)}, f32[8,128]{1,0:T(8,128)S(1)}, u32[]{:S(2)}, u32[]{:S(2)}) collective-permute-start(f32[8,128]{1,0:T(8,128)S(1)} %get-tuple-element.74.refs_3_), channel_id=1, source_target_pairs={{8,10},{12,14},{18,16},{22,20},{9,11},{13,15},{19,17},{23,21}} | collective-permute-start | bytes 12296 | tf_op jit(solution)/shard_map/ppermute | solution.py:531
  77.0 24.8 %collective-permute-start.5 = (f32[2,4,328,128]{3,2,1,0:T(8,128)S(1)}, f32[2,4,328,128]{3,2,1,0:T(8,128)S(1)}, u32[]{:S(2)}, u32[]{:S(2)}) collective-permute-start(f32[2,4,328,128]{3,2,1,0:T(8,128)S(1)} %get-tuple-element.76), channel_id=1, source_target_pairs={{2,3},{3,2},{6,7},{7,6},{10,11},{11,10},{14,15},{15,14},{16,17},{1... | collective-permute-start | bytes 4030472 | tf_op jit(solution)/shard_map/ppermute | solution.py:513
  98.7 47.3 %collective-permute-start.10 = (f32[2,4,72,324]{3,2,1,0:T(8,128)S(1)}, f32[2,4,72,324]{3,2,1,0:T(8,128)S(1)}, u32[]{:S(2)}, u32[]{:S(2)}) collective-permute-start(f32[2,4,72,324]{3,2,1,0:T(8,128)S(1)} %get-tuple-element.87), channel_id=1, source_target_pairs={{2,3},{3,2},{6,7},{7,6},{10,11},{11,10},{14,15},{15,14},{16,17},{1... | collective-permute-start | bytes 2239496 | tf_op jit(solution)/shard_map/ppermute | solution.py:513
  100.5 54.4 %collective-permute-start.11 = (bf16[2,4,328,128]{3,2,1,0:T(8,128)(2,1)S(1)}, bf16[2,4,328,128]{3,2,1,0:T(8,128)(2,1)S(1)}, u32[]{:S(2)}, u32[]{:S(2)}) collective-permute-start(bf16[2,4,328,128]{3,2,1,0:T(8,128)(2,1)S(1)} %get-tuple-element.90.refs_1_), channel_id=1, source_target_pairs={{16,0},{17,1},{20,4},{21,5},{24,8},{25,9},{28,12},{29,13},{2,18},{... | collective-permute-start | bytes 2015240 | tf_op jit(solution)/shard_map/ppermute | solution.py:520
  102.9 54.8 %collective-permute-start.12 = (bf16[2,4,328,128]{3,2,1,0:T(8,128)(2,1)S(1)}, bf16[2,4,328,128]{3,2,1,0:T(8,128)(2,1)S(1)}, u32[]{:S(2)}, u32[]{:S(2)}) collective-permute-start(bf16[2,4,328,128]{3,2,1,0:T(8,128)(2,1)S(1)} %get-tuple-element.91.refs_2_), channel_id=1, source_target_pairs={{16,0},{17,1},{20,4},{21,5},{24,8},{25,9},{28,12},{29,13},{2,18},{... | collective-permute-start | bytes 2015240 | tf_op jit(solution)/shard_map/ppermute | solution.py:520
  107.0 41.8 %collective-permute-start.9 = (f32[4,328,384]{2,1,0:T(8,128)S(1)}, f32[4,328,384]{2,1,0:T(8,128)S(1)}, u32[]{:S(2)}, u32[]{:S(2)}) collective-permute-start(f32[4,328,384]{2,1,0:T(8,128)S(1)} %get-tuple-element.84.refs_3_), channel_id=1, source_target_pairs={{0,2},{1,3},{4,6},{5,7},{8,10},{9,11},{12,14},{13,15},{18,16},{19,... | collective-permute-start | bytes 6045704 | tf_op jit(solution)/shard_map/ppermute | solution.py:537
  146.7 23.3 %collective-permute-start.15 = (bf16[2,4,72,324]{3,2,1,0:T(8,128)(2,1)S(1)}, bf16[2,4,72,324]{3,2,1,0:T(8,128)(2,1)S(1)}, u32[]{:S(2)}, u32[]{:S(2)}) collective-permute-start(bf16[2,4,72,324]{3,2,1,0:T(8,128)(2,1)S(1)} %get-tuple-element.89.refs_1_), channel_id=1, source_target_pairs={{16,0},{17,1},{20,4},{21,5},{24,8},{25,9},{28,12},{29,13},{2,18},{... | collective-permute-start | bytes 1119752 | tf_op jit(solution)/shard_map/ppermute | solution.py:520
  148.0 12.5 %collective-permute-start.13 = (bf16[2,2,2,328,128]{4,3,2,1,0:T(8,128)(2,1)S(1)}, bf16[2,2,2,328,128]{4,3,2,1,0:T(8,128)(2,1)S(1)}, u32[]{:S(2)}, u32[]{:S(2)}) collective-permute-start(bf16[2,2,2,328,128]{4,3,2,1,0:T(8,128)(2,1)S(1)} %get-tuple-element.103), channel_id=1, source_target_pairs={{2,3},{3,2},{6,7},{7,6},{10,11},{11,10},{14,15},{15,14},{16,17},{1... | collective-permute-start | bytes 2015240 | tf_op jit(solution)/shard_map/ppermute | solution.py:525
  148.8 11.7 %collective-permute-start.14 = (bf16[1,2,2,72,324]{4,3,2,1,0:T(8,128)(2,1)S(1)}, bf16[1,2,2,72,324]{4,3,2,1,0:T(8,128)(2,1)S(1)}, u32[]{:S(2)}, u32[]{:S(2)}) collective-permute-start(bf16[1,2,2,72,324]{4,3,2,1,0:T(8,128)(2,1)S(1)} %get-tuple-element.104), channel_id=1, source_target_pairs={{2,3},{3,2},{6,7},{7,6},{10,11},{11,10},{14,15},{15,14},{16,17},{1... | collective-permute-start | bytes 559880 | tf_op jit(solution)/shard_map/ppermute | solution.py:525

commit v17 on v16

--- a/solution.py
+++ b/solution.py
@@ -479,8 +479,8 @@
     at = jnp.stack([x, receiver])
 
     partner = lax.ppermute(amplitudes, "state", [(s, s ^ 1) for s in range(blocks)])
-    first = amplitudes[:, :, :LANES].transpose(0, 2, 1)
-    first, later = lax.optimization_barrier((first.reshape(states * LANES, depth), amplitudes))
+    first = amplitudes[:, :, :LANES].transpose(2, 0, 1)
+    first, later = lax.optimization_barrier((first, amplitudes))
     got = [lax.ppermute(first, both, over)]
     own = later.transpose(0, 2, 1)
     partner, own = lax.optimization_barrier((partner, own))
@@ -498,6 +498,8 @@
     last, token = lax.optimization_barrier((chunk[full], token))
     got.append(lax.ppermute(last, both, over))
     keep, token = near_keep(det, own, partner, (token,))
+    raw, token = lax.optimization_barrier((got[0], token))
+    got[0] = raw.transpose(1, 0, 2).reshape(states * LANES, depth)
     def terms(k, mine, done, declared=0):
         wire, start = (0, 0) if k == 0 else (2, 0) if k == full else (1, states * LANES * (k - 1))
         return far_terms(at, own, got[wire], start, widths[k], k < full, mine, done, declared)

time: 174 us -> 171 us (0.983)
  waiting for transfers between devices: 37 us -> 34 us
    ppermute x1, waiting for transfers between devices: 9.63 us -> 6.7 us  [paired(): doubled = lax.ppermute(doubled, both, first_across)]
where the time goes in v17:
time: 171 us; the launch traced here: 170 us
  starting transfers between devices  62.3 us (36%)
  Pallas kernels  43.8 us (26%)
  waiting for transfers between devices  34 us (20%)
  local copies, waits for them, and re-layouts  29.4 us (17%)
    pallas_call x20, Pallas kernels, call(): return lambda *operands: kernel(*operands, *after)  43.8 us
    ppermute x1, starting transfers between devices, paired(): given = lax.ppermute(share, both, to_second)  38.1 us
    ppermute x1, waiting for transfers between devices, paired(): crossed = lax.ppermute(crossed, 'det', [(0, 1), (1, 0)])  18.4 us
    ppermute x3, waiting for transfers between devices, sum_up(): theirs[k] = lax.ppermute(codes[k], both, back)  8.83 us
    optimization_barrier x1, local copies, waits for them, and re-layouts, paired(): partner, own = lax.optimization_barrier((partner, own))  7.35 us
    ppermute x1, starting transfers between devices, paired(): got = [lax.ppermute(first, both, over)]  6.81 us
    ppermute x1, waiting for transfers between devices, paired(): doubled = lax.ppermute(doubled, both, first_across)  6.7 us
    optimization_barrier x1, local copies, waits for them, and re-layouts, paired(): first, later = lax.optimization_barrier((first, amplitudes))  5.42 us
  transfers between devices with their start and end apart: 16, of which 4 were waited for; matrix products, arithmetic and copies ran while one was open for 14% of the time, Pallas kernels for 24%

profile of v17, /device:TPU:0, one launch (start us, length us, event | category | flops | bytes accessed | tf_op | source)
XLA Modules:
  0.0 170.3 jit_solution(15812040518631009378)
XLA Ops:
  0.0 0.5 collective-permute-start
  0.5 2.6 %slice_bitcast_fusion.refs_3_ = bf16[128,4,2048]{2,1,0:T(4,128)(2,1)S(1)} fusion(bf16[4,2048,324]{1,0,2:T(4,128)(2,1)} %param.1), kind=kLoop, calls=%fused_computation.2 | loop fusion | bytes 4194304 | tf_op jit(solution)/shard_map/transpose | solution.py:482
  3.1 6.8 %collective-permute-start.4 = (bf16[128,4,2048]{2,1,0:T(4,128)(2,1)S(1)}, bf16[128,4,2048]{2,1,0:T(4,128)(2,1)}, u32[]{:S(2)}, u32[]{:S(2)}) collective-permute-start(bf16[128,4,2048]{2,1,0:T(4,128)(2,1)S(1)} %slice_bitcast_fusion.refs_3_), channel_id=1, source_target_pairs={{0,16},{1,17},{4,20},{5,21},{8,24},{9,25},{12,28},{13,29},{18,2},{... | collective-permute-start | bytes 6291464 | tf_op jit(solution)/shard_map/ppermute | solution.py:484
  9.9 5.4 %copy.18 = bf16[4,2048,324]{1,2,0:T(8,128)(2,1)S(1)} copy(bf16[4,2048,324]{1,0,2:T(4,128)(2,1)} %param.1) | data formatting | bytes 10616832 | tf_op jit(solution)/shard_map/optimization_barrier | solution.py:483
  15.3 0.0 copy-start
  15.3 0.0 collective-permute-done
  15.3 7.4 %copy.17 = bf16[4,2048,324]{1,2,0:T(8,128)(2,1)S(1)} copy(bf16[4,2048,324]{1,0,2:T(4,128)(2,1)} %collective-permute-done) | data formatting | bytes 10616832 | tf_op jit(solution)/shard_map/optimization_barrier | solution.py:486
  22.7 0.0 copy-start.2
  22.7 5.2 %shard_map.17 = (f32[1744,256]{1,0:T(8,128)}, f32[8,128]{1,0:T(8,128)S(1)}) custom-call(s32[1]{0:T(128)} %bitcast.refs_0_, bf16[4,324,2048]{2,1,0:T(8,128)(2,1)S(1)} %bitcast.14, bf16[4,324,2048]{2,1,0:T(8,128)(2,1)S(1)} %bitcast.27, bf16[128,4,2048]{2,1,0:T(4,128)(2,1)S(1)} %slice_bitcast_fusion.refs_3_), custom_call_target="tpu_custom_call" | custom-call | tf_op jit(solution)/shard_map/pallas_call | solution.py:45
  27.8 0.0 copy-done.2
  27.8 5.0 %shard_map.18 = (f32[1744,256]{1,0:T(8,128)}, f32[8,128]{1,0:T(8,128)S(1)}) custom-call(s32[1]{0:T(128)} %bitcast.refs_0_, bf16[4,324,2048]{2,1,0:T(8,128)(2,1)S(1)} %bitcast.15, bf16[4,324,2048]{2,1,0:T(8,128)(2,1)S(1)} %bitcast.28, f32[8,128]{1,0:T(8,128)S(1)} %get-tuple-element.63.refs_3_), custom_call_target="tpu_custom_call" | custom-call | tf_op jit(solution)/shard_map/pallas_call | solution.py:45
  32.9 1.5 slice.11
  34.4 2.7 %collective-permute-start.3 = (bf16[512,2048]{1,0:T(8,128)(2,1)}, bf16[512,2048]{1,0:T(8,128)(2,1)}, u32[]{:S(2)}, u32[]{:S(2)}) collective-permute-start(bf16[512,2048]{1,0:T(8,128)(2,1)} %bitcast.5), channel_id=1, source_target_pairs={{0,16},{1,17},{4,20},{5,21},{8,24},{9,25},{12,28},{13,29},{18,2},{... | collective-permute-start | bytes 6291464 | tf_op jit(solution)/shard_map/ppermute | solution.py:497
  37.1 3.4 %collective-permute-start.2 = (f32[1744,256]{1,0:T(8,128)}, f32[1744,256]{1,0:T(8,128)}, u32[]{:S(2)}, u32[]{:S(2)}) collective-permute-start(f32[1744,256]{1,0:T(8,128)} %get-tuple-element.71), channel_id=1, source_target_pairs={{0,1},{1,0},{4,5},{5,4},{8,9},{9,8},{12,13},{13,12},{18,19},{19,18... | collective-permute-start | bytes 5357576 | tf_op jit(solution)/shard_map/ppermute | solution.py:492
  40.5 0.6 collective-permute-start.1
  41.1 0.1 pad_add_fusion.refs_0_
  41.2 2.4 %slice.10 = bf16[4,68,2048]{2,1,0:T(8,128)(2,1)} slice(bf16[4,324,2048]{2,1,0:T(8,128)(2,1)} %bitcast.17), slice={[0:4], [256:324], [0:2048]} | slice | bytes 2228224 | tf_op jit(solution)/shard_map/slice | solution.py:495
  43.6 2.3 %reshape.9 = bf16[272,2048]{1,0:T(8,128)(2,1)} reshape(bf16[4,68,2048]{2,1,0:T(8,128)(2,1)} %slice.10) | data formatting | bytes 2228224 | tf_op jit(solution)/shard_map/reshape | solution.py:495
  45.9 2.5 %copy-done.1 = bf16[4,2048,324]{1,2,0:T(8,128)(2,1)S(1)} copy-done((bf16[4,2048,324]{1,2,0:T(8,128)(2,1)S(1)}, bf16[4,2048,324]{1,2,0:T(8,128)(2,1)}, u32[]{:S(2)}) %copy-start.1) | copy-done | bytes 5308440
  48.4 2.5 %copy-done.3 = bf16[4,2048,324]{1,2,0:T(8,128)(2,1)S(1)} copy-done((bf16[4,2048,324]{1,2,0:T(8,128)(2,1)S(1)}, bf16[4,2048,324]{1,2,0:T(8,128)(2,1)}, u32[]{:S(2)}) %copy-start.3) | copy-done | bytes 5308440
  50.9 7.2 %shard_map.19 = (f32[8,324,324]{2,1,0:T(8,128)S(1)}, f32[8,128]{1,0:T(8,128)S(1)}) custom-call(s32[1]{0:T(128)} %bitcast.refs_0_, bf16[4,324,2048]{2,1,0:T(8,128)(2,1)S(1)} %bitcast.18, bf16[4,324,2048]{2,1,0:T(8,128)(2,1)S(1)} %bitcast.29, f32[8,128]{1,0:T(8,128)S(1)} %get-tuple-element.68.refs_3_), custom_call_target="tpu_custom_call" | custom-call | tf_op jit(solution)/shard_map/pallas_call | solution.py:45
  58.2 0.0 collective-permute-done.4
  58.2 2.7 %copy.14 = bf16[4,128,2048]{2,1,0:T(8,128)(2,1)S(1)} copy(bf16[4,128,2048]{2,0,1:T(4,128)(2,1)} %bitcast.6) | data formatting | bytes 4194304 | tf_op jit(solution)/shard_map/transpose | solution.py:502
  61.0 0.7 shard_map.20
  61.6 0.9 collective-permute-start.6
  62.6 2.1 %collective-permute-start.7 = (bf16[272,2048]{1,0:T(8,128)(2,1)S(1)}, bf16[272,2048]{1,0:T(8,128)(2,1)S(1)}, u32[]{:S(2)}, u32[]{:S(2)}) collective-permute-start(bf16[272,2048]{1,0:T(8,128)(2,1)S(1)} %copy-done.4), channel_id=1, source_target_pairs={{0,16},{1,17},{4,20},{5,21},{8,24},{9,25},{12,28},{13,29},{18,2},{... | collective-permute-start | bytes 3342344 | tf_op jit(solution)/shard_map/ppermute | solution.py:499
  64.6 0.7 shard_map.21
  65.3 0.0 collective-permute-done.3.refs_2_
  65.3 1.8 %shard_map.22 = (f32[2,4,328,128]{3,2,1,0:T(8,128)S(1)}, f32[8,128]{1,0:T(8,128)S(1)}) custom-call(s32[2]{0:T(128)S(1)} %pad_add_fusion.refs_0_, bf16[4,324,2048]{2,1,0:T(8,128)(2,1)S(1)} %bitcast.23, bf16[512,2048]{1,0:T(8,128)(2,1)} %collective-permute-done.3.refs_2_, f32[8,128]{1,0:T(8,128)S(1)} %get-tuple-element.77.refs_3_), custom_call_target="tpu_custom_call" | custom-call | tf_op jit(solution)/shard_map/pallas_call | solution.py:45
  67.2 0.7 collective-permute-start.8
  67.9 6.7 %collective-permute-done.2.refs_5_.refs_2_ = f32[1744,256]{1,0:T(8,128)} collective-permute-done((f32[1744,256]{1,0:T(8,128)}, f32[1744,256]{1,0:T(8,128)}, u32[]{:S(2)}, u32[]{:S(2)}) %collective-permute-start.2) | collective-permute-done | bytes 1785888 | tf_op jit(solution)/shard_map/ppermute | solution.py:492
  74.6 0.7 collective-permute-start.5
  75.3 18.4 %collective-permute-done.1.refs_4_.refs_2_ = f32[1744,256]{1,0:T(8,128)} collective-permute-done((f32[1744,256]{1,0:T(8,128)}, f32[1744,256]{1,0:T(8,128)}, u32[]{:S(2)}, u32[]{:S(2)}) %collective-permute-start.1) | collective-permute-done | bytes 1785888 | tf_op jit(solution)/shard_map/ppermute | solution.py:490
  93.7 1.8 %shard_map.23 = (f32[2,4,328,128]{3,2,1,0:T(8,128)S(1)}, f32[8,128]{1,0:T(8,128)S(1)}) custom-call(s32[2]{0:T(128)S(1)} %pad_add_fusion.refs_0_, bf16[4,324,2048]{2,1,0:T(8,128)(2,1)S(1)} %bitcast.24, bf16[512,2048]{1,0:T(8,128)(2,1)} %collective-permute-done.3.refs_2_, f32[8,128]{1,0:T(8,128)S(1)} %get-tuple-element.78.refs_3_, ...), custom_call_target="tpu_custom_call" | custom-call | flops 10000000000 | bytes 100000000 | tf_op jit(solution)/shard_map/pallas_call | solution.py:45
  95.6 0.0 collective-permute-done.7.refs_2_
  95.6 0.7 shard_map.24
  96.2 0.7 collective-permute-start.10
  97.0 0.0 collective-permute-done.6.refs_2_
  97.0 0.0 collective-permute-done.8.refs_4_
  97.0 1.1 shard_map.25
  98.0 1.3 collective-permute-start.11
  99.3 0.0 collective-permute-done.5.refs_2_
  99.4 1.1 shard_map.26
  100.4 1.3 collective-permute-start.12
  101.7 2.8 %shard_map.27 = (f32[4,328,384]{2,1,0:T(8,128)S(1)}, f32[8,128]{1,0:T(8,128)S(1)}) custom-call(s32[2]{0:T(128)S(1)} %pad_add_fusion.refs_0_, f32[8,324,324]{2,1,0:T(8,128)S(1)} %get-tuple-element.69.refs_1_, f32[1744,256]{1,0:T(8,128)} %collective-permute-done.2.refs_5_.refs_2_, f32[8,128]{1,0:T(8,128)S(1)} %get-tuple-element.87.refs_3_), custom_call_target="tpu_custom_call" | custom-call | tf_op jit(solution)/shard_map/pallas_call | solution.py:45
  104.6 38.1 %collective-permute-start.9 = (f32[4,328,384]{2,1,0:T(8,128)S(1)}, f32[4,328,384]{2,1,0:T(8,128)S(1)}, u32[]{:S(2)}, u32[]{:S(2)}) collective-permute-start(f32[4,328,384]{2,1,0:T(8,128)S(1)} %get-tuple-element.88.refs_3_), channel_id=1, source_target_pairs={{0,2},{1,3},{4,6},{5,7},{8,10},{9,11},{12,14},{13,15},{18,16},{19,... | collective-permute-start | bytes 6045704 | tf_op jit(solution)/shard_map/ppermute | solution.py:539
  142.6 0.7 shard_map.28
  143.3 0.0 collective-permute-done.10.refs_2_
  143.3 0.6 shard_map.29
  143.9 0.1 shard_map.30
  144.0 1.3 collective-permute-start.15
  145.3 0.7 collective-permute-start.13
  146.1 0.1 collective-permute-done.9.refs_3_.refs_4_
  146.2 0.7 collective-permute-start.14
  146.9 5.2 %shard_map.32 = (f32[2,324,8,324]{3,2,1,0:T(8,128)}, f32[8,128]{1,0:T(8,128)S(1)}) custom-call(s32[2]{0:T(128)S(1)} %pad_add_fusion.refs_0_, f32[8,324,324]{2,1,0:T(8,128)S(1)} %get-tuple-element.69.refs_1_, f32[1744,256]{1,0:T(8,128)} %collective-permute-done.1.refs_4_.refs_2_, f32[4,328,384]{2,1,0:T(8,128)S(1)} %get-tuple-element.88.refs_3_, ...), custom_call_target="tpu_custom_call" | custom-call | tf_op jit(solution)/shard_map/pallas_call | solution.py:45
  152.1 0.0 collective-permute-done.11.refs_2_
  152.1 3.0 %shard_map.33 = (f32[2,324,8,324]{3,2,1,0:T(8,128)}, f32[8,128]{1,0:T(8,128)S(1)}) custom-call(s32[2]{0:T(128)S(1)} %pad_add_fusion.refs_0_, f32[2,324,8,324]{3,2,1,0:T(8,128)} %get-tuple-element.99.refs_1_, bf16[2,4,328,128]{3,2,1,0:T(8,128)(2,1)S(1)} %collective-permute-done.11.refs_2_, ...), custom_call_target="tpu_custom_call", output_to_operand_aliasing={{0}: (1, {})} | custom-call | flops 10000000000 | bytes 100000000 | tf_op jit(solution)/shard_map/pallas_call | solution.py:45
  155.1 0.0 collective-permute-done.12.refs_2_
  155.1 2.8 %shard_map.34 = (f32[2,324,8,324]{3,2,1,0:T(8,128)}, f32[8,128]{1,0:T(8,128)S(1)}) custom-call(s32[2]{0:T(128)S(1)} %pad_add_fusion.refs_0_, f32[2,324,8,324]{3,2,1,0:T(8,128)} %get-tuple-element.101.refs_1_, bf16[2,4,328,128]{3,2,1,0:T(8,128)(2,1)S(1)} %collective-permute-done.12.refs_2_, ...), custom_call_target="tpu_custom_call", output_to_operand_aliasing={{0}: (1, {})} | custom-call | flops 10000000000 | bytes 100000000 | tf_op jit(solution)/shard_map/pallas_call | solution.py:45
  157.8 0.0 collective-permute-done.13.refs_5_
  157.9 0.0 collective-permute-done.14.refs_6_
  157.9 0.6 shard_map.35
  158.5 8.8 %collective-permute-done.15.refs_2_ = bf16[2,4,72,324]{3,2,1,0:T(8,128)(2,1)S(1)} collective-permute-done((bf16[2,4,72,324]{3,2,1,0:T(8,128)(2,1)S(1)}, bf16[2,4,72,324]{3,2,1,0:T(8,128)(2,1)S(1)}, u32[]{:S(2)}, u32[]{:S(2)}) %collective-permute-start.15) | collective-permute-done | bytes 373280 | tf_op jit(solution)/shard_map/ppermute | solution.py:522
  167.3 2.8 %shard_map.36 = (f32[2,324,8,324]{3,2,1,0:T(8,128)}, f32[8,128]{1,0:T(8,128)}) custom-call(s32[2]{0:T(128)S(1)} %pad_add_fusion.refs_0_, f32[2,324,8,324]{3,2,1,0:T(8,128)} %get-tuple-element.110.refs_1_, bf16[2,4,72,324]{3,2,1,0:T(8,128)(2,1)S(1)} %collective-permute-done.15.refs_2_, ...), custom_call_target="tpu_custom_call", output_to_operand_aliasing={{0}: (1, {})} | custom-call | tf_op jit(solution)/shard_map/pallas_call | solution.py:45
  (11 shorter events, 0.1 us)
Async XLA Ops:
  0.0 15.3 %collective-permute-start = (bf16[4,2048,324]{1,0,2:T(4,128)(2,1)}, bf16[4,2048,324]{1,0,2:T(4,128)(2,1)}, u32[]{:S(2)}, u32[]{:S(2)}) collective-permute-start(bf16[4,2048,324]{1,0,2:T(4,128)(2,1)} %param.1), channel_id=1, source_target_pairs={{0,2},{2,0},{4,6},{6,4},{8,10},{10,8},{12,14},{14,12},{16,18},{18,... | collective-permute-start | bytes 15925256 | tf_op jit(solution)/shard_map/ppermute | solution.py:481
  3.1 55.1 %collective-permute-start.4 = (bf16[128,4,2048]{2,1,0:T(4,128)(2,1)S(1)}, bf16[128,4,2048]{2,1,0:T(4,128)(2,1)}, u32[]{:S(2)}, u32[]{:S(2)}) collective-permute-start(bf16[128,4,2048]{2,1,0:T(4,128)(2,1)S(1)} %slice_bitcast_fusion.refs_3_), channel_id=1, source_target_pairs={{0,16},{1,17},{4,20},{5,21},{8,24},{9,25},{12,28},{13,29},{18,2},{... | collective-permute-start | bytes 6291464 | tf_op jit(solution)/shard_map/ppermute | solution.py:484
  15.3 17.6 %copy-start = (bf16[4,2048,324]{1,2,0:T(8,128)(2,1)}, bf16[4,2048,324]{1,2,0:T(8,128)(2,1)S(1)}, u32[]{:S(2)}) copy-start(bf16[4,2048,324]{1,2,0:T(8,128)(2,1)S(1)} %copy.18) | copy-start | bytes 15925252
  22.7 5.2 %copy-start.2 = (bf16[4,2048,324]{1,2,0:T(8,128)(2,1)}, bf16[4,2048,324]{1,2,0:T(8,128)(2,1)S(1)}, u32[]{:S(2)}) copy-start(bf16[4,2048,324]{1,2,0:T(8,128)(2,1)S(1)} %copy.17) | copy-start | bytes 15925252
  34.4 30.9 %collective-permute-start.3 = (bf16[512,2048]{1,0:T(8,128)(2,1)}, bf16[512,2048]{1,0:T(8,128)(2,1)}, u32[]{:S(2)}, u32[]{:S(2)}) collective-permute-start(bf16[512,2048]{1,0:T(8,128)(2,1)} %bitcast.5), channel_id=1, source_target_pairs={{0,16},{1,17},{4,20},{5,21},{8,24},{9,25},{12,28},{13,29},{18,2},{... | collective-permute-start | bytes 6291464 | tf_op jit(solution)/shard_map/ppermute | solution.py:497
  37.1 37.5 %collective-permute-start.2 = (f32[1744,256]{1,0:T(8,128)}, f32[1744,256]{1,0:T(8,128)}, u32[]{:S(2)}, u32[]{:S(2)}) collective-permute-start(f32[1744,256]{1,0:T(8,128)} %get-tuple-element.71), channel_id=1, source_target_pairs={{0,1},{1,0},{4,5},{5,4},{8,9},{9,8},{12,13},{13,12},{18,19},{19,18... | collective-permute-start | bytes 5357576 | tf_op jit(solution)/shard_map/ppermute | solution.py:492
  40.5 53.2 %collective-permute-start.1 = (f32[1744,256]{1,0:T(8,128)}, f32[1744,256]{1,0:T(8,128)}, u32[]{:S(2)}, u32[]{:S(2)}) collective-permute-start(f32[1744,256]{1,0:T(8,128)} %get-tuple-element.70), channel_id=1, source_target_pairs={{0,1},{1,0},{2,3},{3,2},{4,5},{5,4},{6,7},{7,6},{8,9},{9,8},{10,11... | collective-permute-start | bytes 5357576 | tf_op jit(solution)/shard_map/ppermute | solution.py:490
  43.6 17.3 %slice-start = ((s8[5373952]{0:T(1024)(128)(4,1)}), s8[1179648]{0:T(1024)(128)(4,1)S(1)}, s32[]{:S(2)}) async-start(s8[5373952]{0:T(1024)(128)(4,1)} %bitcast.19), calls=%async_computation | async-start | bytes 2359296
  45.9 2.5 %copy-start.1 = (bf16[4,2048,324]{1,2,0:T(8,128)(2,1)S(1)}, bf16[4,2048,324]{1,2,0:T(8,128)(2,1)}, u32[]{:S(2)}) copy-start(bf16[4,2048,324]{1,2,0:T(8,128)(2,1)} %copy-done) | copy-start | bytes 15925252
  48.4 2.5 %copy-start.3 = (bf16[4,2048,324]{1,2,0:T(8,128)(2,1)S(1)}, bf16[4,2048,324]{1,2,0:T(8,128)(2,1)}, u32[]{:S(2)}) copy-start(bf16[4,2048,324]{1,2,0:T(8,128)(2,1)} %copy-done.2) | copy-start | bytes 15925252
  50.9 10.0 %slice-start.1 = ((s8[5373952]{0:T(1024)(128)(4,1)}), s8[4194304]{0:T(1024)(128)(4,1)S(1)}, s32[]{:S(2)}) async-start(s8[5373952]{0:T(1024)(128)(4,1)} %bitcast.19), calls=%async_computation.1 | async-start | bytes 8388608
  60.9 1.6 copy-start.4
  61.6 35.3 %collective-permute-start.6 = (f32[2,4,328,128]{3,2,1,0:T(8,128)S(1)}, f32[2,4,328,128]{3,2,1,0:T(8,128)S(1)}, u32[]{:S(2)}, u32[]{:S(2)}) collective-permute-start(f32[2,4,328,128]{3,2,1,0:T(8,128)S(1)} %get-tuple-element.82), channel_id=1, source_target_pairs={{2,3},{3,2},{6,7},{7,6},{10,11},{11,10},{14,15},{15,14},{16,17},{1... | collective-permute-start | bytes 4030472 | tf_op jit(solution)/shard_map/ppermute | solution.py:515
  62.6 33.0 %collective-permute-start.7 = (bf16[272,2048]{1,0:T(8,128)(2,1)S(1)}, bf16[272,2048]{1,0:T(8,128)(2,1)S(1)}, u32[]{:S(2)}, u32[]{:S(2)}) collective-permute-start(bf16[272,2048]{1,0:T(8,128)(2,1)S(1)} %copy-done.4), channel_id=1, source_target_pairs={{0,16},{1,17},{4,20},{5,21},{8,24},{9,25},{12,28},{13,29},{18,2},{... | collective-permute-start | bytes 3342344 | tf_op jit(solution)/shard_map/ppermute | solution.py:499
  67.2 29.8 %collective-permute-start.8 = (f32[8,128]{1,0:T(8,128)S(1)}, f32[8,128]{1,0:T(8,128)S(1)}, u32[]{:S(2)}, u32[]{:S(2)}) collective-permute-start(f32[8,128]{1,0:T(8,128)S(1)} %get-tuple-element.78.refs_3_), channel_id=1, source_target_pairs={{8,10},{12,14},{18,16},{22,20},{9,11},{13,15},{19,17},{23,21}} | collective-permute-start | bytes 12296 | tf_op jit(solution)/shard_map/ppermute | solution.py:533
  74.6 24.8 %collective-permute-start.5 = (f32[2,4,328,128]{3,2,1,0:T(8,128)S(1)}, f32[2,4,328,128]{3,2,1,0:T(8,128)S(1)}, u32[]{:S(2)}, u32[]{:S(2)}) collective-permute-start(f32[2,4,328,128]{3,2,1,0:T(8,128)S(1)} %get-tuple-element.80), channel_id=1, source_target_pairs={{2,3},{3,2},{6,7},{7,6},{10,11},{11,10},{14,15},{15,14},{16,17},{1... | collective-permute-start | bytes 4030472 | tf_op jit(solution)/shard_map/ppermute | solution.py:515
  96.2 47.1 %collective-permute-start.10 = (f32[2,4,72,324]{3,2,1,0:T(8,128)S(1)}, f32[2,4,72,324]{3,2,1,0:T(8,128)S(1)}, u32[]{:S(2)}, u32[]{:S(2)}) collective-permute-start(f32[2,4,72,324]{3,2,1,0:T(8,128)S(1)} %get-tuple-element.91), channel_id=1, source_target_pairs={{2,3},{3,2},{6,7},{7,6},{10,11},{11,10},{14,15},{15,14},{16,17},{1... | collective-permute-start | bytes 2239496 | tf_op jit(solution)/shard_map/ppermute | solution.py:515
  98.0 54.0 %collective-permute-start.11 = (bf16[2,4,328,128]{3,2,1,0:T(8,128)(2,1)S(1)}, bf16[2,4,328,128]{3,2,1,0:T(8,128)(2,1)S(1)}, u32[]{:S(2)}, u32[]{:S(2)}) collective-permute-start(bf16[2,4,328,128]{3,2,1,0:T(8,128)(2,1)S(1)} %get-tuple-element.94.refs_1_), channel_id=1, source_target_pairs={{16,0},{17,1},{20,4},{21,5},{24,8},{25,9},{28,12},{29,13},{2,18},{... | collective-permute-start | bytes 2015240 | tf_op jit(solution)/shard_map/ppermute | solution.py:522
  100.4 54.6 %collective-permute-start.12 = (bf16[2,4,328,128]{3,2,1,0:T(8,128)(2,1)S(1)}, bf16[2,4,328,128]{3,2,1,0:T(8,128)(2,1)S(1)}, u32[]{:S(2)}, u32[]{:S(2)}) collective-permute-start(bf16[2,4,328,128]{3,2,1,0:T(8,128)(2,1)S(1)} %get-tuple-element.95.refs_2_), channel_id=1, source_target_pairs={{16,0},{17,1},{20,4},{21,5},{24,8},{25,9},{28,12},{29,13},{2,18},{... | collective-permute-start | bytes 2015240 | tf_op jit(solution)/shard_map/ppermute | solution.py:522
  104.6 41.6 %collective-permute-start.9 = (f32[4,328,384]{2,1,0:T(8,128)S(1)}, f32[4,328,384]{2,1,0:T(8,128)S(1)}, u32[]{:S(2)}, u32[]{:S(2)}) collective-permute-start(f32[4,328,384]{2,1,0:T(8,128)S(1)} %get-tuple-element.88.refs_3_), channel_id=1, source_target_pairs={{0,2},{1,3},{4,6},{5,7},{8,10},{9,11},{12,14},{13,15},{18,16},{19,... | collective-permute-start | bytes 6045704 | tf_op jit(solution)/shard_map/ppermute | solution.py:539
  144.0 23.3 %collective-permute-start.15 = (bf16[2,4,72,324]{3,2,1,0:T(8,128)(2,1)S(1)}, bf16[2,4,72,324]{3,2,1,0:T(8,128)(2,1)S(1)}, u32[]{:S(2)}, u32[]{:S(2)}) collective-permute-start(bf16[2,4,72,324]{3,2,1,0:T(8,128)(2,1)S(1)} %get-tuple-element.93.refs_1_), channel_id=1, source_target_pairs={{16,0},{17,1},{20,4},{21,5},{24,8},{25,9},{28,12},{29,13},{2,18},{... | collective-permute-start | bytes 1119752 | tf_op jit(solution)/shard_map/ppermute | solution.py:522
  145.3 12.5 %collective-permute-start.13 = (bf16[2,2,2,328,128]{4,3,2,1,0:T(8,128)(2,1)S(1)}, bf16[2,2,2,328,128]{4,3,2,1,0:T(8,128)(2,1)S(1)}, u32[]{:S(2)}, u32[]{:S(2)}) collective-permute-start(bf16[2,2,2,328,128]{4,3,2,1,0:T(8,128)(2,1)S(1)} %get-tuple-element.107), channel_id=1, source_target_pairs={{2,3},{3,2},{6,7},{7,6},{10,11},{11,10},{14,15},{15,14},{16,17},{1... | collective-permute-start | bytes 2015240 | tf_op jit(solution)/shard_map/ppermute | solution.py:527
  146.2 11.7 %collective-permute-start.14 = (bf16[1,2,2,72,324]{4,3,2,1,0:T(8,128)(2,1)S(1)}, bf16[1,2,2,72,324]{4,3,2,1,0:T(8,128)(2,1)S(1)}, u32[]{:S(2)}, u32[]{:S(2)}) collective-permute-start(bf16[1,2,2,72,324]{4,3,2,1,0:T(8,128)(2,1)S(1)} %get-tuple-element.108), channel_id=1, source_target_pairs={{2,3},{3,2},{6,7},{7,6},{10,11},{11,10},{14,15},{15,14},{16,17},{1... | collective-permute-start | bytes 559880 | tf_op jit(solution)/shard_map/ppermute | solution.py:527

commit v18 on v17

--- a/solution.py
+++ b/solution.py
@@ -543,8 +543,7 @@
     last, token = cross(late, token, given)
     out, token = near_sum(at, keep, crossed, share, given, states, (token,))
 
-    for k in early:
-        out, token = into_place(0, at, out, *returned([theirs[k]], [k], widths, ops), (token,), LONG)
+    out, token = into_place(0, at, out, *returned([theirs[k] for k in early], early, widths, ops), (token,), 2 * LONG)
     placed = completed([tiles[k] for k in early + late], turned, last, widths, ops)
     out, token = into_place(1, at, out, *placed, (token,), LONG)
     out, token = into_place(0, at, out, *returned([theirs[full]], late, widths, ops), (token,))

time: 171 us -> 171 us (level)
  waiting for transfers between devices: 34 us -> 35.8 us
    ppermute x3, waiting for transfers between devices: 8.83 us -> 10.6 us  [sum_up(): theirs[k] = lax.ppermute(codes[k], both, back)]
    pallas_call x20 -> x19, Pallas kernels: 43.8 us -> 42.1 us  [call(): return lambda *operands: kernel(*operands, *after)]
  transfers between devices with their start and end apart: 16 -> 16, of which waited for: 4 -> 4; matrix products, arithmetic and copies ran while one was open for 14% -> 14% of each run, Pallas kernels for 24% -> 23%
where the time goes in v18:
time: 171 us; the launch traced here: 170 us
  starting transfers between devices  62.3 us (36%)
  Pallas kernels  42.1 us (25%)
  waiting for transfers between devices  35.8 us (21%)
  local copies, waits for them, and re-layouts  29.4 us (17%)
    pallas_call x19, Pallas kernels, call(): return lambda *operands: kernel(*operands, *after)  42.1 us
    ppermute x1, starting transfers between devices, paired(): given = lax.ppermute(share, both, to_second)  38 us
    ppermute x1, waiting for transfers between devices, paired(): crossed = lax.ppermute(crossed, 'det', [(0, 1), (1, 0)])  18.4 us
    ppermute x3, waiting for transfers between devices, sum_up(): theirs[k] = lax.ppermute(codes[k], both, back)  10.6 us
    optimization_barrier x1, local copies, waits for them, and re-layouts, paired(): partner, own = lax.optimization_barrier((partner, own))  7.35 us
    ppermute x1, starting transfers between devices, paired(): got = [lax.ppermute(first, both, over)]  6.81 us
    ppermute x1, waiting for transfers between devices, paired(): doubled = lax.ppermute(doubled, both, first_across)  6.69 us
    optimization_barrier x1, local copies, waits for them, and re-layouts, paired(): first, later = lax.optimization_barrier((first, amplitudes))  5.42 us
  transfers between devices with their start and end apart: 16, of which 4 were waited for; matrix products, arithmetic and copies ran while one was open for 14% of the time, Pallas kernels for 23%

profile of v18, /device:TPU:0, one launch (start us, length us, event | category | flops | bytes accessed | tf_op | source)
XLA Modules:
  0.0 170.3 jit_solution(5656863351049001820)
XLA Ops:
  0.0 0.5 collective-permute-start
  0.5 2.6 %slice_bitcast_fusion.refs_3_ = bf16[128,4,2048]{2,1,0:T(4,128)(2,1)S(1)} fusion(bf16[4,2048,324]{1,0,2:T(4,128)(2,1)} %param.1), kind=kLoop, calls=%fused_computation.2 | loop fusion | bytes 4194304 | tf_op jit(solution)/shard_map/transpose | solution.py:482
  3.1 6.8 %collective-permute-start.4 = (bf16[128,4,2048]{2,1,0:T(4,128)(2,1)S(1)}, bf16[128,4,2048]{2,1,0:T(4,128)(2,1)}, u32[]{:S(2)}, u32[]{:S(2)}) collective-permute-start(bf16[128,4,2048]{2,1,0:T(4,128)(2,1)S(1)} %slice_bitcast_fusion.refs_3_), channel_id=1, source_target_pairs={{0,16},{1,17},{4,20},{5,21},{8,24},{9,25},{12,28},{13,29},{18,2},{... | collective-permute-start | bytes 6291464 | tf_op jit(solution)/shard_map/ppermute | solution.py:484
  9.9 5.4 %copy.17 = bf16[4,2048,324]{1,2,0:T(8,128)(2,1)S(1)} copy(bf16[4,2048,324]{1,0,2:T(4,128)(2,1)} %param.1) | data formatting | bytes 10616832 | tf_op jit(solution)/shard_map/optimization_barrier | solution.py:483
  15.3 0.0 copy-start
  15.3 0.0 collective-permute-done
  15.3 7.4 %copy.16 = bf16[4,2048,324]{1,2,0:T(8,128)(2,1)S(1)} copy(bf16[4,2048,324]{1,0,2:T(4,128)(2,1)} %collective-permute-done) | data formatting | bytes 10616832 | tf_op jit(solution)/shard_map/optimization_barrier | solution.py:486
  22.7 0.0 copy-start.2
  22.7 5.2 %shard_map.17 = (f32[1744,256]{1,0:T(8,128)}, f32[8,128]{1,0:T(8,128)S(1)}) custom-call(s32[1]{0:T(128)} %bitcast.refs_0_, bf16[4,324,2048]{2,1,0:T(8,128)(2,1)S(1)} %bitcast.14, bf16[4,324,2048]{2,1,0:T(8,128)(2,1)S(1)} %bitcast.27, bf16[128,4,2048]{2,1,0:T(4,128)(2,1)S(1)} %slice_bitcast_fusion.refs_3_), custom_call_target="tpu_custom_call" | custom-call | tf_op jit(solution)/shard_map/pallas_call | solution.py:45
  27.9 5.1 %shard_map.18 = (f32[1744,256]{1,0:T(8,128)}, f32[8,128]{1,0:T(8,128)S(1)}) custom-call(s32[1]{0:T(128)} %bitcast.refs_0_, bf16[4,324,2048]{2,1,0:T(8,128)(2,1)S(1)} %bitcast.15, bf16[4,324,2048]{2,1,0:T(8,128)(2,1)S(1)} %bitcast.28, f32[8,128]{1,0:T(8,128)S(1)} %get-tuple-element.61.refs_3_), custom_call_target="tpu_custom_call" | custom-call | tf_op jit(solution)/shard_map/pallas_call | solution.py:45
  32.9 1.5 slice.11
  34.5 2.7 %collective-permute-start.3 = (bf16[512,2048]{1,0:T(8,128)(2,1)}, bf16[512,2048]{1,0:T(8,128)(2,1)}, u32[]{:S(2)}, u32[]{:S(2)}) collective-permute-start(bf16[512,2048]{1,0:T(8,128)(2,1)} %bitcast.5), channel_id=1, source_target_pairs={{0,16},{1,17},{4,20},{5,21},{8,24},{9,25},{12,28},{13,29},{18,2},{... | collective-permute-start | bytes 6291464 | tf_op jit(solution)/shard_map/ppermute | solution.py:497
  37.1 3.4 %collective-permute-start.2 = (f32[1744,256]{1,0:T(8,128)}, f32[1744,256]{1,0:T(8,128)}, u32[]{:S(2)}, u32[]{:S(2)}) collective-permute-start(f32[1744,256]{1,0:T(8,128)} %get-tuple-element.69), channel_id=1, source_target_pairs={{0,1},{1,0},{4,5},{5,4},{8,9},{9,8},{12,13},{13,12},{18,19},{19,18... | collective-permute-start | bytes 5357576 | tf_op jit(solution)/shard_map/ppermute | solution.py:492
  40.5 0.6 collective-permute-start.1
  41.1 0.1 pad_add_fusion.refs_0_
  41.2 2.4 %slice.10 = bf16[4,68,2048]{2,1,0:T(8,128)(2,1)} slice(bf16[4,324,2048]{2,1,0:T(8,128)(2,1)} %bitcast.17), slice={[0:4], [256:324], [0:2048]} | slice | bytes 2228224 | tf_op jit(solution)/shard_map/slice | solution.py:495
  43.7 2.3 %reshape.9 = bf16[272,2048]{1,0:T(8,128)(2,1)} reshape(bf16[4,68,2048]{2,1,0:T(8,128)(2,1)} %slice.10) | data formatting | bytes 2228224 | tf_op jit(solution)/shard_map/reshape | solution.py:495
  45.9 2.5 %copy-done.1 = bf16[4,2048,324]{1,2,0:T(8,128)(2,1)S(1)} copy-done((bf16[4,2048,324]{1,2,0:T(8,128)(2,1)S(1)}, bf16[4,2048,324]{1,2,0:T(8,128)(2,1)}, u32[]{:S(2)}) %copy-start.1) | copy-done | bytes 5308440
  48.5 2.5 %copy-done.3 = bf16[4,2048,324]{1,2,0:T(8,128)(2,1)S(1)} copy-done((bf16[4,2048,324]{1,2,0:T(8,128)(2,1)S(1)}, bf16[4,2048,324]{1,2,0:T(8,128)(2,1)}, u32[]{:S(2)}) %copy-start.3) | copy-done | bytes 5308440
  51.0 7.2 %shard_map.19 = (f32[8,324,324]{2,1,0:T(8,128)S(1)}, f32[8,128]{1,0:T(8,128)S(1)}) custom-call(s32[1]{0:T(128)} %bitcast.refs_0_, bf16[4,324,2048]{2,1,0:T(8,128)(2,1)S(1)} %bitcast.18, bf16[4,324,2048]{2,1,0:T(8,128)(2,1)S(1)} %bitcast.29, f32[8,128]{1,0:T(8,128)S(1)} %get-tuple-element.66.refs_3_), custom_call_target="tpu_custom_call" | custom-call | tf_op jit(solution)/shard_map/pallas_call | solution.py:45
  58.2 0.0 collective-permute-done.4
  58.2 2.7 %copy.13 = bf16[4,128,2048]{2,1,0:T(8,128)(2,1)S(1)} copy(bf16[4,128,2048]{2,0,1:T(4,128)(2,1)} %bitcast.6) | data formatting | bytes 4194304 | tf_op jit(solution)/shard_map/transpose | solution.py:502
  60.9 0.0 slice-done
  61.0 0.0 slice-done.1
  61.0 0.7 shard_map.20
  61.7 0.9 collective-permute-start.6
  62.6 2.1 %collective-permute-start.7 = (bf16[272,2048]{1,0:T(8,128)(2,1)S(1)}, bf16[272,2048]{1,0:T(8,128)(2,1)S(1)}, u32[]{:S(2)}, u32[]{:S(2)}) collective-permute-start(bf16[272,2048]{1,0:T(8,128)(2,1)S(1)} %copy-done.4), channel_id=1, source_target_pairs={{0,16},{1,17},{4,20},{5,21},{8,24},{9,25},{12,28},{13,29},{18,2},{... | collective-permute-start | bytes 3342344 | tf_op jit(solution)/shard_map/ppermute | solution.py:499
  64.7 0.7 shard_map.21
  65.4 0.0 collective-permute-done.3.refs_2_
  65.4 1.8 %shard_map.22 = (f32[2,4,328,128]{3,2,1,0:T(8,128)S(1)}, f32[8,128]{1,0:T(8,128)S(1)}) custom-call(s32[2]{0:T(128)S(1)} %pad_add_fusion.refs_0_, bf16[4,324,2048]{2,1,0:T(8,128)(2,1)S(1)} %bitcast.23, bf16[512,2048]{1,0:T(8,128)(2,1)} %collective-permute-done.3.refs_2_, f32[8,128]{1,0:T(8,128)S(1)} %get-tuple-element.75.refs_3_), custom_call_target="tpu_custom_call" | custom-call | tf_op jit(solution)/shard_map/pallas_call | solution.py:45
  67.2 0.7 collective-permute-start.8
  67.9 6.7 %collective-permute-done.2.refs_5_.refs_2_ = f32[1744,256]{1,0:T(8,128)} collective-permute-done((f32[1744,256]{1,0:T(8,128)}, f32[1744,256]{1,0:T(8,128)}, u32[]{:S(2)}, u32[]{:S(2)}) %collective-permute-start.2) | collective-permute-done | bytes 1785888 | tf_op jit(solution)/shard_map/ppermute | solution.py:492
  74.6 0.7 collective-permute-start.5
  75.3 18.4 %collective-permute-done.1.refs_4_.refs_2_ = f32[1744,256]{1,0:T(8,128)} collective-permute-done((f32[1744,256]{1,0:T(8,128)}, f32[1744,256]{1,0:T(8,128)}, u32[]{:S(2)}, u32[]{:S(2)}) %collective-permute-start.1) | collective-permute-done | bytes 1785888 | tf_op jit(solution)/shard_map/ppermute | solution.py:490
  93.7 1.8 %shard_map.23 = (f32[2,4,328,128]{3,2,1,0:T(8,128)S(1)}, f32[8,128]{1,0:T(8,128)S(1)}) custom-call(s32[2]{0:T(128)S(1)} %pad_add_fusion.refs_0_, bf16[4,324,2048]{2,1,0:T(8,128)(2,1)S(1)} %bitcast.24, bf16[512,2048]{1,0:T(8,128)(2,1)} %collective-permute-done.3.refs_2_, f32[8,128]{1,0:T(8,128)S(1)} %get-tuple-element.76.refs_3_, ...), custom_call_target="tpu_custom_call" | custom-call | flops 10000000000 | bytes 100000000 | tf_op jit(solution)/shard_map/pallas_call | solution.py:45
  95.6 0.0 collective-permute-done.7.refs_2_
  95.6 0.7 shard_map.24
  96.3 0.7 collective-permute-start.10
  97.0 0.0 collective-permute-done.6.refs_2_
  97.0 0.0 collective-permute-done.8.refs_4_
  97.0 1.1 shard_map.25
  98.1 1.3 collective-permute-start.11
  99.4 0.0 collective-permute-done.5.refs_2_
  99.4 1.1 shard_map.26
  100.5 1.3 collective-permute-start.12
  101.8 2.8 %shard_map.27 = (f32[4,328,384]{2,1,0:T(8,128)S(1)}, f32[8,128]{1,0:T(8,128)S(1)}) custom-call(s32[2]{0:T(128)S(1)} %pad_add_fusion.refs_0_, f32[8,324,324]{2,1,0:T(8,128)S(1)} %get-tuple-element.67.refs_1_, f32[1744,256]{1,0:T(8,128)} %collective-permute-done.2.refs_5_.refs_2_, f32[8,128]{1,0:T(8,128)S(1)} %get-tuple-element.85.refs_3_), custom_call_target="tpu_custom_call" | custom-call | tf_op jit(solution)/shard_map/pallas_call | solution.py:45
  104.6 38.0 %collective-permute-start.9 = (f32[4,328,384]{2,1,0:T(8,128)S(1)}, f32[4,328,384]{2,1,0:T(8,128)S(1)}, u32[]{:S(2)}, u32[]{:S(2)}) collective-permute-start(f32[4,328,384]{2,1,0:T(8,128)S(1)} %get-tuple-element.86.refs_3_), channel_id=1, source_target_pairs={{0,2},{1,3},{4,6},{5,7},{8,10},{9,11},{12,14},{13,15},{18,16},{19,... | collective-permute-start | bytes 6045704 | tf_op jit(solution)/shard_map/ppermute | solution.py:539
  142.6 0.7 shard_map.28
  143.3 0.0 collective-permute-done.10.refs_2_
  143.3 0.6 shard_map.29
  143.9 0.1 shard_map.30
  144.0 1.3 collective-permute-start.15
  145.3 0.7 collective-permute-start.13
  146.1 0.1 collective-permute-done.9.refs_3_.refs_4_
  146.2 0.7 collective-permute-start.14
  146.9 5.2 %shard_map.32 = (f32[2,324,8,324]{3,2,1,0:T(8,128)}, f32[8,128]{1,0:T(8,128)S(1)}) custom-call(s32[2]{0:T(128)S(1)} %pad_add_fusion.refs_0_, f32[8,324,324]{2,1,0:T(8,128)S(1)} %get-tuple-element.67.refs_1_, f32[1744,256]{1,0:T(8,128)} %collective-permute-done.1.refs_4_.refs_2_, f32[4,328,384]{2,1,0:T(8,128)S(1)} %get-tuple-element.86.refs_3_, ...), custom_call_target="tpu_custom_call" | custom-call | tf_op jit(solution)/shard_map/pallas_call | solution.py:45
  152.1 0.0 collective-permute-done.11.refs_2_
  152.1 0.0 collective-permute-done.12.refs_3_
  152.1 4.0 %shard_map.33 = (f32[2,324,8,324]{3,2,1,0:T(8,128)}, f32[8,128]{1,0:T(8,128)S(1)}) custom-call(s32[2]{0:T(128)S(1)} %pad_add_fusion.refs_0_, f32[2,324,8,324]{3,2,1,0:T(8,128)} %get-tuple-element.97.refs_1_, bf16[2,4,328,128]{3,2,1,0:T(8,128)(2,1)S(1)} %collective-permute-done.11.refs_2_, ...), custom_call_target="tpu_custom_call", output_to_operand_aliasing={{0}: (1, {})} | custom-call | flops 20000000000 | bytes 200000000 | tf_op jit(solution)/shard_map/pallas_call | solution.py:45
  156.1 0.0 collective-permute-done.13.refs_5_
  156.1 0.0 collective-permute-done.14.refs_6_
  156.1 0.6 shard_map.34
  156.7 10.6 %collective-permute-done.15.refs_2_ = bf16[2,4,72,324]{3,2,1,0:T(8,128)(2,1)S(1)} collective-permute-done((bf16[2,4,72,324]{3,2,1,0:T(8,128)(2,1)S(1)}, bf16[2,4,72,324]{3,2,1,0:T(8,128)(2,1)S(1)}, u32[]{:S(2)}, u32[]{:S(2)}) %collective-permute-start.15) | collective-permute-done | bytes 373280 | tf_op jit(solution)/shard_map/ppermute | solution.py:522
  167.3 2.8 %shard_map.35 = (f32[2,324,8,324]{3,2,1,0:T(8,128)}, f32[8,128]{1,0:T(8,128)}) custom-call(s32[2]{0:T(128)S(1)} %pad_add_fusion.refs_0_, f32[2,324,8,324]{3,2,1,0:T(8,128)} %get-tuple-element.106.refs_1_, bf16[2,4,72,324]{3,2,1,0:T(8,128)(2,1)S(1)} %collective-permute-done.15.refs_2_, ...), custom_call_target="tpu_custom_call", output_to_operand_aliasing={{0}: (1, {})} | custom-call | tf_op jit(solution)/shard_map/pallas_call | solution.py:45
  (10 shorter events, 0.1 us)
Async XLA Ops:
  0.0 15.3 %collective-permute-start = (bf16[4,2048,324]{1,0,2:T(4,128)(2,1)}, bf16[4,2048,324]{1,0,2:T(4,128)(2,1)}, u32[]{:S(2)}, u32[]{:S(2)}) collective-permute-start(bf16[4,2048,324]{1,0,2:T(4,128)(2,1)} %param.1), channel_id=1, source_target_pairs={{0,2},{2,0},{4,6},{6,4},{8,10},{10,8},{12,14},{14,12},{16,18},{18,... | collective-permute-start | bytes 15925256 | tf_op jit(solution)/shard_map/ppermute | solution.py:481
  3.1 55.1 %collective-permute-start.4 = (bf16[128,4,2048]{2,1,0:T(4,128)(2,1)S(1)}, bf16[128,4,2048]{2,1,0:T(4,128)(2,1)}, u32[]{:S(2)}, u32[]{:S(2)}) collective-permute-start(bf16[128,4,2048]{2,1,0:T(4,128)(2,1)S(1)} %slice_bitcast_fusion.refs_3_), channel_id=1, source_target_pairs={{0,16},{1,17},{4,20},{5,21},{8,24},{9,25},{12,28},{13,29},{18,2},{... | collective-permute-start | bytes 6291464 | tf_op jit(solution)/shard_map/ppermute | solution.py:484
  15.3 17.6 %copy-start = (bf16[4,2048,324]{1,2,0:T(8,128)(2,1)}, bf16[4,2048,324]{1,2,0:T(8,128)(2,1)S(1)}, u32[]{:S(2)}) copy-start(bf16[4,2048,324]{1,2,0:T(8,128)(2,1)S(1)} %copy.17) | copy-start | bytes 15925252
  22.7 5.2 %copy-start.2 = (bf16[4,2048,324]{1,2,0:T(8,128)(2,1)}, bf16[4,2048,324]{1,2,0:T(8,128)(2,1)S(1)}, u32[]{:S(2)}) copy-start(bf16[4,2048,324]{1,2,0:T(8,128)(2,1)S(1)} %copy.16) | copy-start | bytes 15925252
  34.5 30.9 %collective-permute-start.3 = (bf16[512,2048]{1,0:T(8,128)(2,1)}, bf16[512,2048]{1,0:T(8,128)(2,1)}, u32[]{:S(2)}, u32[]{:S(2)}) collective-permute-start(bf16[512,2048]{1,0:T(8,128)(2,1)} %bitcast.5), channel_id=1, source_target_pairs={{0,16},{1,17},{4,20},{5,21},{8,24},{9,25},{12,28},{13,29},{18,2},{... | collective-permute-start | bytes 6291464 | tf_op jit(solution)/shard_map/ppermute | solution.py:497
  37.1 37.5 %collective-permute-start.2 = (f32[1744,256]{1,0:T(8,128)}, f32[1744,256]{1,0:T(8,128)}, u32[]{:S(2)}, u32[]{:S(2)}) collective-permute-start(f32[1744,256]{1,0:T(8,128)} %get-tuple-element.69), channel_id=1, source_target_pairs={{0,1},{1,0},{4,5},{5,4},{8,9},{9,8},{12,13},{13,12},{18,19},{19,18... | collective-permute-start | bytes 5357576 | tf_op jit(solution)/shard_map/ppermute | solution.py:492
  40.5 53.2 %collective-permute-start.1 = (f32[1744,256]{1,0:T(8,128)}, f32[1744,256]{1,0:T(8,128)}, u32[]{:S(2)}, u32[]{:S(2)}) collective-permute-start(f32[1744,256]{1,0:T(8,128)} %get-tuple-element.68), channel_id=1, source_target_pairs={{0,1},{1,0},{2,3},{3,2},{4,5},{5,4},{6,7},{7,6},{8,9},{9,8},{10,11... | collective-permute-start | bytes 5357576 | tf_op jit(solution)/shard_map/ppermute | solution.py:490
  43.6 17.3 %slice-start = ((s8[5373952]{0:T(1024)(128)(4,1)}), s8[1179648]{0:T(1024)(128)(4,1)S(1)}, s32[]{:S(2)}) async-start(s8[5373952]{0:T(1024)(128)(4,1)} %bitcast.19), calls=%async_computation | async-start | bytes 2359296
  45.9 2.5 %copy-start.1 = (bf16[4,2048,324]{1,2,0:T(8,128)(2,1)S(1)}, bf16[4,2048,324]{1,2,0:T(8,128)(2,1)}, u32[]{:S(2)}) copy-start(bf16[4,2048,324]{1,2,0:T(8,128)(2,1)} %copy-done) | copy-start | bytes 15925252
  48.4 2.5 %copy-start.3 = (bf16[4,2048,324]{1,2,0:T(8,128)(2,1)S(1)}, bf16[4,2048,324]{1,2,0:T(8,128)(2,1)}, u32[]{:S(2)}) copy-start(bf16[4,2048,324]{1,2,0:T(8,128)(2,1)} %copy-done.2) | copy-start | bytes 15925252
  51.0 10.0 %slice-start.1 = ((s8[5373952]{0:T(1024)(128)(4,1)}), s8[4194304]{0:T(1024)(128)(4,1)S(1)}, s32[]{:S(2)}) async-start(s8[5373952]{0:T(1024)(128)(4,1)} %bitcast.19), calls=%async_computation.1 | async-start | bytes 8388608
  61.0 1.6 copy-start.4
  61.7 35.3 %collective-permute-start.6 = (f32[2,4,328,128]{3,2,1,0:T(8,128)S(1)}, f32[2,4,328,128]{3,2,1,0:T(8,128)S(1)}, u32[]{:S(2)}, u32[]{:S(2)}) collective-permute-start(f32[2,4,328,128]{3,2,1,0:T(8,128)S(1)} %get-tuple-element.80), channel_id=1, source_target_pairs={{2,3},{3,2},{6,7},{7,6},{10,11},{11,10},{14,15},{15,14},{16,17},{1... | collective-permute-start | bytes 4030472 | tf_op jit(solution)/shard_map/ppermute | solution.py:515
  62.6 33.0 %collective-permute-start.7 = (bf16[272,2048]{1,0:T(8,128)(2,1)S(1)}, bf16[272,2048]{1,0:T(8,128)(2,1)S(1)}, u32[]{:S(2)}, u32[]{:S(2)}) collective-permute-start(bf16[272,2048]{1,0:T(8,128)(2,1)S(1)} %copy-done.4), channel_id=1, source_target_pairs={{0,16},{1,17},{4,20},{5,21},{8,24},{9,25},{12,28},{13,29},{18,2},{... | collective-permute-start | bytes 3342344 | tf_op jit(solution)/shard_map/ppermute | solution.py:499
  67.2 29.8 %collective-permute-start.8 = (f32[8,128]{1,0:T(8,128)S(1)}, f32[8,128]{1,0:T(8,128)S(1)}, u32[]{:S(2)}, u32[]{:S(2)}) collective-permute-start(f32[8,128]{1,0:T(8,128)S(1)} %get-tuple-element.76.refs_3_), channel_id=1, source_target_pairs={{8,10},{12,14},{18,16},{22,20},{9,11},{13,15},{19,17},{23,21}} | collective-permute-start | bytes 12296 | tf_op jit(solution)/shard_map/ppermute | solution.py:533
  74.6 24.8 %collective-permute-start.5 = (f32[2,4,328,128]{3,2,1,0:T(8,128)S(1)}, f32[2,4,328,128]{3,2,1,0:T(8,128)S(1)}, u32[]{:S(2)}, u32[]{:S(2)}) collective-permute-start(f32[2,4,328,128]{3,2,1,0:T(8,128)S(1)} %get-tuple-element.78), channel_id=1, source_target_pairs={{2,3},{3,2},{6,7},{7,6},{10,11},{11,10},{14,15},{15,14},{16,17},{1... | collective-permute-start | bytes 4030472 | tf_op jit(solution)/shard_map/ppermute | solution.py:515
  96.3 47.0 %collective-permute-start.10 = (f32[2,4,72,324]{3,2,1,0:T(8,128)S(1)}, f32[2,4,72,324]{3,2,1,0:T(8,128)S(1)}, u32[]{:S(2)}, u32[]{:S(2)}) collective-permute-start(f32[2,4,72,324]{3,2,1,0:T(8,128)S(1)} %get-tuple-element.89), channel_id=1, source_target_pairs={{2,3},{3,2},{6,7},{7,6},{10,11},{11,10},{14,15},{15,14},{16,17},{1... | collective-permute-start | bytes 2239496 | tf_op jit(solution)/shard_map/ppermute | solution.py:515
  98.1 54.0 %collective-permute-start.11 = (bf16[2,4,328,128]{3,2,1,0:T(8,128)(2,1)S(1)}, bf16[2,4,328,128]{3,2,1,0:T(8,128)(2,1)S(1)}, u32[]{:S(2)}, u32[]{:S(2)}) collective-permute-start(bf16[2,4,328,128]{3,2,1,0:T(8,128)(2,1)S(1)} %get-tuple-element.92.refs_1_), channel_id=1, source_target_pairs={{16,0},{17,1},{20,4},{21,5},{24,8},{25,9},{28,12},{29,13},{2,18},{... | collective-permute-start | bytes 2015240 | tf_op jit(solution)/shard_map/ppermute | solution.py:522
  100.5 51.6 %collective-permute-start.12 = (bf16[2,4,328,128]{3,2,1,0:T(8,128)(2,1)S(1)}, bf16[2,4,328,128]{3,2,1,0:T(8,128)(2,1)S(1)}, u32[]{:S(2)}, u32[]{:S(2)}) collective-permute-start(bf16[2,4,328,128]{3,2,1,0:T(8,128)(2,1)S(1)} %get-tuple-element.93.refs_2_), channel_id=1, source_target_pairs={{16,0},{17,1},{20,4},{21,5},{24,8},{25,9},{28,12},{29,13},{2,18},{... | collective-permute-start | bytes 2015240 | tf_op jit(solution)/shard_map/ppermute | solution.py:522
  104.6 41.6 %collective-permute-start.9 = (f32[4,328,384]{2,1,0:T(8,128)S(1)}, f32[4,328,384]{2,1,0:T(8,128)S(1)}, u32[]{:S(2)}, u32[]{:S(2)}) collective-permute-start(f32[4,328,384]{2,1,0:T(8,128)S(1)} %get-tuple-element.86.refs_3_), channel_id=1, source_target_pairs={{0,2},{1,3},{4,6},{5,7},{8,10},{9,11},{12,14},{13,15},{18,16},{19,... | collective-permute-start | bytes 6045704 | tf_op jit(solution)/shard_map/ppermute | solution.py:539
  144.0 23.3 %collective-permute-start.15 = (bf16[2,4,72,324]{3,2,1,0:T(8,128)(2,1)S(1)}, bf16[2,4,72,324]{3,2,1,0:T(8,128)(2,1)S(1)}, u32[]{:S(2)}, u32[]{:S(2)}) collective-permute-start(bf16[2,4,72,324]{3,2,1,0:T(8,128)(2,1)S(1)} %get-tuple-element.91.refs_1_), channel_id=1, source_target_pairs={{16,0},{17,1},{20,4},{21,5},{24,8},{25,9},{28,12},{29,13},{2,18},{... | collective-permute-start | bytes 1119752 | tf_op jit(solution)/shard_map/ppermute | solution.py:522
  145.3 10.7 %collective-permute-start.13 = (bf16[2,2,2,328,128]{4,3,2,1,0:T(8,128)(2,1)S(1)}, bf16[2,2,2,328,128]{4,3,2,1,0:T(8,128)(2,1)S(1)}, u32[]{:S(2)}, u32[]{:S(2)}) collective-permute-start(bf16[2,2,2,328,128]{4,3,2,1,0:T(8,128)(2,1)S(1)} %get-tuple-element.103), channel_id=1, source_target_pairs={{2,3},{3,2},{6,7},{7,6},{10,11},{11,10},{14,15},{15,14},{16,17},{1... | collective-permute-start | bytes 2015240 | tf_op jit(solution)/shard_map/ppermute | solution.py:527
  146.2 9.9 %collective-permute-start.14 = (bf16[1,2,2,72,324]{4,3,2,1,0:T(8,128)(2,1)S(1)}, bf16[1,2,2,72,324]{4,3,2,1,0:T(8,128)(2,1)S(1)}, u32[]{:S(2)}, u32[]{:S(2)}) collective-permute-start(bf16[1,2,2,72,324]{4,3,2,1,0:T(8,128)(2,1)S(1)} %get-tuple-element.104), channel_id=1, source_target_pairs={{2,3},{3,2},{6,7},{7,6},{10,11},{11,10},{14,15},{15,14},{16,17},{1... | collective-permute-start | bytes 559880 | tf_op jit(solution)/shard_map/ppermute | solution.py:527
